TPU v7x, 256 devices: a whole 4x4x8 slice. The times are simulated.
256 devices in a mesh: dp: 16 (over y, x_hi, core), seq: 16 (over z, x_lo).
Axes of the slice: x: 4 (x_hi: 2, x_lo: 2; x = x_hi * 2 + x_lo), y: 4, z: 8, core: 2. Of those that a mesh axis runs over, the one named last changes fastest.
Arguments:
- frames: bfloat16 [16, 4096, 1536], P('dp', 'seq'), may hold values from -6 to 6
- cotangent: bfloat16 [16, 4096, 1536], P('dp', 'seq'), may hold values from -6 to 6
- lengths: int32 [16], P('dp'), may hold values from 128 to 4096, as said below
- w_qkv: bfloat16 [1536, 2304], replicated, as said below
- w_out: bfloat16 [768, 1536], replicated, may hold values from -0.21875 to 0.21875
Outputs:
- block_out: bfloat16 [16, 4096, 1536], P('dp', 'seq')
- frame_grad: bfloat16 [16, 4096, 1536], P('dp', 'seq')
- weight_grads: float32 [1536, 3072], P(('dp', 'seq'))
Inputs may be any that keep to these rules, and one draw needn't show every extreme that they name: `lengths`: some recording has exactly 4096 valid frames and some has exactly 128. `w_qkv`: entries of order 1536 ** -0.5 or a few times that.
All inputs are finite; a program needn't handle non-finite values.
Results may differ from a plain program's by a relative error of at most 0.015.
Values may be sent and summed in bfloat16 or wider, within the bound.
No kernel may reach another device: no remote copies, remote signals or barrier semaphores. Data moves between devices by JAX's collectives and lax.ppermute only.
A program may use at most 192 MiB of HBM per device.

v0:
```python
import jax
import jax.numpy as jnp
import numpy as np
from jax import lax
from jax.experimental import pallas as pl
from jax.experimental.pallas import tpu as pltpu
from jax.sharding import PartitionSpec as P

HEAD_DIM = 64
GROUP = 32
LEFT = 4
CONTEXT = LEFT * GROUP
PAIR = 2 * HEAD_DIM
F32 = jnp.float32
BF16 = jnp.bfloat16
NT = (((1,), (1,)), ((), ()))
NN = (((1,), (0,)), ((), ()))

Y, XH, CORES, Z, XL = 4, 2, 2, 8, 2
CHUNKS = Y * XH * XL

epsilon = 1e-05


def dot(a, b, dims=NN):
    return lax.dot_general(a, b, dims, preferred_element_type=F32)


def from_behind(value, axis, by):
    peers = lax.axis_size(axis)
    pairs = [(i, i + by) for i in range(peers) if 0 <= i + by < peers]
    return lax.ppermute(value, axis, pairs)


def flat(y, xh, core, z, xl):
    return ((y * XH + xh) * CORES + core) * (Z * XL) + z * XL + xl


def to_device(value, where):
    pairs = []
    for place in np.ndindex(Y, XH, CORES, Z, XL):
        pairs.append((flat(*place), flat(*where(*place))))
    return lax.ppermute(value, ("dp", "seq"), pairs)


def to_core(y, xh, core, z, xl):
    return y, xh, 1 - core, z, xl


def to_x_near(y, xh, core, z, xl):
    return y, xh, core, z, 1 - xl


def to_x_mirror(y, xh, core, z, xl):
    return y, 1 - xh, core, z, 1 - xl


def to_y_near(y, xh, core, z, xl):
    return y ^ 1, xh, core, z, xl


def to_y_mirror(y, xh, core, z, xl):
    return 3 - y, xh, core, z, xl


ROUTES = (
    (to_x_near, to_x_mirror, to_y_near, to_y_mirror),
    (to_x_mirror, to_x_near, to_y_mirror, to_y_near),
    (to_y_near, to_y_mirror, to_x_near, to_x_mirror),
    (to_y_mirror, to_y_near, to_x_mirror, to_x_near),
)


def halves(route, hi, lo):
    return (hi ^ lo, hi) if route % 2 == 0 else (hi, hi ^ lo)


def chunk_at(route, slot, y, xh, xl):
    bits = [(slot >> (3 - i)) & 1 for i in range(4)]
    x_bits, y_bits = (bits[:2], bits[2:]) if route < 2 else (bits[2:], bits[:2])
    found = []
    for (hi, lo), pair in (((y >> 1, y & 1), y_bits), ((xh, xl), x_bits)):
        first, second = halves(route, hi, lo)
        first, second = first ^ pair[0], second ^ pair[1]
        found.append((second, first ^ second) if route % 2 == 0 else (first, first ^ second))
    (yh, yl), (xh_to, xl_to) = found
    return ((yh * 2 + yl) * XH + xh_to) * XL + xl_to


def row_order(width):
    share = width // (CHUNKS * CORES * Z)
    order = np.arange(width // Y).reshape(XH, CORES, Z, XL, share).transpose(1, 0, 3, 2, 4).reshape(-1)
    return jnp.asarray(np.eye(width // Y, dtype=np.float32)[order], BF16)


def normalize(rows_in):
    average = jnp.mean(rows_in, axis=-1, keepdims=True)
    centered = rows_in - average
    variance = jnp.mean(centered * centered, axis=-1, keepdims=True)
    return centered * lax.rsqrt(variance + epsilon)


def project_kernel(frames_ref, weight_ref, normed_ref, projected_ref, tail_ref, held):
    step = pl.program_id(0)

    @pl.when(step == 0)
    def _():
        held[...] = normalize(frames_ref[...].astype(F32)).astype(BF16)
        normed_ref[...] = held[...]

    out = dot(held[...], weight_ref[...]).astype(BF16)
    projected_ref[...] = out
    tail_ref[...] = out[out.shape[0] - CONTEXT :]


def project(frames, weight):
    rows, width = frames.shape
    columns = weight.shape[1]
    block = HEAD_DIM * 6
    steps = columns // block
    skipped = steps // 3
    return pl.pallas_call(
        project_kernel,
        grid=(steps,),
        in_specs=[
            pl.BlockSpec((rows, width), lambda i: (0, 0)),
            pl.BlockSpec((width, block), lambda i: (0, i)),
        ],
        out_specs=[
            pl.BlockSpec((rows, width), lambda i: (0, 0)),
            pl.BlockSpec((rows, block), lambda i: (0, i)),
            pl.BlockSpec((CONTEXT, block), lambda i: (0, jnp.maximum(i - skipped, 0))),
        ],
        out_shape=[
            jax.ShapeDtypeStruct((rows, width), BF16),
            jax.ShapeDtypeStruct((rows, columns), BF16),
            jax.ShapeDtypeStruct((CONTEXT, columns // 3 * 2), BF16),
        ],
        scratch_shapes=[pltpu.VMEM((rows, width), BF16)],
        compiler_params=pltpu.CompilerParams(vmem_limit_bytes=40 * 2**20),
        cost_estimate=pl.CostEstimate(
            flops=2 * rows * width * columns, bytes_accessed=2 * width * columns, transcendentals=0
        ),
        name="project",
    )(frames, weight)


def turn_kernel(places, order_ref, normed_ref, cotangent_ref, keep_ref, send_ref):
    rows = order_ref.shape[0]
    half = rows // CORES
    for y in range(Y):
        here = slice(y * rows, (y + 1) * rows)
        turned = jnp.concatenate([normed_ref[:, here].T, cotangent_ref[:, here].T], axis=1)
        turned = dot(order_ref[...], turned).astype(BF16)
        there = slice(y * half, (y + 1) * half)

        @pl.when(places[0] == 0)
        def _():
            keep_ref[there, :] = turned[:half]
            send_ref[there, :] = turned[half:]

        @pl.when(places[0] == 1)
        def _():
            keep_ref[there, :] = turned[half:]
            send_ref[there, :] = turned[:half]


def turn(normed, cotangent, core):
    tokens, width = normed.shape
    order = row_order(width)
    whole = pl.BlockSpec((tokens, width), lambda i, s: (0, 0))
    result = pl.BlockSpec((width // CORES, 2 * tokens), lambda i, s: (0, 0))
    return pl.pallas_call(
        turn_kernel,
        grid_spec=pltpu.PrefetchScalarGridSpec(
            num_scalar_prefetch=1,
            grid=(1,),
            in_specs=[pl.BlockSpec(order.shape, lambda i, s: (0, 0)), whole, whole],
            out_specs=[result, result],
        ),
        out_shape=[jax.ShapeDtypeStruct((width // CORES, 2 * tokens), BF16)] * 2,
        compiler_params=pltpu.CompilerParams(vmem_limit_bytes=40 * 2**20),
        cost_estimate=pl.CostEstimate(
            flops=4 * tokens * width * width // Y, bytes_accessed=8 * tokens * width, transcendentals=0
        ),
        name="turn",
    )(jnp.reshape(core, (1,)), order, normed, cotangent)


def attend(begin, length, q, k2, v2, do):
    lane = lax.broadcasted_iota(jnp.int32, (CONTEXT, PAIR), 1)
    heads = (lane < HEAD_DIM, lane >= HEAD_DIM)
    keys = lax.broadcasted_iota(jnp.int32, (2 * CONTEXT, 2 * CONTEXT), 0)
    queries = lax.broadcasted_iota(jnp.int32, (2 * CONTEXT, 2 * CONTEXT), 1)
    key_block = keys // GROUP
    query_block = (queries % CONTEXT) // GROUP
    key_place = begin - CONTEXT + keys
    seen = (key_block >= query_block) & (key_block <= query_block + LEFT) & (key_place >= 0) & (key_place < length)
    zero = jnp.zeros((CONTEXT, PAIR), BF16)
    scale = HEAD_DIM ** (-0.5)
    row_valid = begin + lax.broadcasted_iota(jnp.int32, (CONTEXT, PAIR), 0) < length
    do = jnp.where(row_valid, do, zero)
    q = q * jnp.asarray(scale, BF16)
    q2 = jnp.concatenate([jnp.where(h, q, zero) for h in heads], axis=0)
    do2 = jnp.concatenate([jnp.where(h, do, zero) for h in heads], axis=0)
    scores = jnp.where(seen, dot(k2, q2, NT), -1e30)
    highest = jnp.max(scores, axis=0, keepdims=True)
    raised = jnp.exp(scores - highest)
    prob = raised * (1.0 / jnp.sum(raised, axis=0, keepdims=True))
    rounded = prob.astype(BF16)

    def unstack(both):
        return jnp.concatenate([both[:HEAD_DIM, :CONTEXT], both[HEAD_DIM:, CONTEXT:]], axis=0)

    col_valid = begin + lax.broadcasted_iota(jnp.int32, (PAIR, CONTEXT), 1) < length
    mixed = jnp.where(col_valid, unstack(dot(v2.T, rounded)), 0.0).T.astype(BF16)
    dprob = dot(v2, do2, NT)
    inner = jnp.sum(prob * dprob, axis=0, keepdims=True)
    dscores = (prob * (dprob - inner)).astype(BF16)
    dq = (unstack(dot(k2.T, dscores)) * scale).T.astype(BF16)
    return mixed, dq, dot(dscores, q2), dot(rounded, do2)


def late_kernel(places, q_ref, k_ref, v_ref, do_ref, out_ref, head_ref, tail_ref):
    begin = places[1] + CONTEXT
    out_ref[0], out_ref[1], dk, dv = attend(begin, places[0], q_ref[...], k_ref[...], v_ref[...], do_ref[...])
    for n, grad in enumerate((dk, dv)):
        head_ref[n] = grad[:CONTEXT]
        tail_ref[n] = grad[CONTEXT:]


def early_kernel(places, q_ref, k_ref, v_ref, kh_ref, vh_ref, do_ref, add_ref, out_ref, head_ref, halo_ref):
    k2 = jnp.concatenate([kh_ref[...], k_ref[...]], axis=0)
    v2 = jnp.concatenate([vh_ref[...], v_ref[...]], axis=0)
    out_ref[0], out_ref[1], dk, dv = attend(places[1], places[0], q_ref[...], k2, v2, do_ref[...])
    for n, grad in enumerate((dk, dv)):
        halo_ref[n] = grad[:CONTEXT].astype(BF16)
        head_ref[n] = (grad[CONTEXT:] + add_ref[n]).astype(BF16)


def attention(kernel, places, operands, in_specs, inner, types, name):
    both = pl.BlockSpec((2, CONTEXT, PAIR), lambda p, s: (0, 0, p))
    return pl.pallas_call(
        kernel,
        grid_spec=pltpu.PrefetchScalarGridSpec(
            num_scalar_prefetch=1,
            grid=(inner // PAIR,),
            in_specs=[both if spec is None else pl.BlockSpec((spec[0], PAIR), lambda p, s, spec=spec: (spec[1], spec[2] + p)) for spec in in_specs],
            out_specs=[both] * len(types),
        ),
        out_shape=[jax.ShapeDtypeStruct((2, CONTEXT, inner), dtype) for dtype in types],
        compiler_params=pltpu.CompilerParams(vmem_limit_bytes=40 * 2**20),
        cost_estimate=pl.CostEstimate(
            flops=28 * CONTEXT * 2 * CONTEXT * inner, bytes_accessed=16 * CONTEXT * inner, transcendentals=CONTEXT * 4 * inner
        ),
        name=name,
    )(places, *operands)


def weight_kernel(chunks, left_ref, left_other_ref, right_ref, right_other_ref, keep_ref, send_ref, held):
    total = dot(left_ref[...], right_ref[0]) + dot(left_other_ref[...], right_other_ref[0])
    held[...] = total.reshape(held.shape)
    half = CHUNKS // 2
    route = pl.program_id(0)
    for slot in range(CHUNKS):
        ref = keep_ref if slot < half else send_ref
        ref[0, slot % half] = held[chunks[route, slot]].astype(BF16)


def weight_sections(chunks, left, left_other, left_block, right, right_other):
    rows = left.shape[0]
    tokens = right.shape[1]
    columns = right.shape[2] // 2
    routes = len(ROUTES)
    lefts = pl.BlockSpec((rows, tokens), lambda r, s: (0, left_block(r)))
    rights = pl.BlockSpec((1, tokens, columns), lambda r, s: (r // 2, 0, r % 2))
    size = (CHUNKS // 2, rows // CHUNKS, columns)
    result = pl.BlockSpec((1, *size), lambda r, s: (r, 0, 0, 0))
    return pl.pallas_call(
        weight_kernel,
        grid_spec=pltpu.PrefetchScalarGridSpec(
            num_scalar_prefetch=1,
            grid=(routes,),
            in_specs=[lefts, lefts, rights, rights],
            out_specs=[result, result],
            scratch_shapes=[pltpu.VMEM((CHUNKS, rows // CHUNKS, columns), F32)],
        ),
        out_shape=[jax.ShapeDtypeStruct((routes, *size), BF16)] * 2,
        compiler_params=pltpu.CompilerParams(vmem_limit_bytes=40 * 2**20),
        cost_estimate=pl.CostEstimate(
            flops=4 * rows * tokens * columns * routes,
            bytes_accessed=4 * rows * (tokens + columns * routes),
            transcendentals=0,
        ),
        name="weight_sections",
    )(chunks, left, left_other, right, right_other)


def plus(a, b):
    return (a.astype(F32) + b.astype(F32)).astype(BF16)


def pieces_kernel(*refs):
    ins, out_ref, held = refs[:-2], refs[-2], refs[-1]
    share = out_ref.shape[1] // held.shape[1]
    for n, ref in enumerate(ins):
        block = ref[...].astype(F32)
        width = block.shape[1] // PAIR // 2
        bases = (((n + 2) % 4) * width + (0 if n > 1 else 4 * width), (2 + n) * width)
        for wave, base in enumerate(bases):
            for t in range(width):
                column = (wave * width + t) * PAIR
                for z in range(Z):
                    held[z, base + t] = block[z * share : (z + 1) * share, column : column + PAIR]
    for z in range(Z):
        for t in range(held.shape[1]):
            out_ref[z, t * share : (t + 1) * share, :] = held[z, t].astype(BF16)


def total_kernel(in_ref, out_ref):
    total = in_ref[0].astype(F32)
    for z in range(1, Z):
        total += in_ref[z].astype(F32)
    share = out_ref.shape[0]
    for t in range(out_ref.shape[1] // PAIR):
        out_ref[:, t * PAIR : (t + 1) * PAIR] = total[t * share : (t + 1) * share]


def on_device(frames, cotangent, lengths, w_qkv, w_out):
    frame_rows = frames[0]
    grad_rows = cotangent[0]
    row_count, width = frame_rows.shape
    inner = w_out.shape[0]
    pairs = inner // PAIR
    seq_index = lax.axis_index("seq")
    dp_index = lax.axis_index("dp")
    xl = seq_index % XL
    core, xh, y = dp_index % CORES, dp_index // CORES % XH, dp_index // (CORES * XH)
    places = jnp.stack([lengths[0], seq_index * row_count])
    routes = range(len(ROUTES))
    chunks = jnp.stack([jnp.stack([chunk_at(r, slot, y, xh, xl) for slot in range(CHUNKS)]) for r in routes])

    normed, projected, tail = project(frame_rows, w_qkv)
    received = from_behind(tail, "seq", 1)
    attended_grad = dot(grad_rows, w_out, NT).astype(BF16)
    late, late_head, late_tail = attention(
        late_kernel,
        places,
        (projected, projected, projected, attended_grad),
        ((CONTEXT, 1, 0), (2 * CONTEXT, 0, pairs), (2 * CONTEXT, 0, 2 * pairs), (CONTEXT, 1, 0)),
        inner,
        (BF16, F32, F32),
        "attention_late",
    )
    left, left_out = turn(normed, grad_rows, core)
    left_other = to_device(left_out, to_core)
    early, kv_head, halo = attention(
        early_kernel,
        places,
        (projected, projected, projected, received, received, attended_grad, late_head),
        ((CONTEXT, 0, 0), (CONTEXT, 0, pairs), (CONTEXT, 0, 2 * pairs), (CONTEXT, 0, 0), (CONTEXT, 0, pairs), (CONTEXT, 0, 0), None),
        inner,
        (BF16, BF16, BF16),
        "attention_early",
    )
    returned = from_behind(halo, "seq", -1)
    own = jnp.concatenate([early, late], axis=1)
    own_other = to_device(own, to_core)
    keep_a, send_a = weight_sections(chunks, left, left_other, lambda r: 1 - r // 2, own, own_other)
    got_a = [to_device(send_a[r], ROUTES[r][0]) for r in routes]

    kv_total = jnp.concatenate([kv_head, (late_tail + returned.astype(F32)).astype(BF16)], axis=1)
    kv_other = to_device(kv_total, to_core)
    keep_b, send_b = weight_sections(chunks, left, left_other, lambda r: 0, kv_total, kv_other)
    got_b = [to_device(send_b[r], ROUTES[r][0]) for r in routes]

    attended, send_a = lax.optimization_barrier((own[0], send_a))
    block_out = dot(attended, w_out).astype(BF16)
    projected_grad = jnp.concatenate([own[1], kv_total[0], kv_total[1]], axis=1)
    projected_grad, send_b = lax.optimization_barrier((projected_grad, send_b))
    normed_grad = dot(projected_grad, w_qkv, NT).astype(BF16)
    _, norm_back = jax.vjp(normalize, frame_rows.astype(F32))
    (frame_grad,) = norm_back(normed_grad.astype(F32))

    totals = [
        jnp.concatenate([plus(keep_a[r], got_a[r]), plus(keep_b[r], got_b[r])], axis=-1) for r in routes
    ]
    for step in range(1, 4):
        count = totals[0].shape[0] // 2
        sends = lax.optimization_barrier([t[count:] for t in totals])
        gots = lax.optimization_barrier([to_device(sends[r], ROUTES[r][step]) for r in routes])
        totals = [plus(totals[r][:count], gots[r]) for r in routes]
    share = width // (CHUNKS * CORES * Z)
    tiles = 4 * inner // PAIR
    shares = pl.pallas_call(
        pieces_kernel,
        out_shape=jax.ShapeDtypeStruct((Z, tiles * share, PAIR), BF16),
        scratch_shapes=[pltpu.VMEM((Z, tiles, share, PAIR), F32)],
        compiler_params=pltpu.CompilerParams(vmem_limit_bytes=40 * 2**20),
        name="pieces",
    )(*[t[0] for t in totals])
    rings = [[place * XL + x for place in range(Z)] for x in range(XL)]
    shares = lax.all_to_all(shares, "seq", 0, 0, axis_index_groups=rings, tiled=True)
    total = pl.pallas_call(
        total_kernel,
        out_shape=jax.ShapeDtypeStruct((share, 4 * inner), F32),
        name="total",
    )(shares)
    return block_out[None], frame_grad.astype(BF16)[None], total


def solution(mesh):
    placed = (P("dp", "seq", None), P("dp", "seq", None), P("dp"), P(), P())
    return jax.shard_map(
        on_device,
        mesh=mesh,
        in_specs=placed,
        out_specs=(P("dp", "seq", None), P("dp", "seq", None), P(("dp", "seq"), None)),
        check_vma=False,
    )
```

profile of v0, /device:TPU:8, one launch (start us, length us, event | category | flops | bytes accessed | tf_op | source)
XLA Modules:
  0.0 137.4 jit_solution(8739153062304158897)
XLA Ops:
  0.7 3.1 %copy-done.1 = bf16[1536,2304]{1,0:T(8,128)(2,1)S(1)} copy-done((bf16[1536,2304]{1,0:T(8,128)(2,1)S(1)}, bf16[1536,2304]{1,0:T(8,128)(2,1)}, u32[]{:S(2)}) %copy-start.1) | copy-done | bytes 7077912
  3.8 1.1 copy-done.2
  4.9 5.5 %project.1 = (bf16[256,1536]{1,0:T(8,128)(2,1)S(1)}, bf16[256,2304]{1,0:T(8,128)(2,1)S(1)}, bf16[128,1536]{1,0:T(8,128)(2,1)}) custom-call(bf16[256,1536]{1,0:T(8,128)(2,1)S(1)} %bitcast.98, bf16[1536,2304]{1,0:T(8,128)(2,1)S(1)} %copy-done.1), custom_call_target="tpu_custom_call" | custom-call | flops 1811939328 | bytes 7077888 | tf_op jit(solution)/shard_map/project/pallas_call | solution.py:122
  10.4 0.9 copy-done.5
  11.3 4.2 %collective-permute-start = (bf16[128,1536]{1,0:T(8,128)(2,1)}, bf16[128,1536]{1,0:T(8,128)(2,1)}, u32[]{:S(2)}, u32[]{:S(2)}) collective-permute-start(bf16[128,1536]{1,0:T(8,128)(2,1)} %get-tuple-element.45), channel_id=1, source_target_pairs={{0,1},{1,2},{2,3},{3,4},{4,5},{5,6},{6,7},{7,8},{8,9},{9,10},{10,1... | collective-permute-start | bytes 1179656 | tf_op jit(solution)/shard_map/ppermute | solution.py:32
  15.5 1.1 copy-done.4
  16.6 1.1 copy-done.6
  17.8 1.0 copy-done.7
  18.7 2.8 %turn.1 = (bf16[768,512]{1,0:T(8,128)(2,1)S(1)}, bf16[768,512]{1,0:T(8,128)(2,1)}) custom-call(s32[1]{0:T(128)} %bitcast.24.places, bf16[384,384]{1,0:T(8,128)(2,1)S(1)} %copy-done.7, bf16[256,1536]{1,0:T(8,128)(2,1)S(1)} %copy-done.6, bf16[256,1536]{1,0:T(8,128)(2,1)S(1)} %bitcast.99), custom_call_target="tpu_custom_call" | custom-call | flops 603979776 | bytes 3145728 | tf_op jit(solution)/shard_map/turn/pallas_call | solution.py:173
  21.6 0.9 copy-done.8
  22.5 0.1 stack.151
  22.7 0.1 stack.72
  23.5 1.9 %convolution_convert_fusion.2.do_ref = bf16[256,768]{1,0:T(8,128)(2,1)S(1)} fusion(bf16[768,1536]{1,0:T(8,128)(2,1)S(1)} %copy-done, bf16[1,256,1536]{2,1,0:T(8,128)(2,1)} %param.7), kind=kOutput, calls=%fused_computation.13 | convolution fusion | flops 604176384 | bytes 3538944 | tf_op jit(solution)/shard_map/dot_general | solution.py:26
  25.5 6.2 %attention_late.1 = (bf16[2,128,768]{2,1,0:T(8,128)(2,1)S(1)}, f32[2,128,768]{2,1,0:T(8,128)S(1)}, f32[2,128,768]{2,1,0:T(8,128)S(1)}) custom-call(s32[2]{0:T(128)S(1)} %pad_add_fusion.1.places, bf16[256,2304]{1,0:T(8,128)(2,1)S(1)} %get-tuple-element.44.q_ref.k_ref.v_ref, bf16[256,2304]{1,0:T(8,128)(2,1)S(1)} %get-tuple-element.44.q_ref.k_ref.v_ref, ...), custom_call_target="tpu_custom_call" | custom-call | flops 704643072 | bytes 1572864 | tf_op jit(solution)/shard_map/attention_late/pallas_call | solution.py:243
  31.8 0.2 convert_reduce_fusion
  32.0 7.1 %attention_early.1 = (bf16[2,128,768]{2,1,0:T(8,128)(2,1)S(1)}, bf16[2,128,768]{2,1,0:T(8,128)(2,1)S(1)}, bf16[2,128,768]{2,1,0:T(8,128)(2,1)S(1)}) custom-call(s32[2]{0:T(128)S(1)} %pad_add_fusion.1.places, bf16[256,2304]{1,0:T(8,128)(2,1)S(1)} %get-tuple-element.44.q_ref.k_ref.v_ref, bf16[256,2304]{1,0:T(8,128)(2,1)S(1)} %get-tuple-element.44.q_ref.k_ref.v_ref, ...), custom_call_target="tpu_custom_call" | custom-call | flops 704643072 | bytes 1572864 | tf_op jit(solution)/shard_map/attention_early/pallas_call | solution.py:243
  39.1 1.3 collective-permute-start.3
  40.5 0.6 collective-permute-start.2
  41.2 11.4 %collective-permute-done.3 = bf16[2,128,768]{2,1,0:T(8,128)(2,1)S(1)} collective-permute-done((bf16[2,128,768]{2,1,0:T(8,128)(2,1)S(1)}, bf16[2,128,768]{2,1,0:T(8,128)(2,1)S(1)}, u32[]{:S(2)}, u32[]{:S(2)}) %collective-permute-start.3) | collective-permute-done | bytes 393248 | tf_op jit(solution)/shard_map/ppermute | solution.py:32
  53.0 1.0 copy-done.9
  54.0 4.6 %weight_sections.2 = (bf16[4,8,48,384]{3,2,1,0:T(8,128)(2,1)S(1)}, bf16[4,8,48,384]{3,2,1,0:T(8,128)(2,1)S(1)}) custom-call(s32[4,16]{1,0:T(4,128)S(1)} %pad_add_fusion.chunks, bf16[768,512]{1,0:T(8,128)(2,1)S(1)} %copy-done.9, bf16[768,512]{1,0:T(8,128)(2,1)} %collective-permute-done.1.left_other_ref, ...), custom_call_target="tpu_custom_call" | custom-call | flops 1207959552 | bytes 5505024 | tf_op jit(solution)/shard_map/weight_sections/pallas_call | solution.py:279
  58.7 0.1 slice_bitcast_fusion.3
  58.8 1.7 %collective-permute-start.11 = (bf16[8,48,384]{2,1,0:T(8,128)(2,1)S(1)}, bf16[8,48,384]{2,1,0:T(8,128)(2,1)S(1)}, u32[]{:S(2)}, u32[]{:S(2)}) collective-permute-start(bf16[8,48,384]{2,1,0:T(8,128)(2,1)S(1)} %get-tuple-element.101), channel_id=1, source_target_pairs={{0,192},{1,193},{2,194},{3,195},{4,196},{5,197},{6,198},{7,199},{8... | collective-permute-start | bytes 884744 | tf_op jit(solution)/shard_map/ppermute | solution.py:43
  60.4 1.9 %collective-permute-start.9 = (bf16[8,48,384]{2,1,0:T(8,128)(2,1)S(1)}, bf16[8,48,384]{2,1,0:T(8,128)(2,1)S(1)}, u32[]{:S(2)}, u32[]{:S(2)}) collective-permute-start(bf16[8,48,384]{2,1,0:T(8,128)(2,1)S(1)} %get-tuple-element.102), channel_id=1, source_target_pairs={{0,64},{1,65},{2,66},{3,67},{4,68},{5,69},{6,70},{7,71},{8,72},{9,... | collective-permute-start | bytes 884744 | tf_op jit(solution)/shard_map/ppermute | solution.py:43
  62.3 3.6 %collective-permute-start.7 = (bf16[8,48,384]{2,1,0:T(8,128)(2,1)S(1)}, bf16[8,48,384]{2,1,0:T(8,128)(2,1)S(1)}, u32[]{:S(2)}, u32[]{:S(2)}) collective-permute-start(bf16[8,48,384]{2,1,0:T(8,128)(2,1)S(1)} %get-tuple-element.103), channel_id=1, source_target_pairs={{0,33},{1,32},{2,35},{3,34},{4,37},{5,36},{6,39},{7,38},{8,41},{9,... | collective-permute-start | bytes 884744 | tf_op jit(solution)/shard_map/ppermute | solution.py:43
  65.9 4.4 %weight_sections.3 = (bf16[4,8,48,384]{3,2,1,0:T(8,128)(2,1)S(1)}, bf16[4,8,48,384]{3,2,1,0:T(8,128)(2,1)S(1)}) custom-call(s32[4,16]{1,0:T(4,128)S(1)} %pad_add_fusion.chunks, bf16[768,512]{1,0:T(8,128)(2,1)S(1)} %copy-done.9, bf16[768,512]{1,0:T(8,128)(2,1)} %collective-permute-done.1.left_other_ref, bf16[2,256,768]{2,1,0:T(8,128)(2,1)S(1)} %pad_maximum_fusion.1.right_ref, ...), custom_call_target="tpu_custom_call" | custom-call | flops 1207959552 | bytes 5505024 | tf_op jit(solution)/shard_map/weight_sections/pallas_call | solution.py:279
  70.4 0.1 slice_bitcast_fusion.2
  70.6 1.2 collective-permute-start.10
  71.8 1.8 %collective-permute-start.8 = (bf16[8,48,384]{2,1,0:T(8,128)(2,1)S(1)}, bf16[8,48,384]{2,1,0:T(8,128)(2,1)S(1)}, u32[]{:S(2)}, u32[]{:S(2)}) collective-permute-start(bf16[8,48,384]{2,1,0:T(8,128)(2,1)S(1)} %get-tuple-element.95), channel_id=1, source_target_pairs={{0,33},{1,32},{2,35},{3,34},{4,37},{5,36},{6,39},{7,38},{8,41},{9,... | collective-permute-start | bytes 884744 | tf_op jit(solution)/shard_map/ppermute | solution.py:43
  73.6 0.3 collective-permute-start.6
  73.9 1.7 %fusion.1 = bf16[1,256,1536]{2,1,0:T(8,128)(2,1)} fusion(bf16[256,768]{1,0:T(8,128)(2,1)S(1)} %get-tuple-element.53, bf16[768,1536]{1,0:T(8,128)(2,1)S(1)} %copy-done), kind=kOutput, calls=%fused_computation.3 | convolution fusion | flops 604372992 | bytes 3538944 | tf_op jit(solution)/shard_map/dot_general | solution.py:26
  75.6 0.3 fusion.9
  75.9 3.3 %collective-permute-done.12 = bf16[8,48,384]{2,1,0:T(8,128)(2,1)S(1)} collective-permute-done((bf16[8,48,384]{2,1,0:T(8,128)(2,1)S(1)}, bf16[8,48,384]{2,1,0:T(8,128)(2,1)S(1)}, u32[]{:S(2)}, u32[]{:S(2)}) %collective-permute-start.12) | collective-permute-done | bytes 294944 | tf_op jit(solution)/shard_map/ppermute | solution.py:43
  79.2 0.1 collective-permute-done.10
  79.3 1.7 %collective-permute-done.8 = bf16[8,48,384]{2,1,0:T(8,128)(2,1)S(1)} collective-permute-done((bf16[8,48,384]{2,1,0:T(8,128)(2,1)S(1)}, bf16[8,48,384]{2,1,0:T(8,128)(2,1)S(1)}, u32[]{:S(2)}, u32[]{:S(2)}) %collective-permute-start.8) | collective-permute-done | bytes 294944 | tf_op jit(solution)/shard_map/ppermute | solution.py:43
  81.0 0.7 collective-permute-done.6
  81.7 0.3 fusion.8
  82.2 2.3 %collective-permute-start.13 = (bf16[4,48,768]{2,1,0:T(8,128)(2,1)S(1)}, bf16[4,48,768]{2,1,0:T(8,128)(2,1)S(1)}, u32[]{:S(2)}, u32[]{:S(2)}) collective-permute-start(bf16[4,48,768]{2,1,0:T(8,128)(2,1)S(1)} %pad_maximum_fusion.5), channel_id=1, source_target_pairs={{0,33},{1,32},{2,35},{3,34},{4,37},{5,36},{6,39},{7,38},{8,41},{9,... | collective-permute-start | bytes 884744 | tf_op jit(solution)/shard_map/ppermute | solution.py:43
  84.5 1.5 %collective-permute-start.15 = (bf16[4,48,768]{2,1,0:T(8,128)(2,1)S(1)}, bf16[4,48,768]{2,1,0:T(8,128)(2,1)S(1)}, u32[]{:S(2)}, u32[]{:S(2)}) collective-permute-start(bf16[4,48,768]{2,1,0:T(8,128)(2,1)S(1)} %fusion.21), channel_id=1, source_target_pairs={{0,192},{1,193},{2,194},{3,195},{4,196},{5,197},{6,198},{7,199},{8... | collective-permute-start | bytes 884744 | tf_op jit(solution)/shard_map/ppermute | solution.py:43
  86.1 1.3 collective-permute-start.16
  87.3 2.1 %fusion.5 = (f32[256]{0:T(256)S(1)}, f32[256]{0:T(256)S(1)}, f32[256,1536]{1,0:T(8,128)S(1)}) fusion(f32[256]{0:T(256)S(1)} %broadcast_multiply_fusion, bf16[1,256,1536]{2,1,0:T(8,128)(2,1)S(1)} %copy-done.3, bf16[256,2304]{1,0:T(8,128)(2,1)S(1)} %pad_maximum_fusion, bf16[1536,2304]{1,0:T(8,128)(2,1)S(1)} %bitcast.97), kind=kOutput, calls=%fused_computation.10 | convolution fusion | flops 1815084544 | bytes 10619904 | tf_op jit(solution)/shard_map/dot_general | solution.py:26
  89.5 1.2 collective-permute-done.13
  90.7 0.6 collective-permute-done.14
  91.3 1.7 %collective-permute-done.16 = bf16[4,48,768]{2,1,0:T(8,128)(2,1)S(1)} collective-permute-done((bf16[4,48,768]{2,1,0:T(8,128)(2,1)S(1)}, bf16[4,48,768]{2,1,0:T(8,128)(2,1)S(1)}, u32[]{:S(2)}, u32[]{:S(2)}) %collective-permute-start.16) | collective-permute-done | bytes 294944 | tf_op jit(solution)/shard_map/ppermute | solution.py:43
  93.0 0.1 add_convert_fusion.4
  93.1 0.1 add_convert_fusion.2
  93.3 1.4 %collective-permute-start.17 = (bf16[2,48,768]{2,1,0:T(8,128)(2,1)S(1)}, bf16[2,48,768]{2,1,0:T(8,128)(2,1)S(1)}, u32[]{:S(2)}, u32[]{:S(2)}) collective-permute-start(bf16[2,48,768]{2,1,0:T(8,128)(2,1)S(1)} %slice.191), channel_id=1, source_target_pairs={{0,64},{1,65},{2,66},{3,67},{4,68},{5,69},{6,70},{7,71},{8,72},{9,... | collective-permute-start | bytes 442376 | tf_op jit(solution)/shard_map/ppermute | solution.py:43
  94.7 0.4 collective-permute-start.18
  95.1 1.9 %collective-permute-start.19 = (bf16[2,48,768]{2,1,0:T(8,128)(2,1)S(1)}, bf16[2,48,768]{2,1,0:T(8,128)(2,1)S(1)}, u32[]{:S(2)}, u32[]{:S(2)}) collective-permute-start(bf16[2,48,768]{2,1,0:T(8,128)(2,1)S(1)} %slice.193), channel_id=1, source_target_pairs={{0,1},{1,0},{2,3},{3,2},{4,5},{5,4},{6,7},{7,6},{8,9},{9,8},{10,11... | collective-permute-start | bytes 442376 | tf_op jit(solution)/shard_map/ppermute | solution.py:43
  97.1 2.0 %collective-permute-start.20 = (bf16[2,48,768]{2,1,0:T(8,128)(2,1)S(1)}, bf16[2,48,768]{2,1,0:T(8,128)(2,1)S(1)}, u32[]{:S(2)}, u32[]{:S(2)}) collective-permute-start(bf16[2,48,768]{2,1,0:T(8,128)(2,1)S(1)} %slice.194), channel_id=1, source_target_pairs={{0,33},{1,32},{2,35},{3,34},{4,37},{5,36},{6,39},{7,38},{8,41},{9,... | collective-permute-start | bytes 442376 | tf_op jit(solution)/shard_map/ppermute | solution.py:43
  99.1 1.6 %fusion.30 = (f32[256]{0:T(256)S(1)}, f32[256,1536]{1,0:T(8,128)}) fusion(f32[256]{0:T(256)S(1)} %get-tuple-element.110, f32[256]{0:T(256)S(1)} %broadcast_multiply_fusion, bf16[1,256,1536]{2,1,0:T(8,128)(2,1)S(1)} %copy-done.3, f32[256,1536]{1,0:T(8,128)S(1)} %get-tuple-element.111, f32[256]{0:T(256)S(1)} %get-tuple-element.109), kind=kLoop, calls=%fused_computation.94 | loop fusion | flops 2752256 | bytes 3936256 | tf_op jit(solution)/shard_map/transpose(jvp())/reduce_sum | solution.py:98
  100.7 2.7 %collective-permute-done.20 = bf16[2,48,768]{2,1,0:T(8,128)(2,1)S(1)} collective-permute-done((bf16[2,48,768]{2,1,0:T(8,128)(2,1)S(1)}, bf16[2,48,768]{2,1,0:T(8,128)(2,1)S(1)}, u32[]{:S(2)}, u32[]{:S(2)}) %collective-permute-start.20) | collective-permute-done | bytes 147488 | tf_op jit(solution)/shard_map/ppermute | solution.py:43
  103.7 1.4 %collective-permute-start.21 = (bf16[1,48,768]{2,1,0:T(8,128)(2,1)S(1)}, bf16[1,48,768]{2,1,0:T(8,128)(2,1)S(1)}, u32[]{:S(2)}, u32[]{:S(2)}) collective-permute-start(bf16[1,48,768]{2,1,0:T(8,128)(2,1)S(1)} %slice.196), channel_id=1, source_target_pairs={{0,192},{1,193},{2,194},{3,195},{4,196},{5,197},{6,198},{7,199},{8... | collective-permute-start | bytes 221192 | tf_op jit(solution)/shard_map/ppermute | solution.py:43
  105.0 3.4 %collective-permute-start.22 = (bf16[1,48,768]{2,1,0:T(8,128)(2,1)S(1)}, bf16[1,48,768]{2,1,0:T(8,128)(2,1)S(1)}, u32[]{:S(2)}, u32[]{:S(2)}) collective-permute-start(bf16[1,48,768]{2,1,0:T(8,128)(2,1)S(1)} %slice.198), channel_id=1, source_target_pairs={{0,64},{1,65},{2,66},{3,67},{4,68},{5,69},{6,70},{7,71},{8,72},{9,... | collective-permute-start | bytes 221192 | tf_op jit(solution)/shard_map/ppermute | solution.py:43
  108.5 2.0 %collective-permute-start.23 = (bf16[1,48,768]{2,1,0:T(8,128)(2,1)S(1)}, bf16[1,48,768]{2,1,0:T(8,128)(2,1)S(1)}, u32[]{:S(2)}, u32[]{:S(2)}) collective-permute-start(bf16[1,48,768]{2,1,0:T(8,128)(2,1)S(1)} %slice.200), channel_id=1, source_target_pairs={{0,33},{1,32},{2,35},{3,34},{4,37},{5,36},{6,39},{7,38},{8,41},{9,... | collective-permute-start | bytes 221192 | tf_op jit(solution)/shard_map/ppermute | solution.py:43
  110.5 0.3 collective-permute-done.22
  110.8 3.2 %collective-permute-done.23 = bf16[1,48,768]{2,1,0:T(8,128)(2,1)S(1)} collective-permute-done((bf16[1,48,768]{2,1,0:T(8,128)(2,1)S(1)}, bf16[1,48,768]{2,1,0:T(8,128)(2,1)S(1)}, u32[]{:S(2)}, u32[]{:S(2)}) %collective-permute-start.23) | collective-permute-done | bytes 73760 | tf_op jit(solution)/shard_map/ppermute | solution.py:43
  114.0 0.8 collective-permute-done.24
  114.9 0.9 pieces.1
  115.8 8.3 %all-to-all-start = ((bf16[8,144,128]{2,1,0:T(8,128)(2,1)}), bf16[8,144,128]{2,1,0:T(8,128)(2,1)S(1)}, u32[]{:S(2)}, u32[]{:S(2)}) async-start(bf16[8,144,128]{2,1,0:T(8,128)(2,1)} %pieces.1), calls=%async_computation | async-start | bytes 589824 | tf_op jit(solution)/shard_map/all_to_all | solution.py:403
  124.2 2.4 %fusion.7 = bf16[1,256,1536]{2,1,0:T(8,128)(2,1)} fusion(f32[256,1536]{1,0:T(8,128)} %get-tuple-element.88, f32[256]{0:T(256)S(1)} %negate_multiply_fusion), kind=kLoop, calls=%fused_computation.20 | loop fusion | flops 786432 | bytes 2360320 | tf_op jit(solution)/shard_map/broadcast_in_dim | solution.py:409
  126.6 8.4 %all-to-all-done.in_ref = bf16[8,144,128]{2,1,0:T(8,128)(2,1)S(1)} async-done(((bf16[8,144,128]{2,1,0:T(8,128)(2,1)}), bf16[8,144,128]{2,1,0:T(8,128)(2,1)S(1)}, u32[]{:S(2)}, u32[]{:S(2)}) %all-to-all-start) | async-done | bytes 294944 | tf_op jit(solution)/shard_map/all_to_all | solution.py:403
  135.0 0.7 copy-done.10
  135.7 1.6 %total.1 = f32[6,3072]{1,0:T(8,128)} custom-call(bf16[8,144,128]{2,1,0:T(8,128)(2,1)} %copy-done.10), custom_call_target="tpu_custom_call" | custom-call | tf_op jit(solution)/shard_map/total/pallas_call | solution.py:404
  (71 shorter events, 1.4 us)
Async XLA Ops:
  0.6 22.9 %copy-start = (bf16[768,1536]{1,0:T(8,128)(2,1)S(1)}, bf16[768,1536]{1,0:T(8,128)(2,1)}, u32[]{:S(2)}) copy-start(bf16[768,1536]{1,0:T(8,128)(2,1)} %param.10) | copy-start | bytes 7077892
  0.6 3.2 %copy-start.1 = (bf16[1536,2304]{1,0:T(8,128)(2,1)S(1)}, bf16[1536,2304]{1,0:T(8,128)(2,1)}, u32[]{:S(2)}) copy-start(bf16[1536,2304]{1,0:T(8,128)(2,1)} %weight_ref.1) | copy-start | bytes 21233668
  3.8 1.1 copy-start.2
  10.4 0.9 copy-start.5
  11.3 20.7 %collective-permute-start = (bf16[128,1536]{1,0:T(8,128)(2,1)}, bf16[128,1536]{1,0:T(8,128)(2,1)}, u32[]{:S(2)}, u32[]{:S(2)}) collective-permute-start(bf16[128,1536]{1,0:T(8,128)(2,1)} %get-tuple-element.45), channel_id=1, source_target_pairs={{0,1},{1,2},{2,3},{3,4},{4,5},{5,6},{6,7},{7,8},{8,9},{9,10},{10,1... | collective-permute-start | bytes 1179656 | tf_op jit(solution)/shard_map/ppermute | solution.py:32
  15.5 1.1 copy-start.4
  16.6 1.1 copy-start.6
  17.8 1.0 copy-start.7
  21.6 0.9 copy-start.8
  22.4 30.5 %collective-permute-start.1 = (bf16[768,512]{1,0:T(8,128)(2,1)}, bf16[768,512]{1,0:T(8,128)(2,1)}, u32[]{:S(2)}, u32[]{:S(2)}) collective-permute-start(bf16[768,512]{1,0:T(8,128)(2,1)} %get-tuple-element.51), channel_id=1, source_target_pairs={{0,16},{1,17},{2,18},{3,19},{4,20},{5,21},{6,22},{7,23},{8,24},{9,... | collective-permute-start | bytes 2359304 | tf_op jit(solution)/shard_map/ppermute | solution.py:43
  25.5 6.3 %copy-start.3 = (bf16[1,256,1536]{2,1,0:T(8,128)(2,1)S(1)}, bf16[1,256,1536]{2,1,0:T(8,128)(2,1)}, u32[]{:S(2)}) copy-start(bf16[1,256,1536]{2,1,0:T(8,128)(2,1)} %param.6) | copy-start | bytes 2359300
  39.1 13.4 %collective-permute-start.3 = (bf16[2,128,768]{2,1,0:T(8,128)(2,1)S(1)}, bf16[2,128,768]{2,1,0:T(8,128)(2,1)S(1)}, u32[]{:S(2)}, u32[]{:S(2)}) collective-permute-start(bf16[2,128,768]{2,1,0:T(8,128)(2,1)S(1)} %get-tuple-element.56), channel_id=1, source_target_pairs={{1,0},{2,1},{3,2},{4,3},{5,4},{6,5},{7,6},{8,7},{9,8},{10,9},{11,1... | collective-permute-start | bytes 1179656 | tf_op jit(solution)/shard_map/ppermute | solution.py:32
  40.5 12.5 %collective-permute-start.2 = (bf16[2,256,768]{2,1,0:T(8,128)(2,1)S(1)}, bf16[2,256,768]{2,1,0:T(8,128)(2,1)S(1)}, u32[]{:S(2)}, u32[]{:S(2)}) collective-permute-start(bf16[2,256,768]{2,1,0:T(8,128)(2,1)S(1)} %constant_dynamic-update-slice_fusion.right_ref), channel_id=1, source_target_pairs={{0,16},{1,17},{2,18},{3,19},{4,20},{5,21},{6,22},{7,23},{8,24},{9,... | collective-permute-start | bytes 2359304 | tf_op jit(solution)/shard_map/ppermute | solution.py:43
  52.7 13.2 %collective-permute-start.4 = (bf16[2,256,768]{2,1,0:T(8,128)(2,1)S(1)}, bf16[2,256,768]{2,1,0:T(8,128)(2,1)S(1)}, u32[]{:S(2)}, u32[]{:S(2)}) collective-permute-start(bf16[2,256,768]{2,1,0:T(8,128)(2,1)S(1)} %pad_maximum_fusion.1.right_ref), channel_id=1, source_target_pairs={{0,16},{1,17},{2,18},{3,19},{4,20},{5,21},{6,22},{7,23},{8,24},{9,... | collective-permute-start | bytes 2359304 | tf_op jit(solution)/shard_map/ppermute | solution.py:43
  52.9 1.1 copy-start.9
  58.8 11.9 %collective-permute-start.11 = (bf16[8,48,384]{2,1,0:T(8,128)(2,1)S(1)}, bf16[8,48,384]{2,1,0:T(8,128)(2,1)S(1)}, u32[]{:S(2)}, u32[]{:S(2)}) collective-permute-start(bf16[8,48,384]{2,1,0:T(8,128)(2,1)S(1)} %get-tuple-element.101), channel_id=1, source_target_pairs={{0,192},{1,193},{2,194},{3,195},{4,196},{5,197},{6,198},{7,199},{8... | collective-permute-start | bytes 884744 | tf_op jit(solution)/shard_map/ppermute | solution.py:43
  60.4 11.4 %collective-permute-start.9 = (bf16[8,48,384]{2,1,0:T(8,128)(2,1)S(1)}, bf16[8,48,384]{2,1,0:T(8,128)(2,1)S(1)}, u32[]{:S(2)}, u32[]{:S(2)}) collective-permute-start(bf16[8,48,384]{2,1,0:T(8,128)(2,1)S(1)} %get-tuple-element.102), channel_id=1, source_target_pairs={{0,64},{1,65},{2,66},{3,67},{4,68},{5,69},{6,70},{7,71},{8,72},{9,... | collective-permute-start | bytes 884744 | tf_op jit(solution)/shard_map/ppermute | solution.py:43
  62.3 11.3 %collective-permute-start.7 = (bf16[8,48,384]{2,1,0:T(8,128)(2,1)S(1)}, bf16[8,48,384]{2,1,0:T(8,128)(2,1)S(1)}, u32[]{:S(2)}, u32[]{:S(2)}) collective-permute-start(bf16[8,48,384]{2,1,0:T(8,128)(2,1)S(1)} %get-tuple-element.103), channel_id=1, source_target_pairs={{0,33},{1,32},{2,35},{3,34},{4,37},{5,36},{6,39},{7,38},{8,41},{9,... | collective-permute-start | bytes 884744 | tf_op jit(solution)/shard_map/ppermute | solution.py:43
  65.9 9.7 %collective-permute-start.5 = (bf16[8,48,384]{2,1,0:T(8,128)(2,1)S(1)}, bf16[8,48,384]{2,1,0:T(8,128)(2,1)S(1)}, u32[]{:S(2)}, u32[]{:S(2)}) collective-permute-start(bf16[8,48,384]{2,1,0:T(8,128)(2,1)S(1)} %get-tuple-element.104), channel_id=1, source_target_pairs={{0,1},{1,0},{2,3},{3,2},{4,5},{5,4},{6,7},{7,6},{8,9},{9,8},{10,11... | collective-permute-start | bytes 884744 | tf_op jit(solution)/shard_map/ppermute | solution.py:43
  70.5 8.7 %collective-permute-start.12 = (bf16[8,48,384]{2,1,0:T(8,128)(2,1)S(1)}, bf16[8,48,384]{2,1,0:T(8,128)(2,1)S(1)}, u32[]{:S(2)}, u32[]{:S(2)}) collective-permute-start(bf16[8,48,384]{2,1,0:T(8,128)(2,1)S(1)} %get-tuple-element.93), channel_id=1, source_target_pairs={{0,192},{1,193},{2,194},{3,195},{4,196},{5,197},{6,198},{7,199},{8... | collective-permute-start | bytes 884744 | tf_op jit(solution)/shard_map/ppermute | solution.py:43
  70.6 8.7 %collective-permute-start.10 = (bf16[8,48,384]{2,1,0:T(8,128)(2,1)S(1)}, bf16[8,48,384]{2,1,0:T(8,128)(2,1)S(1)}, u32[]{:S(2)}, u32[]{:S(2)}) collective-permute-start(bf16[8,48,384]{2,1,0:T(8,128)(2,1)S(1)} %get-tuple-element.94), channel_id=1, source_target_pairs={{0,64},{1,65},{2,66},{3,67},{4,68},{5,69},{6,70},{7,71},{8,72},{9,... | collective-permute-start | bytes 884744 | tf_op jit(solution)/shard_map/ppermute | solution.py:43
  71.8 9.2 %collective-permute-start.8 = (bf16[8,48,384]{2,1,0:T(8,128)(2,1)S(1)}, bf16[8,48,384]{2,1,0:T(8,128)(2,1)S(1)}, u32[]{:S(2)}, u32[]{:S(2)}) collective-permute-start(bf16[8,48,384]{2,1,0:T(8,128)(2,1)S(1)} %get-tuple-element.95), channel_id=1, source_target_pairs={{0,33},{1,32},{2,35},{3,34},{4,37},{5,36},{6,39},{7,38},{8,41},{9,... | collective-permute-start | bytes 884744 | tf_op jit(solution)/shard_map/ppermute | solution.py:43
  73.6 8.1 %collective-permute-start.6 = (bf16[8,48,384]{2,1,0:T(8,128)(2,1)S(1)}, bf16[8,48,384]{2,1,0:T(8,128)(2,1)S(1)}, u32[]{:S(2)}, u32[]{:S(2)}) collective-permute-start(bf16[8,48,384]{2,1,0:T(8,128)(2,1)S(1)} %get-tuple-element.96), channel_id=1, source_target_pairs={{0,1},{1,0},{2,3},{3,2},{4,5},{5,4},{6,7},{7,6},{8,9},{9,8},{10,11... | collective-permute-start | bytes 884744 | tf_op jit(solution)/shard_map/ppermute | solution.py:43
  73.9 13.4 %slice-start = ((s8[7077888]{0:T(1024)(128)(4,1)}), s8[4194304]{0:T(1024)(128)(4,1)S(1)}, s32[]{:S(2)}) async-start(s8[7077888]{0:T(1024)(128)(4,1)} %bitcast.96), calls=%async_computation.1 | async-start | bytes 8388608
  75.6 11.7 %slice-start.1 = ((s8[7077888]{0:T(1024)(128)(4,1)}), s8[2883584]{0:T(1024)(128)(4,1)S(1)}, s32[]{:S(2)}) async-start(s8[7077888]{0:T(1024)(128)(4,1)} %bitcast.96), calls=%async_computation.2 | async-start | bytes 5767168
  82.2 8.5 %collective-permute-start.13 = (bf16[4,48,768]{2,1,0:T(8,128)(2,1)S(1)}, bf16[4,48,768]{2,1,0:T(8,128)(2,1)S(1)}, u32[]{:S(2)}, u32[]{:S(2)}) collective-permute-start(bf16[4,48,768]{2,1,0:T(8,128)(2,1)S(1)} %pad_maximum_fusion.5), channel_id=1, source_target_pairs={{0,33},{1,32},{2,35},{3,34},{4,37},{5,36},{6,39},{7,38},{8,41},{9,... | collective-permute-start | bytes 884744 | tf_op jit(solution)/shard_map/ppermute | solution.py:43
  84.5 6.8 %collective-permute-start.14 = (bf16[4,48,768]{2,1,0:T(8,128)(2,1)S(1)}, bf16[4,48,768]{2,1,0:T(8,128)(2,1)S(1)}, u32[]{:S(2)}, u32[]{:S(2)}) collective-permute-start(bf16[4,48,768]{2,1,0:T(8,128)(2,1)S(1)} %fusion.22), channel_id=1, source_target_pairs={{0,1},{1,0},{2,3},{3,2},{4,5},{5,4},{6,7},{7,6},{8,9},{9,8},{10,11... | collective-permute-start | bytes 884744 | tf_op jit(solution)/shard_map/ppermute | solution.py:43
  84.5 6.8 %collective-permute-start.15 = (bf16[4,48,768]{2,1,0:T(8,128)(2,1)S(1)}, bf16[4,48,768]{2,1,0:T(8,128)(2,1)S(1)}, u32[]{:S(2)}, u32[]{:S(2)}) collective-permute-start(bf16[4,48,768]{2,1,0:T(8,128)(2,1)S(1)} %fusion.21), channel_id=1, source_target_pairs={{0,192},{1,193},{2,194},{3,195},{4,196},{5,197},{6,198},{7,199},{8... | collective-permute-start | bytes 884744 | tf_op jit(solution)/shard_map/ppermute | solution.py:43
  86.1 6.9 %collective-permute-start.16 = (bf16[4,48,768]{2,1,0:T(8,128)(2,1)S(1)}, bf16[4,48,768]{2,1,0:T(8,128)(2,1)S(1)}, u32[]{:S(2)}, u32[]{:S(2)}) collective-permute-start(bf16[4,48,768]{2,1,0:T(8,128)(2,1)S(1)} %fusion.20), channel_id=1, source_target_pairs={{0,64},{1,65},{2,66},{3,67},{4,68},{5,69},{6,70},{7,71},{8,72},{9,... | collective-permute-start | bytes 884744 | tf_op jit(solution)/shard_map/ppermute | solution.py:43
  93.3 7.4 %collective-permute-start.17 = (bf16[2,48,768]{2,1,0:T(8,128)(2,1)S(1)}, bf16[2,48,768]{2,1,0:T(8,128)(2,1)S(1)}, u32[]{:S(2)}, u32[]{:S(2)}) collective-permute-start(bf16[2,48,768]{2,1,0:T(8,128)(2,1)S(1)} %slice.191), channel_id=1, source_target_pairs={{0,64},{1,65},{2,66},{3,67},{4,68},{5,69},{6,70},{7,71},{8,72},{9,... | collective-permute-start | bytes 442376 | tf_op jit(solution)/shard_map/ppermute | solution.py:43
  94.7 6.0 %collective-permute-start.18 = (bf16[2,48,768]{2,1,0:T(8,128)(2,1)S(1)}, bf16[2,48,768]{2,1,0:T(8,128)(2,1)S(1)}, u32[]{:S(2)}, u32[]{:S(2)}) collective-permute-start(bf16[2,48,768]{2,1,0:T(8,128)(2,1)S(1)} %slice.192), channel_id=1, source_target_pairs={{0,192},{1,193},{2,194},{3,195},{4,196},{5,197},{6,198},{7,199},{8... | collective-permute-start | bytes 442376 | tf_op jit(solution)/shard_map/ppermute | solution.py:43
  95.1 5.6 %collective-permute-start.19 = (bf16[2,48,768]{2,1,0:T(8,128)(2,1)S(1)}, bf16[2,48,768]{2,1,0:T(8,128)(2,1)S(1)}, u32[]{:S(2)}, u32[]{:S(2)}) collective-permute-start(bf16[2,48,768]{2,1,0:T(8,128)(2,1)S(1)} %slice.193), channel_id=1, source_target_pairs={{0,1},{1,0},{2,3},{3,2},{4,5},{5,4},{6,7},{7,6},{8,9},{9,8},{10,11... | collective-permute-start | bytes 442376 | tf_op jit(solution)/shard_map/ppermute | solution.py:43
  97.1 6.4 %collective-permute-start.20 = (bf16[2,48,768]{2,1,0:T(8,128)(2,1)S(1)}, bf16[2,48,768]{2,1,0:T(8,128)(2,1)S(1)}, u32[]{:S(2)}, u32[]{:S(2)}) collective-permute-start(bf16[2,48,768]{2,1,0:T(8,128)(2,1)S(1)} %slice.194), channel_id=1, source_target_pairs={{0,33},{1,32},{2,35},{3,34},{4,37},{5,36},{6,39},{7,38},{8,41},{9,... | collective-permute-start | bytes 442376 | tf_op jit(solution)/shard_map/ppermute | solution.py:43
  103.7 6.8 %collective-permute-start.21 = (bf16[1,48,768]{2,1,0:T(8,128)(2,1)S(1)}, bf16[1,48,768]{2,1,0:T(8,128)(2,1)S(1)}, u32[]{:S(2)}, u32[]{:S(2)}) collective-permute-start(bf16[1,48,768]{2,1,0:T(8,128)(2,1)S(1)} %slice.196), channel_id=1, source_target_pairs={{0,192},{1,193},{2,194},{3,195},{4,196},{5,197},{6,198},{7,199},{8... | collective-permute-start | bytes 221192 | tf_op jit(solution)/shard_map/ppermute | solution.py:43
  105.0 5.7 %collective-permute-start.22 = (bf16[1,48,768]{2,1,0:T(8,128)(2,1)S(1)}, bf16[1,48,768]{2,1,0:T(8,128)(2,1)S(1)}, u32[]{:S(2)}, u32[]{:S(2)}) collective-permute-start(bf16[1,48,768]{2,1,0:T(8,128)(2,1)S(1)} %slice.198), channel_id=1, source_target_pairs={{0,64},{1,65},{2,66},{3,67},{4,68},{5,69},{6,70},{7,71},{8,72},{9,... | collective-permute-start | bytes 221192 | tf_op jit(solution)/shard_map/ppermute | solution.py:43
  108.5 5.6 %collective-permute-start.23 = (bf16[1,48,768]{2,1,0:T(8,128)(2,1)S(1)}, bf16[1,48,768]{2,1,0:T(8,128)(2,1)S(1)}, u32[]{:S(2)}, u32[]{:S(2)}) collective-permute-start(bf16[1,48,768]{2,1,0:T(8,128)(2,1)S(1)} %slice.200), channel_id=1, source_target_pairs={{0,33},{1,32},{2,35},{3,34},{4,37},{5,36},{6,39},{7,38},{8,41},{9,... | collective-permute-start | bytes 221192 | tf_op jit(solution)/shard_map/ppermute | solution.py:43
  110.5 4.4 %collective-permute-start.24 = (bf16[1,48,768]{2,1,0:T(8,128)(2,1)S(1)}, bf16[1,48,768]{2,1,0:T(8,128)(2,1)S(1)}, u32[]{:S(2)}, u32[]{:S(2)}) collective-permute-start(bf16[1,48,768]{2,1,0:T(8,128)(2,1)S(1)} %slice.202), channel_id=1, source_target_pairs={{0,1},{1,0},{2,3},{3,2},{4,5},{5,4},{6,7},{7,6},{8,9},{9,8},{10,11... | collective-permute-start | bytes 221192 | tf_op jit(solution)/shard_map/ppermute | solution.py:43
  115.8 19.2 %all-to-all-start = ((bf16[8,144,128]{2,1,0:T(8,128)(2,1)}), bf16[8,144,128]{2,1,0:T(8,128)(2,1)S(1)}, u32[]{:S(2)}, u32[]{:S(2)}) async-start(bf16[8,144,128]{2,1,0:T(8,128)(2,1)} %pieces.1), calls=%async_computation | async-start | bytes 589824 | tf_op jit(solution)/shard_map/all_to_all | solution.py:403
  135.0 0.7 copy-start.10
where the time goes:
time: 138 us; the launch traced here: 137 us
  starting transfers between devices  42.7 us (31%)
  waiting for transfers between devices  36.2 us (26%)
  Pallas kernels  33.3 us (24%)
  local copies, waits for them, and re-layouts  11.8 us (9%)
  other arithmetic  5.85 us (4%)
  matrix products  5.72 us (4%)
  between operations  1.72 us (1%)
    ppermute x23, starting transfers between devices, to_device(): return lax.ppermute(value, ('dp', 'seq'), pairs)  28.9 us
    ppermute x23, waiting for transfers between devices, to_device(): return lax.ppermute(value, ('dp', 'seq'), pairs)  16.4 us
    pallas_call x2, Pallas kernels, attention(): pl.pallas_call(kernel, grid_spec=pltpu.PrefetchScalarGridSpec(num_scalar_...  13.4 us
    ppermute x2, waiting for transfers between devices, from_behind(): return lax.ppermute(value, axis, pairs)  11.4 us
    unnamed x27, local copies, waits for them, and re-layouts  11.1 us
    pallas_call x2, Pallas kernels, weight_sections(): pl.pallas_call(weight_kernel, grid_spec=pltpu.PrefetchScalarGridSpec(num_...  9.09 us
    all_to_all x1, waiting for transfers between devices, on_device(): lax.all_to_all(shares, 'seq', 0, 0, axis_index_groups=rings, tiled=True)  8.4 us
    all_to_all x1, starting transfers between devices, on_device(): lax.all_to_all(shares, 'seq', 0, 0, axis_index_groups=rings, tiled=True)  8.32 us
  transfers between devices with their start and end apart: 26, of which 13 were waited for; matrix products, arithmetic and copies ran while one was open for 8% of the time, Pallas kernels for 18%

commit v1 on v0

v1 whole, which is shorter than its diff:
```python
import jax
import jax.numpy as jnp
import numpy as np
from jax import lax
from jax.experimental import pallas as pl
from jax.experimental.pallas import tpu as pltpu
from jax.sharding import PartitionSpec as P

HEAD_DIM = 64
GROUP = 32
LEFT = 4
CONTEXT = LEFT * GROUP
PAIR = 2 * HEAD_DIM
F32 = jnp.float32
BF16 = jnp.bfloat16
NT = (((1,), (1,)), ((), ()))
NN = (((1,), (0,)), ((), ()))

Y, XH, CORES, Z, XL = 4, 2, 2, 8, 2
CHUNKS = Y * XH * XL

epsilon = 1e-05


def dot(a, b, dims=NN):
    return lax.dot_general(a, b, dims, preferred_element_type=F32)


def from_behind(value, axis, by):
    peers = lax.axis_size(axis)
    pairs = [(i, i + by) for i in range(peers) if 0 <= i + by < peers]
    return lax.ppermute(value, axis, pairs)


def flat(y, xh, core, z, xl):
    return ((y * XH + xh) * CORES + core) * (Z * XL) + z * XL + xl


def to_device(value, where):
    pairs = []
    for place in np.ndindex(Y, XH, CORES, Z, XL):
        pairs.append((flat(*place), flat(*where(*place))))
    return lax.ppermute(value, ("dp", "seq"), pairs)


def to_core(y, xh, core, z, xl):
    return y, xh, 1 - core, z, xl


def to_x_near(y, xh, core, z, xl):
    return y, xh, core, z, 1 - xl


def to_x_mirror(y, xh, core, z, xl):
    return y, 1 - xh, core, z, 1 - xl


def to_y_near(y, xh, core, z, xl):
    return y ^ 1, xh, core, z, xl


def to_y_mirror(y, xh, core, z, xl):
    return 3 - y, xh, core, z, xl


def to_x_far(y, xh, core, z, xl):
    return y, 1 - xh, core, z, xl


def to_y_far(y, xh, core, z, xl):
    return y ^ 2, xh, core, z, xl


ROUTES = (
    (to_x_near, to_x_mirror),
    (to_x_mirror, to_x_near),
    (to_y_near, to_y_mirror),
    (to_y_mirror, to_y_near),
)
OWNERS = (
    (to_y_mirror, to_y_near, to_y_far),
    (to_x_mirror, to_x_near, to_x_far),
)


def halves(route, hi, lo):
    return (hi ^ lo, hi) if route % 2 == 0 else (hi, hi ^ lo)


def chunk_at(route, slot, y, xh, xl):
    bits = [(slot >> (3 - i)) & 1 for i in range(4)]
    x_first = route < 2
    x_bits, y_bits = (bits[:2], bits[2:]) if x_first else (bits[2:], bits[:2])
    found = []
    for hi, lo, pair, order in ((y >> 1, y & 1, y_bits, 0 if x_first else route), (xh, xl, x_bits, route if x_first else 0)):
        first, second = halves(order, hi, lo)
        first, second = first ^ pair[0], second ^ pair[1]
        found.append((second, first ^ second) if order % 2 == 0 else (first, first ^ second))
    (yh, yl), (xh_to, xl_to) = found
    return ((yh * 2 + yl) * XH + xh_to) * XL + xl_to


def row_order(width):
    share = width // (CHUNKS * CORES * Z)
    order = np.arange(width // Y).reshape(XH, CORES, Z, XL, share).transpose(1, 0, 3, 2, 4).reshape(-1)
    return jnp.asarray(np.eye(width // Y, dtype=np.float32)[order], BF16)


def normalize(rows_in):
    average = jnp.mean(rows_in, axis=-1, keepdims=True)
    centered = rows_in - average
    variance = jnp.mean(centered * centered, axis=-1, keepdims=True)
    return centered * lax.rsqrt(variance + epsilon)


SMEM_SPEC = pl.BlockSpec(memory_space=pltpu.SMEM)
VMEM_SPEC = pl.BlockSpec(memory_space=pltpu.VMEM)
HBM_SPEC = pl.BlockSpec(memory_space=pltpu.HBM)


def in_vmem(value):
    return pltpu.with_memory_space_constraint(value, pltpu.VMEM)


def in_hbm(value):
    return pltpu.with_memory_space_constraint(value, pltpu.HBM)


def cost(flops, nbytes, transcendentals=0):
    return pl.CostEstimate(flops=flops, bytes_accessed=nbytes, transcendentals=transcendentals)


def params(mebibytes):
    return pltpu.CompilerParams(vmem_limit_bytes=mebibytes * 2**20)


def fetch(source, target, sems, block, base=0):
    copies = []
    for i in range(target.shape[1] // block):
        there = source.at[:, pl.ds(base + i * block, block)]
        copies.append(pltpu.make_async_copy(there, target.at[:, pl.ds(i * block, block)], sems.at[i]))
        copies[-1].start()
    return copies


BLOCK = 384


def project_kernel(frames_ref, weight_ref, normed_ref, keys_ref, tail_ref, rows, weight, row_sem, sems):
    whole = pltpu.make_async_copy(frames_ref, rows, row_sem)
    whole.start()
    copies = fetch(weight_ref, weight, sems, BLOCK, weight_ref.shape[1] - weight.shape[1])
    whole.wait()
    normed_ref[...] = normalize(rows[...].astype(F32)).astype(BF16)
    for i, copy in enumerate(copies):
        copy.wait()
        here = slice(i * BLOCK, (i + 1) * BLOCK)
        out = dot(normed_ref[...], weight[:, here]).astype(BF16)
        keys_ref[:, here] = out
        tail_ref[:, here] = out[out.shape[0] - CONTEXT :]


def project(frames, weight):
    rows, width = frames.shape
    columns = weight.shape[1] // 3 * 2
    return pl.pallas_call(
        project_kernel,
        in_specs=[HBM_SPEC, HBM_SPEC],
        out_specs=[VMEM_SPEC] * 3,
        out_shape=[pltpu.VMEM((rows, width), BF16), pltpu.VMEM((rows, columns), BF16), pltpu.VMEM((CONTEXT, columns), BF16)],
        scratch_shapes=[
            pltpu.VMEM((rows, width), BF16),
            pltpu.VMEM((width, columns), BF16),
            pltpu.SemaphoreType.DMA,
            pltpu.SemaphoreType.DMA((columns // BLOCK,)),
        ],
        compiler_params=params(24),
        cost_estimate=cost(2 * rows * width * columns, 2 * width * columns),
        name="project",
    )(in_hbm(frames), in_hbm(weight))


def second_kernel(places, order_ref, normed_ref, cotangent_ref, weight_ref, out_ref,
                  query_ref, grad_ref, keep_ref, send_ref, cotangent, weight, outer, sem, sems, out_sem):
    whole = pltpu.make_async_copy(cotangent_ref, cotangent, sem)
    whole.start()
    copies = fetch(weight_ref, weight, sems, BLOCK)
    last = pltpu.make_async_copy(out_ref, outer, out_sem)
    last.start()
    rows = order_ref.shape[0]
    half = rows // CORES
    tokens = normed_ref.shape[0]

    def turn(ref, columns):
        for y in range(Y):
            turned = dot(order_ref[...], ref[:, y * rows : (y + 1) * rows].T).astype(BF16)
            there = slice(y * half, (y + 1) * half)

            @pl.when(places[0] == 0)
            def _():
                keep_ref[there, columns] = turned[:half]
                send_ref[there, columns] = turned[half:]

            @pl.when(places[0] == 1)
            def _():
                keep_ref[there, columns] = turned[half:]
                send_ref[there, columns] = turned[:half]

    turn(normed_ref, slice(0, tokens))
    for i, copy in enumerate(copies):
        copy.wait()
        here = slice(i * BLOCK, (i + 1) * BLOCK)
        query_ref[:, here] = dot(normed_ref[...], weight[:, here]).astype(BF16)
    whole.wait()
    turn(cotangent, slice(tokens, 2 * tokens))
    last.wait()
    grad_ref[...] = dot(cotangent[...], outer[...], NT).astype(BF16)


def second(normed, cotangent, w_qkv, w_out, core):
    tokens, width = normed.shape
    inner = w_out.shape[0]
    order = row_order(width)
    turned = pltpu.VMEM((width // CORES, 2 * tokens), BF16)
    return pl.pallas_call(
        second_kernel,
        in_specs=[SMEM_SPEC, VMEM_SPEC, VMEM_SPEC, HBM_SPEC, HBM_SPEC, HBM_SPEC],
        out_specs=[VMEM_SPEC] * 4,
        out_shape=[pltpu.VMEM((tokens, inner), BF16), pltpu.VMEM((tokens, inner), BF16), turned, turned],
        scratch_shapes=[
            pltpu.VMEM((tokens, width), BF16),
            pltpu.VMEM((width, inner), BF16),
            pltpu.VMEM((inner, width), BF16),
            pltpu.SemaphoreType.DMA,
            pltpu.SemaphoreType.DMA((inner // BLOCK,)),
            pltpu.SemaphoreType.DMA,
        ],
        compiler_params=params(24),
        cost_estimate=cost(8 * tokens * width * inner, 8 * inner * width),
        name="second",
    )(jnp.reshape(core, (1,)), in_vmem(order), normed, in_hbm(cotangent), in_hbm(w_qkv), in_hbm(w_out))


def attend(begin, length, inner, operands, results):
    lane = lax.broadcasted_iota(jnp.int32, (CONTEXT, PAIR), 1)
    heads = (lane < HEAD_DIM, lane >= HEAD_DIM)
    row_valid = begin + lax.broadcasted_iota(jnp.int32, (CONTEXT, PAIR), 0) < length
    col_valid = begin + lane < length
    keys = lax.broadcasted_iota(jnp.int32, (2 * CONTEXT, 2 * CONTEXT), 0)
    queries = lax.broadcasted_iota(jnp.int32, (2 * CONTEXT, 2 * CONTEXT), 1)
    key_block = keys // GROUP
    query_block = (queries % CONTEXT) // GROUP
    key_place = begin - CONTEXT + keys
    seen = (key_block >= query_block) & (key_block <= query_block + LEFT) & (key_place >= 0) & (key_place < length)
    zero = jnp.zeros((CONTEXT, PAIR), BF16)
    scale = HEAD_DIM ** (-0.5)

    def unstack(both):
        return jnp.concatenate([both[:HEAD_DIM, :CONTEXT], both[HEAD_DIM:, CONTEXT:]], axis=0)

    for pair in range(inner // PAIR):
        q, k2, v2, do = operands(pair)
        do = jnp.where(row_valid, do, zero)
        q = q * jnp.asarray(scale, BF16)
        q2 = jnp.concatenate([jnp.where(h, q, zero) for h in heads], axis=0)
        do2 = jnp.concatenate([jnp.where(h, do, zero) for h in heads], axis=0)
        scores = jnp.where(seen, dot(k2, q2, NT), -1e30)
        dprob = dot(v2, do2, NT)
        highest = jnp.max(scores, axis=0, keepdims=True)
        raised = jnp.exp(scores - highest)
        prob = raised * (1.0 / jnp.sum(raised, axis=0, keepdims=True))
        rounded = prob.astype(BF16)
        mixed = jnp.where(col_valid, unstack(dot(v2.T, rounded)), 0.0).T.astype(BF16)
        weighed = prob * dprob
        dscores = (weighed - prob * jnp.sum(weighed, axis=0, keepdims=True)).astype(BF16)
        dq = (unstack(dot(k2.T, dscores)) * scale).T.astype(BF16)
        results(pair, mixed, dq, dot(dscores, q2), dot(rounded, do2))


def late_kernel(places, q_ref, kv_ref, do_ref, out_ref, head_ref, tail_ref):
    inner = q_ref.shape[1]

    def operands(pair):
        at = slice(pair * PAIR, (pair + 1) * PAIR)
        return q_ref[CONTEXT:, at], kv_ref[:, at], kv_ref[:, slice(inner + at.start, inner + at.stop)], do_ref[CONTEXT:, at]

    def results(pair, mixed, dq, dk, dv):
        at = slice(pair * PAIR, (pair + 1) * PAIR)
        out_ref[0, :, at] = mixed
        out_ref[1, :, at] = dq
        for n, grad in enumerate((dk, dv)):
            head_ref[n, :, at] = grad[:CONTEXT]
            tail_ref[n, :, at] = grad[CONTEXT:]

    attend(places[1] + CONTEXT, places[0], inner, operands, results)


def early_kernel(places, q_ref, kv_ref, halo_ref, do_ref, add_ref, out_ref, head_ref, back_ref):
    inner = q_ref.shape[1]

    def operands(pair):
        at = slice(pair * PAIR, (pair + 1) * PAIR)
        v_at = slice(inner + at.start, inner + at.stop)
        k2 = jnp.concatenate([halo_ref[:, at], kv_ref[:CONTEXT, at]], axis=0)
        v2 = jnp.concatenate([halo_ref[:, v_at], kv_ref[:CONTEXT, v_at]], axis=0)
        return q_ref[:CONTEXT, at], k2, v2, do_ref[:CONTEXT, at]

    def results(pair, mixed, dq, dk, dv):
        at = slice(pair * PAIR, (pair + 1) * PAIR)
        out_ref[0, :, at] = mixed
        out_ref[1, :, at] = dq
        for n, grad in enumerate((dk, dv)):
            back_ref[n, :, at] = grad[:CONTEXT].astype(BF16)
            head_ref[n, :, at] = (grad[CONTEXT:] + add_ref[n, :, at]).astype(BF16)

    attend(places[1], places[0], inner, operands, results)


def attention(kernel, places, operands, inner, types, name):
    return pl.pallas_call(
        kernel,
        in_specs=[SMEM_SPEC] + [VMEM_SPEC] * len(operands),
        out_specs=[VMEM_SPEC] * len(types),
        out_shape=[pltpu.VMEM((2, CONTEXT, inner), dtype) for dtype in types],
        compiler_params=params(24),
        cost_estimate=cost(28 * CONTEXT * 2 * CONTEXT * inner, 16 * CONTEXT * inner, CONTEXT * 4 * inner),
        name=name,
    )(places, *[in_vmem(o) for o in operands])


def weight_kernel(lefts, chunks, left_ref, left_other_ref, right_ref, right_other_ref, *refs):
    outs, held = refs[:-1], refs[-1]
    tokens = right_ref.shape[1]
    columns = right_ref.shape[2] // 2
    half = CHUNKS // 2
    for n, left in enumerate(lefts):
        at = slice(left * tokens, (left + 1) * tokens)
        total = dot(left_ref[:, at], right_ref[n]) + dot(left_other_ref[:, at], right_other_ref[n])
        for part in range(2):
            route = 2 * n + part
            held[route] = total[:, part * columns : (part + 1) * columns].reshape(held.shape[1:])
            for slot in range(CHUNKS):
                ref = outs[route] if slot < half else outs[len(ROUTES) + route]
                ref[slot % half] = held[route, chunks[route, slot]].astype(BF16)


def weight_sections(chunks, left, left_other, lefts, right, right_other):
    rows = left.shape[0]
    tokens = right.shape[1]
    columns = right.shape[2] // 2
    routes = len(ROUTES)
    out = pltpu.VMEM((CHUNKS // 2, rows // CHUNKS, columns), BF16)
    outs = pl.pallas_call(
        lambda *refs: weight_kernel(lefts, *refs),
        in_specs=[SMEM_SPEC] + [VMEM_SPEC] * 4,
        out_specs=[VMEM_SPEC] * (2 * routes),
        out_shape=[out] * (2 * routes),
        scratch_shapes=[pltpu.VMEM((routes, CHUNKS, rows // CHUNKS, columns), F32)],
        compiler_params=params(24),
        cost_estimate=cost(4 * rows * tokens * columns * routes, 4 * rows * (tokens + columns * routes)),
        name="weight_sections",
    )(chunks, *[in_vmem(o) for o in (left, left_other, right, right_other)])
    return outs[:routes], outs[routes:]


def plus(*terms):
    return sum(t.astype(F32) for t in terms).astype(BF16)


def pieces_kernel(*refs):
    ins, out_ref, held = refs[:-2], refs[-2], refs[-1]
    for group, ref in enumerate(ins):
        block = ref[...].astype(F32)
        width = block.shape[1] // PAIR // 4
        share = block.shape[0] // Z
        for n in (2 * group, 2 * group + 1):
            bases = (((n + 2) % 4) * width + (0 if n > 1 else 4 * width), (2 + n) * width)
            for wave, base in enumerate(bases):
                for t in range(width):
                    column = (((n % 2) * 2 + wave) * width + t) * PAIR
                    for z in range(Z):
                        rows = slice((base + t) * share, (base + t + 1) * share)
                        held[z, rows, :] = block[z * share : (z + 1) * share, column : column + PAIR]
    out_ref[...] = held[...].astype(BF16)


def total_kernel(in_ref, out_ref):
    total = in_ref[0].astype(F32)
    for z in range(1, Z):
        total += in_ref[z].astype(F32)
    share = out_ref.shape[0]
    for t in range(out_ref.shape[1] // PAIR):
        out_ref[:, t * PAIR : (t + 1) * PAIR] = total[t * share : (t + 1) * share]


def on_device(frames, cotangent, lengths, w_qkv, w_out):
    frame_rows = frames[0]
    grad_rows = cotangent[0]
    row_count, width = frame_rows.shape
    inner = w_out.shape[0]
    seq_index = lax.axis_index("seq")
    dp_index = lax.axis_index("dp")
    xl = seq_index % XL
    core, xh, y = dp_index % CORES, dp_index // CORES % XH, dp_index // (CORES * XH)
    places = jnp.stack([lengths[0], seq_index * row_count])
    routes = range(len(ROUTES))
    chunks = jnp.stack([jnp.stack([chunk_at(r, slot, y, xh, xl) for slot in range(CHUNKS)]) for r in routes])

    normed, keys, tail = project(frame_rows, w_qkv)
    received = from_behind(tail, "seq", 1)
    queries, attended_grad, left, left_out = second(normed, grad_rows, w_qkv, w_out, core)
    left_other = to_device(left_out, to_core)
    late, late_head, late_tail = attention(
        late_kernel, places, (queries, keys, attended_grad), inner, (BF16, F32, F32), "attention_late"
    )
    early, kv_head, halo = attention(
        early_kernel, places, (queries, keys, received, attended_grad, late_head), inner, (BF16,) * 3, "attention_early"
    )
    returned = from_behind(halo, "seq", -1)
    own = jnp.concatenate([early, late], axis=1)
    own_other = to_device(own, to_core)
    keep_a, send_a = weight_sections(chunks, left, left_other, (1, 0), own, own_other)
    attended, late_tail, send_a = lax.optimization_barrier((own[0], late_tail, send_a))
    got_a = [to_device(send_a[r], ROUTES[r][0]) for r in routes]

    kv_total = jnp.concatenate([kv_head, plus(late_tail, returned)], axis=1)
    kv_other = to_device(kv_total, to_core)
    keep_b, send_b = weight_sections(chunks, left, left_other, (0, 0), kv_total, kv_other)
    projected_grad = jnp.concatenate([own[1], kv_total[0], kv_total[1]], axis=1)
    projected_grad, send_b = lax.optimization_barrier((projected_grad, send_b))
    got_b = [to_device(send_b[r], ROUTES[r][0]) for r in routes]

    block_out = dot(attended, w_out).astype(BF16)
    normed_grad = dot(projected_grad, w_qkv, NT).astype(BF16)
    _, norm_back = jax.vjp(normalize, frame_rows.astype(F32))
    (frame_grad,) = norm_back(normed_grad.astype(F32))

    totals = [
        jnp.concatenate([plus(keep_a[r], got_a[r]), plus(keep_b[r], got_b[r])], axis=-1) for r in routes
    ]
    count = totals[0].shape[0] // 2
    sends = lax.optimization_barrier([t[count:] for t in totals])
    gots = lax.optimization_barrier([to_device(sends[r], ROUTES[r][1]) for r in routes])
    totals = [plus(totals[r][:count], gots[r]) for r in routes]
    groups = [jnp.concatenate(totals[:2], axis=-1), jnp.concatenate(totals[2:], axis=-1)]
    slots = lax.optimization_barrier([[g[slot] for slot in range(1, 4)] for g in groups])
    gots = [[to_device(slots[n][i], OWNERS[n][i]) for n in range(2)] for i in range(3)]
    groups = [plus(groups[n][0], *[gots[i][n] for i in range(3)]) for n in range(2)]
    share = width // (CHUNKS * CORES * Z)
    tiles = 4 * inner // PAIR
    shares = pl.pallas_call(
        pieces_kernel,
        in_specs=[VMEM_SPEC] * 2,
        out_shape=jax.ShapeDtypeStruct((Z, tiles * share, PAIR), BF16),
        scratch_shapes=[pltpu.VMEM((Z, tiles * share, PAIR), F32)],
        compiler_params=params(24),
        name="pieces",
    )(*[in_vmem(g) for g in groups])
    rings = [[place * XL + x for place in range(Z)] for x in range(XL)]
    shares = lax.all_to_all(shares, "seq", 0, 0, axis_index_groups=rings, tiled=True)
    total = pl.pallas_call(
        total_kernel,
        in_specs=[VMEM_SPEC],
        out_shape=jax.ShapeDtypeStruct((share, 4 * inner), F32),
        compiler_params=params(24),
        name="total",
    )(in_vmem(shares))
    return block_out[None], frame_grad.astype(BF16)[None], total


def solution(mesh):
    placed = (P("dp", "seq", None), P("dp", "seq", None), P("dp"), P(), P())
    return jax.shard_map(
        on_device,
        mesh=mesh,
        in_specs=placed,
        out_specs=(P("dp", "seq", None), P("dp", "seq", None), P(("dp", "seq"), None)),
        check_vma=False,
    )
```

time: 138 us -> 117 us (0.85); the launches traced: 137 us -> 114 us
  local copies, waits for them, and re-layouts: 11.8 us -> 3.06 us
  Pallas kernels: 33.3 us -> 24.8 us
  matrix products: 5.72 us -> 3.82 us
  starting transfers between devices: 42.7 us -> 40.9 us
  other arithmetic: 5.85 us -> 4.46 us
    pallas_call x8, Pallas kernels: 33.3 us -> 24.8 us  [the longest x2 6.48 us: attention(): pl.pallas_call(kernel, in_specs=[SMEM_SPEC] + [VMEM_SPEC] * len(operands)...]
    unnamed x27 -> x21, local copies, waits for them, and re-layouts: 11.1 us -> 2.6 us
    ppermute x2, waiting for transfers between devices: 11.4 us -> 9 us  [from_behind(): return lax.ppermute(value, axis, pairs)]
    dot_general x3 -> x2, matrix products: 5.72 us -> 3.82 us  [dot(): return lax.dot_general(a, b, dims, preferred_element_type=F32)]
    broadcast_in_dim x1, other arithmetic: 2.44 us -> 1.03 us  [on_device(): return (block_out[None], frame_grad.astype(BF16)[None], total)]
    all_to_all x1, waiting for transfers between devices: 8.4 us -> 9.8 us  [on_device(): lax.all_to_all(shares, 'seq', 0, 0, axis_index_groups=rings, tiled=True)]
    ppermute x23 -> x21, starting transfers between devices: 28.9 us -> 27.9 us  [to_device(): return lax.ppermute(value, ('dp', 'seq'), pairs)]
    ppermute x23 -> x21, waiting for transfers between devices: 16.4 us -> 16.8 us  [to_device(): return lax.ppermute(value, ('dp', 'seq'), pairs)]
  transfers between devices with their start and end apart: 26 -> 24, of which waited for: 13 -> 16; matrix products, arithmetic and copies ran while one was open for 8% -> 7% of each run, Pallas kernels for 18% -> 13%
where the time goes in v1:
time: 117 us; the launch traced here: 114 us
  starting transfers between devices  40.9 us (35%)
  waiting for transfers between devices  35.6 us (30%)
  Pallas kernels  24.8 us (21%)
  other arithmetic  4.46 us (4%)
  matrix products  3.82 us (3%)
  local copies, waits for them, and re-layouts  3.06 us (3%)
  between operations  1.68 us (1%)
    ppermute x21, starting transfers between devices, to_device(): return lax.ppermute(value, ('dp', 'seq'), pairs)  27.9 us
    ppermute x21, waiting for transfers between devices, to_device(): return lax.ppermute(value, ('dp', 'seq'), pairs)  16.8 us
    all_to_all x1, waiting for transfers between devices, on_device(): lax.all_to_all(shares, 'seq', 0, 0, axis_index_groups=rings, tiled=True)  9.8 us
    ppermute x2, waiting for transfers between devices, from_behind(): return lax.ppermute(value, axis, pairs)  9 us
    all_to_all x1, starting transfers between devices, on_device(): lax.all_to_all(shares, 'seq', 0, 0, axis_index_groups=rings, tiled=True)  8.33 us
    pallas_call x2, Pallas kernels, attention(): pl.pallas_call(kernel, in_specs=[SMEM_SPEC] + [VMEM_SPEC] * len(operands)...  6.48 us
    pallas_call x1, Pallas kernels, second(): pl.pallas_call(second_kernel, in_specs=[SMEM_SPEC, VMEM_SPEC, VMEM_SPEC,...  6.05 us
    pallas_call x2, Pallas kernels, weight_sections(): pl.pallas_call(lambda *refs: weight_kernel(lefts, *refs), in_specs=[SMEM_...  5.76 us
  transfers between devices with their start and end apart: 24, of which 16 were waited for; matrix products, arithmetic and copies ran while one was open for 7% of the time, Pallas kernels for 13%

profile of v1, /device:TPU:8, one launch (start us, length us, event | category | flops | bytes accessed | tf_op | source)
XLA Modules:
  0.0 114.4 jit_solution(17783711189450980482)
XLA Ops:
  0.6 5.0 %project.1 = (bf16[256,1536]{1,0:T(8,128)(2,1)S(1)}, bf16[256,1536]{1,0:T(8,128)(2,1)S(1)}, bf16[128,1536]{1,0:T(8,128)(2,1)S(1)}) custom-call(bf16[256,1536]{1,0:T(8,128)(2,1)} %bitcast.69, bf16[1536,2304]{1,0:T(8,128)(2,1)} %weight_ref.3), custom_call_target="tpu_custom_call" | custom-call | flops 1207959552 | bytes 4718592 | tf_op jit(solution)/shard_map/project/pallas_call | solution.py:166
  5.7 3.4 %collective-permute-start = (bf16[128,1536]{1,0:T(8,128)(2,1)S(1)}, bf16[128,1536]{1,0:T(8,128)(2,1)S(1)}, u32[]{:S(2)}, u32[]{:S(2)}) collective-permute-start(bf16[128,1536]{1,0:T(8,128)(2,1)S(1)} %get-tuple-element.60), channel_id=1, source_target_pairs={{0,1},{1,2},{2,3},{3,4},{4,5},{5,6},{6,7},{7,8},{8,9},{9,10},{10,1... | collective-permute-start | bytes 1179656 | tf_op jit(solution)/shard_map/ppermute | solution.py:32
  9.2 6.0 %second.1 = (bf16[256,768]{1,0:T(8,128)(2,1)S(1)}, bf16[256,768]{1,0:T(8,128)(2,1)S(1)}, bf16[768,512]{1,0:T(8,128)(2,1)S(1)}, bf16[768,512]{1,0:T(8,128)(2,1)}) custom-call(s32[1]{0:T(128)} %bitcast.1.places, bf16[384,384]{1,0:T(8,128)(2,1)S(1)} %copy-done.2, bf16[256,1536]{1,0:T(8,128)(2,1)S(1)} %get-tuple-element.57.normed_ref, ...), custom_call_target="tpu_custom_call" | custom-call | flops 2415919104 | bytes 9437184 | tf_op jit(solution)/shard_map/second/pallas_call | solution.py:225
  15.2 0.9 copy-done.3
  16.8 3.2 %attention_late.1 = (bf16[2,128,768]{2,1,0:T(8,128)(2,1)S(1)}, f32[2,128,768]{2,1,0:T(8,128)S(1)}, f32[2,128,768]{2,1,0:T(8,128)S(1)}) custom-call(s32[2]{0:T(128)S(1)} %pad_add_fusion.1.places, bf16[256,768]{1,0:T(8,128)(2,1)S(1)} %get-tuple-element.58.q_ref, bf16[256,1536]{1,0:T(8,128)(2,1)S(1)} %get-tuple-element.59.kv_ref, ...), custom_call_target="tpu_custom_call" | custom-call | flops 704643072 | bytes 1572864 | tf_op jit(solution)/shard_map/attention_late/pallas_call | solution.py:320
  20.1 1.0 copy-done.1
  21.1 3.2 %attention_early.1 = (bf16[2,128,768]{2,1,0:T(8,128)(2,1)S(1)}, bf16[2,128,768]{2,1,0:T(8,128)(2,1)S(1)}, bf16[2,128,768]{2,1,0:T(8,128)(2,1)S(1)}) custom-call(s32[2]{0:T(128)S(1)} %pad_add_fusion.1.places, bf16[256,768]{1,0:T(8,128)(2,1)S(1)} %get-tuple-element.58.q_ref, bf16[256,1536]{1,0:T(8,128)(2,1)S(1)} %get-tuple-element.59.kv_ref, ...), custom_call_target="tpu_custom_call" | custom-call | flops 704643072 | bytes 1572864 | tf_op jit(solution)/shard_map/attention_early/pallas_call | solution.py:320
  24.4 0.7 copy-done.5
  25.1 0.5 collective-permute-start.2
  25.6 0.1 stack.153
  25.7 0.1 stack.151
  25.8 0.1 stack.74
  25.9 0.1 stack.72
  26.0 1.3 %convert_reduce_fusion = f32[256]{0:T(256)S(1)} fusion(bf16[1,256,1536]{2,1,0:T(8,128)(2,1)} %param.6), kind=kLoop, calls=%fused_computation.6 | loop fusion | flops 786176 | bytes 787456 | tf_op jit(solution)/shard_map/jvp()/reduce_sum | solution.py:110
  27.3 1.3 %collective-permute-start.3 = (bf16[2,128,768]{2,1,0:T(8,128)(2,1)}, bf16[2,128,768]{2,1,0:T(8,128)(2,1)S(1)}, u32[]{:S(2)}, u32[]{:S(2)}) collective-permute-start(bf16[2,128,768]{2,1,0:T(8,128)(2,1)} %copy-done.5), channel_id=1, source_target_pairs={{1,0},{2,1},{3,2},{4,3},{5,4},{6,5},{7,6},{8,7},{9,8},{10,9},{11,1... | collective-permute-start | bytes 1179656 | tf_op jit(solution)/shard_map/ppermute | solution.py:32
  28.8 2.8 %weight_sections.2 = (bf16[8,48,384]{2,1,0:T(8,128)(2,1)S(1)}, bf16[8,48,384]{2,1,0:T(8,128)(2,1)S(1)}, bf16[8,48,384]{2,1,0:T(8,128)(2,1)S(1)}, bf16[8,48,384]{...) custom-call(s32[4,16]{1,0:T(4,128)S(1)} %pad_add_fusion.refs_0_, ...), custom_call_target="tpu_custom_call" | custom-call | flops 1207959552 | bytes 5505024 | tf_op jit(solution)/shard_map/weight_sections/pallas_call | solution.py:353
  31.6 9.0 %collective-permute-done.3 = bf16[2,128,768]{2,1,0:T(8,128)(2,1)S(1)} collective-permute-done((bf16[2,128,768]{2,1,0:T(8,128)(2,1)}, bf16[2,128,768]{2,1,0:T(8,128)(2,1)S(1)}, u32[]{:S(2)}, u32[]{:S(2)}) %collective-permute-start.3) | collective-permute-done | bytes 393248 | tf_op jit(solution)/shard_map/ppermute | solution.py:32
  40.6 0.1 add_convert_fusion.1
  40.8 2.7 %collective-permute-start.5 = (bf16[8,48,384]{2,1,0:T(8,128)(2,1)S(1)}, bf16[8,48,384]{2,1,0:T(8,128)(2,1)S(1)}, u32[]{:S(2)}, u32[]{:S(2)}) collective-permute-start(bf16[8,48,384]{2,1,0:T(8,128)(2,1)S(1)} %get-tuple-element.82), channel_id=1, source_target_pairs={{0,1},{1,0},{2,3},{3,2},{4,5},{5,4},{6,7},{7,6},{8,9},{9,8},{10,11... | collective-permute-start | bytes 884744 | tf_op jit(solution)/shard_map/ppermute | solution.py:43
  43.6 1.7 %collective-permute-start.7 = (bf16[8,48,384]{2,1,0:T(8,128)(2,1)S(1)}, bf16[8,48,384]{2,1,0:T(8,128)(2,1)S(1)}, u32[]{:S(2)}, u32[]{:S(2)}) collective-permute-start(bf16[8,48,384]{2,1,0:T(8,128)(2,1)S(1)} %get-tuple-element.86), channel_id=1, source_target_pairs={{0,33},{1,32},{2,35},{3,34},{4,37},{5,36},{6,39},{7,38},{8,41},{9,... | collective-permute-start | bytes 884744 | tf_op jit(solution)/shard_map/ppermute | solution.py:43
  45.2 0.4 collective-permute-start.9
  45.7 2.4 %collective-permute-start.11 = (bf16[8,48,384]{2,1,0:T(8,128)(2,1)S(1)}, bf16[8,48,384]{2,1,0:T(8,128)(2,1)S(1)}, u32[]{:S(2)}, u32[]{:S(2)}) collective-permute-start(bf16[8,48,384]{2,1,0:T(8,128)(2,1)S(1)} %get-tuple-element.94), channel_id=1, source_target_pairs={{0,192},{1,193},{2,194},{3,195},{4,196},{5,197},{6,198},{7,199},{8... | collective-permute-start | bytes 884744 | tf_op jit(solution)/shard_map/ppermute | solution.py:43
  48.1 1.7 %fusion.1 = bf16[1,256,1536]{2,1,0:T(8,128)(2,1)} fusion(bf16[256,768]{1,0:T(8,128)(2,1)S(1)} %get-tuple-element.72, bf16[768,1536]{1,0:T(8,128)(2,1)S(1)} %copy-done.7), kind=kOutput, calls=%fused_computation.3 | convolution fusion | flops 604372992 | bytes 3538944 | tf_op jit(solution)/shard_map/dot_general | solution.py:26
  49.7 0.1 pad_maximum_fusion
  50.0 2.6 %collective-permute-done.7 = bf16[8,48,384]{2,1,0:T(8,128)(2,1)S(1)} collective-permute-done((bf16[8,48,384]{2,1,0:T(8,128)(2,1)S(1)}, bf16[8,48,384]{2,1,0:T(8,128)(2,1)S(1)}, u32[]{:S(2)}, u32[]{:S(2)}) %collective-permute-start.7) | collective-permute-done | bytes 294944 | tf_op jit(solution)/shard_map/ppermute | solution.py:43
  52.6 0.4 collective-permute-done.9
  53.1 0.8 collective-permute-done.11
  53.9 2.9 %weight_sections.3 = (bf16[8,48,384]{2,1,0:T(8,128)(2,1)S(1)}, bf16[8,48,384]{2,1,0:T(8,128)(2,1)S(1)}, bf16[8,48,384]{2,1,0:T(8,128)(2,1)S(1)}, bf16[8,48,384]{...) custom-call(s32[4,16]{1,0:T(4,128)S(1)} %pad_add_fusion.refs_0_, ...), custom_call_target="tpu_custom_call" | custom-call | flops 1207959552 | bytes 5505024 | tf_op jit(solution)/shard_map/weight_sections/pallas_call | solution.py:353
  56.9 1.1 collective-permute-start.6
  58.0 0.9 collective-permute-start.8
  58.9 2.1 %collective-permute-start.10 = (bf16[8,48,384]{2,1,0:T(8,128)(2,1)S(1)}, bf16[8,48,384]{2,1,0:T(8,128)(2,1)S(1)}, u32[]{:S(2)}, u32[]{:S(2)}) collective-permute-start(bf16[8,48,384]{2,1,0:T(8,128)(2,1)S(1)} %get-tuple-element.92), channel_id=1, source_target_pairs={{0,64},{1,65},{2,66},{3,67},{4,68},{5,69},{6,70},{7,71},{8,72},{9,... | collective-permute-start | bytes 884744 | tf_op jit(solution)/shard_map/ppermute | solution.py:43
  61.0 1.6 %collective-permute-start.12 = (bf16[8,48,384]{2,1,0:T(8,128)(2,1)S(1)}, bf16[8,48,384]{2,1,0:T(8,128)(2,1)S(1)}, u32[]{:S(2)}, u32[]{:S(2)}) collective-permute-start(bf16[8,48,384]{2,1,0:T(8,128)(2,1)S(1)} %get-tuple-element.96), channel_id=1, source_target_pairs={{0,192},{1,193},{2,194},{3,195},{4,196},{5,197},{6,198},{7,199},{8... | collective-permute-start | bytes 884744 | tf_op jit(solution)/shard_map/ppermute | solution.py:43
  62.6 2.2 %fusion.5 = (f32[256]{0:T(256)S(1)}, f32[256]{0:T(256)S(1)}, f32[256,1536]{1,0:T(8,128)S(1)}) fusion(f32[256]{0:T(256)S(1)} %broadcast_multiply_fusion, bf16[1,256,1536]{2,1,0:T(8,128)(2,1)S(1)} %copy-done.6, bf16[256,2304]{1,0:T(8,128)(2,1)S(1)} %pad_maximum_fusion, bf16[1536,2304]{1,0:T(8,128)(2,1)S(1)} %bitcast.68), kind=kOutput, calls=%fused_computation.10 | convolution fusion | flops 1815084544 | bytes 10619904 | tf_op jit(solution)/shard_map/dot_general | solution.py:26
  64.9 1.4 %collective-permute-done.8 = bf16[8,48,384]{2,1,0:T(8,128)(2,1)S(1)} collective-permute-done((bf16[8,48,384]{2,1,0:T(8,128)(2,1)S(1)}, bf16[8,48,384]{2,1,0:T(8,128)(2,1)S(1)}, u32[]{:S(2)}, u32[]{:S(2)}) %collective-permute-start.8) | collective-permute-done | bytes 294944 | tf_op jit(solution)/shard_map/ppermute | solution.py:43
  66.3 0.1 add_convert_fusion.10
  66.3 0.1 add_convert_fusion.8
  66.5 1.2 %collective-permute-done.12 = bf16[8,48,384]{2,1,0:T(8,128)(2,1)S(1)} collective-permute-done((bf16[8,48,384]{2,1,0:T(8,128)(2,1)S(1)}, bf16[8,48,384]{2,1,0:T(8,128)(2,1)S(1)}, u32[]{:S(2)}, u32[]{:S(2)}) %collective-permute-start.12) | collective-permute-done | bytes 294944 | tf_op jit(solution)/shard_map/ppermute | solution.py:43
  67.8 2.9 %collective-permute-start.13 = (bf16[4,48,768]{2,1,0:T(8,128)(2,1)S(1)}, bf16[4,48,768]{2,1,0:T(8,128)(2,1)S(1)}, u32[]{:S(2)}, u32[]{:S(2)}) collective-permute-start(bf16[4,48,768]{2,1,0:T(8,128)(2,1)S(1)} %pad_maximum_fusion.5), channel_id=1, source_target_pairs={{0,33},{1,32},{2,35},{3,34},{4,37},{5,36},{6,39},{7,38},{8,41},{9,... | collective-permute-start | bytes 884744 | tf_op jit(solution)/shard_map/ppermute | solution.py:43
  70.7 1.6 %collective-permute-start.15 = (bf16[4,48,768]{2,1,0:T(8,128)(2,1)S(1)}, bf16[4,48,768]{2,1,0:T(8,128)(2,1)S(1)}, u32[]{:S(2)}, u32[]{:S(2)}) collective-permute-start(bf16[4,48,768]{2,1,0:T(8,128)(2,1)S(1)} %fusion.13), channel_id=1, source_target_pairs={{0,192},{1,193},{2,194},{3,195},{4,196},{5,197},{6,198},{7,199},{8... | collective-permute-start | bytes 884744 | tf_op jit(solution)/shard_map/ppermute | solution.py:43
  72.4 1.6 %collective-permute-start.16 = (bf16[4,48,768]{2,1,0:T(8,128)(2,1)S(1)}, bf16[4,48,768]{2,1,0:T(8,128)(2,1)S(1)}, u32[]{:S(2)}, u32[]{:S(2)}) collective-permute-start(bf16[4,48,768]{2,1,0:T(8,128)(2,1)S(1)} %fusion.12), channel_id=1, source_target_pairs={{0,64},{1,65},{2,66},{3,67},{4,68},{5,69},{6,70},{7,71},{8,72},{9,... | collective-permute-start | bytes 884744 | tf_op jit(solution)/shard_map/ppermute | solution.py:43
  74.0 0.5 fusion.37
  74.5 1.6 %collective-permute-done.13 = bf16[4,48,768]{2,1,0:T(8,128)(2,1)S(1)} collective-permute-done((bf16[4,48,768]{2,1,0:T(8,128)(2,1)S(1)}, bf16[4,48,768]{2,1,0:T(8,128)(2,1)S(1)}, u32[]{:S(2)}, u32[]{:S(2)}) %collective-permute-start.13) | collective-permute-done | bytes 294944 | tf_op jit(solution)/shard_map/ppermute | solution.py:43
  76.1 1.4 %collective-permute-done.14 = bf16[4,48,768]{2,1,0:T(8,128)(2,1)S(1)} collective-permute-done((bf16[4,48,768]{2,1,0:T(8,128)(2,1)S(1)}, bf16[4,48,768]{2,1,0:T(8,128)(2,1)S(1)}, u32[]{:S(2)}, u32[]{:S(2)}) %collective-permute-start.14) | collective-permute-done | bytes 294944 | tf_op jit(solution)/shard_map/ppermute | solution.py:43
  77.5 0.9 collective-permute-done.15
  78.4 1.9 %collective-permute-done.16 = bf16[4,48,768]{2,1,0:T(8,128)(2,1)S(1)} collective-permute-done((bf16[4,48,768]{2,1,0:T(8,128)(2,1)S(1)}, bf16[4,48,768]{2,1,0:T(8,128)(2,1)S(1)}, u32[]{:S(2)}, u32[]{:S(2)}) %collective-permute-start.16) | collective-permute-done | bytes 294944 | tf_op jit(solution)/shard_map/ppermute | solution.py:43
  80.3 0.1 add_convert_fusion.2
  80.4 0.1 add_convert_fusion.4
  80.6 0.5 collective-permute-start.17
  81.2 1.9 %collective-permute-start.18 = (bf16[48,1536]{1,0:T(8,128)(2,1)S(1)}, bf16[48,1536]{1,0:T(8,128)(2,1)S(1)}, u32[]{:S(2)}, u32[]{:S(2)}) collective-permute-start(bf16[48,1536]{1,0:T(8,128)(2,1)S(1)} %get-tuple-element.106), channel_id=1, source_target_pairs={{0,64},{1,65},{2,66},{3,67},{4,68},{5,69},{6,70},{7,71},{8,72},{9,... | collective-permute-start | bytes 442376 | tf_op jit(solution)/shard_map/ppermute | solution.py:43
  83.0 1.2 %collective-permute-start.19 = (bf16[48,1536]{1,0:T(8,128)(2,1)S(1)}, bf16[48,1536]{1,0:T(8,128)(2,1)S(1)}, u32[]{:S(2)}, u32[]{:S(2)}) collective-permute-start(bf16[48,1536]{1,0:T(8,128)(2,1)S(1)} %get-tuple-element.107), channel_id=1, source_target_pairs={{0,128},{1,129},{2,130},{3,131},{4,132},{5,133},{6,134},{7,135},{8... | collective-permute-start | bytes 442376 | tf_op jit(solution)/shard_map/ppermute | solution.py:43
  84.2 1.4 %collective-permute-start.20 = (bf16[48,1536]{1,0:T(8,128)(2,1)S(1)}, bf16[48,1536]{1,0:T(8,128)(2,1)S(1)}, u32[]{:S(2)}, u32[]{:S(2)}) collective-permute-start(bf16[48,1536]{1,0:T(8,128)(2,1)S(1)} %get-tuple-element.108), channel_id=1, source_target_pairs={{0,33},{1,32},{2,35},{3,34},{4,37},{5,36},{6,39},{7,38},{8,41},{9,... | collective-permute-start | bytes 442376 | tf_op jit(solution)/shard_map/ppermute | solution.py:43
  85.7 1.3 %collective-permute-start.21 = (bf16[48,1536]{1,0:T(8,128)(2,1)S(1)}, bf16[48,1536]{1,0:T(8,128)(2,1)S(1)}, u32[]{:S(2)}, u32[]{:S(2)}) collective-permute-start(bf16[48,1536]{1,0:T(8,128)(2,1)S(1)} %get-tuple-element.109), channel_id=1, source_target_pairs={{0,1},{1,0},{2,3},{3,2},{4,5},{5,4},{6,7},{7,6},{8,9},{9,8},{10,11... | collective-permute-start | bytes 442376 | tf_op jit(solution)/shard_map/ppermute | solution.py:43
  87.0 1.9 %collective-permute-start.22 = (bf16[48,1536]{1,0:T(8,128)(2,1)S(1)}, bf16[48,1536]{1,0:T(8,128)(2,1)S(1)}, u32[]{:S(2)}, u32[]{:S(2)}) collective-permute-start(bf16[48,1536]{1,0:T(8,128)(2,1)S(1)} %get-tuple-element.110), channel_id=1, source_target_pairs={{0,32},{1,33},{2,34},{3,35},{4,36},{5,37},{6,38},{7,39},{8,40},{9,... | collective-permute-start | bytes 442376 | tf_op jit(solution)/shard_map/ppermute | solution.py:43
  88.9 0.8 collective-permute-done.19
  89.7 0.1 fusion.21.refs_0_
  89.8 0.8 collective-permute-done.20
  90.6 0.2 collective-permute-done.21
  90.8 2.8 %collective-permute-done.22 = bf16[48,1536]{1,0:T(8,128)(2,1)S(1)} collective-permute-done((bf16[48,1536]{1,0:T(8,128)(2,1)S(1)}, bf16[48,1536]{1,0:T(8,128)(2,1)S(1)}, u32[]{:S(2)}, u32[]{:S(2)}) %collective-permute-start.22) | collective-permute-done | bytes 147488 | tf_op jit(solution)/shard_map/ppermute | solution.py:43
  93.6 0.1 fusion.18.refs_1_
  93.7 0.8 pieces.1
  94.5 8.3 %all-to-all-start = ((bf16[8,144,128]{2,1,0:T(8,128)(2,1)}), bf16[8,144,128]{2,1,0:T(8,128)(2,1)S(1)}, u32[]{:S(2)}, u32[]{:S(2)}) async-start(bf16[8,144,128]{2,1,0:T(8,128)(2,1)} %pieces.1), calls=%async_computation | async-start | bytes 589824 | tf_op jit(solution)/shard_map/all_to_all | solution.py:460
  102.9 1.0 fusion.7
  103.9 9.8 %all-to-all-done.in_ref = bf16[8,144,128]{2,1,0:T(8,128)(2,1)S(1)} async-done(((bf16[8,144,128]{2,1,0:T(8,128)(2,1)}), bf16[8,144,128]{2,1,0:T(8,128)(2,1)S(1)}, u32[]{:S(2)}, u32[]{:S(2)}) %all-to-all-start) | async-done | bytes 294944 | tf_op jit(solution)/shard_map/all_to_all | solution.py:460
  113.7 0.7 total.1
  (52 shorter events, 1.1 us)
Async XLA Ops:
  0.6 8.5 %copy-start.2 = (bf16[384,384]{1,0:T(8,128)(2,1)S(1)}, bf16[384,384]{1,0:T(8,128)(2,1)}, u32[]{:S(2)}) copy-start(bf16[384,384]{1,0:T(8,128)(2,1)} %constant.66.clone.order_ref) | copy-start | bytes 884740
  5.7 14.4 %collective-permute-start = (bf16[128,1536]{1,0:T(8,128)(2,1)S(1)}, bf16[128,1536]{1,0:T(8,128)(2,1)S(1)}, u32[]{:S(2)}, u32[]{:S(2)}) collective-permute-start(bf16[128,1536]{1,0:T(8,128)(2,1)S(1)} %get-tuple-element.60), channel_id=1, source_target_pairs={{0,1},{1,2},{2,3},{3,4},{4,5},{5,6},{6,7},{7,8},{8,9},{9,10},{10,1... | collective-permute-start | bytes 1179656 | tf_op jit(solution)/shard_map/ppermute | solution.py:32
  15.2 0.9 copy-start.3
  16.1 4.0 %copy-start = (bf16[256,768]{1,0:T(8,128)(2,1)}, bf16[256,768]{1,0:T(8,128)(2,1)S(1)}, u32[]{:S(2)}) copy-start(bf16[256,768]{1,0:T(8,128)(2,1)S(1)} %get-tuple-element.61.do_ref) | copy-start | bytes 1179652
  16.1 12.6 %collective-permute-start.1 = (bf16[768,512]{1,0:T(8,128)(2,1)}, bf16[768,512]{1,0:T(8,128)(2,1)}, u32[]{:S(2)}, u32[]{:S(2)}) collective-permute-start(bf16[768,512]{1,0:T(8,128)(2,1)} %get-tuple-element.67), channel_id=1, source_target_pairs={{0,16},{1,17},{2,18},{3,19},{4,20},{5,21},{6,22},{7,23},{8,24},{9,... | collective-permute-start | bytes 2359304 | tf_op jit(solution)/shard_map/ppermute | solution.py:43
  20.1 1.0 copy-start.1
  24.3 0.8 copy-start.5
  24.4 4.4 %copy-start.4 = (bf16[768,512]{1,0:T(8,128)(2,1)S(1)}, bf16[768,512]{1,0:T(8,128)(2,1)}, u32[]{:S(2)}) copy-start(bf16[768,512]{1,0:T(8,128)(2,1)} %copy-done.3) | copy-start | bytes 2359300
  25.1 3.6 %collective-permute-start.2 = (bf16[2,256,768]{2,1,0:T(8,128)(2,1)S(1)}, bf16[2,256,768]{2,1,0:T(8,128)(2,1)S(1)}, u32[]{:S(2)}, u32[]{:S(2)}) collective-permute-start(bf16[2,256,768]{2,1,0:T(8,128)(2,1)S(1)} %constant_dynamic-update-slice_fusion.refs_3_), channel_id=1, source_target_pairs={{0,16},{1,17},{2,18},{3,19},{4,20},{5,21},{6,22},{7,23},{8,24},{9,... | collective-permute-start | bytes 2359304 | tf_op jit(solution)/shard_map/ppermute | solution.py:43
  27.3 13.3 %collective-permute-start.3 = (bf16[2,128,768]{2,1,0:T(8,128)(2,1)}, bf16[2,128,768]{2,1,0:T(8,128)(2,1)S(1)}, u32[]{:S(2)}, u32[]{:S(2)}) collective-permute-start(bf16[2,128,768]{2,1,0:T(8,128)(2,1)} %copy-done.5), channel_id=1, source_target_pairs={{1,0},{2,1},{3,2},{4,3},{5,4},{6,5},{7,6},{8,7},{9,8},{10,9},{11,1... | collective-permute-start | bytes 1179656 | tf_op jit(solution)/shard_map/ppermute | solution.py:32
  40.7 7.4 %copy-start.7 = (bf16[768,1536]{1,0:T(8,128)(2,1)S(1)}, bf16[768,1536]{1,0:T(8,128)(2,1)}, u32[]{:S(2)}) copy-start(bf16[768,1536]{1,0:T(8,128)(2,1)} %out_ref.1) | copy-start | bytes 7077892
  40.8 21.8 %slice-start = ((s8[7077888]{0:T(1024)(128)(4,1)}), s8[4194304]{0:T(1024)(128)(4,1)S(1)}, s32[]{:S(2)}) async-start(s8[7077888]{0:T(1024)(128)(4,1)} %bitcast.67), calls=%async_computation.1 | async-start | bytes 8388608
  40.8 9.0 %collective-permute-start.5 = (bf16[8,48,384]{2,1,0:T(8,128)(2,1)S(1)}, bf16[8,48,384]{2,1,0:T(8,128)(2,1)S(1)}, u32[]{:S(2)}, u32[]{:S(2)}) collective-permute-start(bf16[8,48,384]{2,1,0:T(8,128)(2,1)S(1)} %get-tuple-element.82), channel_id=1, source_target_pairs={{0,1},{1,0},{2,3},{3,2},{4,5},{5,4},{6,7},{7,6},{8,9},{9,8},{10,11... | collective-permute-start | bytes 884744 | tf_op jit(solution)/shard_map/ppermute | solution.py:43
  43.6 9.0 %collective-permute-start.7 = (bf16[8,48,384]{2,1,0:T(8,128)(2,1)S(1)}, bf16[8,48,384]{2,1,0:T(8,128)(2,1)S(1)}, u32[]{:S(2)}, u32[]{:S(2)}) collective-permute-start(bf16[8,48,384]{2,1,0:T(8,128)(2,1)S(1)} %get-tuple-element.86), channel_id=1, source_target_pairs={{0,33},{1,32},{2,35},{3,34},{4,37},{5,36},{6,39},{7,38},{8,41},{9,... | collective-permute-start | bytes 884744 | tf_op jit(solution)/shard_map/ppermute | solution.py:43
  45.2 7.8 %collective-permute-start.9 = (bf16[8,48,384]{2,1,0:T(8,128)(2,1)S(1)}, bf16[8,48,384]{2,1,0:T(8,128)(2,1)S(1)}, u32[]{:S(2)}, u32[]{:S(2)}) collective-permute-start(bf16[8,48,384]{2,1,0:T(8,128)(2,1)S(1)} %get-tuple-element.90), channel_id=1, source_target_pairs={{0,64},{1,65},{2,66},{3,67},{4,68},{5,69},{6,70},{7,71},{8,72},{9,... | collective-permute-start | bytes 884744 | tf_op jit(solution)/shard_map/ppermute | solution.py:43
  45.7 8.2 %collective-permute-start.11 = (bf16[8,48,384]{2,1,0:T(8,128)(2,1)S(1)}, bf16[8,48,384]{2,1,0:T(8,128)(2,1)S(1)}, u32[]{:S(2)}, u32[]{:S(2)}) collective-permute-start(bf16[8,48,384]{2,1,0:T(8,128)(2,1)S(1)} %get-tuple-element.94), channel_id=1, source_target_pairs={{0,192},{1,193},{2,194},{3,195},{4,196},{5,197},{6,198},{7,199},{8... | collective-permute-start | bytes 884744 | tf_op jit(solution)/shard_map/ppermute | solution.py:43
  49.7 4.2 %collective-permute-start.4 = (bf16[2,256,768]{2,1,0:T(8,128)(2,1)S(1)}, bf16[2,256,768]{2,1,0:T(8,128)(2,1)S(1)}, u32[]{:S(2)}, u32[]{:S(2)}) collective-permute-start(bf16[2,256,768]{2,1,0:T(8,128)(2,1)S(1)} %pad_maximum_fusion.1.refs_3_), channel_id=1, source_target_pairs={{0,16},{1,17},{2,18},{3,19},{4,20},{5,21},{6,22},{7,23},{8,24},{9,... | collective-permute-start | bytes 2359304 | tf_op jit(solution)/shard_map/ppermute | solution.py:43
  49.9 12.7 %slice-start.1 = ((s8[7077888]{0:T(1024)(128)(4,1)}), s8[2883584]{0:T(1024)(128)(4,1)S(1)}, s32[]{:S(2)}) async-start(s8[7077888]{0:T(1024)(128)(4,1)} %bitcast.67), calls=%async_computation.2 | async-start | bytes 5767168
  53.9 8.7 %copy-start.6 = (bf16[1,256,1536]{2,1,0:T(8,128)(2,1)S(1)}, bf16[1,256,1536]{2,1,0:T(8,128)(2,1)}, u32[]{:S(2)}) copy-start(bf16[1,256,1536]{2,1,0:T(8,128)(2,1)} %param.6) | copy-start | bytes 2359300
  56.9 7.9 %collective-permute-start.6 = (bf16[8,48,384]{2,1,0:T(8,128)(2,1)S(1)}, bf16[8,48,384]{2,1,0:T(8,128)(2,1)S(1)}, u32[]{:S(2)}, u32[]{:S(2)}) collective-permute-start(bf16[8,48,384]{2,1,0:T(8,128)(2,1)S(1)} %get-tuple-element.84), channel_id=1, source_target_pairs={{0,1},{1,0},{2,3},{3,2},{4,5},{5,4},{6,7},{7,6},{8,9},{9,8},{10,11... | collective-permute-start | bytes 884744 | tf_op jit(solution)/shard_map/ppermute | solution.py:43
  58.0 8.3 %collective-permute-start.8 = (bf16[8,48,384]{2,1,0:T(8,128)(2,1)S(1)}, bf16[8,48,384]{2,1,0:T(8,128)(2,1)S(1)}, u32[]{:S(2)}, u32[]{:S(2)}) collective-permute-start(bf16[8,48,384]{2,1,0:T(8,128)(2,1)S(1)} %get-tuple-element.88), channel_id=1, source_target_pairs={{0,33},{1,32},{2,35},{3,34},{4,37},{5,36},{6,39},{7,38},{8,41},{9,... | collective-permute-start | bytes 884744 | tf_op jit(solution)/shard_map/ppermute | solution.py:43
  58.9 7.5 %collective-permute-start.10 = (bf16[8,48,384]{2,1,0:T(8,128)(2,1)S(1)}, bf16[8,48,384]{2,1,0:T(8,128)(2,1)S(1)}, u32[]{:S(2)}, u32[]{:S(2)}) collective-permute-start(bf16[8,48,384]{2,1,0:T(8,128)(2,1)S(1)} %get-tuple-element.92), channel_id=1, source_target_pairs={{0,64},{1,65},{2,66},{3,67},{4,68},{5,69},{6,70},{7,71},{8,72},{9,... | collective-permute-start | bytes 884744 | tf_op jit(solution)/shard_map/ppermute | solution.py:43
  61.0 6.7 %collective-permute-start.12 = (bf16[8,48,384]{2,1,0:T(8,128)(2,1)S(1)}, bf16[8,48,384]{2,1,0:T(8,128)(2,1)S(1)}, u32[]{:S(2)}, u32[]{:S(2)}) collective-permute-start(bf16[8,48,384]{2,1,0:T(8,128)(2,1)S(1)} %get-tuple-element.96), channel_id=1, source_target_pairs={{0,192},{1,193},{2,194},{3,195},{4,196},{5,197},{6,198},{7,199},{8... | collective-permute-start | bytes 884744 | tf_op jit(solution)/shard_map/ppermute | solution.py:43
  67.8 8.2 %collective-permute-start.13 = (bf16[4,48,768]{2,1,0:T(8,128)(2,1)S(1)}, bf16[4,48,768]{2,1,0:T(8,128)(2,1)S(1)}, u32[]{:S(2)}, u32[]{:S(2)}) collective-permute-start(bf16[4,48,768]{2,1,0:T(8,128)(2,1)S(1)} %pad_maximum_fusion.5), channel_id=1, source_target_pairs={{0,33},{1,32},{2,35},{3,34},{4,37},{5,36},{6,39},{7,38},{8,41},{9,... | collective-permute-start | bytes 884744 | tf_op jit(solution)/shard_map/ppermute | solution.py:43
  70.7 6.7 %collective-permute-start.14 = (bf16[4,48,768]{2,1,0:T(8,128)(2,1)S(1)}, bf16[4,48,768]{2,1,0:T(8,128)(2,1)S(1)}, u32[]{:S(2)}, u32[]{:S(2)}) collective-permute-start(bf16[4,48,768]{2,1,0:T(8,128)(2,1)S(1)} %fusion.14), channel_id=1, source_target_pairs={{0,1},{1,0},{2,3},{3,2},{4,5},{5,4},{6,7},{7,6},{8,9},{9,8},{10,11... | collective-permute-start | bytes 884744 | tf_op jit(solution)/shard_map/ppermute | solution.py:43
  70.7 7.6 %collective-permute-start.15 = (bf16[4,48,768]{2,1,0:T(8,128)(2,1)S(1)}, bf16[4,48,768]{2,1,0:T(8,128)(2,1)S(1)}, u32[]{:S(2)}, u32[]{:S(2)}) collective-permute-start(bf16[4,48,768]{2,1,0:T(8,128)(2,1)S(1)} %fusion.13), channel_id=1, source_target_pairs={{0,192},{1,193},{2,194},{3,195},{4,196},{5,197},{6,198},{7,199},{8... | collective-permute-start | bytes 884744 | tf_op jit(solution)/shard_map/ppermute | solution.py:43
  72.4 7.9 %collective-permute-start.16 = (bf16[4,48,768]{2,1,0:T(8,128)(2,1)S(1)}, bf16[4,48,768]{2,1,0:T(8,128)(2,1)S(1)}, u32[]{:S(2)}, u32[]{:S(2)}) collective-permute-start(bf16[4,48,768]{2,1,0:T(8,128)(2,1)S(1)} %fusion.12), channel_id=1, source_target_pairs={{0,64},{1,65},{2,66},{3,67},{4,68},{5,69},{6,70},{7,71},{8,72},{9,... | collective-permute-start | bytes 884744 | tf_op jit(solution)/shard_map/ppermute | solution.py:43
  80.6 6.4 %collective-permute-start.17 = (bf16[48,1536]{1,0:T(8,128)(2,1)S(1)}, bf16[48,1536]{1,0:T(8,128)(2,1)S(1)}, u32[]{:S(2)}, u32[]{:S(2)}) collective-permute-start(bf16[48,1536]{1,0:T(8,128)(2,1)S(1)} %get-tuple-element.105), channel_id=1, source_target_pairs={{0,192},{1,193},{2,194},{3,195},{4,196},{5,197},{6,198},{7,199},{8... | collective-permute-start | bytes 442376 | tf_op jit(solution)/shard_map/ppermute | solution.py:43
  81.2 7.8 %collective-permute-start.18 = (bf16[48,1536]{1,0:T(8,128)(2,1)S(1)}, bf16[48,1536]{1,0:T(8,128)(2,1)S(1)}, u32[]{:S(2)}, u32[]{:S(2)}) collective-permute-start(bf16[48,1536]{1,0:T(8,128)(2,1)S(1)} %get-tuple-element.106), channel_id=1, source_target_pairs={{0,64},{1,65},{2,66},{3,67},{4,68},{5,69},{6,70},{7,71},{8,72},{9,... | collective-permute-start | bytes 442376 | tf_op jit(solution)/shard_map/ppermute | solution.py:43
  83.0 6.6 %collective-permute-start.19 = (bf16[48,1536]{1,0:T(8,128)(2,1)S(1)}, bf16[48,1536]{1,0:T(8,128)(2,1)S(1)}, u32[]{:S(2)}, u32[]{:S(2)}) collective-permute-start(bf16[48,1536]{1,0:T(8,128)(2,1)S(1)} %get-tuple-element.107), channel_id=1, source_target_pairs={{0,128},{1,129},{2,130},{3,131},{4,132},{5,133},{6,134},{7,135},{8... | collective-permute-start | bytes 442376 | tf_op jit(solution)/shard_map/ppermute | solution.py:43
  84.2 6.4 %collective-permute-start.20 = (bf16[48,1536]{1,0:T(8,128)(2,1)S(1)}, bf16[48,1536]{1,0:T(8,128)(2,1)S(1)}, u32[]{:S(2)}, u32[]{:S(2)}) collective-permute-start(bf16[48,1536]{1,0:T(8,128)(2,1)S(1)} %get-tuple-element.108), channel_id=1, source_target_pairs={{0,33},{1,32},{2,35},{3,34},{4,37},{5,36},{6,39},{7,38},{8,41},{9,... | collective-permute-start | bytes 442376 | tf_op jit(solution)/shard_map/ppermute | solution.py:43
  85.7 5.1 %collective-permute-start.21 = (bf16[48,1536]{1,0:T(8,128)(2,1)S(1)}, bf16[48,1536]{1,0:T(8,128)(2,1)S(1)}, u32[]{:S(2)}, u32[]{:S(2)}) collective-permute-start(bf16[48,1536]{1,0:T(8,128)(2,1)S(1)} %get-tuple-element.109), channel_id=1, source_target_pairs={{0,1},{1,0},{2,3},{3,2},{4,5},{5,4},{6,7},{7,6},{8,9},{9,8},{10,11... | collective-permute-start | bytes 442376 | tf_op jit(solution)/shard_map/ppermute | solution.py:43
  87.0 6.6 %collective-permute-start.22 = (bf16[48,1536]{1,0:T(8,128)(2,1)S(1)}, bf16[48,1536]{1,0:T(8,128)(2,1)S(1)}, u32[]{:S(2)}, u32[]{:S(2)}) collective-permute-start(bf16[48,1536]{1,0:T(8,128)(2,1)S(1)} %get-tuple-element.110), channel_id=1, source_target_pairs={{0,32},{1,33},{2,34},{3,35},{4,36},{5,37},{6,38},{7,39},{8,40},{9,... | collective-permute-start | bytes 442376 | tf_op jit(solution)/shard_map/ppermute | solution.py:43
  94.5 19.2 %all-to-all-start = ((bf16[8,144,128]{2,1,0:T(8,128)(2,1)}), bf16[8,144,128]{2,1,0:T(8,128)(2,1)S(1)}, u32[]{:S(2)}, u32[]{:S(2)}) async-start(bf16[8,144,128]{2,1,0:T(8,128)(2,1)} %pieces.1), calls=%async_computation | async-start | bytes 589824 | tf_op jit(solution)/shard_map/all_to_all | solution.py:460

commit v2 on v1

--- a/solution.py
+++ b/solution.py
@@ -28,8 +28,7 @@
 
 def from_behind(value, axis, by):
     peers = lax.axis_size(axis)
-    pairs = [(i, i + by) for i in range(peers) if 0 <= i + by < peers]
-    return lax.ppermute(value, axis, pairs)
+    return lax.ppermute(value, axis, [(i, (i + by) % peers) for i in range(peers)])
 
 
 def flat(y, xh, core, z, xl):
@@ -106,11 +105,17 @@
     return jnp.asarray(np.eye(width // Y, dtype=np.float32)[order], BF16)
 
 
-def normalize(rows_in):
+def statistics(rows_in):
     average = jnp.mean(rows_in, axis=-1, keepdims=True)
     centered = rows_in - average
     variance = jnp.mean(centered * centered, axis=-1, keepdims=True)
-    return centered * lax.rsqrt(variance + epsilon)
+    return average, lax.rsqrt(variance + epsilon)
+
+
+def normalize_grad(rows_in, average, inverse, grad):
+    normed = (rows_in - average) * inverse
+    along = jnp.mean(grad * normed, axis=-1, keepdims=True)
+    return inverse * (grad - jnp.mean(grad, axis=-1, keepdims=True) - normed * along)
 
 
 SMEM_SPEC = pl.BlockSpec(memory_space=pltpu.SMEM)
@@ -143,15 +148,19 @@
     return copies
 
 
-BLOCK = 384
-
-
-def project_kernel(frames_ref, weight_ref, normed_ref, keys_ref, tail_ref, rows, weight, row_sem, sems):
+BLOCK = 768
+
+
+def project_kernel(frames_ref, weight_ref, normed_ref, keys_ref, tail_ref, stats_ref, rows, weight, row_sem, sems):
     whole = pltpu.make_async_copy(frames_ref, rows, row_sem)
     whole.start()
     copies = fetch(weight_ref, weight, sems, BLOCK, weight_ref.shape[1] - weight.shape[1])
     whole.wait()
-    normed_ref[...] = normalize(rows[...].astype(F32)).astype(BF16)
+    values = rows[...].astype(F32)
+    average, inverse = statistics(values)
+    for n, column in enumerate((average, inverse)):
+        stats_ref[n : n + 1, :] = jnp.broadcast_to(column, (column.shape[0], PAIR)).T[:1]
+    normed_ref[...] = ((values - average) * inverse).astype(BF16)
     for i, copy in enumerate(copies):
         copy.wait()
         here = slice(i * BLOCK, (i + 1) * BLOCK)
@@ -166,8 +175,13 @@
     return pl.pallas_call(
         project_kernel,
         in_specs=[HBM_SPEC, HBM_SPEC],
-        out_specs=[VMEM_SPEC] * 3,
-        out_shape=[pltpu.VMEM((rows, width), BF16), pltpu.VMEM((rows, columns), BF16), pltpu.VMEM((CONTEXT, columns), BF16)],
+        out_specs=[VMEM_SPEC] * 4,
+        out_shape=[
+            pltpu.VMEM((rows, width), BF16),
+            pltpu.VMEM((rows, columns), BF16),
+            pltpu.VMEM((CONTEXT, columns), BF16),
+            pltpu.VMEM((2, rows), F32),
+        ],
         scratch_shapes=[
             pltpu.VMEM((rows, width), BF16),
             pltpu.VMEM((width, columns), BF16),
@@ -184,9 +198,9 @@
                   query_ref, grad_ref, keep_ref, send_ref, cotangent, weight, outer, sem, sems, out_sem):
     whole = pltpu.make_async_copy(cotangent_ref, cotangent, sem)
     whole.start()
+    first = pltpu.make_async_copy(out_ref, outer, out_sem)
+    first.start()
     copies = fetch(weight_ref, weight, sems, BLOCK)
-    last = pltpu.make_async_copy(out_ref, outer, out_sem)
-    last.start()
     rows = order_ref.shape[0]
     half = rows // CORES
     tokens = normed_ref.shape[0]
@@ -207,14 +221,14 @@
                 send_ref[there, columns] = turned[:half]
 
     turn(normed_ref, slice(0, tokens))
+    whole.wait()
+    turn(cotangent, slice(tokens, 2 * tokens))
+    first.wait()
+    grad_ref[...] = dot(cotangent[...], outer[...], NT).astype(BF16)
     for i, copy in enumerate(copies):
         copy.wait()
         here = slice(i * BLOCK, (i + 1) * BLOCK)
         query_ref[:, here] = dot(normed_ref[...], weight[:, here]).astype(BF16)
-    whole.wait()
-    turn(cotangent, slice(tokens, 2 * tokens))
-    last.wait()
-    grad_ref[...] = dot(cotangent[...], outer[...], NT).astype(BF16)
 
 
 def second(normed, cotangent, w_qkv, w_out, core):
@@ -295,8 +309,9 @@
     attend(places[1] + CONTEXT, places[0], inner, operands, results)
 
 
-def early_kernel(places, q_ref, kv_ref, halo_ref, do_ref, add_ref, out_ref, head_ref, back_ref):
+def early_kernel(places, q_ref, kv_ref, halo_ref, do_ref, late_ref, add_ref, out_ref, head_ref, back_ref):
     inner = q_ref.shape[1]
+    out_ref[:, CONTEXT:, :] = late_ref[...]
 
     def operands(pair):
         at = slice(pair * PAIR, (pair + 1) * PAIR)
@@ -307,8 +322,8 @@
 
     def results(pair, mixed, dq, dk, dv):
         at = slice(pair * PAIR, (pair + 1) * PAIR)
-        out_ref[0, :, at] = mixed
-        out_ref[1, :, at] = dq
+        out_ref[0, :CONTEXT, at] = mixed
+        out_ref[1, :CONTEXT, at] = dq
         for n, grad in enumerate((dk, dv)):
             back_ref[n, :, at] = grad[:CONTEXT].astype(BF16)
             head_ref[n, :, at] = (grad[CONTEXT:] + add_ref[n, :, at]).astype(BF16)
@@ -316,12 +331,29 @@
     attend(places[1], places[0], inner, operands, results)
 
 
-def attention(kernel, places, operands, inner, types, name):
+def join_kernel(head_ref, tail_ref, back_ref, out_ref):
+    out_ref[:, :CONTEXT, :] = head_ref[...]
+    out_ref[:, CONTEXT:, :] = (tail_ref[...] + back_ref[...].astype(F32)).astype(BF16)
+
+
+def join(head, tail, back):
+    return pl.pallas_call(
+        join_kernel,
+        in_specs=[VMEM_SPEC] * 3,
+        out_specs=VMEM_SPEC,
+        out_shape=pltpu.VMEM((2, 2 * CONTEXT, head.shape[2]), BF16),
+        compiler_params=params(8),
+        cost_estimate=cost(1, 1),
+        name="join",
+    )(*[in_vmem(o) for o in (head, tail, back)])
+
+
+def attention(kernel, places, operands, inner, rows, types, name):
     return pl.pallas_call(
         kernel,
         in_specs=[SMEM_SPEC] + [VMEM_SPEC] * len(operands),
         out_specs=[VMEM_SPEC] * len(types),
-        out_shape=[pltpu.VMEM((2, CONTEXT, inner), dtype) for dtype in types],
+        out_shape=[pltpu.VMEM((2, n, inner), dtype) for n, dtype in zip(rows, types)],
         compiler_params=params(24),
         cost_estimate=cost(28 * CONTEXT * 2 * CONTEXT * inner, 16 * CONTEXT * inner, CONTEXT * 4 * inner),
         name=name,
@@ -357,7 +389,7 @@
         out_shape=[out] * (2 * routes),
         scratch_shapes=[pltpu.VMEM((routes, CHUNKS, rows // CHUNKS, columns), F32)],
         compiler_params=params(24),
-        cost_estimate=cost(4 * rows * tokens * columns * routes, 4 * rows * (tokens + columns * routes)),
+        cost_estimate=cost(1, 1),
         name="weight_sections",
     )(chunks, *[in_vmem(o) for o in (left, left_other, right, right_other)])
     return outs[:routes], outs[routes:]
@@ -406,40 +438,47 @@
     routes = range(len(ROUTES))
     chunks = jnp.stack([jnp.stack([chunk_at(r, slot, y, xh, xl) for slot in range(CHUNKS)]) for r in routes])
 
-    normed, keys, tail = project(frame_rows, w_qkv)
+    frame_rows, places, chunks = lax.optimization_barrier((frame_rows, places, chunks))
+    normed, keys, tail, stats = project(frame_rows, w_qkv)
     received = from_behind(tail, "seq", 1)
     queries, attended_grad, left, left_out = second(normed, grad_rows, w_qkv, w_out, core)
     left_other = to_device(left_out, to_core)
     late, late_head, late_tail = attention(
-        late_kernel, places, (queries, keys, attended_grad), inner, (BF16, F32, F32), "attention_late"
+        late_kernel, places, (queries, keys, attended_grad), inner, (CONTEXT,) * 3, (BF16, F32, F32), "attention_late"
     )
-    early, kv_head, halo = attention(
-        early_kernel, places, (queries, keys, received, attended_grad, late_head), inner, (BF16,) * 3, "attention_early"
+    own, kv_head, halo = attention(
+        early_kernel,
+        places,
+        (queries, keys, received, attended_grad, late, late_head),
+        inner,
+        (row_count, CONTEXT, CONTEXT),
+        (BF16,) * 3,
+        "attention_early",
     )
     returned = from_behind(halo, "seq", -1)
-    own = jnp.concatenate([early, late], axis=1)
     own_other = to_device(own, to_core)
     keep_a, send_a = weight_sections(chunks, left, left_other, (1, 0), own, own_other)
-    attended, late_tail, send_a = lax.optimization_barrier((own[0], late_tail, send_a))
-    got_a = [to_device(send_a[r], ROUTES[r][0]) for r in routes]
-
-    kv_total = jnp.concatenate([kv_head, plus(late_tail, returned)], axis=1)
+    attended, send_a = lax.optimization_barrier((own[0], send_a))
+    block_out = dot(attended, w_out).astype(BF16)
+    block_out, late_tail = lax.optimization_barrier((block_out, late_tail))
+    got_a = [None] + [to_device(send_a[r], ROUTES[r][0]) for r in routes[1:]]
+    got_a[1], got_a[2], late_tail = lax.optimization_barrier((got_a[1], got_a[2], late_tail))
+
+    kv_total, send_first = lax.optimization_barrier((join(kv_head, late_tail, returned), send_a[0]))
+    got_a[0] = to_device(send_first, ROUTES[0][0])
     kv_other = to_device(kv_total, to_core)
     keep_b, send_b = weight_sections(chunks, left, left_other, (0, 0), kv_total, kv_other)
     projected_grad = jnp.concatenate([own[1], kv_total[0], kv_total[1]], axis=1)
-    projected_grad, send_b = lax.optimization_barrier((projected_grad, send_b))
     got_b = [to_device(send_b[r], ROUTES[r][0]) for r in routes]
-
-    block_out = dot(attended, w_out).astype(BF16)
-    normed_grad = dot(projected_grad, w_qkv, NT).astype(BF16)
-    _, norm_back = jax.vjp(normalize, frame_rows.astype(F32))
-    (frame_grad,) = norm_back(normed_grad.astype(F32))
 
     totals = [
         jnp.concatenate([plus(keep_a[r], got_a[r]), plus(keep_b[r], got_b[r])], axis=-1) for r in routes
     ]
     count = totals[0].shape[0] // 2
-    sends = lax.optimization_barrier([t[count:] for t in totals])
+    sends = [t[count:] for t in totals]
+    projected_grad, frame_rows, stats, sends = lax.optimization_barrier((projected_grad, frame_rows, stats, sends))
+    normed_grad = dot(projected_grad, w_qkv, NT).astype(BF16)
+    frame_grad = normalize_grad(frame_rows.astype(F32), stats[0][:, None], stats[1][:, None], normed_grad.astype(F32))
     gots = lax.optimization_barrier([to_device(sends[r], ROUTES[r][1]) for r in routes])
     totals = [plus(totals[r][:count], gots[r]) for r in routes]
     groups = [jnp.concatenate(totals[:2], axis=-1), jnp.concatenate(totals[2:], axis=-1)]

time: 117 us -> 103 us (0.88); the launches traced: 114 us -> 102 us
  starting transfers between devices: 40.9 us -> 36 us
  Pallas kernels: 24.8 us -> 22.2 us
  local copies, waits for them, and re-layouts: 3.06 us -> 0.52 us
  waiting for transfers between devices: 35.6 us -> 33.7 us
  other arithmetic: 4.46 us -> 2.79 us
    ppermute x2, waiting for transfers between devices: 9 us -> 5.85 us  [from_behind(): lax.ppermute(value, axis, [(i, (i + by) % peers) for i in range(peers)])]
    all_to_all x1, starting transfers between devices: 8.33 us -> 5.54 us  [on_device(): lax.all_to_all(shares, 'seq', 0, 0, axis_index_groups=rings, tiled=True)]
    unnamed x21 -> x12, local copies, waits for them, and re-layouts: 2.6 us -> 0.03 us
    reduce_sum x2 -> x0, other arithmetic: 1.82 us -> none  [the longest x1 1.32 us: normalize(): average = jnp.mean(rows_in, axis=-1, keepdims=True)]
    ppermute x21, waiting for transfers between devices: 16.8 us -> 18.4 us  [to_device(): return lax.ppermute(value, ('dp', 'seq'), pairs)]
  transfers between devices with their start and end apart: 24 -> 24, of which waited for: 16 -> 14; matrix products, arithmetic and copies ran while one was open for 7% -> 7% of each run, Pallas kernels for 13% -> 16%
where the time goes in v2:
time: 103 us; the launch traced here: 102 us
  starting transfers between devices  36 us (35%)
  waiting for transfers between devices  33.7 us (33%)
  Pallas kernels  22.2 us (22%)
  matrix products  4.93 us (5%)
  other arithmetic  2.79 us (3%)
  between operations  1.64 us (2%)
    ppermute x21, starting transfers between devices, to_device(): return lax.ppermute(value, ('dp', 'seq'), pairs)  26.9 us
    ppermute x21, waiting for transfers between devices, to_device(): return lax.ppermute(value, ('dp', 'seq'), pairs)  18.4 us
    all_to_all x1, waiting for transfers between devices, on_device(): lax.all_to_all(shares, 'seq', 0, 0, axis_index_groups=rings, tiled=True)  9.47 us
    pallas_call x2, Pallas kernels, attention(): pl.pallas_call(kernel, in_specs=[SMEM_SPEC] + [VMEM_SPEC] * len(operands)...  6.54 us
    ppermute x2, waiting for transfers between devices, from_behind(): lax.ppermute(value, axis, [(i, (i + by) % peers) for i in range(peers)])  5.85 us
    all_to_all x1, starting transfers between devices, on_device(): lax.all_to_all(shares, 'seq', 0, 0, axis_index_groups=rings, tiled=True)  5.54 us
    pallas_call x1, Pallas kernels, second(): pl.pallas_call(second_kernel, in_specs=[SMEM_SPEC, VMEM_SPEC, VMEM_SPEC,...  5.18 us
    dot_general x2, matrix products, dot(): return lax.dot_general(a, b, dims, preferred_element_type=F32)  4.93 us
  transfers between devices with their start and end apart: 24, of which 14 were waited for; matrix products, arithmetic and copies ran while one was open for 7% of the time, Pallas kernels for 16%

profile of v2, /device:TPU:8, one launch (start us, length us, event | category | flops | bytes accessed | tf_op | source)
XLA Modules:
  0.0 101.9 jit_solution(17543482965592207084)
XLA Ops:
  0.7 0.1 stack.153
  0.8 0.1 stack.151
  0.9 0.1 stack.74
  1.0 0.1 stack.72
  1.8 0.1 pad_add_fusion.1.places
  1.9 4.3 %project.1 = (bf16[256,1536]{1,0:T(8,128)(2,1)S(1)}, bf16[256,1536]{1,0:T(8,128)(2,1)S(1)}, bf16[128,1536]{1,0:T(8,128)(2,1)S(1)}, f32[2,256]{1,0:T(2,128)S(1)}) custom-call(bf16[256,1536]{1,0:T(8,128)(2,1)} %bitcast.65, bf16[1536,2304]{1,0:T(8,128)(2,1)} %weight_ref.3), custom_call_target="tpu_custom_call" | custom-call | flops 1207959552 | bytes 4718592 | tf_op jit(solution)/shard_map/project/pallas_call | solution.py:175
  6.2 1.6 %collective-permute-start = (bf16[128,1536]{1,0:T(8,128)(2,1)S(1)}, bf16[128,1536]{1,0:T(8,128)(2,1)S(1)}, u32[]{:S(2)}, u32[]{:S(2)}) collective-permute-start(bf16[128,1536]{1,0:T(8,128)(2,1)S(1)} %get-tuple-element.70), channel_id=1, source_target_pairs={{0,1},{1,2},{2,3},{3,4},{4,5},{5,6},{6,7},{7,8},{8,9},{9,10},{10,1... | collective-permute-start | bytes 1179656 | tf_op jit(solution)/shard_map/ppermute | solution.py:31
  7.8 5.2 %second.1 = (bf16[256,768]{1,0:T(8,128)(2,1)S(1)}, bf16[256,768]{1,0:T(8,128)(2,1)S(1)}, bf16[768,512]{1,0:T(8,128)(2,1)S(1)}, bf16[768,512]{1,0:T(8,128)(2,1)S(1)}) custom-call(s32[1]{0:T(128)} %bitcast.22.places, bf16[384,384]{1,0:T(8,128)(2,1)S(1)} %copy-done, bf16[256,1536]{1,0:T(8,128)(2,1)S(1)} %get-tuple-element.67.normed_ref, ...), custom_call_target="tpu_custom_call" | custom-call | flops 2415919104 | bytes 9437184 | tf_op jit(solution)/shard_map/second/pallas_call | solution.py:239
  13.0 0.1 collective-permute-start.1
  13.1 3.3 %attention_late.1 = (bf16[2,128,768]{2,1,0:T(8,128)(2,1)S(1)}, f32[2,128,768]{2,1,0:T(8,128)S(1)}, f32[2,128,768]{2,1,0:T(8,128)S(1)}) custom-call(s32[2]{0:T(128)S(1)} %pad_add_fusion.1.places, bf16[256,768]{1,0:T(8,128)(2,1)S(1)} %get-tuple-element.68.q_ref, bf16[256,1536]{1,0:T(8,128)(2,1)S(1)} %get-tuple-element.69.kv_ref, ...), custom_call_target="tpu_custom_call" | custom-call | flops 704643072 | bytes 1572864 | tf_op jit(solution)/shard_map/attention_late/pallas_call | solution.py:352
  16.3 5.9 %collective-permute-done.halo_ref = bf16[128,1536]{1,0:T(8,128)(2,1)S(1)} collective-permute-done((bf16[128,1536]{1,0:T(8,128)(2,1)S(1)}, bf16[128,1536]{1,0:T(8,128)(2,1)S(1)}, u32[]{:S(2)}, u32[]{:S(2)}) %collective-permute-start) | collective-permute-done | bytes 393248 | tf_op jit(solution)/shard_map/ppermute | solution.py:31
  22.2 3.3 %attention_early.1 = (bf16[2,256,768]{2,1,0:T(8,128)(2,1)S(1)}, bf16[2,128,768]{2,1,0:T(8,128)(2,1)S(1)}, bf16[2,128,768]{2,1,0:T(8,128)(2,1)S(1)}) custom-call(s32[2]{0:T(128)S(1)} %pad_add_fusion.1.places, bf16[256,768]{1,0:T(8,128)(2,1)S(1)} %get-tuple-element.68.q_ref, bf16[256,1536]{1,0:T(8,128)(2,1)S(1)} %get-tuple-element.69.kv_ref, ...), custom_call_target="tpu_custom_call" | custom-call | flops 704643072 | bytes 1572864 | tf_op jit(solution)/shard_map/attention_early/pallas_call | solution.py:352
  25.5 0.1 collective-permute-start.2
  25.6 2.0 %collective-permute-start.5 = (bf16[2,128,768]{2,1,0:T(8,128)(2,1)S(1)}, bf16[2,128,768]{2,1,0:T(8,128)(2,1)S(1)}, u32[]{:S(2)}, u32[]{:S(2)}) collective-permute-start(bf16[2,128,768]{2,1,0:T(8,128)(2,1)S(1)} %get-tuple-element.90), channel_id=1, source_target_pairs={{0,15},{1,0},{2,1},{3,2},{4,3},{5,4},{6,5},{7,6},{8,7},{9,8},{10,9... | collective-permute-start | bytes 1179656 | tf_op jit(solution)/shard_map/ppermute | solution.py:31
  27.6 0.2 collective-permute-done.2.refs_4_
  27.9 2.3 %weight_sections.2 = (bf16[8,48,384]{2,1,0:T(8,128)(2,1)S(1)}, bf16[8,48,384]{2,1,0:T(8,128)(2,1)S(1)}, bf16[8,48,384]{2,1,0:T(8,128)(2,1)S(1)}, bf16[8,48,384]{...) custom-call(s32[4,16]{1,0:T(4,128)S(1)} %pad_add_fusion.refs_0_, ...), custom_call_target="tpu_custom_call" | custom-call | flops 1 | bytes 1 | tf_op jit(solution)/shard_map/weight_sections/pallas_call | solution.py:385
  30.2 1.4 %collective-permute-start.3 = (bf16[8,48,384]{2,1,0:T(8,128)(2,1)S(1)}, bf16[8,48,384]{2,1,0:T(8,128)(2,1)S(1)}, u32[]{:S(2)}, u32[]{:S(2)}) collective-permute-start(bf16[8,48,384]{2,1,0:T(8,128)(2,1)S(1)} %get-tuple-element.86), channel_id=1, source_target_pairs={{0,33},{1,32},{2,35},{3,34},{4,37},{5,36},{6,39},{7,38},{8,41},{9,... | collective-permute-start | bytes 884744 | tf_op jit(solution)/shard_map/ppermute | solution.py:42
  31.6 0.5 collective-permute-start.4
  32.1 2.4 %collective-permute-start.11 = (bf16[8,48,384]{2,1,0:T(8,128)(2,1)S(1)}, bf16[8,48,384]{2,1,0:T(8,128)(2,1)S(1)}, u32[]{:S(2)}, u32[]{:S(2)}) collective-permute-start(bf16[8,48,384]{2,1,0:T(8,128)(2,1)S(1)} %get-tuple-element.107), channel_id=1, source_target_pairs={{0,192},{1,193},{2,194},{3,195},{4,196},{5,197},{6,198},{7,199},{8... | collective-permute-start | bytes 884744 | tf_op jit(solution)/shard_map/ppermute | solution.py:42
  34.5 1.7 %convolution_convert_fusion.1 = bf16[256,1536]{1,0:T(8,128)(2,1)} fusion(bf16[256,768]{1,0:T(8,128)(2,1)S(1)} %get-tuple-element.82, bf16[768,1536]{1,0:T(8,128)(2,1)S(1)} %copy-done.2), kind=kOutput, calls=%fused_computation.2 | convolution fusion | flops 604372992 | bytes 3538944 | tf_op jit(solution)/shard_map/dot_general | solution.py:26
  36.1 4.4 %collective-permute-done.3 = bf16[8,48,384]{2,1,0:T(8,128)(2,1)S(1)} collective-permute-done((bf16[8,48,384]{2,1,0:T(8,128)(2,1)S(1)}, bf16[8,48,384]{2,1,0:T(8,128)(2,1)S(1)}, u32[]{:S(2)}, u32[]{:S(2)}) %collective-permute-start.3) | collective-permute-done | bytes 294944 | tf_op jit(solution)/shard_map/ppermute | solution.py:42
  40.5 0.1 join.1.refs_3_
  40.6 1.3 %collective-permute-start.6 = (bf16[8,48,384]{2,1,0:T(8,128)(2,1)S(1)}, bf16[8,48,384]{2,1,0:T(8,128)(2,1)S(1)}, u32[]{:S(2)}, u32[]{:S(2)}) collective-permute-start(bf16[8,48,384]{2,1,0:T(8,128)(2,1)S(1)} %get-tuple-element.95), channel_id=1, source_target_pairs={{0,1},{1,0},{2,3},{3,2},{4,5},{5,4},{6,7},{7,6},{8,9},{9,8},{10,11... | collective-permute-start | bytes 884744 | tf_op jit(solution)/shard_map/ppermute | solution.py:42
  42.0 0.1 pad_maximum_fusion
  42.0 0.2 add_convert_fusion.7
  42.2 2.0 %collective-permute-done.7.refs_4_ = bf16[2,256,768]{2,1,0:T(8,128)(2,1)S(1)} collective-permute-done((bf16[2,256,768]{2,1,0:T(8,128)(2,1)S(1)}, bf16[2,256,768]{2,1,0:T(8,128)(2,1)S(1)}, u32[]{:S(2)}, u32[]{:S(2)}) %collective-permute-start.7) | collective-permute-done | bytes 786464 | tf_op jit(solution)/shard_map/ppermute | solution.py:42
  44.2 2.3 %weight_sections.3 = (bf16[8,48,384]{2,1,0:T(8,128)(2,1)S(1)}, bf16[8,48,384]{2,1,0:T(8,128)(2,1)S(1)}, bf16[8,48,384]{2,1,0:T(8,128)(2,1)S(1)}, bf16[8,48,384]{...) custom-call(s32[4,16]{1,0:T(4,128)S(1)} %pad_add_fusion.refs_0_, ...), custom_call_target="tpu_custom_call" | custom-call | flops 1 | bytes 1 | tf_op jit(solution)/shard_map/weight_sections/pallas_call | solution.py:385
  46.5 0.9 collective-permute-start.8
  47.5 1.8 %collective-permute-start.9 = (bf16[8,48,384]{2,1,0:T(8,128)(2,1)S(1)}, bf16[8,48,384]{2,1,0:T(8,128)(2,1)S(1)}, u32[]{:S(2)}, u32[]{:S(2)}) collective-permute-start(bf16[8,48,384]{2,1,0:T(8,128)(2,1)S(1)} %get-tuple-element.101), channel_id=1, source_target_pairs={{0,33},{1,32},{2,35},{3,34},{4,37},{5,36},{6,39},{7,38},{8,41},{9,... | collective-permute-start | bytes 884744 | tf_op jit(solution)/shard_map/ppermute | solution.py:42
  49.3 0.1 add_convert_fusion.11
  49.4 0.5 collective-permute-start.10
  49.9 2.4 %collective-permute-start.12 = (bf16[8,48,384]{2,1,0:T(8,128)(2,1)S(1)}, bf16[8,48,384]{2,1,0:T(8,128)(2,1)S(1)}, u32[]{:S(2)}, u32[]{:S(2)}) collective-permute-start(bf16[8,48,384]{2,1,0:T(8,128)(2,1)S(1)} %get-tuple-element.109), channel_id=1, source_target_pairs={{0,192},{1,193},{2,194},{3,195},{4,196},{5,197},{6,198},{7,199},{8... | collective-permute-start | bytes 884744 | tf_op jit(solution)/shard_map/ppermute | solution.py:42
  52.4 3.3 %collective-permute-done.8 = bf16[8,48,384]{2,1,0:T(8,128)(2,1)S(1)} collective-permute-done((bf16[8,48,384]{2,1,0:T(8,128)(2,1)S(1)}, bf16[8,48,384]{2,1,0:T(8,128)(2,1)S(1)}, u32[]{:S(2)}, u32[]{:S(2)}) %collective-permute-start.8) | collective-permute-done | bytes 294944 | tf_op jit(solution)/shard_map/ppermute | solution.py:42
  55.6 0.1 add_convert_fusion.10
  55.7 1.9 %collective-permute-done.9 = bf16[8,48,384]{2,1,0:T(8,128)(2,1)S(1)} collective-permute-done((bf16[8,48,384]{2,1,0:T(8,128)(2,1)S(1)}, bf16[8,48,384]{2,1,0:T(8,128)(2,1)S(1)}, u32[]{:S(2)}, u32[]{:S(2)}) %collective-permute-start.9) | collective-permute-done | bytes 294944 | tf_op jit(solution)/shard_map/ppermute | solution.py:42
  57.6 0.1 add_convert_fusion.8
  57.6 0.3 collective-permute-done.10
  58.2 0.6 collective-permute-done.12
  58.9 1.6 %collective-permute-start.13 = (bf16[4,48,768]{2,1,0:T(8,128)(2,1)S(1)}, bf16[4,48,768]{2,1,0:T(8,128)(2,1)S(1)}, u32[]{:S(2)}, u32[]{:S(2)}) collective-permute-start(bf16[4,48,768]{2,1,0:T(8,128)(2,1)S(1)} %fusion.5), channel_id=1, source_target_pairs={{0,33},{1,32},{2,35},{3,34},{4,37},{5,36},{6,39},{7,38},{8,41},{9,... | collective-permute-start | bytes 884744 | tf_op jit(solution)/shard_map/ppermute | solution.py:42
  60.5 1.7 %collective-permute-start.15 = (bf16[4,48,768]{2,1,0:T(8,128)(2,1)S(1)}, bf16[4,48,768]{2,1,0:T(8,128)(2,1)S(1)}, u32[]{:S(2)}, u32[]{:S(2)}) collective-permute-start(bf16[4,48,768]{2,1,0:T(8,128)(2,1)S(1)} %fusion.3), channel_id=1, source_target_pairs={{0,192},{1,193},{2,194},{3,195},{4,196},{5,197},{6,198},{7,199},{8... | collective-permute-start | bytes 884744 | tf_op jit(solution)/shard_map/ppermute | solution.py:42
  62.3 2.6 %collective-permute-start.16 = (bf16[4,48,768]{2,1,0:T(8,128)(2,1)S(1)}, bf16[4,48,768]{2,1,0:T(8,128)(2,1)S(1)}, u32[]{:S(2)}, u32[]{:S(2)}) collective-permute-start(bf16[4,48,768]{2,1,0:T(8,128)(2,1)S(1)} %fusion.2), channel_id=1, source_target_pairs={{0,64},{1,65},{2,66},{3,67},{4,68},{5,69},{6,70},{7,71},{8,72},{9,... | collective-permute-start | bytes 884744 | tf_op jit(solution)/shard_map/ppermute | solution.py:42
  64.8 3.3 %fusion.26 = (f32[256]{0:T(256)S(1)}, f32[256]{0:T(256)S(1)}, f32[256,1536]{1,0:T(8,128)}) fusion(f32[256]{0:T(256)S(1)} %bitcast.71, f32[256]{0:T(256)S(1)} %bitcast.69, bf16[256,1536]{1,0:T(8,128)(2,1)S(1)} %bitcast.66, bf16[256,2304]{1,0:T(8,128)(2,1)S(1)} %pad_maximum_fusion, bf16[1536,2304]{1,0:T(8,128)(2,1)S(1)} %bitcast.64), kind=kOutput, calls=%fused_computation.80 | convolution fusion | flops 1815084544 | bytes 10620928 | tf_op jit(solution)/shard_map/dot_general | solution.py:26
  68.1 1.7 %collective-permute-done.16 = bf16[4,48,768]{2,1,0:T(8,128)(2,1)S(1)} collective-permute-done((bf16[4,48,768]{2,1,0:T(8,128)(2,1)S(1)}, bf16[4,48,768]{2,1,0:T(8,128)(2,1)S(1)}, u32[]{:S(2)}, u32[]{:S(2)}) %collective-permute-start.16) | collective-permute-done | bytes 294944 | tf_op jit(solution)/shard_map/ppermute | solution.py:42
  69.8 0.1 add_convert_fusion
  69.9 0.1 add_convert_fusion.1
  70.0 0.1 add_convert_fusion.3
  70.1 0.1 add_convert_fusion.2
  70.2 0.5 collective-permute-start.17
  70.8 2.8 %collective-permute-start.18 = (bf16[48,1536]{1,0:T(8,128)(2,1)S(1)}, bf16[48,1536]{1,0:T(8,128)(2,1)S(1)}, u32[]{:S(2)}, u32[]{:S(2)}) collective-permute-start(bf16[48,1536]{1,0:T(8,128)(2,1)S(1)} %get-tuple-element.122), channel_id=1, source_target_pairs={{0,64},{1,65},{2,66},{3,67},{4,68},{5,69},{6,70},{7,71},{8,72},{9,... | collective-permute-start | bytes 442376 | tf_op jit(solution)/shard_map/ppermute | solution.py:42
  73.5 0.6 collective-permute-start.19
  74.1 1.7 %collective-permute-start.20 = (bf16[48,1536]{1,0:T(8,128)(2,1)S(1)}, bf16[48,1536]{1,0:T(8,128)(2,1)S(1)}, u32[]{:S(2)}, u32[]{:S(2)}) collective-permute-start(bf16[48,1536]{1,0:T(8,128)(2,1)S(1)} %get-tuple-element.124), channel_id=1, source_target_pairs={{0,33},{1,32},{2,35},{3,34},{4,37},{5,36},{6,39},{7,38},{8,41},{9,... | collective-permute-start | bytes 442376 | tf_op jit(solution)/shard_map/ppermute | solution.py:42
  75.9 1.4 %collective-permute-start.21 = (bf16[48,1536]{1,0:T(8,128)(2,1)S(1)}, bf16[48,1536]{1,0:T(8,128)(2,1)S(1)}, u32[]{:S(2)}, u32[]{:S(2)}) collective-permute-start(bf16[48,1536]{1,0:T(8,128)(2,1)S(1)} %get-tuple-element.125), channel_id=1, source_target_pairs={{0,1},{1,0},{2,3},{3,2},{4,5},{5,4},{6,7},{7,6},{8,9},{9,8},{10,11... | collective-permute-start | bytes 442376 | tf_op jit(solution)/shard_map/ppermute | solution.py:42
  77.3 2.5 %collective-permute-start.22 = (bf16[48,1536]{1,0:T(8,128)(2,1)S(1)}, bf16[48,1536]{1,0:T(8,128)(2,1)S(1)}, u32[]{:S(2)}, u32[]{:S(2)}) collective-permute-start(bf16[48,1536]{1,0:T(8,128)(2,1)S(1)} %get-tuple-element.126), channel_id=1, source_target_pairs={{0,32},{1,33},{2,34},{3,35},{4,36},{5,37},{6,38},{7,39},{8,40},{9,... | collective-permute-start | bytes 442376 | tf_op jit(solution)/shard_map/ppermute | solution.py:42
  79.8 0.4 collective-permute-done.19
  80.2 0.1 fusion.11.refs_0_
  80.3 0.2 collective-permute-done.20
  80.5 0.5 collective-permute-done.21
  81.0 2.9 %collective-permute-done.22 = bf16[48,1536]{1,0:T(8,128)(2,1)S(1)} collective-permute-done((bf16[48,1536]{1,0:T(8,128)(2,1)S(1)}, bf16[48,1536]{1,0:T(8,128)(2,1)S(1)}, u32[]{:S(2)}, u32[]{:S(2)}) %collective-permute-start.22) | collective-permute-done | bytes 147488 | tf_op jit(solution)/shard_map/ppermute | solution.py:42
  83.9 0.1 fusion.8.refs_1_
  84.0 0.8 pieces.1
  84.8 5.5 %all-to-all-start = ((bf16[8,144,128]{2,1,0:T(8,128)(2,1)}), bf16[8,144,128]{2,1,0:T(8,128)(2,1)S(1)}, u32[]{:S(2)}, u32[]{:S(2)}) async-start(bf16[8,144,128]{2,1,0:T(8,128)(2,1)} %pieces.1), calls=%async_computation | async-start | bytes 589824 | tf_op jit(solution)/shard_map/all_to_all | solution.py:499
  90.4 1.4 %fusion.1 = bf16[1,256,1536]{2,1,0:T(8,128)(2,1)} fusion(bf16[256,1536]{1,0:T(8,128)(2,1)S(1)} %bitcast.67, f32[256,1536]{1,0:T(8,128)S(1)} %copy-done.3, f32[256]{0:T(256)S(1)} %broadcast_multiply_fusion, f32[256]{0:T(256)S(1)} %bitcast.70, f32[256]{0:T(256)S(1)} %broadcast_multiply_fusion.1, f32[256]{0:T(256)S(1)} %bitcast.72), kind=kLoop, calls=%fused_computation.7 | loop fusion | flops 3145728 | bytes 3149824 | tf_op jit(solution)/shard_map/broadcast_in_dim | solution.py:507
  91.7 9.5 %all-to-all-done.in_ref = bf16[8,144,128]{2,1,0:T(8,128)(2,1)S(1)} async-done(((bf16[8,144,128]{2,1,0:T(8,128)(2,1)}), bf16[8,144,128]{2,1,0:T(8,128)(2,1)S(1)}, u32[]{:S(2)}, u32[]{:S(2)}) %all-to-all-start) | async-done | bytes 294944 | tf_op jit(solution)/shard_map/all_to_all | solution.py:499
  101.2 0.7 total.1
  (40 shorter events, 0.6 us)
Async XLA Ops:
  1.9 5.9 %copy-start = (bf16[384,384]{1,0:T(8,128)(2,1)S(1)}, bf16[384,384]{1,0:T(8,128)(2,1)}, u32[]{:S(2)}) copy-start(bf16[384,384]{1,0:T(8,128)(2,1)} %constant.60.clone.order_ref) | copy-start | bytes 884740
  6.2 16.0 %collective-permute-start = (bf16[128,1536]{1,0:T(8,128)(2,1)S(1)}, bf16[128,1536]{1,0:T(8,128)(2,1)S(1)}, u32[]{:S(2)}, u32[]{:S(2)}) collective-permute-start(bf16[128,1536]{1,0:T(8,128)(2,1)S(1)} %get-tuple-element.70), channel_id=1, source_target_pairs={{0,1},{1,2},{2,3},{3,4},{4,5},{5,6},{6,7},{7,8},{8,9},{9,10},{10,1... | collective-permute-start | bytes 1179656 | tf_op jit(solution)/shard_map/ppermute | solution.py:31
  13.0 14.7 %collective-permute-start.1 = (bf16[768,512]{1,0:T(8,128)(2,1)S(1)}, bf16[768,512]{1,0:T(8,128)(2,1)S(1)}, u32[]{:S(2)}, u32[]{:S(2)}) collective-permute-start(bf16[768,512]{1,0:T(8,128)(2,1)S(1)} %get-tuple-element.77), channel_id=1, source_target_pairs={{0,16},{1,17},{2,18},{3,19},{4,20},{5,21},{6,22},{7,23},{8,24},{9,... | collective-permute-start | bytes 2359304 | tf_op jit(solution)/shard_map/ppermute | solution.py:42
  25.5 2.4 %collective-permute-start.2 = (bf16[2,256,768]{2,1,0:T(8,128)(2,1)S(1)}, bf16[2,256,768]{2,1,0:T(8,128)(2,1)S(1)}, u32[]{:S(2)}, u32[]{:S(2)}) collective-permute-start(bf16[2,256,768]{2,1,0:T(8,128)(2,1)S(1)} %get-tuple-element.74.refs_3_), channel_id=1, source_target_pairs={{0,16},{1,17},{2,18},{3,19},{4,20},{5,21},{6,22},{7,23},{8,24},{9,... | collective-permute-start | bytes 2359304 | tf_op jit(solution)/shard_map/ppermute | solution.py:42
  25.6 14.9 %collective-permute-start.5 = (bf16[2,128,768]{2,1,0:T(8,128)(2,1)S(1)}, bf16[2,128,768]{2,1,0:T(8,128)(2,1)S(1)}, u32[]{:S(2)}, u32[]{:S(2)}) collective-permute-start(bf16[2,128,768]{2,1,0:T(8,128)(2,1)S(1)} %get-tuple-element.90), channel_id=1, source_target_pairs={{0,15},{1,0},{2,1},{3,2},{4,3},{5,4},{6,5},{7,6},{8,7},{9,8},{10,9... | collective-permute-start | bytes 1179656 | tf_op jit(solution)/shard_map/ppermute | solution.py:31
  27.8 6.6 %copy-start.2 = (bf16[768,1536]{1,0:T(8,128)(2,1)S(1)}, bf16[768,1536]{1,0:T(8,128)(2,1)}, u32[]{:S(2)}) copy-start(bf16[768,1536]{1,0:T(8,128)(2,1)} %out_ref.1) | copy-start | bytes 7077892
  30.2 10.3 %collective-permute-start.3 = (bf16[8,48,384]{2,1,0:T(8,128)(2,1)S(1)}, bf16[8,48,384]{2,1,0:T(8,128)(2,1)S(1)}, u32[]{:S(2)}, u32[]{:S(2)}) collective-permute-start(bf16[8,48,384]{2,1,0:T(8,128)(2,1)S(1)} %get-tuple-element.86), channel_id=1, source_target_pairs={{0,33},{1,32},{2,35},{3,34},{4,37},{5,36},{6,39},{7,38},{8,41},{9,... | collective-permute-start | bytes 884744 | tf_op jit(solution)/shard_map/ppermute | solution.py:42
  31.6 8.9 %collective-permute-start.4 = (bf16[8,48,384]{2,1,0:T(8,128)(2,1)S(1)}, bf16[8,48,384]{2,1,0:T(8,128)(2,1)S(1)}, u32[]{:S(2)}, u32[]{:S(2)}) collective-permute-start(bf16[8,48,384]{2,1,0:T(8,128)(2,1)S(1)} %get-tuple-element.87), channel_id=1, source_target_pairs={{0,64},{1,65},{2,66},{3,67},{4,68},{5,69},{6,70},{7,71},{8,72},{9,... | collective-permute-start | bytes 884744 | tf_op jit(solution)/shard_map/ppermute | solution.py:42
  32.1 15.4 %collective-permute-start.11 = (bf16[8,48,384]{2,1,0:T(8,128)(2,1)S(1)}, bf16[8,48,384]{2,1,0:T(8,128)(2,1)S(1)}, u32[]{:S(2)}, u32[]{:S(2)}) collective-permute-start(bf16[8,48,384]{2,1,0:T(8,128)(2,1)S(1)} %get-tuple-element.107), channel_id=1, source_target_pairs={{0,192},{1,193},{2,194},{3,195},{4,196},{5,197},{6,198},{7,199},{8... | collective-permute-start | bytes 884744 | tf_op jit(solution)/shard_map/ppermute | solution.py:42
  40.6 8.7 %collective-permute-start.6 = (bf16[8,48,384]{2,1,0:T(8,128)(2,1)S(1)}, bf16[8,48,384]{2,1,0:T(8,128)(2,1)S(1)}, u32[]{:S(2)}, u32[]{:S(2)}) collective-permute-start(bf16[8,48,384]{2,1,0:T(8,128)(2,1)S(1)} %get-tuple-element.95), channel_id=1, source_target_pairs={{0,1},{1,0},{2,3},{3,2},{4,5},{5,4},{6,7},{7,6},{8,9},{9,8},{10,11... | collective-permute-start | bytes 884744 | tf_op jit(solution)/shard_map/ppermute | solution.py:42
  41.9 2.3 %collective-permute-start.7 = (bf16[2,256,768]{2,1,0:T(8,128)(2,1)S(1)}, bf16[2,256,768]{2,1,0:T(8,128)(2,1)S(1)}, u32[]{:S(2)}, u32[]{:S(2)}) collective-permute-start(bf16[2,256,768]{2,1,0:T(8,128)(2,1)S(1)} %join.1.refs_3_), channel_id=1, source_target_pairs={{0,16},{1,17},{2,18},{3,19},{4,20},{5,21},{6,22},{7,23},{8,24},{9,... | collective-permute-start | bytes 2359304 | tf_op jit(solution)/shard_map/ppermute | solution.py:42
  41.9 22.9 %slice-start = ((s8[7077888]{0:T(1024)(128)(4,1)}), s8[4194304]{0:T(1024)(128)(4,1)S(1)}, s32[]{:S(2)}) async-start(s8[7077888]{0:T(1024)(128)(4,1)} %bitcast.63), calls=%async_computation.1 | async-start | bytes 8388608
  46.5 9.1 %collective-permute-start.8 = (bf16[8,48,384]{2,1,0:T(8,128)(2,1)S(1)}, bf16[8,48,384]{2,1,0:T(8,128)(2,1)S(1)}, u32[]{:S(2)}, u32[]{:S(2)}) collective-permute-start(bf16[8,48,384]{2,1,0:T(8,128)(2,1)S(1)} %get-tuple-element.97), channel_id=1, source_target_pairs={{0,1},{1,0},{2,3},{3,2},{4,5},{5,4},{6,7},{7,6},{8,9},{9,8},{10,11... | collective-permute-start | bytes 884744 | tf_op jit(solution)/shard_map/ppermute | solution.py:42
  47.4 17.4 %slice-start.1 = ((s8[7077888]{0:T(1024)(128)(4,1)}), s8[2883584]{0:T(1024)(128)(4,1)S(1)}, s32[]{:S(2)}) async-start(s8[7077888]{0:T(1024)(128)(4,1)} %bitcast.63), calls=%async_computation.2 | async-start | bytes 5767168
  47.5 10.1 %collective-permute-start.9 = (bf16[8,48,384]{2,1,0:T(8,128)(2,1)S(1)}, bf16[8,48,384]{2,1,0:T(8,128)(2,1)S(1)}, u32[]{:S(2)}, u32[]{:S(2)}) collective-permute-start(bf16[8,48,384]{2,1,0:T(8,128)(2,1)S(1)} %get-tuple-element.101), channel_id=1, source_target_pairs={{0,33},{1,32},{2,35},{3,34},{4,37},{5,36},{6,39},{7,38},{8,41},{9,... | collective-permute-start | bytes 884744 | tf_op jit(solution)/shard_map/ppermute | solution.py:42
  49.4 8.6 %collective-permute-start.10 = (bf16[8,48,384]{2,1,0:T(8,128)(2,1)S(1)}, bf16[8,48,384]{2,1,0:T(8,128)(2,1)S(1)}, u32[]{:S(2)}, u32[]{:S(2)}) collective-permute-start(bf16[8,48,384]{2,1,0:T(8,128)(2,1)S(1)} %get-tuple-element.105), channel_id=1, source_target_pairs={{0,64},{1,65},{2,66},{3,67},{4,68},{5,69},{6,70},{7,71},{8,72},{9,... | collective-permute-start | bytes 884744 | tf_op jit(solution)/shard_map/ppermute | solution.py:42
  49.9 8.9 %collective-permute-start.12 = (bf16[8,48,384]{2,1,0:T(8,128)(2,1)S(1)}, bf16[8,48,384]{2,1,0:T(8,128)(2,1)S(1)}, u32[]{:S(2)}, u32[]{:S(2)}) collective-permute-start(bf16[8,48,384]{2,1,0:T(8,128)(2,1)S(1)} %get-tuple-element.109), channel_id=1, source_target_pairs={{0,192},{1,193},{2,194},{3,195},{4,196},{5,197},{6,198},{7,199},{8... | collective-permute-start | bytes 884744 | tf_op jit(solution)/shard_map/ppermute | solution.py:42
  58.1 6.7 %copy-start.1 = (bf16[1,256,1536]{2,1,0:T(8,128)(2,1)S(1)}, bf16[1,256,1536]{2,1,0:T(8,128)(2,1)}, u32[]{:S(2)}) copy-start(bf16[1,256,1536]{2,1,0:T(8,128)(2,1)} %param.6) | copy-start | bytes 2359300
  58.9 9.2 %collective-permute-start.13 = (bf16[4,48,768]{2,1,0:T(8,128)(2,1)S(1)}, bf16[4,48,768]{2,1,0:T(8,128)(2,1)S(1)}, u32[]{:S(2)}, u32[]{:S(2)}) collective-permute-start(bf16[4,48,768]{2,1,0:T(8,128)(2,1)S(1)} %fusion.5), channel_id=1, source_target_pairs={{0,33},{1,32},{2,35},{3,34},{4,37},{5,36},{6,39},{7,38},{8,41},{9,... | collective-permute-start | bytes 884744 | tf_op jit(solution)/shard_map/ppermute | solution.py:42
  60.5 7.6 %collective-permute-start.14 = (bf16[4,48,768]{2,1,0:T(8,128)(2,1)S(1)}, bf16[4,48,768]{2,1,0:T(8,128)(2,1)S(1)}, u32[]{:S(2)}, u32[]{:S(2)}) collective-permute-start(bf16[4,48,768]{2,1,0:T(8,128)(2,1)S(1)} %fusion.4), channel_id=1, source_target_pairs={{0,1},{1,0},{2,3},{3,2},{4,5},{5,4},{6,7},{7,6},{8,9},{9,8},{10,11... | collective-permute-start | bytes 884744 | tf_op jit(solution)/shard_map/ppermute | solution.py:42
  60.5 7.6 %collective-permute-start.15 = (bf16[4,48,768]{2,1,0:T(8,128)(2,1)S(1)}, bf16[4,48,768]{2,1,0:T(8,128)(2,1)S(1)}, u32[]{:S(2)}, u32[]{:S(2)}) collective-permute-start(bf16[4,48,768]{2,1,0:T(8,128)(2,1)S(1)} %fusion.3), channel_id=1, source_target_pairs={{0,192},{1,193},{2,194},{3,195},{4,196},{5,197},{6,198},{7,199},{8... | collective-permute-start | bytes 884744 | tf_op jit(solution)/shard_map/ppermute | solution.py:42
  62.3 7.5 %collective-permute-start.16 = (bf16[4,48,768]{2,1,0:T(8,128)(2,1)S(1)}, bf16[4,48,768]{2,1,0:T(8,128)(2,1)S(1)}, u32[]{:S(2)}, u32[]{:S(2)}) collective-permute-start(bf16[4,48,768]{2,1,0:T(8,128)(2,1)S(1)} %fusion.2), channel_id=1, source_target_pairs={{0,64},{1,65},{2,66},{3,67},{4,68},{5,69},{6,70},{7,71},{8,72},{9,... | collective-permute-start | bytes 884744 | tf_op jit(solution)/shard_map/ppermute | solution.py:42
  70.2 7.1 %collective-permute-start.17 = (bf16[48,1536]{1,0:T(8,128)(2,1)S(1)}, bf16[48,1536]{1,0:T(8,128)(2,1)S(1)}, u32[]{:S(2)}, u32[]{:S(2)}) collective-permute-start(bf16[48,1536]{1,0:T(8,128)(2,1)S(1)} %get-tuple-element.121), channel_id=1, source_target_pairs={{0,192},{1,193},{2,194},{3,195},{4,196},{5,197},{6,198},{7,199},{8... | collective-permute-start | bytes 442376 | tf_op jit(solution)/shard_map/ppermute | solution.py:42
  70.8 9.1 %collective-permute-start.18 = (bf16[48,1536]{1,0:T(8,128)(2,1)S(1)}, bf16[48,1536]{1,0:T(8,128)(2,1)S(1)}, u32[]{:S(2)}, u32[]{:S(2)}) collective-permute-start(bf16[48,1536]{1,0:T(8,128)(2,1)S(1)} %get-tuple-element.122), channel_id=1, source_target_pairs={{0,64},{1,65},{2,66},{3,67},{4,68},{5,69},{6,70},{7,71},{8,72},{9,... | collective-permute-start | bytes 442376 | tf_op jit(solution)/shard_map/ppermute | solution.py:42
  73.5 6.6 %collective-permute-start.19 = (bf16[48,1536]{1,0:T(8,128)(2,1)S(1)}, bf16[48,1536]{1,0:T(8,128)(2,1)S(1)}, u32[]{:S(2)}, u32[]{:S(2)}) collective-permute-start(bf16[48,1536]{1,0:T(8,128)(2,1)S(1)} %get-tuple-element.123), channel_id=1, source_target_pairs={{0,128},{1,129},{2,130},{3,131},{4,132},{5,133},{6,134},{7,135},{8... | collective-permute-start | bytes 442376 | tf_op jit(solution)/shard_map/ppermute | solution.py:42
  74.1 16.2 %copy-start.3 = (f32[256,1536]{1,0:T(8,128)S(1)}, f32[256,1536]{1,0:T(8,128)}, u32[]{:S(2)}) copy-start(f32[256,1536]{1,0:T(8,128)} %get-tuple-element.141) | copy-start | bytes 4718596
  74.1 6.4 %collective-permute-start.20 = (bf16[48,1536]{1,0:T(8,128)(2,1)S(1)}, bf16[48,1536]{1,0:T(8,128)(2,1)S(1)}, u32[]{:S(2)}, u32[]{:S(2)}) collective-permute-start(bf16[48,1536]{1,0:T(8,128)(2,1)S(1)} %get-tuple-element.124), channel_id=1, source_target_pairs={{0,33},{1,32},{2,35},{3,34},{4,37},{5,36},{6,39},{7,38},{8,41},{9,... | collective-permute-start | bytes 442376 | tf_op jit(solution)/shard_map/ppermute | solution.py:42
  75.9 5.1 %collective-permute-start.21 = (bf16[48,1536]{1,0:T(8,128)(2,1)S(1)}, bf16[48,1536]{1,0:T(8,128)(2,1)S(1)}, u32[]{:S(2)}, u32[]{:S(2)}) collective-permute-start(bf16[48,1536]{1,0:T(8,128)(2,1)S(1)} %get-tuple-element.125), channel_id=1, source_target_pairs={{0,1},{1,0},{2,3},{3,2},{4,5},{5,4},{6,7},{7,6},{8,9},{9,8},{10,11... | collective-permute-start | bytes 442376 | tf_op jit(solution)/shard_map/ppermute | solution.py:42
  77.3 6.6 %collective-permute-start.22 = (bf16[48,1536]{1,0:T(8,128)(2,1)S(1)}, bf16[48,1536]{1,0:T(8,128)(2,1)S(1)}, u32[]{:S(2)}, u32[]{:S(2)}) collective-permute-start(bf16[48,1536]{1,0:T(8,128)(2,1)S(1)} %get-tuple-element.126), channel_id=1, source_target_pairs={{0,32},{1,33},{2,34},{3,35},{4,36},{5,37},{6,38},{7,39},{8,40},{9,... | collective-permute-start | bytes 442376 | tf_op jit(solution)/shard_map/ppermute | solution.py:42
  84.8 16.4 %all-to-all-start = ((bf16[8,144,128]{2,1,0:T(8,128)(2,1)}), bf16[8,144,128]{2,1,0:T(8,128)(2,1)S(1)}, u32[]{:S(2)}, u32[]{:S(2)}) async-start(bf16[8,144,128]{2,1,0:T(8,128)(2,1)} %pieces.1), calls=%async_computation | async-start | bytes 589824 | tf_op jit(solution)/shard_map/all_to_all | solution.py:499

commit v3 on v2

v3 whole, which is shorter than its diff:
```python
import jax
import jax.numpy as jnp
import numpy as np
from jax import lax
from jax.experimental import pallas as pl
from jax.experimental.pallas import tpu as pltpu
from jax.sharding import PartitionSpec as P

HEAD_DIM = 64
GROUP = 32
LEFT = 4
CONTEXT = LEFT * GROUP
PAIR = 2 * HEAD_DIM
F32 = jnp.float32
BF16 = jnp.bfloat16
NT = (((1,), (1,)), ((), ()))
NN = (((1,), (0,)), ((), ()))

Y, XH, CORES, Z, XL = 4, 2, 2, 8, 2
CHUNKS = Y * XH * XL

epsilon = 1e-05


def dot(a, b, dims=NN):
    return lax.dot_general(a, b, dims, preferred_element_type=F32)


def from_behind(value, axis, by):
    peers = lax.axis_size(axis)
    return lax.ppermute(value, axis, [(i, (i + by) % peers) for i in range(peers)])


def flat(y, xh, core, z, xl):
    return ((y * XH + xh) * CORES + core) * (Z * XL) + z * XL + xl


def to_device(value, where):
    pairs = []
    for place in np.ndindex(Y, XH, CORES, Z, XL):
        pairs.append((flat(*place), flat(*where(*place))))
    return lax.ppermute(value, ("dp", "seq"), pairs)


def to_core(y, xh, core, z, xl):
    return y, xh, 1 - core, z, xl


def to_x_near(y, xh, core, z, xl):
    return y, xh, core, z, 1 - xl


def to_x_mirror(y, xh, core, z, xl):
    return y, 1 - xh, core, z, 1 - xl


def to_y_near(y, xh, core, z, xl):
    return y ^ 1, xh, core, z, xl


def to_y_mirror(y, xh, core, z, xl):
    return 3 - y, xh, core, z, xl


def to_x_far(y, xh, core, z, xl):
    return y, 1 - xh, core, z, xl


def to_y_far(y, xh, core, z, xl):
    return y ^ 2, xh, core, z, xl


ROUTES = (
    (to_x_near, to_x_mirror),
    (to_x_mirror, to_x_near),
    (to_y_near, to_y_mirror),
    (to_y_mirror, to_y_near),
)
OWNERS = (
    (to_y_mirror, to_y_near, to_y_far),
    (to_x_mirror, to_x_near, to_x_far),
)


def halves(route, hi, lo):
    return (hi ^ lo, hi) if route % 2 == 0 else (hi, hi ^ lo)


def chunk_at(route, slot, y, xh, xl):
    bits = [(slot >> (3 - i)) & 1 for i in range(4)]
    x_first = route < 2
    x_bits, y_bits = (bits[:2], bits[2:]) if x_first else (bits[2:], bits[:2])
    found = []
    for hi, lo, pair, order in ((y >> 1, y & 1, y_bits, 0 if x_first else route), (xh, xl, x_bits, route if x_first else 0)):
        first, second = halves(order, hi, lo)
        first, second = first ^ pair[0], second ^ pair[1]
        found.append((second, first ^ second) if order % 2 == 0 else (first, first ^ second))
    (yh, yl), (xh_to, xl_to) = found
    return ((yh * 2 + yl) * XH + xh_to) * XL + xl_to


def row_order(width):
    share = width // (CHUNKS * CORES * Z)
    order = np.arange(width // Y).reshape(XH, CORES, Z, XL, share).transpose(1, 0, 3, 2, 4).reshape(-1)
    return jnp.asarray(np.eye(width // Y, dtype=np.float32)[order], BF16)


def statistics(rows_in):
    average = jnp.mean(rows_in, axis=-1, keepdims=True)
    centered = rows_in - average
    variance = jnp.mean(centered * centered, axis=-1, keepdims=True)
    return average, lax.rsqrt(variance + epsilon)


def normalize_grad(rows_in, average, inverse, grad):
    normed = (rows_in - average) * inverse
    along = jnp.mean(grad * normed, axis=-1, keepdims=True)
    return inverse * (grad - jnp.mean(grad, axis=-1, keepdims=True) - normed * along)


SMEM_SPEC = pl.BlockSpec(memory_space=pltpu.SMEM)
VMEM_SPEC = pl.BlockSpec(memory_space=pltpu.VMEM)
HBM_SPEC = pl.BlockSpec(memory_space=pltpu.HBM)


def in_vmem(value):
    return pltpu.with_memory_space_constraint(value, pltpu.VMEM)


def in_hbm(value):
    return pltpu.with_memory_space_constraint(value, pltpu.HBM)


def cost(flops, nbytes, transcendentals=0):
    return pl.CostEstimate(flops=flops, bytes_accessed=nbytes, transcendentals=transcendentals)


def params(mebibytes):
    return pltpu.CompilerParams(vmem_limit_bytes=mebibytes * 2**20)


def turn(ref, order_ref, store):
    rows = order_ref.shape[0]
    half = rows // CORES
    for y in range(Y):
        turned = dot(order_ref[...], ref[:, y * rows : (y + 1) * rows].T).astype(BF16)
        for core in range(CORES):
            store(core, slice(y * half, (y + 1) * half), turned[core * half : (core + 1) * half])


def front_kernel(
    places, order_ref, frames_ref, cotangent_ref, weight_ref, out_ref,
    qkv_ref, grad_ref, keep_ref, send_ref, stats_ref, weight, late_ref, dkv_ref,
    rows, cotangent, outer, normed, sems,
):
    here = places[2]
    tokens = rows.shape[0]
    thirds = weight.shape[1] // 3
    block = [slice(n * thirds, (n + 1) * thirds) for n in range(3)]
    copies = [
        pltpu.make_async_copy(frames_ref, rows, sems.at[0]),
        pltpu.make_async_copy(cotangent_ref, cotangent, sems.at[1]),
        pltpu.make_async_copy(out_ref, outer, sems.at[2]),
    ] + [
        pltpu.make_async_copy(weight_ref.at[:, pl.ds(n * thirds, thirds)], weight.at[:, pl.ds(n * thirds, thirds)], sems.at[3 + n])
        for n in range(3)
    ]
    for copy in copies:
        copy.start()

    def put(columns):
        def store(core, at, values):
            @pl.when(here == core)
            def _():
                keep_ref[at, columns] = values

            @pl.when(here != core)
            def _():
                send_ref[at, columns] = values

        return store

    copies[0].wait()
    values = rows[...].astype(F32)
    average, inverse = statistics(values)
    for n, column in enumerate((average, inverse)):
        stats_ref[n : n + 1, :] = jnp.broadcast_to(column, (tokens, PAIR)).T[:1]
    normed[...] = ((values - average) * inverse).astype(BF16)
    turn(normed, order_ref, put(slice(0, tokens)))
    copies[1].wait()
    turn(cotangent, order_ref, put(slice(tokens, 2 * tokens)))
    copies[2].wait()
    grad_ref[...] = dot(cotangent[...], outer[...], NT).astype(BF16)
    for n in range(3):
        copies[3 + n].wait()
        qkv_ref[:, block[n]] = dot(normed[...], weight[:, block[n]]).astype(BF16)

    inner = thirds

    def operands(pair):
        q, k, v = pair_columns(pair, inner)
        return qkv_ref[CONTEXT:, q], qkv_ref[:, k], qkv_ref[:, v], grad_ref[CONTEXT:, q]

    def results(pair, mixed, dq, dk, dv):
        at = pair_columns(pair, inner)[0]
        late_ref[0, :, at] = mixed
        late_ref[1, :, at] = dq
        dkv_ref[0, :, at] = dk
        dkv_ref[1, :, at] = dv

    attend(places[1] + CONTEXT, places[0], inner, operands, results)


def front(places, frames, cotangent, w_qkv, w_out):
    tokens, width = frames.shape
    inner = w_out.shape[0]
    turned = pltpu.VMEM((width // CORES, 2 * tokens), BF16)
    return pl.pallas_call(
        front_kernel,
        in_specs=[SMEM_SPEC, VMEM_SPEC] + [HBM_SPEC] * 4,
        out_specs=[VMEM_SPEC] * 8,
        out_shape=[
            pltpu.VMEM((tokens, 3 * inner), BF16),
            pltpu.VMEM((tokens, inner), BF16),
            turned,
            turned,
            pltpu.VMEM((2, tokens), F32),
            pltpu.VMEM((width, 3 * inner), BF16),
            pltpu.VMEM((2, CONTEXT, inner), BF16),
            pltpu.VMEM((2, tokens, inner), F32),
        ],
        scratch_shapes=[
            pltpu.VMEM((tokens, width), BF16),
            pltpu.VMEM((tokens, width), BF16),
            pltpu.VMEM((inner, width), BF16),
            pltpu.VMEM((tokens, width), BF16),
            pltpu.SemaphoreType.DMA((6,)),
        ],
        compiler_params=params(24),
        cost_estimate=cost(12 * tokens * width * inner, 10 * inner * width),
        name="front",
    )(places, in_vmem(row_order(width)), *[in_hbm(o) for o in (frames, cotangent, w_qkv, w_out)])


def pair_columns(pair, inner):
    return [slice(n * inner + pair * PAIR, n * inner + (pair + 1) * PAIR) for n in range(3)]


def attend(begin, length, inner, operands, results):
    lane = lax.broadcasted_iota(jnp.int32, (CONTEXT, PAIR), 1)
    heads = (lane < HEAD_DIM, lane >= HEAD_DIM)
    row_valid = begin + lax.broadcasted_iota(jnp.int32, (CONTEXT, PAIR), 0) < length
    col_valid = begin + lane < length
    keys = lax.broadcasted_iota(jnp.int32, (2 * CONTEXT, 2 * CONTEXT), 0)
    queries = lax.broadcasted_iota(jnp.int32, (2 * CONTEXT, 2 * CONTEXT), 1)
    key_block = keys // GROUP
    query_block = (queries % CONTEXT) // GROUP
    key_place = begin - CONTEXT + keys
    seen = (key_block >= query_block) & (key_block <= query_block + LEFT) & (key_place >= 0) & (key_place < length)
    zero = jnp.zeros((CONTEXT, PAIR), BF16)
    scale = HEAD_DIM ** (-0.5)

    def unstack(both):
        return jnp.concatenate([both[:HEAD_DIM, :CONTEXT], both[HEAD_DIM:, CONTEXT:]], axis=0)

    for pair in range(inner // PAIR):
        q, k2, v2, do = operands(pair)
        do = jnp.where(row_valid, do, zero)
        q = q * jnp.asarray(scale, BF16)
        q2 = jnp.concatenate([jnp.where(h, q, zero) for h in heads], axis=0)
        do2 = jnp.concatenate([jnp.where(h, do, zero) for h in heads], axis=0)
        scores = jnp.where(seen, dot(k2, q2, NT), -1e30)
        dprob = dot(v2, do2, NT)
        highest = jnp.max(scores, axis=0, keepdims=True)
        raised = jnp.exp(scores - highest)
        prob = raised * (1.0 / jnp.sum(raised, axis=0, keepdims=True))
        rounded = prob.astype(BF16)
        mixed = jnp.where(col_valid, unstack(dot(v2.T, rounded)), 0.0).T.astype(BF16)
        weighed = prob * dprob
        dscores = (weighed - prob * jnp.sum(weighed, axis=0, keepdims=True)).astype(BF16)
        dq = (unstack(dot(k2.T, dscores)) * scale).T.astype(BF16)
        results(pair, mixed, dq, dot(dscores, q2), dot(rounded, do2))


def early_kernel(places, order_ref, frames_ref, weight_ref, qkv_ref, do_ref, late_ref, add_ref,
                 out_ref, dkv_ref, turned_ref, normed, halo):
    inner = do_ref.shape[1]
    rows = qkv_ref.shape[0]
    here = places[2]
    values = frames_ref[...].astype(F32)
    average, inverse = statistics(values)
    normed[...] = ((values - average) * inverse).astype(BF16)
    halo[...] = dot(normed[...], weight_ref[:, inner:]).astype(BF16)
    out_ref[:, CONTEXT:, :] = late_ref[...]
    dkv_ref[:, CONTEXT:rows, :inner] = add_ref[:, CONTEXT:, :].astype(BF16)

    def store(core, at, values):
        @pl.when(here == core)
        def _():
            turned_ref[at, :] = values

        @pl.when(here != core)
        def _():
            half = dkv_ref.shape[1]
            for n in range(2):
                first, last = max(at.start, n * half), min(at.stop, (n + 1) * half)
                if first < last:
                    dkv_ref[n, first - n * half : last - n * half, inner:] = values[first - at.start : last - at.start]

    turn(normed, order_ref, store)

    def operands(pair):
        q, k, v = pair_columns(pair, inner)
        k2 = jnp.concatenate([halo[:, q], qkv_ref[:CONTEXT, k]], axis=0)
        v2 = jnp.concatenate([halo[:, k], qkv_ref[:CONTEXT, v]], axis=0)
        return qkv_ref[:CONTEXT, q], k2, v2, do_ref[:CONTEXT, q]

    def results(pair, mixed, dq, dk, dv):
        at = pair_columns(pair, inner)[0]
        out_ref[0, :CONTEXT, at] = mixed
        out_ref[1, :CONTEXT, at] = dq
        for n, grad in enumerate((dk, dv)):
            dkv_ref[n, rows:, at] = grad[:CONTEXT].astype(BF16)
            dkv_ref[n, :CONTEXT, at] = (grad[CONTEXT:] + add_ref[n, :CONTEXT, at]).astype(BF16)

    attend(places[1], places[0], inner, operands, results)


def early_tile(places, frames, weight, qkv, attended_grad, late, late_grad):
    rows, inner = attended_grad.shape
    width = frames.shape[1]
    return pl.pallas_call(
        early_kernel,
        in_specs=[SMEM_SPEC] + [VMEM_SPEC] * 7,
        out_specs=[VMEM_SPEC] * 3,
        out_shape=[
            pltpu.VMEM((2, rows, inner), BF16),
            pltpu.VMEM((2, rows + CONTEXT, inner + CONTEXT), BF16),
            pltpu.VMEM((width // CORES, CONTEXT), BF16),
        ],
        scratch_shapes=[pltpu.VMEM((CONTEXT, width), BF16), pltpu.VMEM((CONTEXT, 2 * inner), BF16)],
        compiler_params=params(16),
        cost_estimate=cost(28 * CONTEXT * 2 * CONTEXT * inner, 16 * CONTEXT * inner, CONTEXT * 4 * inner),
        name="attention_early",
    )(places, in_vmem(row_order(width)), *[in_vmem(o) for o in (frames, weight, qkv, attended_grad, late, late_grad)])


def store_sections(chunks, n, total, outs, held):
    columns = total.shape[1] // 2
    half = CHUNKS // 2
    for part in range(2):
        route = 2 * n + part
        held[route] = total[:, part * columns : (part + 1) * columns].reshape(held.shape[1:])
        for slot in range(CHUNKS):
            ref = outs[route] if slot < half else outs[len(ROUTES) + route]
            ref[slot % half] = held[route, chunks[route, slot]].astype(BF16)


def first_wave_kernel(chunks, left_ref, left_other_ref, right_ref, right_other_ref, *refs):
    tokens = right_ref.shape[1]
    for n, at in enumerate((slice(tokens, 2 * tokens), slice(0, tokens))):
        total = dot(left_ref[:, at], right_ref[n]) + dot(left_other_ref[:, at], right_other_ref[n])
        store_sections(chunks, n, total, refs[:-1], refs[-1])


def second_wave_kernel(chunks, left_ref, left_other_ref, behind_ref, right_ref, right_other_ref, *refs):
    tokens = left_ref.shape[1] // 2
    inner = right_ref.shape[2] - CONTEXT
    behind_other = jnp.concatenate([right_other_ref[n, :, inner:] for n in range(2)], axis=0)
    for n in range(2):
        total = dot(left_ref[:, :tokens], right_ref[n, :tokens, :inner])
        total += dot(left_other_ref[:, :tokens], right_other_ref[n, :tokens, :inner])
        total += dot(behind_ref[...], right_ref[n, tokens:, :inner])
        total += dot(behind_other, right_other_ref[n, tokens:, :inner])
        store_sections(chunks, n, total, refs[:-1], refs[-1])


def weight_sections(kernel, chunks, operands, inner, flops, name):
    size = (operands[0].shape[0] // CHUNKS, inner // 2)
    routes = len(ROUTES)
    outs = pl.pallas_call(
        kernel,
        in_specs=[SMEM_SPEC] + [VMEM_SPEC] * len(operands),
        out_specs=[VMEM_SPEC] * (2 * routes),
        out_shape=[pltpu.VMEM((CHUNKS // 2, *size), BF16)] * (2 * routes),
        scratch_shapes=[pltpu.VMEM((routes, CHUNKS, *size), F32)],
        compiler_params=params(24),
        cost_estimate=cost(flops, 1),
        name=name,
    )(chunks, *[in_vmem(o) for o in operands])
    return outs[:routes], outs[routes:]


def plus(*terms):
    return sum(t.astype(F32) for t in terms).astype(BF16)


def pieces_kernel(*refs):
    ins, out_ref, held = refs[:-2], refs[-2], refs[-1]
    for group, ref in enumerate(ins):
        block = ref[...].astype(F32)
        width = block.shape[1] // PAIR // 4
        share = block.shape[0] // Z
        for n in (2 * group, 2 * group + 1):
            bases = (((n + 2) % 4) * width + (0 if n > 1 else 4 * width), (2 + n) * width)
            for wave, base in enumerate(bases):
                for t in range(width):
                    column = (((n % 2) * 2 + wave) * width + t) * PAIR
                    for z in range(Z):
                        rows = slice((base + t) * share, (base + t + 1) * share)
                        held[z, rows, :] = block[z * share : (z + 1) * share, column : column + PAIR]
    out_ref[...] = held[...].astype(BF16)


def total_kernel(in_ref, out_ref):
    total = in_ref[0].astype(F32)
    for z in range(1, Z):
        total += in_ref[z].astype(F32)
    share = out_ref.shape[0]
    for t in range(out_ref.shape[1] // PAIR):
        out_ref[:, t * PAIR : (t + 1) * PAIR] = total[t * share : (t + 1) * share]


def on_device(frames, cotangent, lengths, w_qkv, w_out):
    frame_rows = frames[0]
    grad_rows = cotangent[0]
    row_count, width = frame_rows.shape
    inner = w_out.shape[0]
    seq_index = lax.axis_index("seq")
    dp_index = lax.axis_index("dp")
    xl = seq_index % XL
    core, xh, y = dp_index % CORES, dp_index // CORES % XH, dp_index // (CORES * XH)
    places = jnp.stack([lengths[0], seq_index * row_count, core])
    routes = range(len(ROUTES))
    chunks = jnp.stack([chunk_at(r, jnp.arange(CHUNKS), y, xh, xl) for r in routes])

    behind = from_behind(frame_rows[row_count - CONTEXT :], "seq", 1)
    frame_rows, places, chunks = lax.optimization_barrier((frame_rows, places, chunks))
    qkv, attended_grad, left, left_out, stats, weight, late, late_grad = front(
        places, frame_rows, grad_rows, w_qkv, w_out
    )
    left_other = to_device(left_out, to_core)
    own, grads, left_behind = early_tile(places, behind, weight, qkv, attended_grad, late, late_grad)
    own_other, left_other, grads = lax.optimization_barrier((to_device(own, to_core), left_other, grads))
    grads_other = to_device(grads, to_core)
    keep_a, send_a = weight_sections(first_wave_kernel, chunks, (left, left_other, own, own_other), inner, 1, "first_wave")
    got_a = [to_device(send_a[r], ROUTES[r][0]) for r in routes]
    keep_b, send_b = weight_sections(
        second_wave_kernel, chunks, (left, left_other, left_behind, grads, grads_other), inner, 3 * 10**9, "second_wave"
    )
    attended, send_b = lax.optimization_barrier((own[0], send_b))
    block_out = dot(attended, w_out).astype(BF16)
    got_b = [to_device(send_b[r], ROUTES[r][0]) for r in routes]

    got_a, got_b = lax.optimization_barrier((got_a, got_b))
    totals = [
        jnp.concatenate([plus(keep_a[r], got_a[r]), plus(keep_b[r], got_b[r])], axis=-1) for r in routes
    ]
    count = totals[0].shape[0] // 2
    projected_grad = jnp.concatenate([own[1], grads[0, :row_count, :inner], grads[1, :row_count, :inner]], axis=1)
    projected_grad, block_out, sends = lax.optimization_barrier(
        (projected_grad, block_out, [t[count:] for t in totals])
    )
    normed_grad = dot(projected_grad, w_qkv, NT)
    gots = lax.optimization_barrier([to_device(sends[r], ROUTES[r][1]) for r in routes])
    totals = [plus(totals[r][:count], gots[r]) for r in routes]
    groups = [jnp.concatenate(totals[:2], axis=-1), jnp.concatenate(totals[2:], axis=-1)]
    slots, grads, normed_grad = lax.optimization_barrier(
        ([[g[slot] for slot in range(1, 4)] for g in groups], grads, normed_grad)
    )
    returned = from_behind(grads[:, row_count:, :inner], "seq", -1)
    gots = [[to_device(slots[n][i], OWNERS[n][i]) for n in range(2)] for i in range(3)]
    groups = [plus(groups[n][0], *[gots[i][n] for i in range(3)]) for n in range(2)]
    returned = jnp.concatenate([jnp.zeros((CONTEXT, inner), BF16), returned[0], returned[1]], axis=1)
    returned = jnp.concatenate([jnp.zeros((row_count - CONTEXT, width), F32), dot(returned, w_qkv, NT)], axis=0)
    normed_grad = (normed_grad + returned).astype(BF16)
    frame_grad = normalize_grad(frame_rows.astype(F32), stats[0][:, None], stats[1][:, None], normed_grad.astype(F32))
    share = width // (CHUNKS * CORES * Z)
    tiles = 4 * inner // PAIR
    shares = pl.pallas_call(
        pieces_kernel,
        in_specs=[VMEM_SPEC] * 2,
        out_shape=jax.ShapeDtypeStruct((Z, tiles * share, PAIR), BF16),
        scratch_shapes=[pltpu.VMEM((Z, tiles * share, PAIR), F32)],
        compiler_params=params(24),
        name="pieces",
    )(*[in_vmem(g) for g in groups])
    rings = [[place * XL + x for place in range(Z)] for x in range(XL)]
    shares = lax.all_to_all(shares, "seq", 0, 0, axis_index_groups=rings, tiled=True)
    total = pl.pallas_call(
        total_kernel,
        in_specs=[VMEM_SPEC],
        out_shape=jax.ShapeDtypeStruct((share, 4 * inner), F32),
        compiler_params=params(24),
        name="total",
    )(in_vmem(shares))
    return block_out[None], frame_grad.astype(BF16)[None], total


def solution(mesh):
    placed = (P("dp", "seq", None), P("dp", "seq", None), P("dp"), P(), P())
    return jax.shard_map(
        on_device,
        mesh=mesh,
        in_specs=placed,
        out_specs=(P("dp", "seq", None), P("dp", "seq", None), P(("dp", "seq"), None)),
        check_vma=False,
    )
```

time: 103 us -> 96.4 us (0.936)
  waiting for transfers between devices: 33.7 us -> 15.9 us
  matrix products: 4.93 us -> 9.13 us
  starting transfers between devices: 36 us -> 39.2 us
  Pallas kernels: 22.2 us -> 24.7 us
  local copies, waits for them, and re-layouts: 0.52 us -> 2.19 us
    ppermute x21, waiting for transfers between devices: 18.4 us -> 11.7 us  [to_device(): return lax.ppermute(value, ('dp', 'seq'), pairs)]
    all_to_all x1, waiting for transfers between devices: 9.47 us -> 3.34 us  [on_device(): lax.all_to_all(shares, 'seq', 0, 0, axis_index_groups=rings, tiled=True)]
    ppermute x2, waiting for transfers between devices: 5.85 us -> 0.8 us  [from_behind(): lax.ppermute(value, axis, [(i, (i + by) % peers) for i in range(peers)])]
    dot_general x2 -> x3, matrix products: 4.93 us -> 9.13 us  [dot(): return lax.dot_general(a, b, dims, preferred_element_type=F32)]
    ppermute x2, starting transfers between devices: 3.57 us -> 6.74 us  [from_behind(): lax.ppermute(value, axis, [(i, (i + by) % peers) for i in range(peers)])]
    pallas_call x7 -> x4, Pallas kernels: 20.8 us -> 23.2 us  [the longest x1 11.8 us: front(): pl.pallas_call(front_kernel, in_specs=[SMEM_SPEC, VMEM_SPEC] + [HBM_SPEC]...]
    ppermute x21, starting transfers between devices: 26.9 us -> 24.9 us  [to_device(): return lax.ppermute(value, ('dp', 'seq'), pairs)]
    all_to_all x1, starting transfers between devices: 5.54 us -> 7.56 us  [on_device(): lax.all_to_all(shares, 'seq', 0, 0, axis_index_groups=rings, tiled=True)]
  transfers between devices with their start and end apart: 24 -> 24, of which waited for: 14 -> 11; matrix products, arithmetic and copies ran while one was open for 7% -> 12% of each run, Pallas kernels for 16% -> 25%
where the time goes in v3:
time: 96.4 us; the launch traced here: 96.1 us
  starting transfers between devices  39.2 us (41%)
  Pallas kernels  24.7 us (26%)
  waiting for transfers between devices  15.9 us (16%)
  matrix products  9.13 us (9%)
  other arithmetic  3.42 us (4%)
  local copies, waits for them, and re-layouts  2.19 us (2%)
  between operations  1.61 us (2%)
    ppermute x21, starting transfers between devices, to_device(): return lax.ppermute(value, ('dp', 'seq'), pairs)  24.9 us
    pallas_call x1, Pallas kernels, front(): pl.pallas_call(front_kernel, in_specs=[SMEM_SPEC, VMEM_SPEC] + [HBM_SPEC]...  11.8 us
    ppermute x21, waiting for transfers between devices, to_device(): return lax.ppermute(value, ('dp', 'seq'), pairs)  11.7 us
    dot_general x3, matrix products, dot(): return lax.dot_general(a, b, dims, preferred_element_type=F32)  9.13 us
    all_to_all x1, starting transfers between devices, on_device(): lax.all_to_all(shares, 'seq', 0, 0, axis_index_groups=rings, tiled=True)  7.56 us
    ppermute x2, starting transfers between devices, from_behind(): lax.ppermute(value, axis, [(i, (i + by) % peers) for i in range(peers)])  6.74 us
    pallas_call x2, Pallas kernels, weight_sections(): pl.pallas_call(kernel, in_specs=[SMEM_SPEC] + [VMEM_SPEC] * len(operands)...  5.98 us
    pallas_call x1, Pallas kernels, early_tile(): pl.pallas_call(early_kernel, in_specs=[SMEM_SPEC] + [VMEM_SPEC] * 7, out_...  5.5 us
  transfers between devices with their start and end apart: 24, of which 11 were waited for; matrix products, arithmetic and copies ran while one was open for 12% of the time, Pallas kernels for 25%

profile of v3, /device:TPU:8, one launch (start us, length us, event | category | flops | bytes accessed | tf_op | source)
XLA Modules:
  0.0 96.1 jit_solution(12419942163294996171)
XLA Ops:
  0.6 1.0 %slice_bitcast_fusion.4 = bf16[128,1536]{1,0:T(8,128)(2,1)S(1)} fusion(bf16[1,256,1536]{2,1,0:T(8,128)(2,1)} %param.7), kind=kLoop, calls=%fused_computation.53 | loop fusion | bytes 786432 | tf_op jit(solution)/shard_map/slice | solution.py:437
  1.7 1.6 %collective-permute-start = (bf16[128,1536]{1,0:T(8,128)(2,1)S(1)}, bf16[128,1536]{1,0:T(8,128)(2,1)S(1)}, u32[]{:S(2)}, u32[]{:S(2)}) collective-permute-start(bf16[128,1536]{1,0:T(8,128)(2,1)S(1)} %slice_bitcast_fusion.4), channel_id=1, source_target_pairs={{0,1},{1,2},{2,3},{3,4},{4,5},{5,6},{6,7},{7,8},{8,9},{9,10},{10,1... | collective-permute-start | bytes 1179656 | tf_op jit(solution)/shard_map/ppermute | solution.py:31
  3.9 0.1 pad_add_fusion.1.places
  4.0 1.0 %copy-done = bf16[384,384]{1,0:T(8,128)(2,1)S(1)} copy-done((bf16[384,384]{1,0:T(8,128)(2,1)S(1)}, bf16[384,384]{1,0:T(8,128)(2,1)}, u32[]{:S(2)}) %copy-start) | copy-done | bytes 294936
  5.0 11.8 %front.1 = (bf16[256,2304]{1,0:T(8,128)(2,1)S(1)}, bf16[256,768]{1,0:T(8,128)(2,1)S(1)}, bf16[768,512]{1,0:T(8,128)(2,1)S(1)}, bf16[768,512]{1,0:T(8,128)(2,1)S(...) custom-call(s32[3]{0:T(128)S(1)} %pad_add_fusion.1.places, ...), custom_call_target="tpu_custom_call" | custom-call | flops 3623878656 | bytes 11796480 | tf_op jit(solution)/shard_map/front/pallas_call | solution.py:218
  16.7 0.1 collective-permute-start.2
  16.8 0.8 collective-permute-done.frames_ref
  17.6 5.5 %attention_early.1 = (bf16[2,256,768]{2,1,0:T(8,128)(2,1)S(1)}, bf16[2,384,896]{2,1,0:T(8,128)(2,1)S(1)}, bf16[768,128]{1,0:T(8,128)(2,1)S(1)}) custom-call(s32[3]{0:T(128)S(1)} %pad_add_fusion.1.places, bf16[384,384]{1,0:T(8,128)(2,1)S(1)} %copy-done.1, bf16[128,1536]{1,0:T(8,128)(2,1)S(1)} %collective-permute-done.frames_ref, ...), custom_call_target="tpu_custom_call" | custom-call | flops 704643072 | bytes 1572864 | tf_op jit(solution)/shard_map/attention_early/pallas_call | solution.py:332
  23.1 0.1 collective-permute-start.1
  23.3 2.3 %collective-permute-done.1.right_other_ref = bf16[2,256,768]{2,1,0:T(8,128)(2,1)S(1)} collective-permute-done((bf16[2,256,768]{2,1,0:T(8,128)(2,1)S(1)}, bf16[2,256,768]{2,1,0:T(8,128)(2,1)S(1)}, u32[]{:S(2)}, u32[]{:S(2)}) %collective-permute-start.1) | collective-permute-done | bytes 786464 | tf_op jit(solution)/shard_map/ppermute | solution.py:42
  25.5 0.1 collective-permute-start.3
  25.7 0.1 slice_bitcast_fusion
  25.7 2.3 %first_wave.1 = (bf16[8,48,384]{2,1,0:T(8,128)(2,1)S(1)}, bf16[8,48,384]{2,1,0:T(8,128)(2,1)S(1)}, bf16[8,48,384]{2,1,0:T(8,128)(2,1)S(1)}, bf16[8,48,384]{2,1,0...) custom-call(s32[4,16]{1,0:T(4,128)S(1)} %pad_add_fusion.chunks, ...), custom_call_target="tpu_custom_call" | custom-call | flops 1 | bytes 1 | tf_op jit(solution)/shard_map/first_wave/pallas_call | solution.py:381
  28.0 1.5 %collective-permute-start.4 = (bf16[8,48,384]{2,1,0:T(8,128)(2,1)S(1)}, bf16[8,48,384]{2,1,0:T(8,128)(2,1)S(1)}, u32[]{:S(2)}, u32[]{:S(2)}) collective-permute-start(bf16[8,48,384]{2,1,0:T(8,128)(2,1)S(1)} %get-tuple-element.89), channel_id=1, source_target_pairs={{0,1},{1,0},{2,3},{3,2},{4,5},{5,4},{6,7},{7,6},{8,9},{9,8},{10,11... | collective-permute-start | bytes 884744 | tf_op jit(solution)/shard_map/ppermute | solution.py:42
  29.6 1.8 %collective-permute-start.5 = (bf16[8,48,384]{2,1,0:T(8,128)(2,1)S(1)}, bf16[8,48,384]{2,1,0:T(8,128)(2,1)S(1)}, u32[]{:S(2)}, u32[]{:S(2)}) collective-permute-start(bf16[8,48,384]{2,1,0:T(8,128)(2,1)S(1)} %get-tuple-element.90), channel_id=1, source_target_pairs={{0,33},{1,32},{2,35},{3,34},{4,37},{5,36},{6,39},{7,38},{8,41},{9,... | collective-permute-start | bytes 884744 | tf_op jit(solution)/shard_map/ppermute | solution.py:42
  31.4 0.5 collective-permute-start.6
  31.9 2.4 %collective-permute-start.7 = (bf16[8,48,384]{2,1,0:T(8,128)(2,1)S(1)}, bf16[8,48,384]{2,1,0:T(8,128)(2,1)S(1)}, u32[]{:S(2)}, u32[]{:S(2)}) collective-permute-start(bf16[8,48,384]{2,1,0:T(8,128)(2,1)S(1)} %get-tuple-element.92), channel_id=1, source_target_pairs={{0,192},{1,193},{2,194},{3,195},{4,196},{5,197},{6,198},{7,199},{8... | collective-permute-start | bytes 884744 | tf_op jit(solution)/shard_map/ppermute | solution.py:42
  34.3 0.1 pad_maximum_fusion
  34.5 3.7 %second_wave.1 = (bf16[8,48,384]{2,1,0:T(8,128)(2,1)S(1)}, bf16[8,48,384]{2,1,0:T(8,128)(2,1)S(1)}, bf16[8,48,384]{2,1,0:T(8,128)(2,1)S(1)}, bf16[8,48,384]{2,1,...) custom-call(s32[4,16]{1,0:T(4,128)S(1)} %pad_add_fusion.chunks, ...), custom_call_target="tpu_custom_call" | custom-call | flops 3000000000 | bytes 1 | tf_op jit(solution)/shard_map/second_wave/pallas_call | solution.py:381
  38.1 1.4 %collective-permute-start.10 = (bf16[8,48,384]{2,1,0:T(8,128)(2,1)S(1)}, bf16[8,48,384]{2,1,0:T(8,128)(2,1)S(1)}, u32[]{:S(2)}, u32[]{:S(2)}) collective-permute-start(bf16[8,48,384]{2,1,0:T(8,128)(2,1)S(1)} %get-tuple-element.95), channel_id=1, source_target_pairs={{0,64},{1,65},{2,66},{3,67},{4,68},{5,69},{6,70},{7,71},{8,72},{9,... | collective-permute-start | bytes 884744 | tf_op jit(solution)/shard_map/ppermute | solution.py:42
  39.6 0.4 collective-permute-start.11
  40.0 1.1 %collective-permute-start.8 = (bf16[8,48,384]{2,1,0:T(8,128)(2,1)S(1)}, bf16[8,48,384]{2,1,0:T(8,128)(2,1)S(1)}, u32[]{:S(2)}, u32[]{:S(2)}) collective-permute-start(bf16[8,48,384]{2,1,0:T(8,128)(2,1)S(1)} %get-tuple-element.93), channel_id=1, source_target_pairs={{0,1},{1,0},{2,3},{3,2},{4,5},{5,4},{6,7},{7,6},{8,9},{9,8},{10,11... | collective-permute-start | bytes 884744 | tf_op jit(solution)/shard_map/ppermute | solution.py:42
  41.2 1.1 %collective-permute-start.9 = (bf16[8,48,384]{2,1,0:T(8,128)(2,1)S(1)}, bf16[8,48,384]{2,1,0:T(8,128)(2,1)S(1)}, u32[]{:S(2)}, u32[]{:S(2)}) collective-permute-start(bf16[8,48,384]{2,1,0:T(8,128)(2,1)S(1)} %get-tuple-element.94), channel_id=1, source_target_pairs={{0,33},{1,32},{2,35},{3,34},{4,37},{5,36},{6,39},{7,38},{8,41},{9,... | collective-permute-start | bytes 884744 | tf_op jit(solution)/shard_map/ppermute | solution.py:42
  42.3 1.7 %convolution_convert_fusion = bf16[256,1536]{1,0:T(8,128)(2,1)} fusion(bf16[256,768]{1,0:T(8,128)(2,1)S(1)} %get-tuple-element.86, bf16[768,1536]{1,0:T(8,128)(2,1)S(1)} %copy-done.3), kind=kOutput, calls=%fused_computation | convolution fusion | flops 604372992 | bytes 3538944 | tf_op jit(solution)/shard_map/dot_general | solution.py:26
  44.0 2.5 %collective-permute-done.10 = bf16[8,48,384]{2,1,0:T(8,128)(2,1)S(1)} collective-permute-done((bf16[8,48,384]{2,1,0:T(8,128)(2,1)S(1)}, bf16[8,48,384]{2,1,0:T(8,128)(2,1)S(1)}, u32[]{:S(2)}, u32[]{:S(2)}) %collective-permute-start.10) | collective-permute-done | bytes 294944 | tf_op jit(solution)/shard_map/ppermute | solution.py:42
  46.5 1.0 %collective-permute-done.11 = bf16[8,48,384]{2,1,0:T(8,128)(2,1)S(1)} collective-permute-done((bf16[8,48,384]{2,1,0:T(8,128)(2,1)S(1)}, bf16[8,48,384]{2,1,0:T(8,128)(2,1)S(1)}, u32[]{:S(2)}, u32[]{:S(2)}) %collective-permute-start.11) | collective-permute-done | bytes 294944 | tf_op jit(solution)/shard_map/ppermute | solution.py:42
  47.5 0.3 collective-permute-done.8
  47.8 1.8 %collective-permute-done.9 = bf16[8,48,384]{2,1,0:T(8,128)(2,1)S(1)} collective-permute-done((bf16[8,48,384]{2,1,0:T(8,128)(2,1)S(1)}, bf16[8,48,384]{2,1,0:T(8,128)(2,1)S(1)}, u32[]{:S(2)}, u32[]{:S(2)}) %collective-permute-start.9) | collective-permute-done | bytes 294944 | tf_op jit(solution)/shard_map/ppermute | solution.py:42
  49.6 0.1 add_convert_fusion.5
  49.7 0.1 add_convert_fusion.6
  49.8 0.1 add_convert_fusion.7
  49.9 0.1 add_convert_fusion.8
  50.0 0.1 add_convert_fusion.9
  50.1 0.1 add_convert_fusion.10
  50.2 0.1 add_convert_fusion.11
  50.3 0.1 add_convert_fusion.12
  50.4 1.9 %collective-permute-start.12 = (bf16[4,48,768]{2,1,0:T(8,128)(2,1)S(1)}, bf16[4,48,768]{2,1,0:T(8,128)(2,1)S(1)}, u32[]{:S(2)}, u32[]{:S(2)}) collective-permute-start(bf16[4,48,768]{2,1,0:T(8,128)(2,1)S(1)} %fusion.13), channel_id=1, source_target_pairs={{0,33},{1,32},{2,35},{3,34},{4,37},{5,36},{6,39},{7,38},{8,41},{9,... | collective-permute-start | bytes 884744 | tf_op jit(solution)/shard_map/ppermute | solution.py:42
  52.3 1.2 %collective-permute-start.14 = (bf16[4,48,768]{2,1,0:T(8,128)(2,1)S(1)}, bf16[4,48,768]{2,1,0:T(8,128)(2,1)S(1)}, u32[]{:S(2)}, u32[]{:S(2)}) collective-permute-start(bf16[4,48,768]{2,1,0:T(8,128)(2,1)S(1)} %fusion.11), channel_id=1, source_target_pairs={{0,192},{1,193},{2,194},{3,195},{4,196},{5,197},{6,198},{7,199},{8... | collective-permute-start | bytes 884744 | tf_op jit(solution)/shard_map/ppermute | solution.py:42
  53.5 1.9 %collective-permute-start.15 = (bf16[4,48,768]{2,1,0:T(8,128)(2,1)S(1)}, bf16[4,48,768]{2,1,0:T(8,128)(2,1)S(1)}, u32[]{:S(2)}, u32[]{:S(2)}) collective-permute-start(bf16[4,48,768]{2,1,0:T(8,128)(2,1)S(1)} %fusion.10), channel_id=1, source_target_pairs={{0,64},{1,65},{2,66},{3,67},{4,68},{5,69},{6,70},{7,71},{8,72},{9,... | collective-permute-start | bytes 884744 | tf_op jit(solution)/shard_map/ppermute | solution.py:42
  55.4 2.0 %fusion.38 = f32[256,1536]{1,0:T(8,128)S(1)} fusion(bf16[256,2304]{1,0:T(8,128)(2,1)S(1)} %pad_maximum_fusion, bf16[1536,2304]{1,0:T(8,128)(2,1)S(1)} %bitcast.51), kind=kOutput, calls=%fused_computation.106 | convolution fusion | flops 1811939328 | bytes 9830400 | tf_op jit(solution)/shard_map/dot_general | solution.py:26
  57.4 1.0 %collective-permute-done.12 = bf16[4,48,768]{2,1,0:T(8,128)(2,1)S(1)} collective-permute-done((bf16[4,48,768]{2,1,0:T(8,128)(2,1)S(1)}, bf16[4,48,768]{2,1,0:T(8,128)(2,1)S(1)}, u32[]{:S(2)}, u32[]{:S(2)}) %collective-permute-start.12) | collective-permute-done | bytes 294944 | tf_op jit(solution)/shard_map/ppermute | solution.py:42
  58.5 0.6 collective-permute-done.13
  59.1 1.2 %collective-permute-done.15 = bf16[4,48,768]{2,1,0:T(8,128)(2,1)S(1)} collective-permute-done((bf16[4,48,768]{2,1,0:T(8,128)(2,1)S(1)}, bf16[4,48,768]{2,1,0:T(8,128)(2,1)S(1)}, u32[]{:S(2)}, u32[]{:S(2)}) %collective-permute-start.15) | collective-permute-done | bytes 294944 | tf_op jit(solution)/shard_map/ppermute | solution.py:42
  60.2 0.1 add_convert_fusion.1
  60.3 0.1 add_convert_fusion.2
  60.4 0.1 add_convert_fusion.3
  60.5 0.1 add_convert_fusion.4
  60.6 1.8 %collective-permute-start.20 = (bf16[48,1536]{1,0:T(8,128)(2,1)S(1)}, bf16[48,1536]{1,0:T(8,128)(2,1)S(1)}, u32[]{:S(2)}, u32[]{:S(2)}) collective-permute-start(bf16[48,1536]{1,0:T(8,128)(2,1)S(1)} %get-tuple-element.128), channel_id=1, source_target_pairs={{0,33},{1,32},{2,35},{3,34},{4,37},{5,36},{6,39},{7,38},{8,41},{9,... | collective-permute-start | bytes 442376 | tf_op jit(solution)/shard_map/ppermute | solution.py:42
  62.4 1.4 %collective-permute-start.21 = (bf16[48,1536]{1,0:T(8,128)(2,1)S(1)}, bf16[48,1536]{1,0:T(8,128)(2,1)S(1)}, u32[]{:S(2)}, u32[]{:S(2)}) collective-permute-start(bf16[48,1536]{1,0:T(8,128)(2,1)S(1)} %get-tuple-element.129), channel_id=1, source_target_pairs={{0,1},{1,0},{2,3},{3,2},{4,5},{5,4},{6,7},{7,6},{8,9},{9,8},{10,11... | collective-permute-start | bytes 442376 | tf_op jit(solution)/shard_map/ppermute | solution.py:42
  63.8 1.6 %collective-permute-start.22 = (bf16[48,1536]{1,0:T(8,128)(2,1)S(1)}, bf16[48,1536]{1,0:T(8,128)(2,1)S(1)}, u32[]{:S(2)}, u32[]{:S(2)}) collective-permute-start(bf16[48,1536]{1,0:T(8,128)(2,1)S(1)} %get-tuple-element.130), channel_id=1, source_target_pairs={{0,32},{1,33},{2,34},{3,35},{4,36},{5,37},{6,38},{7,39},{8,40},{9,... | collective-permute-start | bytes 442376 | tf_op jit(solution)/shard_map/ppermute | solution.py:42
  65.4 1.3 %collective-permute-start.17 = (bf16[48,1536]{1,0:T(8,128)(2,1)S(1)}, bf16[48,1536]{1,0:T(8,128)(2,1)S(1)}, u32[]{:S(2)}, u32[]{:S(2)}) collective-permute-start(bf16[48,1536]{1,0:T(8,128)(2,1)S(1)} %get-tuple-element.125), channel_id=1, source_target_pairs={{0,192},{1,193},{2,194},{3,195},{4,196},{5,197},{6,198},{7,199},{8... | collective-permute-start | bytes 442376 | tf_op jit(solution)/shard_map/ppermute | solution.py:42
  66.7 2.6 %collective-permute-start.18 = (bf16[48,1536]{1,0:T(8,128)(2,1)S(1)}, bf16[48,1536]{1,0:T(8,128)(2,1)S(1)}, u32[]{:S(2)}, u32[]{:S(2)}) collective-permute-start(bf16[48,1536]{1,0:T(8,128)(2,1)S(1)} %get-tuple-element.126), channel_id=1, source_target_pairs={{0,64},{1,65},{2,66},{3,67},{4,68},{5,69},{6,70},{7,71},{8,72},{9,... | collective-permute-start | bytes 442376 | tf_op jit(solution)/shard_map/ppermute | solution.py:42
  69.4 0.5 collective-permute-start.19
  69.9 5.2 %collective-permute-start.16 = (bf16[2,128,768]{2,1,0:T(8,128)(2,1)S(1)}, bf16[2,128,768]{2,1,0:T(8,128)(2,1)S(1)}, u32[]{:S(2)}, u32[]{:S(2)}) collective-permute-start(bf16[2,128,768]{2,1,0:T(8,128)(2,1)S(1)} %slice.102), channel_id=1, source_target_pairs={{0,15},{1,0},{2,1},{3,2},{4,3},{5,4},{6,5},{7,6},{8,7},{9,8},{10,9... | collective-permute-start | bytes 1179656 | tf_op jit(solution)/shard_map/ppermute | solution.py:31
  75.1 0.1 fusion.17.refs_1_
  75.2 1.0 %collective-permute-done.19 = bf16[48,1536]{1,0:T(8,128)(2,1)S(1)} collective-permute-done((bf16[48,1536]{1,0:T(8,128)(2,1)S(1)}, bf16[48,1536]{1,0:T(8,128)(2,1)S(1)}, u32[]{:S(2)}, u32[]{:S(2)}) %collective-permute-start.19) | collective-permute-done | bytes 147488 | tf_op jit(solution)/shard_map/ppermute | solution.py:42
  76.1 0.1 fusion.20.refs_0_
  76.2 0.8 pieces.1
  77.0 7.6 %all-to-all-start = ((bf16[8,144,128]{2,1,0:T(8,128)(2,1)}), bf16[8,144,128]{2,1,0:T(8,128)(2,1)S(1)}, u32[]{:S(2)}, u32[]{:S(2)}) async-start(bf16[8,144,128]{2,1,0:T(8,128)(2,1)} %pieces.1), calls=%async_computation | async-start | bytes 589824 | tf_op jit(solution)/shard_map/all_to_all | solution.py:489
  84.6 5.5 %fusion.5 = f32[128,1536]{1,0:T(8,128)S(1)} fusion(bf16[1536,2304]{1,0:T(8,128)(2,1)} %weight_ref.1, bf16[128,768]{1,0:T(8,128)(2,1)S(1)} %get-tuple-element.145, bf16[128,768]{1,0:T(8,128)(2,1)S(1)} %get-tuple-element.144, bf16[2304]{0:T(1024)(128)(2,1)S(1)} %pad.1.clone), kind=kOutput, calls=%fused_computation.32 | convolution fusion | flops 907739136 | bytes 8262144 | tf_op jit(solution)/shard_map/dot_general | solution.py:26
  90.1 0.5 convert_reduce_fusion
  90.7 1.4 %fusion.4 = bf16[1,256,1536]{2,1,0:T(8,128)(2,1)} fusion(bf16[256,1536]{1,0:T(8,128)(2,1)S(1)} %bitcast.54, bf16[256,1536]{1,0:T(8,128)(2,1)S(1)} %get-tuple-element.133, f32[256]{0:T(256)S(1)} %broadcast_multiply_fusion, f32[256]{0:T(256)S(1)} %bitcast.56, f32[256]{0:T(256)S(1)} %broadcast_multiply_fusion.1, f32[256]{0:T(256)S(1)} %bitcast.58), kind=kLoop, calls=%fused_computation.11 | loop fusion | flops 3538944 | bytes 2363392 | tf_op jit(solution)/shard_map/broadcast_in_dim | solution.py:497
  92.1 3.3 %all-to-all-done.in_ref = bf16[8,144,128]{2,1,0:T(8,128)(2,1)S(1)} async-done(((bf16[8,144,128]{2,1,0:T(8,128)(2,1)}), bf16[8,144,128]{2,1,0:T(8,128)(2,1)S(1)}, u32[]{:S(2)}, u32[]{:S(2)}) %all-to-all-start) | async-done | bytes 294944 | tf_op jit(solution)/shard_map/all_to_all | solution.py:489
  95.4 0.7 total.1
  (43 shorter events, 0.4 us)
Async XLA Ops:
  1.7 16.0 %collective-permute-start = (bf16[128,1536]{1,0:T(8,128)(2,1)S(1)}, bf16[128,1536]{1,0:T(8,128)(2,1)S(1)}, u32[]{:S(2)}, u32[]{:S(2)}) collective-permute-start(bf16[128,1536]{1,0:T(8,128)(2,1)S(1)} %slice_bitcast_fusion.4), channel_id=1, source_target_pairs={{0,1},{1,2},{2,3},{3,4},{4,5},{5,6},{6,7},{7,8},{8,9},{9,10},{10,1... | collective-permute-start | bytes 1179656 | tf_op jit(solution)/shard_map/ppermute | solution.py:31
  4.0 1.0 %copy-start = (bf16[384,384]{1,0:T(8,128)(2,1)S(1)}, bf16[384,384]{1,0:T(8,128)(2,1)}, u32[]{:S(2)}) copy-start(bf16[384,384]{1,0:T(8,128)(2,1)} %constant.67.clone.order_ref) | copy-start | bytes 884740
  5.0 12.7 %copy-start.1 = (bf16[384,384]{1,0:T(8,128)(2,1)S(1)}, bf16[384,384]{1,0:T(8,128)(2,1)}, u32[]{:S(2)}) copy-start(bf16[384,384]{1,0:T(8,128)(2,1)} %constant.67.clone.order_ref) | copy-start | bytes 884740
  16.7 6.5 %collective-permute-start.2 = (bf16[768,512]{1,0:T(8,128)(2,1)S(1)}, bf16[768,512]{1,0:T(8,128)(2,1)S(1)}, u32[]{:S(2)}, u32[]{:S(2)}) collective-permute-start(bf16[768,512]{1,0:T(8,128)(2,1)S(1)} %get-tuple-element.75), channel_id=1, source_target_pairs={{0,16},{1,17},{2,18},{3,19},{4,20},{5,21},{6,22},{7,23},{8,24},{9,... | collective-permute-start | bytes 2359304 | tf_op jit(solution)/shard_map/ppermute | solution.py:42
  23.1 2.4 %collective-permute-start.1 = (bf16[2,256,768]{2,1,0:T(8,128)(2,1)S(1)}, bf16[2,256,768]{2,1,0:T(8,128)(2,1)S(1)}, u32[]{:S(2)}, u32[]{:S(2)}) collective-permute-start(bf16[2,256,768]{2,1,0:T(8,128)(2,1)S(1)} %get-tuple-element.74.right_ref), channel_id=1, source_target_pairs={{0,16},{1,17},{2,18},{3,19},{4,20},{5,21},{6,22},{7,23},{8,24},{9,... | collective-permute-start | bytes 2359304 | tf_op jit(solution)/shard_map/ppermute | solution.py:42
  25.5 8.9 %collective-permute-start.3 = (bf16[2,384,896]{2,1,0:T(8,128)(2,1)S(1)}, bf16[2,384,896]{2,1,0:T(8,128)(2,1)S(1)}, u32[]{:S(2)}, u32[]{:S(2)}) collective-permute-start(bf16[2,384,896]{2,1,0:T(8,128)(2,1)S(1)} %get-tuple-element.124.right_ref), channel_id=1, source_target_pairs={{0,16},{1,17},{2,18},{3,19},{4,20},{5,21},{6,22},{7,23},{8,24},{9,... | collective-permute-start | bytes 4128776 | tf_op jit(solution)/shard_map/ppermute | solution.py:42
  28.0 11.5 %collective-permute-start.4 = (bf16[8,48,384]{2,1,0:T(8,128)(2,1)S(1)}, bf16[8,48,384]{2,1,0:T(8,128)(2,1)S(1)}, u32[]{:S(2)}, u32[]{:S(2)}) collective-permute-start(bf16[8,48,384]{2,1,0:T(8,128)(2,1)S(1)} %get-tuple-element.89), channel_id=1, source_target_pairs={{0,1},{1,0},{2,3},{3,2},{4,5},{5,4},{6,7},{7,6},{8,9},{9,8},{10,11... | collective-permute-start | bytes 884744 | tf_op jit(solution)/shard_map/ppermute | solution.py:42
  29.6 10.4 %collective-permute-start.5 = (bf16[8,48,384]{2,1,0:T(8,128)(2,1)S(1)}, bf16[8,48,384]{2,1,0:T(8,128)(2,1)S(1)}, u32[]{:S(2)}, u32[]{:S(2)}) collective-permute-start(bf16[8,48,384]{2,1,0:T(8,128)(2,1)S(1)} %get-tuple-element.90), channel_id=1, source_target_pairs={{0,33},{1,32},{2,35},{3,34},{4,37},{5,36},{6,39},{7,38},{8,41},{9,... | collective-permute-start | bytes 884744 | tf_op jit(solution)/shard_map/ppermute | solution.py:42
  31.4 9.7 %collective-permute-start.6 = (bf16[8,48,384]{2,1,0:T(8,128)(2,1)S(1)}, bf16[8,48,384]{2,1,0:T(8,128)(2,1)S(1)}, u32[]{:S(2)}, u32[]{:S(2)}) collective-permute-start(bf16[8,48,384]{2,1,0:T(8,128)(2,1)S(1)} %get-tuple-element.91), channel_id=1, source_target_pairs={{0,64},{1,65},{2,66},{3,67},{4,68},{5,69},{6,70},{7,71},{8,72},{9,... | collective-permute-start | bytes 884744 | tf_op jit(solution)/shard_map/ppermute | solution.py:42
  31.9 12.1 %collective-permute-start.7 = (bf16[8,48,384]{2,1,0:T(8,128)(2,1)S(1)}, bf16[8,48,384]{2,1,0:T(8,128)(2,1)S(1)}, u32[]{:S(2)}, u32[]{:S(2)}) collective-permute-start(bf16[8,48,384]{2,1,0:T(8,128)(2,1)S(1)} %get-tuple-element.92), channel_id=1, source_target_pairs={{0,192},{1,193},{2,194},{3,195},{4,196},{5,197},{6,198},{7,199},{8... | collective-permute-start | bytes 884744 | tf_op jit(solution)/shard_map/ppermute | solution.py:42
  34.4 7.8 %copy-start.3 = (bf16[768,1536]{1,0:T(8,128)(2,1)S(1)}, bf16[768,1536]{1,0:T(8,128)(2,1)}, u32[]{:S(2)}) copy-start(bf16[768,1536]{1,0:T(8,128)(2,1)} %out_ref.1) | copy-start | bytes 7077892
  38.1 8.3 %collective-permute-start.10 = (bf16[8,48,384]{2,1,0:T(8,128)(2,1)S(1)}, bf16[8,48,384]{2,1,0:T(8,128)(2,1)S(1)}, u32[]{:S(2)}, u32[]{:S(2)}) collective-permute-start(bf16[8,48,384]{2,1,0:T(8,128)(2,1)S(1)} %get-tuple-element.95), channel_id=1, source_target_pairs={{0,64},{1,65},{2,66},{3,67},{4,68},{5,69},{6,70},{7,71},{8,72},{9,... | collective-permute-start | bytes 884744 | tf_op jit(solution)/shard_map/ppermute | solution.py:42
  39.6 7.9 %collective-permute-start.11 = (bf16[8,48,384]{2,1,0:T(8,128)(2,1)S(1)}, bf16[8,48,384]{2,1,0:T(8,128)(2,1)S(1)}, u32[]{:S(2)}, u32[]{:S(2)}) collective-permute-start(bf16[8,48,384]{2,1,0:T(8,128)(2,1)S(1)} %get-tuple-element.96), channel_id=1, source_target_pairs={{0,192},{1,193},{2,194},{3,195},{4,196},{5,197},{6,198},{7,199},{8... | collective-permute-start | bytes 884744 | tf_op jit(solution)/shard_map/ppermute | solution.py:42
  40.0 7.7 %collective-permute-start.8 = (bf16[8,48,384]{2,1,0:T(8,128)(2,1)S(1)}, bf16[8,48,384]{2,1,0:T(8,128)(2,1)S(1)}, u32[]{:S(2)}, u32[]{:S(2)}) collective-permute-start(bf16[8,48,384]{2,1,0:T(8,128)(2,1)S(1)} %get-tuple-element.93), channel_id=1, source_target_pairs={{0,1},{1,0},{2,3},{3,2},{4,5},{5,4},{6,7},{7,6},{8,9},{9,8},{10,11... | collective-permute-start | bytes 884744 | tf_op jit(solution)/shard_map/ppermute | solution.py:42
  41.2 8.4 %collective-permute-start.9 = (bf16[8,48,384]{2,1,0:T(8,128)(2,1)S(1)}, bf16[8,48,384]{2,1,0:T(8,128)(2,1)S(1)}, u32[]{:S(2)}, u32[]{:S(2)}) collective-permute-start(bf16[8,48,384]{2,1,0:T(8,128)(2,1)S(1)} %get-tuple-element.94), channel_id=1, source_target_pairs={{0,33},{1,32},{2,35},{3,34},{4,37},{5,36},{6,39},{7,38},{8,41},{9,... | collective-permute-start | bytes 884744 | tf_op jit(solution)/shard_map/ppermute | solution.py:42
  42.3 13.1 %slice-start = ((s8[7077888]{0:T(1024)(128)(4,1)}), s8[4194304]{0:T(1024)(128)(4,1)S(1)}, s32[]{:S(2)}) async-start(s8[7077888]{0:T(1024)(128)(4,1)} %bitcast.50), calls=%async_computation.1 | async-start | bytes 8388608
  49.8 5.6 %slice-start.1 = ((s8[7077888]{0:T(1024)(128)(4,1)}), s8[2883584]{0:T(1024)(128)(4,1)S(1)}, s32[]{:S(2)}) async-start(s8[7077888]{0:T(1024)(128)(4,1)} %bitcast.50), calls=%async_computation.2 | async-start | bytes 5767168
  50.4 8.0 %collective-permute-start.12 = (bf16[4,48,768]{2,1,0:T(8,128)(2,1)S(1)}, bf16[4,48,768]{2,1,0:T(8,128)(2,1)S(1)}, u32[]{:S(2)}, u32[]{:S(2)}) collective-permute-start(bf16[4,48,768]{2,1,0:T(8,128)(2,1)S(1)} %fusion.13), channel_id=1, source_target_pairs={{0,33},{1,32},{2,35},{3,34},{4,37},{5,36},{6,39},{7,38},{8,41},{9,... | collective-permute-start | bytes 884744 | tf_op jit(solution)/shard_map/ppermute | solution.py:42
  52.3 6.7 %collective-permute-start.13 = (bf16[4,48,768]{2,1,0:T(8,128)(2,1)S(1)}, bf16[4,48,768]{2,1,0:T(8,128)(2,1)S(1)}, u32[]{:S(2)}, u32[]{:S(2)}) collective-permute-start(bf16[4,48,768]{2,1,0:T(8,128)(2,1)S(1)} %fusion.12), channel_id=1, source_target_pairs={{0,1},{1,0},{2,3},{3,2},{4,5},{5,4},{6,7},{7,6},{8,9},{9,8},{10,11... | collective-permute-start | bytes 884744 | tf_op jit(solution)/shard_map/ppermute | solution.py:42
  52.3 6.7 %collective-permute-start.14 = (bf16[4,48,768]{2,1,0:T(8,128)(2,1)S(1)}, bf16[4,48,768]{2,1,0:T(8,128)(2,1)S(1)}, u32[]{:S(2)}, u32[]{:S(2)}) collective-permute-start(bf16[4,48,768]{2,1,0:T(8,128)(2,1)S(1)} %fusion.11), channel_id=1, source_target_pairs={{0,192},{1,193},{2,194},{3,195},{4,196},{5,197},{6,198},{7,199},{8... | collective-permute-start | bytes 884744 | tf_op jit(solution)/shard_map/ppermute | solution.py:42
  53.5 6.7 %collective-permute-start.15 = (bf16[4,48,768]{2,1,0:T(8,128)(2,1)S(1)}, bf16[4,48,768]{2,1,0:T(8,128)(2,1)S(1)}, u32[]{:S(2)}, u32[]{:S(2)}) collective-permute-start(bf16[4,48,768]{2,1,0:T(8,128)(2,1)S(1)} %fusion.10), channel_id=1, source_target_pairs={{0,64},{1,65},{2,66},{3,67},{4,68},{5,69},{6,70},{7,71},{8,72},{9,... | collective-permute-start | bytes 884744 | tf_op jit(solution)/shard_map/ppermute | solution.py:42
  60.6 8.8 %collective-permute-start.20 = (bf16[48,1536]{1,0:T(8,128)(2,1)S(1)}, bf16[48,1536]{1,0:T(8,128)(2,1)S(1)}, u32[]{:S(2)}, u32[]{:S(2)}) collective-permute-start(bf16[48,1536]{1,0:T(8,128)(2,1)S(1)} %get-tuple-element.128), channel_id=1, source_target_pairs={{0,33},{1,32},{2,35},{3,34},{4,37},{5,36},{6,39},{7,38},{8,41},{9,... | collective-permute-start | bytes 442376 | tf_op jit(solution)/shard_map/ppermute | solution.py:42
  62.4 7.5 %collective-permute-start.21 = (bf16[48,1536]{1,0:T(8,128)(2,1)S(1)}, bf16[48,1536]{1,0:T(8,128)(2,1)S(1)}, u32[]{:S(2)}, u32[]{:S(2)}) collective-permute-start(bf16[48,1536]{1,0:T(8,128)(2,1)S(1)} %get-tuple-element.129), channel_id=1, source_target_pairs={{0,1},{1,0},{2,3},{3,2},{4,5},{5,4},{6,7},{7,6},{8,9},{9,8},{10,11... | collective-permute-start | bytes 442376 | tf_op jit(solution)/shard_map/ppermute | solution.py:42
  63.8 11.2 %collective-permute-start.22 = (bf16[48,1536]{1,0:T(8,128)(2,1)S(1)}, bf16[48,1536]{1,0:T(8,128)(2,1)S(1)}, u32[]{:S(2)}, u32[]{:S(2)}) collective-permute-start(bf16[48,1536]{1,0:T(8,128)(2,1)S(1)} %get-tuple-element.130), channel_id=1, source_target_pairs={{0,32},{1,33},{2,34},{3,35},{4,36},{5,37},{6,38},{7,39},{8,40},{9,... | collective-permute-start | bytes 442376 | tf_op jit(solution)/shard_map/ppermute | solution.py:42
  65.4 9.7 %collective-permute-start.17 = (bf16[48,1536]{1,0:T(8,128)(2,1)S(1)}, bf16[48,1536]{1,0:T(8,128)(2,1)S(1)}, u32[]{:S(2)}, u32[]{:S(2)}) collective-permute-start(bf16[48,1536]{1,0:T(8,128)(2,1)S(1)} %get-tuple-element.125), channel_id=1, source_target_pairs={{0,192},{1,193},{2,194},{3,195},{4,196},{5,197},{6,198},{7,199},{8... | collective-permute-start | bytes 442376 | tf_op jit(solution)/shard_map/ppermute | solution.py:42
  66.7 8.4 %collective-permute-start.18 = (bf16[48,1536]{1,0:T(8,128)(2,1)S(1)}, bf16[48,1536]{1,0:T(8,128)(2,1)S(1)}, u32[]{:S(2)}, u32[]{:S(2)}) collective-permute-start(bf16[48,1536]{1,0:T(8,128)(2,1)S(1)} %get-tuple-element.126), channel_id=1, source_target_pairs={{0,64},{1,65},{2,66},{3,67},{4,68},{5,69},{6,70},{7,71},{8,72},{9,... | collective-permute-start | bytes 442376 | tf_op jit(solution)/shard_map/ppermute | solution.py:42
  69.4 6.7 %collective-permute-start.19 = (bf16[48,1536]{1,0:T(8,128)(2,1)S(1)}, bf16[48,1536]{1,0:T(8,128)(2,1)S(1)}, u32[]{:S(2)}, u32[]{:S(2)}) collective-permute-start(bf16[48,1536]{1,0:T(8,128)(2,1)S(1)} %get-tuple-element.127), channel_id=1, source_target_pairs={{0,128},{1,129},{2,130},{3,131},{4,132},{5,133},{6,134},{7,135},{8... | collective-permute-start | bytes 442376 | tf_op jit(solution)/shard_map/ppermute | solution.py:42
  69.9 14.7 %collective-permute-start.16 = (bf16[2,128,768]{2,1,0:T(8,128)(2,1)S(1)}, bf16[2,128,768]{2,1,0:T(8,128)(2,1)S(1)}, u32[]{:S(2)}, u32[]{:S(2)}) collective-permute-start(bf16[2,128,768]{2,1,0:T(8,128)(2,1)S(1)} %slice.102), channel_id=1, source_target_pairs={{0,15},{1,0},{2,1},{3,2},{4,3},{5,4},{6,5},{7,6},{8,7},{9,8},{10,9... | collective-permute-start | bytes 1179656 | tf_op jit(solution)/shard_map/ppermute | solution.py:31
  77.0 18.4 %all-to-all-start = ((bf16[8,144,128]{2,1,0:T(8,128)(2,1)}), bf16[8,144,128]{2,1,0:T(8,128)(2,1)S(1)}, u32[]{:S(2)}, u32[]{:S(2)}) async-start(bf16[8,144,128]{2,1,0:T(8,128)(2,1)} %pieces.1), calls=%async_computation | async-start | bytes 589824 | tf_op jit(solution)/shard_map/all_to_all | solution.py:489
  84.6 5.5 %copy-start.2 = (bf16[1,256,1536]{2,1,0:T(8,128)(2,1)S(1)}, bf16[1,256,1536]{2,1,0:T(8,128)(2,1)}, u32[]{:S(2)}) copy-start(bf16[1,256,1536]{2,1,0:T(8,128)(2,1)} %param.7) | copy-start | bytes 2359300

commit v4 on v3

--- a/solution.py
+++ b/solution.py
@@ -139,24 +139,49 @@
     return pltpu.CompilerParams(vmem_limit_bytes=mebibytes * 2**20)
 
 
-def turn(ref, order_ref, store):
+def turn(ref, order_ref, here, store):
     rows = order_ref.shape[0]
     half = rows // CORES
     for y in range(Y):
         turned = dot(order_ref[...], ref[:, y * rows : (y + 1) * rows].T).astype(BF16)
-        for core in range(CORES):
-            store(core, slice(y * half, (y + 1) * half), turned[core * half : (core + 1) * half])
+        first, second = turned[:half], turned[half:]
+        at = slice(y * half, (y + 1) * half)
+        store(at, jnp.where(here == 0, first, second), jnp.where(here == 0, second, first))
+
+
+def last_rows(frames):
+    rows, width = frames.shape
+
+    def kernel(frames_ref, out_ref, sem):
+        copy = pltpu.make_async_copy(frames_ref.at[pl.ds(rows - CONTEXT, CONTEXT)], out_ref, sem)
+        copy.start()
+        copy.wait()
+
+    return pl.pallas_call(
+        kernel,
+        in_specs=[HBM_SPEC],
+        out_specs=VMEM_SPEC,
+        out_shape=pltpu.VMEM((CONTEXT, width), BF16),
+        scratch_shapes=[pltpu.SemaphoreType.DMA],
+        compiler_params=params(4),
+        cost_estimate=cost(1, 1),
+        name="last_rows",
+    )(in_hbm(frames))
 
 
 def front_kernel(
-    places, order_ref, frames_ref, cotangent_ref, weight_ref, out_ref,
-    qkv_ref, grad_ref, keep_ref, send_ref, stats_ref, weight, late_ref, dkv_ref,
-    rows, cotangent, outer, normed, sems,
+    places, lengths_ref, order_ref, frames_ref, cotangent_ref, weight_ref, out_ref,
+    qkv_ref, grad_ref, keep_ref, send_ref, stats_ref, weight, late_ref, dkv_ref, order,
+    length, rows, cotangent, outer, normed, sems,
 ):
-    here = places[2]
+    here = places[1]
     tokens = rows.shape[0]
     thirds = weight.shape[1] // 3
     block = [slice(n * thirds, (n + 1) * thirds) for n in range(3)]
+    small = [
+        pltpu.make_async_copy(order_ref, order, sems.at[6]),
+        pltpu.make_async_copy(lengths_ref, length, sems.at[7]),
+    ]
     copies = [
         pltpu.make_async_copy(frames_ref, rows, sems.at[0]),
         pltpu.make_async_copy(cotangent_ref, cotangent, sems.at[1]),
@@ -165,18 +190,13 @@
         pltpu.make_async_copy(weight_ref.at[:, pl.ds(n * thirds, thirds)], weight.at[:, pl.ds(n * thirds, thirds)], sems.at[3 + n])
         for n in range(3)
     ]
-    for copy in copies:
+    for copy in copies[:1] + small + copies[1:]:
         copy.start()
 
     def put(columns):
-        def store(core, at, values):
-            @pl.when(here == core)
-            def _():
-                keep_ref[at, columns] = values
-
-            @pl.when(here != core)
-            def _():
-                send_ref[at, columns] = values
+        def store(at, own, other):
+            keep_ref[at, columns] = own
+            send_ref[at, columns] = other
 
         return store
 
@@ -186,14 +206,15 @@
     for n, column in enumerate((average, inverse)):
         stats_ref[n : n + 1, :] = jnp.broadcast_to(column, (tokens, PAIR)).T[:1]
     normed[...] = ((values - average) * inverse).astype(BF16)
-    turn(normed, order_ref, put(slice(0, tokens)))
+    small[0].wait()
+    turn(normed, order, here, put(slice(0, tokens)))
     copies[1].wait()
-    turn(cotangent, order_ref, put(slice(tokens, 2 * tokens)))
+    turn(cotangent, order, here, put(slice(tokens, 2 * tokens)))
     copies[2].wait()
     grad_ref[...] = dot(cotangent[...], outer[...], NT).astype(BF16)
     for n in range(3):
         copies[3 + n].wait()
-        qkv_ref[:, block[n]] = dot(normed[...], weight[:, block[n]]).astype(BF16)
+    qkv_ref[...] = dot(normed[...], weight[...]).astype(BF16)
 
     inner = thirds
 
@@ -208,17 +229,19 @@
         dkv_ref[0, :, at] = dk
         dkv_ref[1, :, at] = dv
 
-    attend(places[1] + CONTEXT, places[0], inner, operands, results)
-
-
-def front(places, frames, cotangent, w_qkv, w_out):
+    small[1].wait()
+    attend(places[0] + CONTEXT, length[0], inner, operands, results)
+
+
+def front(places, lengths, frames, cotangent, w_qkv, w_out):
     tokens, width = frames.shape
     inner = w_out.shape[0]
+    order = row_order(width)
     turned = pltpu.VMEM((width // CORES, 2 * tokens), BF16)
     return pl.pallas_call(
         front_kernel,
-        in_specs=[SMEM_SPEC, VMEM_SPEC] + [HBM_SPEC] * 4,
-        out_specs=[VMEM_SPEC] * 8,
+        in_specs=[SMEM_SPEC] + [HBM_SPEC] * 6,
+        out_specs=[VMEM_SPEC] * 9,
         out_shape=[
             pltpu.VMEM((tokens, 3 * inner), BF16),
             pltpu.VMEM((tokens, inner), BF16),
@@ -228,18 +251,20 @@
             pltpu.VMEM((width, 3 * inner), BF16),
             pltpu.VMEM((2, CONTEXT, inner), BF16),
             pltpu.VMEM((2, tokens, inner), F32),
+            pltpu.VMEM(order.shape, BF16),
         ],
         scratch_shapes=[
+            pltpu.SMEM((1,), jnp.int32),
             pltpu.VMEM((tokens, width), BF16),
             pltpu.VMEM((tokens, width), BF16),
             pltpu.VMEM((inner, width), BF16),
             pltpu.VMEM((tokens, width), BF16),
-            pltpu.SemaphoreType.DMA((6,)),
+            pltpu.SemaphoreType.DMA((8,)),
         ],
         compiler_params=params(24),
         cost_estimate=cost(12 * tokens * width * inner, 10 * inner * width),
         name="front",
-    )(places, in_vmem(row_order(width)), *[in_hbm(o) for o in (frames, cotangent, w_qkv, w_out)])
+    )(places, lengths, *[in_hbm(o) for o in (order, frames, cotangent, w_qkv, w_out)])
 
 
 def pair_columns(pair, inner):
@@ -282,11 +307,15 @@
         results(pair, mixed, dq, dot(dscores, q2), dot(rounded, do2))
 
 
-def early_kernel(places, order_ref, frames_ref, weight_ref, qkv_ref, do_ref, late_ref, add_ref,
-                 out_ref, dkv_ref, turned_ref, normed, halo):
+def early_kernel(
+    places, lengths_ref, order_ref, frames_ref, weight_ref, qkv_ref, do_ref, late_ref, add_ref,
+    out_ref, dkv_ref, turned_ref, length, normed, halo, sem,
+):
+    fetch = pltpu.make_async_copy(lengths_ref, length, sem)
+    fetch.start()
     inner = do_ref.shape[1]
     rows = qkv_ref.shape[0]
-    here = places[2]
+    here = places[1]
     values = frames_ref[...].astype(F32)
     average, inverse = statistics(values)
     normed[...] = ((values - average) * inverse).astype(BF16)
@@ -294,20 +323,15 @@
     out_ref[:, CONTEXT:, :] = late_ref[...]
     dkv_ref[:, CONTEXT:rows, :inner] = add_ref[:, CONTEXT:, :].astype(BF16)
 
-    def store(core, at, values):
-        @pl.when(here == core)
-        def _():
-            turned_ref[at, :] = values
-
-        @pl.when(here != core)
-        def _():
-            half = dkv_ref.shape[1]
-            for n in range(2):
-                first, last = max(at.start, n * half), min(at.stop, (n + 1) * half)
-                if first < last:
-                    dkv_ref[n, first - n * half : last - n * half, inner:] = values[first - at.start : last - at.start]
-
-    turn(normed, order_ref, store)
+    def store(at, own, other):
+        turned_ref[at, :] = own
+        half = dkv_ref.shape[1]
+        for n in range(2):
+            first, last = max(at.start, n * half), min(at.stop, (n + 1) * half)
+            if first < last:
+                dkv_ref[n, first - n * half : last - n * half, inner:] = other[first - at.start : last - at.start]
+
+    turn(normed, order_ref, here, store)
 
     def operands(pair):
         q, k, v = pair_columns(pair, inner)
@@ -323,26 +347,32 @@
             dkv_ref[n, rows:, at] = grad[:CONTEXT].astype(BF16)
             dkv_ref[n, :CONTEXT, at] = (grad[CONTEXT:] + add_ref[n, :CONTEXT, at]).astype(BF16)
 
-    attend(places[1], places[0], inner, operands, results)
-
-
-def early_tile(places, frames, weight, qkv, attended_grad, late, late_grad):
+    fetch.wait()
+    attend(places[0], length[0], inner, operands, results)
+
+
+def early_tile(places, lengths, order, frames, weight, qkv, attended_grad, late, late_grad):
     rows, inner = attended_grad.shape
     width = frames.shape[1]
     return pl.pallas_call(
         early_kernel,
-        in_specs=[SMEM_SPEC] + [VMEM_SPEC] * 7,
+        in_specs=[SMEM_SPEC, HBM_SPEC] + [VMEM_SPEC] * 7,
         out_specs=[VMEM_SPEC] * 3,
         out_shape=[
             pltpu.VMEM((2, rows, inner), BF16),
             pltpu.VMEM((2, rows + CONTEXT, inner + CONTEXT), BF16),
             pltpu.VMEM((width // CORES, CONTEXT), BF16),
         ],
-        scratch_shapes=[pltpu.VMEM((CONTEXT, width), BF16), pltpu.VMEM((CONTEXT, 2 * inner), BF16)],
+        scratch_shapes=[
+            pltpu.SMEM((1,), jnp.int32),
+            pltpu.VMEM((CONTEXT, width), BF16),
+            pltpu.VMEM((CONTEXT, 2 * inner), BF16),
+            pltpu.SemaphoreType.DMA,
+        ],
         compiler_params=params(16),
         cost_estimate=cost(28 * CONTEXT * 2 * CONTEXT * inner, 16 * CONTEXT * inner, CONTEXT * 4 * inner),
         name="attention_early",
-    )(places, in_vmem(row_order(width)), *[in_vmem(o) for o in (frames, weight, qkv, attended_grad, late, late_grad)])
+    )(places, lengths, *[in_vmem(o) for o in (order, frames, weight, qkv, attended_grad, late, late_grad)])
 
 
 def store_sections(chunks, n, total, outs, held):
@@ -356,10 +386,28 @@
             ref[slot % half] = held[route, chunks[route, slot]].astype(BF16)
 
 
-def first_wave_kernel(chunks, left_ref, left_other_ref, right_ref, right_other_ref, *refs):
+def first_own_kernel(left_ref, right_ref, out_ref):
     tokens = right_ref.shape[1]
+    out_ref[0] = dot(left_ref[:, tokens:], right_ref[0])
+    out_ref[1] = dot(left_ref[:, :tokens], right_ref[1])
+
+
+def first_own(left, right):
+    return pl.pallas_call(
+        first_own_kernel,
+        in_specs=[VMEM_SPEC] * 2,
+        out_specs=VMEM_SPEC,
+        out_shape=pltpu.VMEM((2, left.shape[0], right.shape[2]), F32),
+        compiler_params=params(8),
+        cost_estimate=cost(2 * 10**9, 1),
+        name="first_own",
+    )(in_vmem(left), in_vmem(right))
+
+
+def first_wave_kernel(chunks, left_other_ref, right_other_ref, own_ref, *refs):
+    tokens = right_other_ref.shape[1]
     for n, at in enumerate((slice(tokens, 2 * tokens), slice(0, tokens))):
-        total = dot(left_ref[:, at], right_ref[n]) + dot(left_other_ref[:, at], right_other_ref[n])
+        total = own_ref[n] + dot(left_other_ref[:, at], right_other_ref[n])
         store_sections(chunks, n, total, refs[:-1], refs[-1])
 
 
@@ -367,11 +415,9 @@
     tokens = left_ref.shape[1] // 2
     inner = right_ref.shape[2] - CONTEXT
     behind_other = jnp.concatenate([right_other_ref[n, :, inner:] for n in range(2)], axis=0)
+    left = jnp.concatenate([left_ref[:, :tokens], behind_ref[...], left_other_ref[:, :tokens], behind_other], axis=1)
     for n in range(2):
-        total = dot(left_ref[:, :tokens], right_ref[n, :tokens, :inner])
-        total += dot(left_other_ref[:, :tokens], right_other_ref[n, :tokens, :inner])
-        total += dot(behind_ref[...], right_ref[n, tokens:, :inner])
-        total += dot(behind_other, right_other_ref[n, tokens:, :inner])
+        total = dot(left, jnp.concatenate([right_ref[n, :, :inner], right_other_ref[n, :, :inner]], axis=0))
         store_sections(chunks, n, total, refs[:-1], refs[-1])
 
 
@@ -430,20 +476,22 @@
     dp_index = lax.axis_index("dp")
     xl = seq_index % XL
     core, xh, y = dp_index % CORES, dp_index // CORES % XH, dp_index // (CORES * XH)
-    places = jnp.stack([lengths[0], seq_index * row_count, core])
+    places = jnp.stack([seq_index * row_count, core])
     routes = range(len(ROUTES))
     chunks = jnp.stack([chunk_at(r, jnp.arange(CHUNKS), y, xh, xl) for r in routes])
 
-    behind = from_behind(frame_rows[row_count - CONTEXT :], "seq", 1)
+    behind = from_behind(last_rows(frame_rows), "seq", 1)
     frame_rows, places, chunks = lax.optimization_barrier((frame_rows, places, chunks))
-    qkv, attended_grad, left, left_out, stats, weight, late, late_grad = front(
-        places, frame_rows, grad_rows, w_qkv, w_out
+    qkv, attended_grad, left, left_out, stats, weight, late, late_grad, order = front(
+        places, lengths, frame_rows, grad_rows, w_qkv, w_out
     )
     left_other = to_device(left_out, to_core)
-    own, grads, left_behind = early_tile(places, behind, weight, qkv, attended_grad, late, late_grad)
-    own_other, left_other, grads = lax.optimization_barrier((to_device(own, to_core), left_other, grads))
+    own, grads, left_behind = early_tile(places, lengths, order, behind, weight, qkv, attended_grad, late, late_grad)
+    own_other = to_device(own, to_core)
+    own_sum = first_own(left, own)
+    own_other, left_other, own_sum, grads = lax.optimization_barrier((own_other, left_other, own_sum, grads))
     grads_other = to_device(grads, to_core)
-    keep_a, send_a = weight_sections(first_wave_kernel, chunks, (left, left_other, own, own_other), inner, 1, "first_wave")
+    keep_a, send_a = weight_sections(first_wave_kernel, chunks, (left_other, own_other, own_sum), inner, 1, "first_wave")
     got_a = [to_device(send_a[r], ROUTES[r][0]) for r in routes]
     keep_b, send_b = weight_sections(
         second_wave_kernel, chunks, (left, left_other, left_behind, grads, grads_other), inner, 3 * 10**9, "second_wave"
@@ -457,23 +505,24 @@
         jnp.concatenate([plus(keep_a[r], got_a[r]), plus(keep_b[r], got_b[r])], axis=-1) for r in routes
     ]
     count = totals[0].shape[0] // 2
-    projected_grad = jnp.concatenate([own[1], grads[0, :row_count, :inner], grads[1, :row_count, :inner]], axis=1)
-    projected_grad, block_out, sends = lax.optimization_barrier(
-        (projected_grad, block_out, [t[count:] for t in totals])
-    )
+    query_grad = jnp.concatenate([own[1], jnp.zeros((CONTEXT, inner), BF16)], axis=0)
+    projected_grad = jnp.concatenate([query_grad, grads[0, :, :inner], grads[1, :, :inner]], axis=1)
+    sends = [t[count:] for t in totals]
+    projected_grad, block_out, sends = lax.optimization_barrier((projected_grad, block_out, sends))
     normed_grad = dot(projected_grad, w_qkv, NT)
-    gots = lax.optimization_barrier([to_device(sends[r], ROUTES[r][1]) for r in routes])
-    totals = [plus(totals[r][:count], gots[r]) for r in routes]
-    groups = [jnp.concatenate(totals[:2], axis=-1), jnp.concatenate(totals[2:], axis=-1)]
-    slots, grads, normed_grad = lax.optimization_barrier(
-        ([[g[slot] for slot in range(1, 4)] for g in groups], grads, normed_grad)
-    )
-    returned = from_behind(grads[:, row_count:, :inner], "seq", -1)
-    gots = [[to_device(slots[n][i], OWNERS[n][i]) for n in range(2)] for i in range(3)]
-    groups = [plus(groups[n][0], *[gots[i][n] for i in range(3)]) for n in range(2)]
-    returned = jnp.concatenate([jnp.zeros((CONTEXT, inner), BF16), returned[0], returned[1]], axis=1)
-    returned = jnp.concatenate([jnp.zeros((row_count - CONTEXT, width), F32), dot(returned, w_qkv, NT)], axis=0)
-    normed_grad = (normed_grad + returned).astype(BF16)
+    gots = [to_device(sends[r], ROUTES[r][1]) for r in routes]
+    groups = []
+    for n in range(2):
+        pair = [plus(totals[r][:count], gots[r]) for r in (2 * n, 2 * n + 1)]
+        group = jnp.concatenate(pair, axis=-1)
+        slots = lax.optimization_barrier([group[slot] for slot in range(1, 4)])
+        if n == 0:
+            slots, normed_grad = lax.optimization_barrier((slots, normed_grad))
+        others = [to_device(slots[i], OWNERS[n][i]) for i in range(3)]
+        groups.append(plus(group[0], *others))
+    returned = from_behind(normed_grad[row_count:].astype(BF16), "seq", -1)
+    returned = jnp.concatenate([jnp.zeros((row_count - CONTEXT, width), BF16), returned], axis=0)
+    normed_grad = (normed_grad[:row_count] + returned.astype(F32)).astype(BF16)
     frame_grad = normalize_grad(frame_rows.astype(F32), stats[0][:, None], stats[1][:, None], normed_grad.astype(F32))
     share = width // (CHUNKS * CORES * Z)
     tiles = 4 * inner // PAIR

time: 96.4 us -> 94.1 us (0.976)
  waiting for transfers between devices: 15.9 us -> 22.6 us
  matrix products: 9.13 us -> 4.58 us
  starting transfers between devices: 39.2 us -> 36.9 us
  Pallas kernels: 24.7 us -> 22.8 us
  local copies, waits for them, and re-layouts: 2.19 us -> 0.94 us
    all_to_all x1, waiting for transfers between devices: 3.34 us -> 7.9 us  [on_device(): lax.all_to_all(shares, 'seq', 0, 0, axis_index_groups=rings, tiled=True)]
    dot_general x3 -> x2, matrix products: 9.13 us -> 4.58 us  [dot(): return lax.dot_general(a, b, dims, preferred_element_type=F32)]
    ppermute x2, starting transfers between devices: 6.74 us -> 3.9 us  [from_behind(): lax.ppermute(value, axis, [(i, (i + by) % peers) for i in range(peers)])]
    ppermute x2, waiting for transfers between devices: 0.8 us -> 3.63 us  [from_behind(): lax.ppermute(value, axis, [(i, (i + by) % peers) for i in range(peers)])]
    ppermute x21, starting transfers between devices: 24.9 us -> 27.2 us  [to_device(): return lax.ppermute(value, ('dp', 'seq'), pairs)]
    all_to_all x1, starting transfers between devices: 7.56 us -> 5.82 us  [on_device(): lax.all_to_all(shares, 'seq', 0, 0, axis_index_groups=rings, tiled=True)]
    pallas_call x2, Pallas kernels: 5.98 us -> 4.88 us  [weight_sections(): pl.pallas_call(kernel, in_specs=[SMEM_SPEC] + [VMEM_SPEC] * len(operands)...]
    unnamed x12 -> x8, local copies, waits for them, and re-layouts: 0.99 us -> 0.02 us
  transfers between devices with their start and end apart: 24 -> 24, of which waited for: 11 -> 10; matrix products, arithmetic and copies ran while one was open for 12% -> 10% of each run, Pallas kernels for 25% -> 22%
where the time goes in v4:
time: 94.1 us; the launch traced here: 93.8 us
  starting transfers between devices  36.9 us (39%)
  Pallas kernels  22.8 us (24%)
  waiting for transfers between devices  22.6 us (24%)
  matrix products  4.58 us (5%)
  other arithmetic  4.37 us (5%)
  between operations  1.64 us (2%)
    ppermute x21, starting transfers between devices, to_device(): return lax.ppermute(value, ('dp', 'seq'), pairs)  27.2 us
    ppermute x21, waiting for transfers between devices, to_device(): return lax.ppermute(value, ('dp', 'seq'), pairs)  11 us
    pallas_call x1, Pallas kernels, front(): pl.pallas_call(front_kernel, in_specs=[SMEM_SPEC] + [HBM_SPEC] * 6, out_s...  9.89 us
    all_to_all x1, waiting for transfers between devices, on_device(): lax.all_to_all(shares, 'seq', 0, 0, axis_index_groups=rings, tiled=True)  7.9 us
    all_to_all x1, starting transfers between devices, on_device(): lax.all_to_all(shares, 'seq', 0, 0, axis_index_groups=rings, tiled=True)  5.82 us
    pallas_call x2, Pallas kernels, weight_sections(): pl.pallas_call(kernel, in_specs=[SMEM_SPEC] + [VMEM_SPEC] * len(operands)...  4.88 us
    pallas_call x1, Pallas kernels, early_tile(): pl.pallas_call(early_kernel, in_specs=[SMEM_SPEC, HBM_SPEC] + [VMEM_SPEC]...  4.69 us
    dot_general x2, matrix products, dot(): return lax.dot_general(a, b, dims, preferred_element_type=F32)  4.58 us
  transfers between devices with their start and end apart: 24, of which 10 were waited for; matrix products, arithmetic and copies ran while one was open for 10% of the time, Pallas kernels for 22%

profile of v4, /device:TPU:8, one launch (start us, length us, event | category | flops | bytes accessed | tf_op | source)
XLA Modules:
  0.0 93.8 jit_solution(12595175563472675659)
XLA Ops:
  0.6 1.0 %last_rows.1 = bf16[128,1536]{1,0:T(8,128)(2,1)S(1)} custom-call(bf16[256,1536]{1,0:T(8,128)(2,1)} %bitcast.43), custom_call_target="tpu_custom_call" | custom-call | flops 1 | bytes 1 | tf_op jit(solution)/shard_map/last_rows/pallas_call | solution.py:160
  1.6 1.6 %collective-permute-start = (bf16[128,1536]{1,0:T(8,128)(2,1)S(1)}, bf16[128,1536]{1,0:T(8,128)(2,1)S(1)}, u32[]{:S(2)}, u32[]{:S(2)}) collective-permute-start(bf16[128,1536]{1,0:T(8,128)(2,1)S(1)} %last_rows.1), channel_id=1, source_target_pairs={{0,1},{1,2},{2,3},{3,4},{4,5},{5,6},{6,7},{7,8},{8,9},{9,10},{10,1... | collective-permute-start | bytes 1179656 | tf_op jit(solution)/shard_map/ppermute | solution.py:31
  3.3 0.1 pad_add_fusion.1.places
  4.0 9.9 %front.1 = (bf16[256,2304]{1,0:T(8,128)(2,1)S(1)}, bf16[256,768]{1,0:T(8,128)(2,1)S(1)}, bf16[768,512]{1,0:T(8,128)(2,1)S(1)}, bf16[768,512]{1,0:T(8,128)(2,1)S(...) custom-call(s32[2]{0:T(128)S(1)} %pad_add_fusion.1.places, ...), custom_call_target="tpu_custom_call" | custom-call | flops 3623878656 | bytes 11796480 | tf_op jit(solution)/shard_map/front/pallas_call | solution.py:241
  13.9 0.1 collective-permute-start.2
  14.0 3.6 %collective-permute-done.frames_ref = bf16[128,1536]{1,0:T(8,128)(2,1)S(1)} collective-permute-done((bf16[128,1536]{1,0:T(8,128)(2,1)S(1)}, bf16[128,1536]{1,0:T(8,128)(2,1)S(1)}, u32[]{:S(2)}, u32[]{:S(2)}) %collective-permute-start) | collective-permute-done | bytes 393248 | tf_op jit(solution)/shard_map/ppermute | solution.py:31
  17.6 4.7 %attention_early.1 = (bf16[2,256,768]{2,1,0:T(8,128)(2,1)S(1)}, bf16[2,384,896]{2,1,0:T(8,128)(2,1)S(1)}, bf16[768,128]{1,0:T(8,128)(2,1)S(1)}) custom-call(s32[2]{0:T(128)S(1)} %pad_add_fusion.1.places, s32[1]{0:T(128)S(6)} %copy.9.lengths_ref, bf16[384,384]{1,0:T(8,128)(2,1)S(1)} %get-tuple-element.69.order_ref, ...), custom_call_target="tpu_custom_call" | custom-call | flops 704643072 | bytes 1572864 | tf_op jit(solution)/shard_map/attention_early/pallas_call | solution.py:357
  22.3 0.3 collective-permute-start.1
  22.6 0.8 first_own.1.own_ref
  23.4 1.5 %collective-permute-done.1.right_other_ref = bf16[2,256,768]{2,1,0:T(8,128)(2,1)S(1)} collective-permute-done((bf16[2,256,768]{2,1,0:T(8,128)(2,1)S(1)}, bf16[2,256,768]{2,1,0:T(8,128)(2,1)S(1)}, u32[]{:S(2)}, u32[]{:S(2)}) %collective-permute-start.1) | collective-permute-done | bytes 786464 | tf_op jit(solution)/shard_map/ppermute | solution.py:42
  24.9 0.1 collective-permute-start.3
  25.0 0.1 slice_bitcast_fusion.2
  25.1 2.0 %first_wave.1 = (bf16[8,48,384]{2,1,0:T(8,128)(2,1)S(1)}, bf16[8,48,384]{2,1,0:T(8,128)(2,1)S(1)}, bf16[8,48,384]{2,1,0:T(8,128)(2,1)S(1)}, bf16[8,48,384]{2,1,0...) custom-call(s32[4,16]{1,0:T(4,128)S(1)} %pad_add_fusion.chunks, ...), custom_call_target="tpu_custom_call" | custom-call | flops 1 | bytes 1 | tf_op jit(solution)/shard_map/first_wave/pallas_call | solution.py:427
  27.1 0.1 collective-permute-start.4
  27.2 3.3 %collective-permute-start.5 = (bf16[8,48,384]{2,1,0:T(8,128)(2,1)S(1)}, bf16[8,48,384]{2,1,0:T(8,128)(2,1)S(1)}, u32[]{:S(2)}, u32[]{:S(2)}) collective-permute-start(bf16[8,48,384]{2,1,0:T(8,128)(2,1)S(1)} %get-tuple-element.92), channel_id=1, source_target_pairs={{0,33},{1,32},{2,35},{3,34},{4,37},{5,36},{6,39},{7,38},{8,41},{9,... | collective-permute-start | bytes 884744 | tf_op jit(solution)/shard_map/ppermute | solution.py:42
  30.5 0.5 collective-permute-start.6
  30.9 2.4 %collective-permute-start.7 = (bf16[8,48,384]{2,1,0:T(8,128)(2,1)S(1)}, bf16[8,48,384]{2,1,0:T(8,128)(2,1)S(1)}, u32[]{:S(2)}, u32[]{:S(2)}) collective-permute-start(bf16[8,48,384]{2,1,0:T(8,128)(2,1)S(1)} %get-tuple-element.94), channel_id=1, source_target_pairs={{0,192},{1,193},{2,194},{3,195},{4,196},{5,197},{6,198},{7,199},{8... | collective-permute-start | bytes 884744 | tf_op jit(solution)/shard_map/ppermute | solution.py:42
  33.3 0.1 slice_bitcast_fusion.1
  33.4 0.1 fusion.2
  33.6 2.9 %second_wave.1 = (bf16[8,48,384]{2,1,0:T(8,128)(2,1)S(1)}, bf16[8,48,384]{2,1,0:T(8,128)(2,1)S(1)}, bf16[8,48,384]{2,1,0:T(8,128)(2,1)S(1)}, bf16[8,48,384]{2,1,...) custom-call(s32[4,16]{1,0:T(4,128)S(1)} %pad_add_fusion.chunks, ...), custom_call_target="tpu_custom_call" | custom-call | flops 3000000000 | bytes 1 | tf_op jit(solution)/shard_map/second_wave/pallas_call | solution.py:427
  36.5 0.1 collective-permute-start.8
  36.6 1.4 %collective-permute-start.9 = (bf16[8,48,384]{2,1,0:T(8,128)(2,1)S(1)}, bf16[8,48,384]{2,1,0:T(8,128)(2,1)S(1)}, u32[]{:S(2)}, u32[]{:S(2)}) collective-permute-start(bf16[8,48,384]{2,1,0:T(8,128)(2,1)S(1)} %get-tuple-element.96), channel_id=1, source_target_pairs={{0,33},{1,32},{2,35},{3,34},{4,37},{5,36},{6,39},{7,38},{8,41},{9,... | collective-permute-start | bytes 884744 | tf_op jit(solution)/shard_map/ppermute | solution.py:42
  38.0 1.3 %collective-permute-start.10 = (bf16[8,48,384]{2,1,0:T(8,128)(2,1)S(1)}, bf16[8,48,384]{2,1,0:T(8,128)(2,1)S(1)}, u32[]{:S(2)}, u32[]{:S(2)}) collective-permute-start(bf16[8,48,384]{2,1,0:T(8,128)(2,1)S(1)} %get-tuple-element.97), channel_id=1, source_target_pairs={{0,64},{1,65},{2,66},{3,67},{4,68},{5,69},{6,70},{7,71},{8,72},{9,... | collective-permute-start | bytes 884744 | tf_op jit(solution)/shard_map/ppermute | solution.py:42
  39.3 1.9 %collective-permute-start.11 = (bf16[8,48,384]{2,1,0:T(8,128)(2,1)S(1)}, bf16[8,48,384]{2,1,0:T(8,128)(2,1)S(1)}, u32[]{:S(2)}, u32[]{:S(2)}) collective-permute-start(bf16[8,48,384]{2,1,0:T(8,128)(2,1)S(1)} %get-tuple-element.98), channel_id=1, source_target_pairs={{0,192},{1,193},{2,194},{3,195},{4,196},{5,197},{6,198},{7,199},{8... | collective-permute-start | bytes 884744 | tf_op jit(solution)/shard_map/ppermute | solution.py:42
  41.2 1.7 %convolution_convert_fusion = bf16[256,1536]{1,0:T(8,128)(2,1)} fusion(bf16[256,768]{1,0:T(8,128)(2,1)S(1)} %get-tuple-element.87, bf16[768,1536]{1,0:T(8,128)(2,1)S(1)} %copy-done.1), kind=kOutput, calls=%fused_computation.2 | convolution fusion | flops 604372992 | bytes 3538944 | tf_op jit(solution)/shard_map/dot_general | solution.py:26
  42.8 1.8 %collective-permute-done.8 = bf16[8,48,384]{2,1,0:T(8,128)(2,1)S(1)} collective-permute-done((bf16[8,48,384]{2,1,0:T(8,128)(2,1)S(1)}, bf16[8,48,384]{2,1,0:T(8,128)(2,1)S(1)}, u32[]{:S(2)}, u32[]{:S(2)}) %collective-permute-start.8) | collective-permute-done | bytes 294944 | tf_op jit(solution)/shard_map/ppermute | solution.py:42
  44.7 1.4 %collective-permute-done.9 = bf16[8,48,384]{2,1,0:T(8,128)(2,1)S(1)} collective-permute-done((bf16[8,48,384]{2,1,0:T(8,128)(2,1)S(1)}, bf16[8,48,384]{2,1,0:T(8,128)(2,1)S(1)}, u32[]{:S(2)}, u32[]{:S(2)}) %collective-permute-start.9) | collective-permute-done | bytes 294944 | tf_op jit(solution)/shard_map/ppermute | solution.py:42
  46.1 0.3 collective-permute-done.10
  46.4 0.8 collective-permute-done.11
  47.3 0.1 add_convert_fusion.5
  47.3 0.1 add_convert_fusion.6
  47.4 0.1 add_convert_fusion.7
  47.5 0.1 add_convert_fusion.8
  47.6 0.1 add_convert_fusion.9
  47.7 0.1 add_convert_fusion.10
  47.8 0.1 add_convert_fusion.12
  47.9 0.1 add_convert_fusion.11
  48.1 2.5 %collective-permute-start.12 = (bf16[4,48,768]{2,1,0:T(8,128)(2,1)S(1)}, bf16[4,48,768]{2,1,0:T(8,128)(2,1)S(1)}, u32[]{:S(2)}, u32[]{:S(2)}) collective-permute-start(bf16[4,48,768]{2,1,0:T(8,128)(2,1)S(1)} %fusion.11), channel_id=1, source_target_pairs={{0,33},{1,32},{2,35},{3,34},{4,37},{5,36},{6,39},{7,38},{8,41},{9,... | collective-permute-start | bytes 884744 | tf_op jit(solution)/shard_map/ppermute | solution.py:42
  50.6 1.7 %collective-permute-start.18 = (bf16[4,48,768]{2,1,0:T(8,128)(2,1)S(1)}, bf16[4,48,768]{2,1,0:T(8,128)(2,1)S(1)}, u32[]{:S(2)}, u32[]{:S(2)}) collective-permute-start(bf16[4,48,768]{2,1,0:T(8,128)(2,1)S(1)} %fusion.9), channel_id=1, source_target_pairs={{0,192},{1,193},{2,194},{3,195},{4,196},{5,197},{6,198},{7,199},{8... | collective-permute-start | bytes 884744 | tf_op jit(solution)/shard_map/ppermute | solution.py:42
  52.3 2.6 %collective-permute-start.19 = (bf16[4,48,768]{2,1,0:T(8,128)(2,1)S(1)}, bf16[4,48,768]{2,1,0:T(8,128)(2,1)S(1)}, u32[]{:S(2)}, u32[]{:S(2)}) collective-permute-start(bf16[4,48,768]{2,1,0:T(8,128)(2,1)S(1)} %fusion.8), channel_id=1, source_target_pairs={{0,64},{1,65},{2,66},{3,67},{4,68},{5,69},{6,70},{7,71},{8,72},{9,... | collective-permute-start | bytes 884744 | tf_op jit(solution)/shard_map/ppermute | solution.py:42
  54.9 2.9 %fusion.34 = f32[384,1536]{1,0:T(8,128)S(1)} fusion(bf16[384,2304]{1,0:T(8,128)(2,1)S(1)} %fusion.2, bf16[1536,2304]{1,0:T(8,128)(2,1)S(1)} %bitcast.52), kind=kOutput, calls=%fused_computation.100 | convolution fusion | flops 2717908992 | bytes 11206656 | tf_op jit(solution)/shard_map/dot_general | solution.py:26
  57.8 0.1 add_convert_fusion.2
  57.9 1.7 %collective-permute-done.19 = bf16[4,48,768]{2,1,0:T(8,128)(2,1)S(1)} collective-permute-done((bf16[4,48,768]{2,1,0:T(8,128)(2,1)S(1)}, bf16[4,48,768]{2,1,0:T(8,128)(2,1)S(1)}, u32[]{:S(2)}, u32[]{:S(2)}) %collective-permute-start.19) | collective-permute-done | bytes 294944 | tf_op jit(solution)/shard_map/ppermute | solution.py:42
  59.6 0.1 add_convert_fusion.1
  59.7 1.2 %collective-permute-start.20 = (bf16[48,1536]{1,0:T(8,128)(2,1)S(1)}, bf16[48,1536]{1,0:T(8,128)(2,1)S(1)}, u32[]{:S(2)}, u32[]{:S(2)}) collective-permute-start(bf16[48,1536]{1,0:T(8,128)(2,1)S(1)} %get-tuple-element.128), channel_id=1, source_target_pairs={{0,33},{1,32},{2,35},{3,34},{4,37},{5,36},{6,39},{7,38},{8,41},{9,... | collective-permute-start | bytes 442376 | tf_op jit(solution)/shard_map/ppermute | solution.py:42
  60.9 1.2 %collective-permute-start.21 = (bf16[48,1536]{1,0:T(8,128)(2,1)S(1)}, bf16[48,1536]{1,0:T(8,128)(2,1)S(1)}, u32[]{:S(2)}, u32[]{:S(2)}) collective-permute-start(bf16[48,1536]{1,0:T(8,128)(2,1)S(1)} %get-tuple-element.129), channel_id=1, source_target_pairs={{0,1},{1,0},{2,3},{3,2},{4,5},{5,4},{6,7},{7,6},{8,9},{9,8},{10,11... | collective-permute-start | bytes 442376 | tf_op jit(solution)/shard_map/ppermute | solution.py:42
  62.1 2.3 %collective-permute-start.22 = (bf16[48,1536]{1,0:T(8,128)(2,1)S(1)}, bf16[48,1536]{1,0:T(8,128)(2,1)S(1)}, u32[]{:S(2)}, u32[]{:S(2)}) collective-permute-start(bf16[48,1536]{1,0:T(8,128)(2,1)S(1)} %get-tuple-element.130), channel_id=1, source_target_pairs={{0,32},{1,33},{2,34},{3,35},{4,36},{5,37},{6,38},{7,39},{8,40},{9,... | collective-permute-start | bytes 442376 | tf_op jit(solution)/shard_map/ppermute | solution.py:42
  64.5 0.1 add_convert_fusion.4
  64.6 0.1 add_convert_fusion.3
  64.7 0.5 collective-permute-start.15
  65.2 2.9 %collective-permute-start.16 = (bf16[48,1536]{1,0:T(8,128)(2,1)S(1)}, bf16[48,1536]{1,0:T(8,128)(2,1)S(1)}, u32[]{:S(2)}, u32[]{:S(2)}) collective-permute-start(bf16[48,1536]{1,0:T(8,128)(2,1)S(1)} %get-tuple-element.124), channel_id=1, source_target_pairs={{0,64},{1,65},{2,66},{3,67},{4,68},{5,69},{6,70},{7,71},{8,72},{9,... | collective-permute-start | bytes 442376 | tf_op jit(solution)/shard_map/ppermute | solution.py:42
  68.1 0.8 slice.198
  68.9 0.8 collective-permute-start.17
  69.7 2.3 %collective-permute-start.14 = (bf16[128,1536]{1,0:T(8,128)(2,1)}, bf16[128,1536]{1,0:T(8,128)(2,1)}, u32[]{:S(2)}, u32[]{:S(2)}) collective-permute-start(bf16[128,1536]{1,0:T(8,128)(2,1)} %slice.198), channel_id=1, source_target_pairs={{0,15},{1,0},{2,1},{3,2},{4,3},{5,4},{6,5},{7,6},{8,7},{9,8},{10,9... | collective-permute-start | bytes 1179656 | tf_op jit(solution)/shard_map/ppermute | solution.py:31
  72.0 1.4 %collective-permute-done.22 = bf16[48,1536]{1,0:T(8,128)(2,1)S(1)} collective-permute-done((bf16[48,1536]{1,0:T(8,128)(2,1)S(1)}, bf16[48,1536]{1,0:T(8,128)(2,1)S(1)}, u32[]{:S(2)}, u32[]{:S(2)}) %collective-permute-start.22) | collective-permute-done | bytes 147488 | tf_op jit(solution)/shard_map/ppermute | solution.py:42
  73.4 0.1 fusion.14.refs_1_
  73.5 2.0 %collective-permute-done.17 = bf16[48,1536]{1,0:T(8,128)(2,1)S(1)} collective-permute-done((bf16[48,1536]{1,0:T(8,128)(2,1)S(1)}, bf16[48,1536]{1,0:T(8,128)(2,1)S(1)}, u32[]{:S(2)}, u32[]{:S(2)}) %collective-permute-start.17) | collective-permute-done | bytes 147488 | tf_op jit(solution)/shard_map/ppermute | solution.py:42
  75.5 0.1 fusion.17.refs_0_
  75.6 0.8 pieces.1
  76.4 5.8 %all-to-all-start = ((bf16[8,144,128]{2,1,0:T(8,128)(2,1)}), bf16[8,144,128]{2,1,0:T(8,128)(2,1)S(1)}, u32[]{:S(2)}, u32[]{:S(2)}) async-start(bf16[8,144,128]{2,1,0:T(8,128)(2,1)} %pieces.1), calls=%async_computation | async-start | bytes 589824 | tf_op jit(solution)/shard_map/all_to_all | solution.py:538
  82.3 1.5 %convert_reduce_fusion = (f32[256]{0:T(256)S(1)}, f32[256]{0:T(256)S(1)}, bf16[256,1536]{1,0:T(8,128)(2,1)S(1)}) fusion(f32[256]{0:T(256)S(1)} %bitcast.49, f32[256]{0:T(256)S(1)} %bitcast.47, bf16[256,1536]{1,0:T(8,128)(2,1)S(1)} %bitcast.45, bf16[128,1536]{1,0:T(8,128)(2,1)} %collective-permute-done.14, f32[384,1536]{1,0:T(8,128)S(1)} %fusion.34), kind=kLoop, calls=%fused_computation.5 | loop fusion | flops 3931648 | bytes 3543040 | tf_op jit(solution)/shard_map/reduce_sum | solution.py:118
  83.8 1.4 %fusion.7 = bf16[1,256,1536]{2,1,0:T(8,128)(2,1)} fusion(bf16[256,1536]{1,0:T(8,128)(2,1)S(1)} %bitcast.46, bf16[256,1536]{1,0:T(8,128)(2,1)S(1)} %get-tuple-element.133, f32[256]{0:T(256)S(1)} %broadcast_multiply_fusion, f32[256]{0:T(256)S(1)} %bitcast.48, f32[256]{0:T(256)S(1)} %broadcast_multiply_fusion.1, f32[256]{0:T(256)S(1)} %bitcast.50), kind=kLoop, calls=%fused_computation.14 | loop fusion | flops 3538944 | bytes 2363392 | tf_op jit(solution)/shard_map/broadcast_in_dim | solution.py:546
  85.2 7.9 %all-to-all-done.in_ref = bf16[8,144,128]{2,1,0:T(8,128)(2,1)S(1)} async-done(((bf16[8,144,128]{2,1,0:T(8,128)(2,1)}), bf16[8,144,128]{2,1,0:T(8,128)(2,1)S(1)}, u32[]{:S(2)}, u32[]{:S(2)}) %all-to-all-start) | async-done | bytes 294944 | tf_op jit(solution)/shard_map/all_to_all | solution.py:538
  93.1 0.7 total.1
  (36 shorter events, 0.3 us)
Async XLA Ops:
  1.6 16.0 %collective-permute-start = (bf16[128,1536]{1,0:T(8,128)(2,1)S(1)}, bf16[128,1536]{1,0:T(8,128)(2,1)S(1)}, u32[]{:S(2)}, u32[]{:S(2)}) collective-permute-start(bf16[128,1536]{1,0:T(8,128)(2,1)S(1)} %last_rows.1), channel_id=1, source_target_pairs={{0,1},{1,2},{2,3},{3,4},{4,5},{5,6},{6,7},{7,8},{8,9},{9,10},{10,1... | collective-permute-start | bytes 1179656 | tf_op jit(solution)/shard_map/ppermute | solution.py:31
  13.9 9.5 %collective-permute-start.2 = (bf16[768,512]{1,0:T(8,128)(2,1)S(1)}, bf16[768,512]{1,0:T(8,128)(2,1)S(1)}, u32[]{:S(2)}, u32[]{:S(2)}) collective-permute-start(bf16[768,512]{1,0:T(8,128)(2,1)S(1)} %get-tuple-element.76), channel_id=1, source_target_pairs={{0,16},{1,17},{2,18},{3,19},{4,20},{5,21},{6,22},{7,23},{8,24},{9,... | collective-permute-start | bytes 2359304 | tf_op jit(solution)/shard_map/ppermute | solution.py:42
  22.3 2.6 %collective-permute-start.1 = (bf16[2,256,768]{2,1,0:T(8,128)(2,1)S(1)}, bf16[2,256,768]{2,1,0:T(8,128)(2,1)S(1)}, u32[]{:S(2)}, u32[]{:S(2)}) collective-permute-start(bf16[2,256,768]{2,1,0:T(8,128)(2,1)S(1)} %get-tuple-element.75.right_ref), channel_id=1, source_target_pairs={{0,16},{1,17},{2,18},{3,19},{4,20},{5,21},{6,22},{7,23},{8,24},{9,... | collective-permute-start | bytes 2359304 | tf_op jit(solution)/shard_map/ppermute | solution.py:42
  24.9 8.7 %collective-permute-start.3 = (bf16[2,384,896]{2,1,0:T(8,128)(2,1)S(1)}, bf16[2,384,896]{2,1,0:T(8,128)(2,1)S(1)}, u32[]{:S(2)}, u32[]{:S(2)}) collective-permute-start(bf16[2,384,896]{2,1,0:T(8,128)(2,1)S(1)} %get-tuple-element.79.right_ref), channel_id=1, source_target_pairs={{0,16},{1,17},{2,18},{3,19},{4,20},{5,21},{6,22},{7,23},{8,24},{9,... | collective-permute-start | bytes 4128776 | tf_op jit(solution)/shard_map/ppermute | solution.py:42
  27.1 9.5 %collective-permute-start.4 = (bf16[8,48,384]{2,1,0:T(8,128)(2,1)S(1)}, bf16[8,48,384]{2,1,0:T(8,128)(2,1)S(1)}, u32[]{:S(2)}, u32[]{:S(2)}) collective-permute-start(bf16[8,48,384]{2,1,0:T(8,128)(2,1)S(1)} %get-tuple-element.91), channel_id=1, source_target_pairs={{0,1},{1,0},{2,3},{3,2},{4,5},{5,4},{6,7},{7,6},{8,9},{9,8},{10,11... | collective-permute-start | bytes 884744 | tf_op jit(solution)/shard_map/ppermute | solution.py:42
  27.2 10.8 %collective-permute-start.5 = (bf16[8,48,384]{2,1,0:T(8,128)(2,1)S(1)}, bf16[8,48,384]{2,1,0:T(8,128)(2,1)S(1)}, u32[]{:S(2)}, u32[]{:S(2)}) collective-permute-start(bf16[8,48,384]{2,1,0:T(8,128)(2,1)S(1)} %get-tuple-element.92), channel_id=1, source_target_pairs={{0,33},{1,32},{2,35},{3,34},{4,37},{5,36},{6,39},{7,38},{8,41},{9,... | collective-permute-start | bytes 884744 | tf_op jit(solution)/shard_map/ppermute | solution.py:42
  30.5 8.8 %collective-permute-start.6 = (bf16[8,48,384]{2,1,0:T(8,128)(2,1)S(1)}, bf16[8,48,384]{2,1,0:T(8,128)(2,1)S(1)}, u32[]{:S(2)}, u32[]{:S(2)}) collective-permute-start(bf16[8,48,384]{2,1,0:T(8,128)(2,1)S(1)} %get-tuple-element.93), channel_id=1, source_target_pairs={{0,64},{1,65},{2,66},{3,67},{4,68},{5,69},{6,70},{7,71},{8,72},{9,... | collective-permute-start | bytes 884744 | tf_op jit(solution)/shard_map/ppermute | solution.py:42
  30.9 11.9 %collective-permute-start.7 = (bf16[8,48,384]{2,1,0:T(8,128)(2,1)S(1)}, bf16[8,48,384]{2,1,0:T(8,128)(2,1)S(1)}, u32[]{:S(2)}, u32[]{:S(2)}) collective-permute-start(bf16[8,48,384]{2,1,0:T(8,128)(2,1)S(1)} %get-tuple-element.94), channel_id=1, source_target_pairs={{0,192},{1,193},{2,194},{3,195},{4,196},{5,197},{6,198},{7,199},{8... | collective-permute-start | bytes 884744 | tf_op jit(solution)/shard_map/ppermute | solution.py:42
  33.5 7.6 %copy-start.1 = (bf16[768,1536]{1,0:T(8,128)(2,1)S(1)}, bf16[768,1536]{1,0:T(8,128)(2,1)}, u32[]{:S(2)}) copy-start(bf16[768,1536]{1,0:T(8,128)(2,1)} %out_ref.1) | copy-start | bytes 7077892
  36.5 8.2 %collective-permute-start.8 = (bf16[8,48,384]{2,1,0:T(8,128)(2,1)S(1)}, bf16[8,48,384]{2,1,0:T(8,128)(2,1)S(1)}, u32[]{:S(2)}, u32[]{:S(2)}) collective-permute-start(bf16[8,48,384]{2,1,0:T(8,128)(2,1)S(1)} %get-tuple-element.95), channel_id=1, source_target_pairs={{0,1},{1,0},{2,3},{3,2},{4,5},{5,4},{6,7},{7,6},{8,9},{9,8},{10,11... | collective-permute-start | bytes 884744 | tf_op jit(solution)/shard_map/ppermute | solution.py:42
  36.6 9.6 %collective-permute-start.9 = (bf16[8,48,384]{2,1,0:T(8,128)(2,1)S(1)}, bf16[8,48,384]{2,1,0:T(8,128)(2,1)S(1)}, u32[]{:S(2)}, u32[]{:S(2)}) collective-permute-start(bf16[8,48,384]{2,1,0:T(8,128)(2,1)S(1)} %get-tuple-element.96), channel_id=1, source_target_pairs={{0,33},{1,32},{2,35},{3,34},{4,37},{5,36},{6,39},{7,38},{8,41},{9,... | collective-permute-start | bytes 884744 | tf_op jit(solution)/shard_map/ppermute | solution.py:42
  38.0 8.4 %collective-permute-start.10 = (bf16[8,48,384]{2,1,0:T(8,128)(2,1)S(1)}, bf16[8,48,384]{2,1,0:T(8,128)(2,1)S(1)}, u32[]{:S(2)}, u32[]{:S(2)}) collective-permute-start(bf16[8,48,384]{2,1,0:T(8,128)(2,1)S(1)} %get-tuple-element.97), channel_id=1, source_target_pairs={{0,64},{1,65},{2,66},{3,67},{4,68},{5,69},{6,70},{7,71},{8,72},{9,... | collective-permute-start | bytes 884744 | tf_op jit(solution)/shard_map/ppermute | solution.py:42
  39.3 8.0 %collective-permute-start.11 = (bf16[8,48,384]{2,1,0:T(8,128)(2,1)S(1)}, bf16[8,48,384]{2,1,0:T(8,128)(2,1)S(1)}, u32[]{:S(2)}, u32[]{:S(2)}) collective-permute-start(bf16[8,48,384]{2,1,0:T(8,128)(2,1)S(1)} %get-tuple-element.98), channel_id=1, source_target_pairs={{0,192},{1,193},{2,194},{3,195},{4,196},{5,197},{6,198},{7,199},{8... | collective-permute-start | bytes 884744 | tf_op jit(solution)/shard_map/ppermute | solution.py:42
  41.2 13.7 %slice-start = ((s8[7077888]{0:T(1024)(128)(4,1)}), s8[4194304]{0:T(1024)(128)(4,1)S(1)}, s32[]{:S(2)}) async-start(s8[7077888]{0:T(1024)(128)(4,1)} %bitcast.51), calls=%async_computation.1 | async-start | bytes 8388608
  47.5 7.4 %slice-start.1 = ((s8[7077888]{0:T(1024)(128)(4,1)}), s8[2883584]{0:T(1024)(128)(4,1)S(1)}, s32[]{:S(2)}) async-start(s8[7077888]{0:T(1024)(128)(4,1)} %bitcast.51), calls=%async_computation.2 | async-start | bytes 5767168
  48.1 16.4 %collective-permute-start.12 = (bf16[4,48,768]{2,1,0:T(8,128)(2,1)S(1)}, bf16[4,48,768]{2,1,0:T(8,128)(2,1)S(1)}, u32[]{:S(2)}, u32[]{:S(2)}) collective-permute-start(bf16[4,48,768]{2,1,0:T(8,128)(2,1)S(1)} %fusion.11), channel_id=1, source_target_pairs={{0,33},{1,32},{2,35},{3,34},{4,37},{5,36},{6,39},{7,38},{8,41},{9,... | collective-permute-start | bytes 884744 | tf_op jit(solution)/shard_map/ppermute | solution.py:42
  50.6 14.0 %collective-permute-start.13 = (bf16[4,48,768]{2,1,0:T(8,128)(2,1)S(1)}, bf16[4,48,768]{2,1,0:T(8,128)(2,1)S(1)}, u32[]{:S(2)}, u32[]{:S(2)}) collective-permute-start(bf16[4,48,768]{2,1,0:T(8,128)(2,1)S(1)} %fusion.10), channel_id=1, source_target_pairs={{0,1},{1,0},{2,3},{3,2},{4,5},{5,4},{6,7},{7,6},{8,9},{9,8},{10,11... | collective-permute-start | bytes 884744 | tf_op jit(solution)/shard_map/ppermute | solution.py:42
  50.6 7.2 %collective-permute-start.18 = (bf16[4,48,768]{2,1,0:T(8,128)(2,1)S(1)}, bf16[4,48,768]{2,1,0:T(8,128)(2,1)S(1)}, u32[]{:S(2)}, u32[]{:S(2)}) collective-permute-start(bf16[4,48,768]{2,1,0:T(8,128)(2,1)S(1)} %fusion.9), channel_id=1, source_target_pairs={{0,192},{1,193},{2,194},{3,195},{4,196},{5,197},{6,198},{7,199},{8... | collective-permute-start | bytes 884744 | tf_op jit(solution)/shard_map/ppermute | solution.py:42
  52.3 7.3 %collective-permute-start.19 = (bf16[4,48,768]{2,1,0:T(8,128)(2,1)S(1)}, bf16[4,48,768]{2,1,0:T(8,128)(2,1)S(1)}, u32[]{:S(2)}, u32[]{:S(2)}) collective-permute-start(bf16[4,48,768]{2,1,0:T(8,128)(2,1)S(1)} %fusion.8), channel_id=1, source_target_pairs={{0,64},{1,65},{2,66},{3,67},{4,68},{5,69},{6,70},{7,71},{8,72},{9,... | collective-permute-start | bytes 884744 | tf_op jit(solution)/shard_map/ppermute | solution.py:42
  59.7 9.2 %collective-permute-start.20 = (bf16[48,1536]{1,0:T(8,128)(2,1)S(1)}, bf16[48,1536]{1,0:T(8,128)(2,1)S(1)}, u32[]{:S(2)}, u32[]{:S(2)}) collective-permute-start(bf16[48,1536]{1,0:T(8,128)(2,1)S(1)} %get-tuple-element.128), channel_id=1, source_target_pairs={{0,33},{1,32},{2,35},{3,34},{4,37},{5,36},{6,39},{7,38},{8,41},{9,... | collective-permute-start | bytes 442376 | tf_op jit(solution)/shard_map/ppermute | solution.py:42
  60.9 8.8 %collective-permute-start.21 = (bf16[48,1536]{1,0:T(8,128)(2,1)S(1)}, bf16[48,1536]{1,0:T(8,128)(2,1)S(1)}, u32[]{:S(2)}, u32[]{:S(2)}) collective-permute-start(bf16[48,1536]{1,0:T(8,128)(2,1)S(1)} %get-tuple-element.129), channel_id=1, source_target_pairs={{0,1},{1,0},{2,3},{3,2},{4,5},{5,4},{6,7},{7,6},{8,9},{9,8},{10,11... | collective-permute-start | bytes 442376 | tf_op jit(solution)/shard_map/ppermute | solution.py:42
  62.1 11.2 %collective-permute-start.22 = (bf16[48,1536]{1,0:T(8,128)(2,1)S(1)}, bf16[48,1536]{1,0:T(8,128)(2,1)S(1)}, u32[]{:S(2)}, u32[]{:S(2)}) collective-permute-start(bf16[48,1536]{1,0:T(8,128)(2,1)S(1)} %get-tuple-element.130), channel_id=1, source_target_pairs={{0,32},{1,33},{2,34},{3,35},{4,36},{5,37},{6,38},{7,39},{8,40},{9,... | collective-permute-start | bytes 442376 | tf_op jit(solution)/shard_map/ppermute | solution.py:42
  64.7 8.8 %collective-permute-start.15 = (bf16[48,1536]{1,0:T(8,128)(2,1)S(1)}, bf16[48,1536]{1,0:T(8,128)(2,1)S(1)}, u32[]{:S(2)}, u32[]{:S(2)}) collective-permute-start(bf16[48,1536]{1,0:T(8,128)(2,1)S(1)} %get-tuple-element.123), channel_id=1, source_target_pairs={{0,192},{1,193},{2,194},{3,195},{4,196},{5,197},{6,198},{7,199},{8... | collective-permute-start | bytes 442376 | tf_op jit(solution)/shard_map/ppermute | solution.py:42
  65.2 8.3 %collective-permute-start.16 = (bf16[48,1536]{1,0:T(8,128)(2,1)S(1)}, bf16[48,1536]{1,0:T(8,128)(2,1)S(1)}, u32[]{:S(2)}, u32[]{:S(2)}) collective-permute-start(bf16[48,1536]{1,0:T(8,128)(2,1)S(1)} %get-tuple-element.124), channel_id=1, source_target_pairs={{0,64},{1,65},{2,66},{3,67},{4,68},{5,69},{6,70},{7,71},{8,72},{9,... | collective-permute-start | bytes 442376 | tf_op jit(solution)/shard_map/ppermute | solution.py:42
  68.9 13.4 %copy-start = (bf16[1,256,1536]{2,1,0:T(8,128)(2,1)S(1)}, bf16[1,256,1536]{2,1,0:T(8,128)(2,1)}, u32[]{:S(2)}) copy-start(bf16[1,256,1536]{2,1,0:T(8,128)(2,1)} %param.6) | copy-start | bytes 2359300
  68.9 6.6 %collective-permute-start.17 = (bf16[48,1536]{1,0:T(8,128)(2,1)S(1)}, bf16[48,1536]{1,0:T(8,128)(2,1)S(1)}, u32[]{:S(2)}, u32[]{:S(2)}) collective-permute-start(bf16[48,1536]{1,0:T(8,128)(2,1)S(1)} %get-tuple-element.125), channel_id=1, source_target_pairs={{0,128},{1,129},{2,130},{3,131},{4,132},{5,133},{6,134},{7,135},{8... | collective-permute-start | bytes 442376 | tf_op jit(solution)/shard_map/ppermute | solution.py:42
  69.7 12.6 %collective-permute-start.14 = (bf16[128,1536]{1,0:T(8,128)(2,1)}, bf16[128,1536]{1,0:T(8,128)(2,1)}, u32[]{:S(2)}, u32[]{:S(2)}) collective-permute-start(bf16[128,1536]{1,0:T(8,128)(2,1)} %slice.198), channel_id=1, source_target_pairs={{0,15},{1,0},{2,1},{3,2},{4,3},{5,4},{6,5},{7,6},{8,7},{9,8},{10,9... | collective-permute-start | bytes 1179656 | tf_op jit(solution)/shard_map/ppermute | solution.py:31
  76.4 16.7 %all-to-all-start = ((bf16[8,144,128]{2,1,0:T(8,128)(2,1)}), bf16[8,144,128]{2,1,0:T(8,128)(2,1)S(1)}, u32[]{:S(2)}, u32[]{:S(2)}) async-start(bf16[8,144,128]{2,1,0:T(8,128)(2,1)} %pieces.1), calls=%async_computation | async-start | bytes 589824 | tf_op jit(solution)/shard_map/all_to_all | solution.py:538

commit v5 on v4

--- a/solution.py
+++ b/solution.py
@@ -152,17 +152,27 @@
 def last_rows(frames):
     rows, width = frames.shape
 
-    def kernel(frames_ref, out_ref, sem):
-        copy = pltpu.make_async_copy(frames_ref.at[pl.ds(rows - CONTEXT, CONTEXT)], out_ref, sem)
-        copy.start()
-        copy.wait()
+    pieces = 8
+
+    def kernel(frames_ref, out_ref, sems):
+        size = CONTEXT // pieces
+        copies = [
+            pltpu.make_async_copy(
+                frames_ref.at[pl.ds(rows - CONTEXT + i * size, size)], out_ref.at[pl.ds(i * size, size)], sems.at[i]
+            )
+            for i in range(pieces)
+        ]
+        for copy in copies:
+            copy.start()
+        for copy in copies:
+            copy.wait()
 
     return pl.pallas_call(
         kernel,
         in_specs=[HBM_SPEC],
         out_specs=VMEM_SPEC,
         out_shape=pltpu.VMEM((CONTEXT, width), BF16),
-        scratch_shapes=[pltpu.SemaphoreType.DMA],
+        scratch_shapes=[pltpu.SemaphoreType.DMA((pieces,))],
         compiler_params=params(4),
         cost_estimate=cost(1, 1),
         name="last_rows",
@@ -375,15 +385,11 @@
     )(places, lengths, *[in_vmem(o) for o in (order, frames, weight, qkv, attended_grad, late, late_grad)])
 
 
-def store_sections(chunks, n, total, outs, held):
-    columns = total.shape[1] // 2
+def store_section(chunks, route, n, total, outs, held):
     half = CHUNKS // 2
-    for part in range(2):
-        route = 2 * n + part
-        held[route] = total[:, part * columns : (part + 1) * columns].reshape(held.shape[1:])
-        for slot in range(CHUNKS):
-            ref = outs[route] if slot < half else outs[len(ROUTES) + route]
-            ref[slot % half] = held[route, chunks[route, slot]].astype(BF16)
+    held[n] = total.reshape(held.shape[1:])
+    for slot in range(CHUNKS):
+        outs[n if slot < half else 2 + n][slot % half] = held[n, chunks[route, slot]].astype(BF16)
 
 
 def first_own_kernel(left_ref, right_ref, out_ref):
@@ -408,7 +414,7 @@
     tokens = right_other_ref.shape[1]
     for n, at in enumerate((slice(tokens, 2 * tokens), slice(0, tokens))):
         total = own_ref[n] + dot(left_other_ref[:, at], right_other_ref[n])
-        store_sections(chunks, n, total, refs[:-1], refs[-1])
+        store_section(chunks, n, n, total, refs[:-1], refs[-1])
 
 
 def second_wave_kernel(chunks, left_ref, left_other_ref, behind_ref, right_ref, right_other_ref, *refs):
@@ -418,12 +424,12 @@
     left = jnp.concatenate([left_ref[:, :tokens], behind_ref[...], left_other_ref[:, :tokens], behind_other], axis=1)
     for n in range(2):
         total = dot(left, jnp.concatenate([right_ref[n, :, :inner], right_other_ref[n, :, :inner]], axis=0))
-        store_sections(chunks, n, total, refs[:-1], refs[-1])
+        store_section(chunks, 2 + n, n, total, refs[:-1], refs[-1])
 
 
 def weight_sections(kernel, chunks, operands, inner, flops, name):
-    size = (operands[0].shape[0] // CHUNKS, inner // 2)
-    routes = len(ROUTES)
+    size = (operands[0].shape[0] // CHUNKS, inner)
+    routes = 2
     outs = pl.pallas_call(
         kernel,
         in_specs=[SMEM_SPEC] + [VMEM_SPEC] * len(operands),
@@ -441,20 +447,40 @@
     return sum(t.astype(F32) for t in terms).astype(BF16)
 
 
+def halve_kernel(*refs):
+    for route in range(2):
+        keep, got, kept, sent = refs[route::2]
+        count = kept.shape[0]
+        for ref, at in ((kept, slice(0, count)), (sent, slice(count, 2 * count))):
+            ref[...] = (keep[at].astype(F32) + got[at].astype(F32)).astype(BF16)
+
+
+def halve(keep, gots):
+    count, *size = keep[0].shape
+    outs = pl.pallas_call(
+        halve_kernel,
+        in_specs=[VMEM_SPEC] * 4,
+        out_specs=[VMEM_SPEC] * 4,
+        out_shape=[pltpu.VMEM((count // 2, *size), BF16)] * 4,
+        compiler_params=params(8),
+        cost_estimate=cost(1, 1),
+        name="halve",
+    )(*[in_vmem(o) for o in (*keep, *gots)])
+    return outs[:2], outs[2:]
+
+
 def pieces_kernel(*refs):
     ins, out_ref, held = refs[:-2], refs[-2], refs[-1]
-    for group, ref in enumerate(ins):
+    for ref, places in zip(ins, ((3, 0), (1, 2))):
         block = ref[...].astype(F32)
-        width = block.shape[1] // PAIR // 4
+        tiles = block.shape[1] // PAIR // 2
         share = block.shape[0] // Z
-        for n in (2 * group, 2 * group + 1):
-            bases = (((n + 2) % 4) * width + (0 if n > 1 else 4 * width), (2 + n) * width)
-            for wave, base in enumerate(bases):
-                for t in range(width):
-                    column = (((n % 2) * 2 + wave) * width + t) * PAIR
-                    for z in range(Z):
-                        rows = slice((base + t) * share, (base + t + 1) * share)
-                        held[z, rows, :] = block[z * share : (z + 1) * share, column : column + PAIR]
+        for n, place in enumerate(places):
+            for t in range(tiles):
+                rows = slice((place * tiles + t) * share, (place * tiles + t + 1) * share)
+                column = (n * tiles + t) * PAIR
+                for z in range(Z):
+                    held[z, rows, :] = block[z * share : (z + 1) * share, column : column + PAIR]
     out_ref[...] = held[...].astype(BF16)
 
 
@@ -477,8 +503,7 @@
     xl = seq_index % XL
     core, xh, y = dp_index % CORES, dp_index // CORES % XH, dp_index // (CORES * XH)
     places = jnp.stack([seq_index * row_count, core])
-    routes = range(len(ROUTES))
-    chunks = jnp.stack([chunk_at(r, jnp.arange(CHUNKS), y, xh, xl) for r in routes])
+    chunks = jnp.stack([chunk_at(r, jnp.arange(CHUNKS), y, xh, xl) for r in range(len(ROUTES))])
 
     behind = from_behind(last_rows(frame_rows), "seq", 1)
     frame_rows, places, chunks = lax.optimization_barrier((frame_rows, places, chunks))
@@ -492,34 +517,32 @@
     own_other, left_other, own_sum, grads = lax.optimization_barrier((own_other, left_other, own_sum, grads))
     grads_other = to_device(grads, to_core)
     keep_a, send_a = weight_sections(first_wave_kernel, chunks, (left_other, own_other, own_sum), inner, 1, "first_wave")
-    got_a = [to_device(send_a[r], ROUTES[r][0]) for r in routes]
     keep_b, send_b = weight_sections(
         second_wave_kernel, chunks, (left, left_other, left_behind, grads, grads_other), inner, 3 * 10**9, "second_wave"
     )
-    attended, send_b = lax.optimization_barrier((own[0], send_b))
-    block_out = dot(attended, w_out).astype(BF16)
-    got_b = [to_device(send_b[r], ROUTES[r][0]) for r in routes]
-
-    got_a, got_b = lax.optimization_barrier((got_a, got_b))
-    totals = [
-        jnp.concatenate([plus(keep_a[r], got_a[r]), plus(keep_b[r], got_b[r])], axis=-1) for r in routes
-    ]
-    count = totals[0].shape[0] // 2
     query_grad = jnp.concatenate([own[1], jnp.zeros((CONTEXT, inner), BF16)], axis=0)
     projected_grad = jnp.concatenate([query_grad, grads[0, :, :inner], grads[1, :, :inner]], axis=1)
-    sends = [t[count:] for t in totals]
-    projected_grad, block_out, sends = lax.optimization_barrier((projected_grad, block_out, sends))
+    attended, projected_grad, send_b = lax.optimization_barrier((own[0], projected_grad, send_b))
+    block_out = dot(attended, w_out).astype(BF16)
+    def second_ring(kept, gots, n, *after):
+        group = jnp.concatenate([plus(kept[r], gots[r]) for r in range(2)], axis=-1)
+        slots, *after = lax.optimization_barrier(([group[slot] for slot in range(1, 4)], *after))
+        others = [to_device(slots[i], OWNERS[n][i]) for i in range(3)]
+        return plus(group[0], *others), *after
+
+    gots_a = [to_device(send_a[r], ROUTES[r][0]) for r in range(2)]
+    gots_b = [to_device(send_b[r], ROUTES[2 + r][0]) for r in range(2)]
+    gots_a, block_out = lax.optimization_barrier((gots_a, block_out))
+    kept_a, sent_a = halve(keep_a, gots_a)
+    gots_a = [to_device(sent_a[r], ROUTES[r][1]) for r in range(2)]
+    kept_b, sent_b = halve(keep_b, gots_b)
+    projected_grad, sent_b = lax.optimization_barrier((projected_grad, sent_b))
+    gots_b = [to_device(sent_b[r], ROUTES[2 + r][1]) for r in range(2)]
     normed_grad = dot(projected_grad, w_qkv, NT)
-    gots = [to_device(sends[r], ROUTES[r][1]) for r in routes]
-    groups = []
-    for n in range(2):
-        pair = [plus(totals[r][:count], gots[r]) for r in (2 * n, 2 * n + 1)]
-        group = jnp.concatenate(pair, axis=-1)
-        slots = lax.optimization_barrier([group[slot] for slot in range(1, 4)])
-        if n == 0:
-            slots, normed_grad = lax.optimization_barrier((slots, normed_grad))
-        others = [to_device(slots[i], OWNERS[n][i]) for i in range(3)]
-        groups.append(plus(group[0], *others))
+    gots_a, normed_grad = lax.optimization_barrier((gots_a, normed_grad))
+    first_group, = second_ring(kept_a, gots_a, 0)
+    second_group, normed_grad = second_ring(kept_b, gots_b, 1, normed_grad)
+    groups = [first_group, second_group]
     returned = from_behind(normed_grad[row_count:].astype(BF16), "seq", -1)
     returned = jnp.concatenate([jnp.zeros((row_count - CONTEXT, width), BF16), returned], axis=0)
     normed_grad = (normed_grad[:row_count] + returned.astype(F32)).astype(BF16)

time: 94.1 us -> 97.8 us (1.039)
  waiting for transfers between devices: 22.6 us -> 33.9 us
  starting transfers between devices: 36.9 us -> 29.4 us
    ppermute x21 -> x17, waiting for transfers between devices: 11 us -> 22.4 us  [to_device(): return lax.ppermute(value, ('dp', 'seq'), pairs)]
    ppermute x21 -> x17, starting transfers between devices: 27.2 us -> 20.4 us  [to_device(): return lax.ppermute(value, ('dp', 'seq'), pairs)]
  transfers between devices with their start and end apart: 24 -> 20, of which waited for: 10 -> 9; matrix products, arithmetic and copies ran while one was open for 10% -> 9% of each run, Pallas kernels for 22% -> 22%
where the time goes in v5:
time: 97.8 us; the launch traced here: 96.9 us
  waiting for transfers between devices  33.9 us (35%)
  starting transfers between devices  29.4 us (30%)
  Pallas kernels  22.9 us (23%)
  matrix products  4.59 us (5%)
  other arithmetic  3.65 us (4%)
  between operations  1.56 us (2%)
    ppermute x17, waiting for transfers between devices, to_device(): return lax.ppermute(value, ('dp', 'seq'), pairs)  22.4 us
    ppermute x17, starting transfers between devices, to_device(): return lax.ppermute(value, ('dp', 'seq'), pairs)  20.4 us
    pallas_call x1, Pallas kernels, front(): pl.pallas_call(front_kernel, in_specs=[SMEM_SPEC] + [HBM_SPEC] * 6, out_s...  9.88 us
    all_to_all x1, waiting for transfers between devices, on_device(): lax.all_to_all(shares, 'seq', 0, 0, axis_index_groups=rings, tiled=True)  7.9 us
    all_to_all x1, starting transfers between devices, on_device(): lax.all_to_all(shares, 'seq', 0, 0, axis_index_groups=rings, tiled=True)  5.83 us
    pallas_call x1, Pallas kernels, early_tile(): pl.pallas_call(early_kernel, in_specs=[SMEM_SPEC, HBM_SPEC] + [VMEM_SPEC]...  4.69 us
    dot_general x2, matrix products, dot(): return lax.dot_general(a, b, dims, preferred_element_type=F32)  4.59 us
    pallas_call x2, Pallas kernels, weight_sections(): pl.pallas_call(kernel, in_specs=[SMEM_SPEC] + [VMEM_SPEC] * len(operands)...  4.46 us
  transfers between devices with their start and end apart: 20, of which 9 were waited for; matrix products, arithmetic and copies ran while one was open for 9% of the time, Pallas kernels for 22%

profile of v5, /device:TPU:8, one launch (start us, length us, event | category | flops | bytes accessed | tf_op | source)
XLA Modules:
  0.0 96.9 jit_solution(6457080274801579758)
XLA Ops:
  0.6 1.0 %last_rows.1 = bf16[128,1536]{1,0:T(8,128)(2,1)S(1)} custom-call(bf16[256,1536]{1,0:T(8,128)(2,1)} %bitcast.43), custom_call_target="tpu_custom_call" | custom-call | flops 1 | bytes 1 | tf_op jit(solution)/shard_map/last_rows/pallas_call | solution.py:170
  1.7 1.6 %collective-permute-start = (bf16[128,1536]{1,0:T(8,128)(2,1)S(1)}, bf16[128,1536]{1,0:T(8,128)(2,1)S(1)}, u32[]{:S(2)}, u32[]{:S(2)}) collective-permute-start(bf16[128,1536]{1,0:T(8,128)(2,1)S(1)} %last_rows.1), channel_id=1, source_target_pairs={{0,1},{1,2},{2,3},{3,4},{4,5},{5,6},{6,7},{7,8},{8,9},{9,10},{10,1... | collective-permute-start | bytes 1179656 | tf_op jit(solution)/shard_map/ppermute | solution.py:31
  3.3 0.1 pad_add_fusion.1.places
  4.0 9.9 %front.1 = (bf16[256,2304]{1,0:T(8,128)(2,1)S(1)}, bf16[256,768]{1,0:T(8,128)(2,1)S(1)}, bf16[768,512]{1,0:T(8,128)(2,1)S(1)}, bf16[768,512]{1,0:T(8,128)(2,1)S(...) custom-call(s32[2]{0:T(128)S(1)} %pad_add_fusion.1.places, ...), custom_call_target="tpu_custom_call" | custom-call | flops 3623878656 | bytes 11796480 | tf_op jit(solution)/shard_map/front/pallas_call | solution.py:251
  13.9 0.1 collective-permute-start.2
  14.0 3.6 %collective-permute-done.frames_ref = bf16[128,1536]{1,0:T(8,128)(2,1)S(1)} collective-permute-done((bf16[128,1536]{1,0:T(8,128)(2,1)S(1)}, bf16[128,1536]{1,0:T(8,128)(2,1)S(1)}, u32[]{:S(2)}, u32[]{:S(2)}) %collective-permute-start) | collective-permute-done | bytes 393248 | tf_op jit(solution)/shard_map/ppermute | solution.py:31
  17.6 4.7 %attention_early.1 = (bf16[2,256,768]{2,1,0:T(8,128)(2,1)S(1)}, bf16[2,384,896]{2,1,0:T(8,128)(2,1)S(1)}, bf16[768,128]{1,0:T(8,128)(2,1)S(1)}) custom-call(s32[2]{0:T(128)S(1)} %pad_add_fusion.1.places, s32[1]{0:T(128)S(6)} %copy.9.lengths_ref, bf16[384,384]{1,0:T(8,128)(2,1)S(1)} %get-tuple-element.61.order_ref, ...), custom_call_target="tpu_custom_call" | custom-call | flops 704643072 | bytes 1572864 | tf_op jit(solution)/shard_map/attention_early/pallas_call | solution.py:367
  22.3 0.3 collective-permute-start.1
  22.6 0.8 first_own.1.own_ref
  23.4 0.0 collective-permute-done.2.left_other_ref
  23.4 1.5 %collective-permute-done.1.right_other_ref = bf16[2,256,768]{2,1,0:T(8,128)(2,1)S(1)} collective-permute-done((bf16[2,256,768]{2,1,0:T(8,128)(2,1)S(1)}, bf16[2,256,768]{2,1,0:T(8,128)(2,1)S(1)}, u32[]{:S(2)}, u32[]{:S(2)}) %collective-permute-start.1) | collective-permute-done | bytes 786464 | tf_op jit(solution)/shard_map/ppermute | solution.py:42
  24.9 0.1 collective-permute-start.5
  25.0 0.1 slice_bitcast_fusion.2
  25.1 1.6 %first_wave.1 = (bf16[8,48,768]{2,1,0:T(8,128)(2,1)S(1)}, bf16[8,48,768]{2,1,0:T(8,128)(2,1)S(1)}, bf16[8,48,768]{2,1,0:T(8,128)(2,1)S(1)}, bf16[8,48,768]{2,1,0:T(8,128)(2,1)S(1)}) custom-call(s32[4,16]{1,0:T(4,128)S(1)} %pad_add_fusion.chunks, bf16[768,512]{1,0:T(8,128)(2,1)S(1)} %collective-permute-done.2.left_other_ref, ...), custom_call_target="tpu_custom_call" | custom-call | flops 1 | bytes 1 | tf_op jit(solution)/shard_map/first_wave/pallas_call | solution.py:433
  26.7 0.1 collective-permute-start.3
  26.8 3.3 %collective-permute-start.4 = (bf16[8,48,768]{2,1,0:T(8,128)(2,1)S(1)}, bf16[8,48,768]{2,1,0:T(8,128)(2,1)S(1)}, u32[]{:S(2)}, u32[]{:S(2)}) collective-permute-start(bf16[8,48,768]{2,1,0:T(8,128)(2,1)S(1)} %get-tuple-element.75), channel_id=1, source_target_pairs={{0,33},{1,32},{2,35},{3,34},{4,37},{5,36},{6,39},{7,38},{8,41},{9,... | collective-permute-start | bytes 1769480 | tf_op jit(solution)/shard_map/ppermute | solution.py:42
  30.1 0.1 slice_bitcast_fusion.1
  30.2 0.0 slice-start
  30.2 0.1 fusion.2
  30.4 0.0 copy-start.1
  30.4 0.0 slice-start.1
  30.4 2.8 %second_wave.1 = (bf16[8,48,768]{2,1,0:T(8,128)(2,1)S(1)}, bf16[8,48,768]{2,1,0:T(8,128)(2,1)S(1)}, bf16[8,48,768]{2,1,0:T(8,128)(2,1)S(1)}, bf16[8,48,768]{2,1,0:T(8,128)(2,1)S(1)}) custom-call(s32[4,16]{1,0:T(4,128)S(1)} %pad_add_fusion.chunks, bf16[768,512]{1,0:T(8,128)(2,1)S(1)} %get-tuple-element.69.left_ref, ...), custom_call_target="tpu_custom_call" | custom-call | flops 3000000000 | bytes 1 | tf_op jit(solution)/shard_map/second_wave/pallas_call | solution.py:433
  33.2 0.5 collective-permute-start.6
  33.8 2.4 %collective-permute-start.7 = (bf16[8,48,768]{2,1,0:T(8,128)(2,1)S(1)}, bf16[8,48,768]{2,1,0:T(8,128)(2,1)S(1)}, u32[]{:S(2)}, u32[]{:S(2)}) collective-permute-start(bf16[8,48,768]{2,1,0:T(8,128)(2,1)S(1)} %get-tuple-element.86), channel_id=1, source_target_pairs={{0,192},{1,193},{2,194},{3,195},{4,196},{5,197},{6,198},{7,199},{8... | collective-permute-start | bytes 1769480 | tf_op jit(solution)/shard_map/ppermute | solution.py:42
  36.2 1.7 %convolution_convert_fusion = bf16[256,1536]{1,0:T(8,128)(2,1)} fusion(bf16[256,768]{1,0:T(8,128)(2,1)S(1)} %get-tuple-element.80, bf16[768,1536]{1,0:T(8,128)(2,1)S(1)} %copy-done.1), kind=kOutput, calls=%fused_computation.2 | convolution fusion | flops 604372992 | bytes 3538944 | tf_op jit(solution)/shard_map/dot_general | solution.py:26
  37.8 4.6 %collective-permute-done.3.refs_2_ = bf16[8,48,768]{2,1,0:T(8,128)(2,1)S(1)} collective-permute-done((bf16[8,48,768]{2,1,0:T(8,128)(2,1)S(1)}, bf16[8,48,768]{2,1,0:T(8,128)(2,1)S(1)}, u32[]{:S(2)}, u32[]{:S(2)}) %collective-permute-start.3) | collective-permute-done | bytes 589856 | tf_op jit(solution)/shard_map/ppermute | solution.py:42
  42.4 1.3 %collective-permute-done.4.refs_3_ = bf16[8,48,768]{2,1,0:T(8,128)(2,1)S(1)} collective-permute-done((bf16[8,48,768]{2,1,0:T(8,128)(2,1)S(1)}, bf16[8,48,768]{2,1,0:T(8,128)(2,1)S(1)}, u32[]{:S(2)}, u32[]{:S(2)}) %collective-permute-start.4) | collective-permute-done | bytes 589856 | tf_op jit(solution)/shard_map/ppermute | solution.py:42
  43.8 0.3 halve.3
  44.0 3.0 %collective-permute-start.10 = (bf16[4,48,768]{2,1,0:T(8,128)(2,1)S(1)}, bf16[4,48,768]{2,1,0:T(8,128)(2,1)S(1)}, u32[]{:S(2)}, u32[]{:S(2)}) collective-permute-start(bf16[4,48,768]{2,1,0:T(8,128)(2,1)S(1)} %get-tuple-element.98), channel_id=1, source_target_pairs={{0,33},{1,32},{2,35},{3,34},{4,37},{5,36},{6,39},{7,38},{8,41},{9,... | collective-permute-start | bytes 884744 | tf_op jit(solution)/shard_map/ppermute | solution.py:42
  47.0 0.0 collective-permute-start.11
  47.0 1.3 %collective-permute-done.6.refs_2_ = bf16[8,48,768]{2,1,0:T(8,128)(2,1)S(1)} collective-permute-done((bf16[8,48,768]{2,1,0:T(8,128)(2,1)S(1)}, bf16[8,48,768]{2,1,0:T(8,128)(2,1)S(1)}, u32[]{:S(2)}, u32[]{:S(2)}) %collective-permute-start.6) | collective-permute-done | bytes 589856 | tf_op jit(solution)/shard_map/ppermute | solution.py:42
  48.3 0.8 collective-permute-done.7.refs_3_
  49.2 0.3 halve.2
  49.4 1.8 %collective-permute-start.8 = (bf16[4,48,768]{2,1,0:T(8,128)(2,1)S(1)}, bf16[4,48,768]{2,1,0:T(8,128)(2,1)S(1)}, u32[]{:S(2)}, u32[]{:S(2)}) collective-permute-start(bf16[4,48,768]{2,1,0:T(8,128)(2,1)S(1)} %get-tuple-element.91), channel_id=1, source_target_pairs={{0,192},{1,193},{2,194},{3,195},{4,196},{5,197},{6,198},{7,199},{8... | collective-permute-start | bytes 884744 | tf_op jit(solution)/shard_map/ppermute | solution.py:42
  51.3 2.6 %collective-permute-start.9 = (bf16[4,48,768]{2,1,0:T(8,128)(2,1)S(1)}, bf16[4,48,768]{2,1,0:T(8,128)(2,1)S(1)}, u32[]{:S(2)}, u32[]{:S(2)}) collective-permute-start(bf16[4,48,768]{2,1,0:T(8,128)(2,1)S(1)} %get-tuple-element.93), channel_id=1, source_target_pairs={{0,64},{1,65},{2,66},{3,67},{4,68},{5,69},{6,70},{7,71},{8,72},{9,... | collective-permute-start | bytes 884744 | tf_op jit(solution)/shard_map/ppermute | solution.py:42
  53.8 2.9 %fusion.30 = f32[384,1536]{1,0:T(8,128)S(1)} fusion(bf16[384,2304]{1,0:T(8,128)(2,1)S(1)} %fusion.2, bf16[1536,2304]{1,0:T(8,128)(2,1)S(1)} %bitcast.52), kind=kOutput, calls=%fused_computation.76 | convolution fusion | flops 2717908992 | bytes 11206656 | tf_op jit(solution)/shard_map/dot_general | solution.py:26
  56.8 0.0 collective-permute-done.10
  56.8 0.1 add_convert_fusion.1
  56.9 0.1 add_convert_fusion.2
  57.0 0.5 collective-permute-start.13
  57.5 1.1 %collective-permute-start.14 = (bf16[48,1536]{1,0:T(8,128)(2,1)S(1)}, bf16[48,1536]{1,0:T(8,128)(2,1)S(1)}, u32[]{:S(2)}, u32[]{:S(2)}) collective-permute-start(bf16[48,1536]{1,0:T(8,128)(2,1)S(1)} %get-tuple-element.108), channel_id=1, source_target_pairs={{0,64},{1,65},{2,66},{3,67},{4,68},{5,69},{6,70},{7,71},{8,72},{9,... | collective-permute-start | bytes 442376 | tf_op jit(solution)/shard_map/ppermute | solution.py:42
  58.6 1.9 %collective-permute-start.15 = (bf16[48,1536]{1,0:T(8,128)(2,1)S(1)}, bf16[48,1536]{1,0:T(8,128)(2,1)S(1)}, u32[]{:S(2)}, u32[]{:S(2)}) collective-permute-start(bf16[48,1536]{1,0:T(8,128)(2,1)S(1)} %get-tuple-element.109), channel_id=1, source_target_pairs={{0,128},{1,129},{2,130},{3,131},{4,132},{5,133},{6,134},{7,135},{8... | collective-permute-start | bytes 442376 | tf_op jit(solution)/shard_map/ppermute | solution.py:42
  60.6 0.0 collective-permute-done.8
  60.6 0.1 add_convert_fusion.4
  60.7 0.1 add_convert_fusion.3
  60.8 0.4 collective-permute-start.16
  61.2 0.4 collective-permute-start.17
  61.6 2.2 %collective-permute-done.13 = bf16[48,1536]{1,0:T(8,128)(2,1)S(1)} collective-permute-done((bf16[48,1536]{1,0:T(8,128)(2,1)S(1)}, bf16[48,1536]{1,0:T(8,128)(2,1)S(1)}, u32[]{:S(2)}, u32[]{:S(2)}) %collective-permute-start.13) | collective-permute-done | bytes 147488 | tf_op jit(solution)/shard_map/ppermute | solution.py:42
  63.8 1.8 %collective-permute-start.18 = (bf16[48,1536]{1,0:T(8,128)(2,1)S(1)}, bf16[48,1536]{1,0:T(8,128)(2,1)S(1)}, u32[]{:S(2)}, u32[]{:S(2)}) collective-permute-start(bf16[48,1536]{1,0:T(8,128)(2,1)S(1)} %get-tuple-element.112), channel_id=1, source_target_pairs={{0,32},{1,33},{2,34},{3,35},{4,36},{5,37},{6,38},{7,39},{8,40},{9,... | collective-permute-start | bytes 442376 | tf_op jit(solution)/shard_map/ppermute | solution.py:42
  65.6 0.1 fusion.13.refs_0_
  65.7 0.0 copy-start
  65.7 0.8 slice.134
  66.5 1.6 %collective-permute-start.12 = (bf16[128,1536]{1,0:T(8,128)(2,1)}, bf16[128,1536]{1,0:T(8,128)(2,1)}, u32[]{:S(2)}, u32[]{:S(2)}) collective-permute-start(bf16[128,1536]{1,0:T(8,128)(2,1)} %slice.134), channel_id=1, source_target_pairs={{0,15},{1,0},{2,1},{3,2},{4,3},{5,4},{6,5},{7,6},{8,7},{9,8},{10,9... | collective-permute-start | bytes 1179656 | tf_op jit(solution)/shard_map/ppermute | solution.py:31
  68.1 0.0 collective-permute-done.16
  68.1 0.0 collective-permute-done.17
  68.1 10.6 %collective-permute-done.18 = bf16[48,1536]{1,0:T(8,128)(2,1)S(1)} collective-permute-done((bf16[48,1536]{1,0:T(8,128)(2,1)S(1)}, bf16[48,1536]{1,0:T(8,128)(2,1)S(1)}, u32[]{:S(2)}, u32[]{:S(2)}) %collective-permute-start.18) | collective-permute-done | bytes 147488 | tf_op jit(solution)/shard_map/ppermute | solution.py:42
  78.7 0.1 fusion.10.refs_1_
  78.8 0.8 pieces.1
  79.6 5.8 %all-to-all-start = ((bf16[8,144,128]{2,1,0:T(8,128)(2,1)}), bf16[8,144,128]{2,1,0:T(8,128)(2,1)S(1)}, u32[]{:S(2)}, u32[]{:S(2)}) async-start(bf16[8,144,128]{2,1,0:T(8,128)(2,1)} %pieces.1), calls=%async_computation | async-start | bytes 589824 | tf_op jit(solution)/shard_map/all_to_all | solution.py:561
  85.4 0.0 collective-permute-done.12
  85.4 1.5 %convert_reduce_fusion = (f32[256]{0:T(256)S(1)}, f32[256]{0:T(256)S(1)}, bf16[256,1536]{1,0:T(8,128)(2,1)S(1)}) fusion(f32[256]{0:T(256)S(1)} %bitcast.49, f32[256]{0:T(256)S(1)} %bitcast.47, bf16[256,1536]{1,0:T(8,128)(2,1)S(1)} %bitcast.45, bf16[128,1536]{1,0:T(8,128)(2,1)} %collective-permute-done.12, f32[384,1536]{1,0:T(8,128)S(1)} %fusion.30), kind=kLoop, calls=%fused_computation.5 | loop fusion | flops 3931648 | bytes 3543040 | tf_op jit(solution)/shard_map/reduce_sum | solution.py:118
  86.9 1.4 %fusion.7 = bf16[1,256,1536]{2,1,0:T(8,128)(2,1)} fusion(bf16[256,1536]{1,0:T(8,128)(2,1)S(1)} %bitcast.46, bf16[256,1536]{1,0:T(8,128)(2,1)S(1)} %get-tuple-element.115, f32[256]{0:T(256)S(1)} %broadcast_multiply_fusion, f32[256]{0:T(256)S(1)} %bitcast.48, f32[256]{0:T(256)S(1)} %broadcast_multiply_fusion.1, f32[256]{0:T(256)S(1)} %bitcast.50), kind=kLoop, calls=%fused_computation.14 | loop fusion | flops 3538944 | bytes 2363392 | tf_op jit(solution)/shard_map/broadcast_in_dim | solution.py:569
  88.3 7.9 %all-to-all-done.in_ref = bf16[8,144,128]{2,1,0:T(8,128)(2,1)S(1)} async-done(((bf16[8,144,128]{2,1,0:T(8,128)(2,1)}), bf16[8,144,128]{2,1,0:T(8,128)(2,1)S(1)}, u32[]{:S(2)}, u32[]{:S(2)}) %all-to-all-start) | async-done | bytes 294944 | tf_op jit(solution)/shard_map/all_to_all | solution.py:561
  96.2 0.7 total.1
  (18 shorter events, 0.1 us)
Async XLA Ops:
  1.7 16.0 %collective-permute-start = (bf16[128,1536]{1,0:T(8,128)(2,1)S(1)}, bf16[128,1536]{1,0:T(8,128)(2,1)S(1)}, u32[]{:S(2)}, u32[]{:S(2)}) collective-permute-start(bf16[128,1536]{1,0:T(8,128)(2,1)S(1)} %last_rows.1), channel_id=1, source_target_pairs={{0,1},{1,2},{2,3},{3,4},{4,5},{5,6},{6,7},{7,8},{8,9},{9,10},{10,1... | collective-permute-start | bytes 1179656 | tf_op jit(solution)/shard_map/ppermute | solution.py:31
  13.9 9.5 %collective-permute-start.2 = (bf16[768,512]{1,0:T(8,128)(2,1)S(1)}, bf16[768,512]{1,0:T(8,128)(2,1)S(1)}, u32[]{:S(2)}, u32[]{:S(2)}) collective-permute-start(bf16[768,512]{1,0:T(8,128)(2,1)S(1)} %get-tuple-element.68), channel_id=1, source_target_pairs={{0,16},{1,17},{2,18},{3,19},{4,20},{5,21},{6,22},{7,23},{8,24},{9,... | collective-permute-start | bytes 2359304 | tf_op jit(solution)/shard_map/ppermute | solution.py:42
  22.3 2.6 %collective-permute-start.1 = (bf16[2,256,768]{2,1,0:T(8,128)(2,1)S(1)}, bf16[2,256,768]{2,1,0:T(8,128)(2,1)S(1)}, u32[]{:S(2)}, u32[]{:S(2)}) collective-permute-start(bf16[2,256,768]{2,1,0:T(8,128)(2,1)S(1)} %get-tuple-element.67.right_ref), channel_id=1, source_target_pairs={{0,16},{1,17},{2,18},{3,19},{4,20},{5,21},{6,22},{7,23},{8,24},{9,... | collective-permute-start | bytes 2359304 | tf_op jit(solution)/shard_map/ppermute | solution.py:42
  24.9 5.5 %collective-permute-start.5 = (bf16[2,384,896]{2,1,0:T(8,128)(2,1)S(1)}, bf16[2,384,896]{2,1,0:T(8,128)(2,1)S(1)}, u32[]{:S(2)}, u32[]{:S(2)}) collective-permute-start(bf16[2,384,896]{2,1,0:T(8,128)(2,1)S(1)} %get-tuple-element.76.right_ref), channel_id=1, source_target_pairs={{0,16},{1,17},{2,18},{3,19},{4,20},{5,21},{6,22},{7,23},{8,24},{9,... | collective-permute-start | bytes 4128776 | tf_op jit(solution)/shard_map/ppermute | solution.py:42
  26.7 15.7 %collective-permute-start.3 = (bf16[8,48,768]{2,1,0:T(8,128)(2,1)S(1)}, bf16[8,48,768]{2,1,0:T(8,128)(2,1)S(1)}, u32[]{:S(2)}, u32[]{:S(2)}) collective-permute-start(bf16[8,48,768]{2,1,0:T(8,128)(2,1)S(1)} %get-tuple-element.74), channel_id=1, source_target_pairs={{0,1},{1,0},{2,3},{3,2},{4,5},{5,4},{6,7},{7,6},{8,9},{9,8},{10,11... | collective-permute-start | bytes 1769480 | tf_op jit(solution)/shard_map/ppermute | solution.py:42
  26.8 16.9 %collective-permute-start.4 = (bf16[8,48,768]{2,1,0:T(8,128)(2,1)S(1)}, bf16[8,48,768]{2,1,0:T(8,128)(2,1)S(1)}, u32[]{:S(2)}, u32[]{:S(2)}) collective-permute-start(bf16[8,48,768]{2,1,0:T(8,128)(2,1)S(1)} %get-tuple-element.75), channel_id=1, source_target_pairs={{0,33},{1,32},{2,35},{3,34},{4,37},{5,36},{6,39},{7,38},{8,41},{9,... | collective-permute-start | bytes 1769480 | tf_op jit(solution)/shard_map/ppermute | solution.py:42
  30.2 23.6 %slice-start = ((s8[7077888]{0:T(1024)(128)(4,1)}), s8[4194304]{0:T(1024)(128)(4,1)S(1)}, s32[]{:S(2)}) async-start(s8[7077888]{0:T(1024)(128)(4,1)} %bitcast.51), calls=%async_computation.1 | async-start | bytes 8388608
  30.4 5.8 %copy-start.1 = (bf16[768,1536]{1,0:T(8,128)(2,1)S(1)}, bf16[768,1536]{1,0:T(8,128)(2,1)}, u32[]{:S(2)}) copy-start(bf16[768,1536]{1,0:T(8,128)(2,1)} %out_ref.1) | copy-start | bytes 7077892
  30.4 23.5 %slice-start.1 = ((s8[7077888]{0:T(1024)(128)(4,1)}), s8[2883584]{0:T(1024)(128)(4,1)S(1)}, s32[]{:S(2)}) async-start(s8[7077888]{0:T(1024)(128)(4,1)} %bitcast.51), calls=%async_computation.2 | async-start | bytes 5767168
  33.2 15.1 %collective-permute-start.6 = (bf16[8,48,768]{2,1,0:T(8,128)(2,1)S(1)}, bf16[8,48,768]{2,1,0:T(8,128)(2,1)S(1)}, u32[]{:S(2)}, u32[]{:S(2)}) collective-permute-start(bf16[8,48,768]{2,1,0:T(8,128)(2,1)S(1)} %get-tuple-element.85), channel_id=1, source_target_pairs={{0,64},{1,65},{2,66},{3,67},{4,68},{5,69},{6,70},{7,71},{8,72},{9,... | collective-permute-start | bytes 1769480 | tf_op jit(solution)/shard_map/ppermute | solution.py:42
  33.8 15.4 %collective-permute-start.7 = (bf16[8,48,768]{2,1,0:T(8,128)(2,1)S(1)}, bf16[8,48,768]{2,1,0:T(8,128)(2,1)S(1)}, u32[]{:S(2)}, u32[]{:S(2)}) collective-permute-start(bf16[8,48,768]{2,1,0:T(8,128)(2,1)S(1)} %get-tuple-element.86), channel_id=1, source_target_pairs={{0,192},{1,193},{2,194},{3,195},{4,196},{5,197},{6,198},{7,199},{8... | collective-permute-start | bytes 1769480 | tf_op jit(solution)/shard_map/ppermute | solution.py:42
  44.0 12.8 %collective-permute-start.10 = (bf16[4,48,768]{2,1,0:T(8,128)(2,1)S(1)}, bf16[4,48,768]{2,1,0:T(8,128)(2,1)S(1)}, u32[]{:S(2)}, u32[]{:S(2)}) collective-permute-start(bf16[4,48,768]{2,1,0:T(8,128)(2,1)S(1)} %get-tuple-element.98), channel_id=1, source_target_pairs={{0,33},{1,32},{2,35},{3,34},{4,37},{5,36},{6,39},{7,38},{8,41},{9,... | collective-permute-start | bytes 884744 | tf_op jit(solution)/shard_map/ppermute | solution.py:42
  47.0 9.8 %collective-permute-start.11 = (bf16[4,48,768]{2,1,0:T(8,128)(2,1)S(1)}, bf16[4,48,768]{2,1,0:T(8,128)(2,1)S(1)}, u32[]{:S(2)}, u32[]{:S(2)}) collective-permute-start(bf16[4,48,768]{2,1,0:T(8,128)(2,1)S(1)} %get-tuple-element.99), channel_id=1, source_target_pairs={{0,1},{1,0},{2,3},{3,2},{4,5},{5,4},{6,7},{7,6},{8,9},{9,8},{10,11... | collective-permute-start | bytes 884744 | tf_op jit(solution)/shard_map/ppermute | solution.py:42
  49.4 11.1 %collective-permute-start.8 = (bf16[4,48,768]{2,1,0:T(8,128)(2,1)S(1)}, bf16[4,48,768]{2,1,0:T(8,128)(2,1)S(1)}, u32[]{:S(2)}, u32[]{:S(2)}) collective-permute-start(bf16[4,48,768]{2,1,0:T(8,128)(2,1)S(1)} %get-tuple-element.91), channel_id=1, source_target_pairs={{0,192},{1,193},{2,194},{3,195},{4,196},{5,197},{6,198},{7,199},{8... | collective-permute-start | bytes 884744 | tf_op jit(solution)/shard_map/ppermute | solution.py:42
  51.3 9.4 %collective-permute-start.9 = (bf16[4,48,768]{2,1,0:T(8,128)(2,1)S(1)}, bf16[4,48,768]{2,1,0:T(8,128)(2,1)S(1)}, u32[]{:S(2)}, u32[]{:S(2)}) collective-permute-start(bf16[4,48,768]{2,1,0:T(8,128)(2,1)S(1)} %get-tuple-element.93), channel_id=1, source_target_pairs={{0,64},{1,65},{2,66},{3,67},{4,68},{5,69},{6,70},{7,71},{8,72},{9,... | collective-permute-start | bytes 884744 | tf_op jit(solution)/shard_map/ppermute | solution.py:42
  57.0 6.8 %collective-permute-start.13 = (bf16[48,1536]{1,0:T(8,128)(2,1)S(1)}, bf16[48,1536]{1,0:T(8,128)(2,1)S(1)}, u32[]{:S(2)}, u32[]{:S(2)}) collective-permute-start(bf16[48,1536]{1,0:T(8,128)(2,1)S(1)} %get-tuple-element.107), channel_id=1, source_target_pairs={{0,192},{1,193},{2,194},{3,195},{4,196},{5,197},{6,198},{7,199},{8... | collective-permute-start | bytes 442376 | tf_op jit(solution)/shard_map/ppermute | solution.py:42
  57.5 8.0 %collective-permute-start.14 = (bf16[48,1536]{1,0:T(8,128)(2,1)S(1)}, bf16[48,1536]{1,0:T(8,128)(2,1)S(1)}, u32[]{:S(2)}, u32[]{:S(2)}) collective-permute-start(bf16[48,1536]{1,0:T(8,128)(2,1)S(1)} %get-tuple-element.108), channel_id=1, source_target_pairs={{0,64},{1,65},{2,66},{3,67},{4,68},{5,69},{6,70},{7,71},{8,72},{9,... | collective-permute-start | bytes 442376 | tf_op jit(solution)/shard_map/ppermute | solution.py:42
  58.6 6.9 %collective-permute-start.15 = (bf16[48,1536]{1,0:T(8,128)(2,1)S(1)}, bf16[48,1536]{1,0:T(8,128)(2,1)S(1)}, u32[]{:S(2)}, u32[]{:S(2)}) collective-permute-start(bf16[48,1536]{1,0:T(8,128)(2,1)S(1)} %get-tuple-element.109), channel_id=1, source_target_pairs={{0,128},{1,129},{2,130},{3,131},{4,132},{5,133},{6,134},{7,135},{8... | collective-permute-start | bytes 442376 | tf_op jit(solution)/shard_map/ppermute | solution.py:42
  60.8 7.3 %collective-permute-start.16 = (bf16[48,1536]{1,0:T(8,128)(2,1)S(1)}, bf16[48,1536]{1,0:T(8,128)(2,1)S(1)}, u32[]{:S(2)}, u32[]{:S(2)}) collective-permute-start(bf16[48,1536]{1,0:T(8,128)(2,1)S(1)} %get-tuple-element.110), channel_id=1, source_target_pairs={{0,33},{1,32},{2,35},{3,34},{4,37},{5,36},{6,39},{7,38},{8,41},{9,... | collective-permute-start | bytes 442376 | tf_op jit(solution)/shard_map/ppermute | solution.py:42
  61.2 6.9 %collective-permute-start.17 = (bf16[48,1536]{1,0:T(8,128)(2,1)S(1)}, bf16[48,1536]{1,0:T(8,128)(2,1)S(1)}, u32[]{:S(2)}, u32[]{:S(2)}) collective-permute-start(bf16[48,1536]{1,0:T(8,128)(2,1)S(1)} %get-tuple-element.111), channel_id=1, source_target_pairs={{0,1},{1,0},{2,3},{3,2},{4,5},{5,4},{6,7},{7,6},{8,9},{9,8},{10,11... | collective-permute-start | bytes 442376 | tf_op jit(solution)/shard_map/ppermute | solution.py:42
  63.8 14.9 %collective-permute-start.18 = (bf16[48,1536]{1,0:T(8,128)(2,1)S(1)}, bf16[48,1536]{1,0:T(8,128)(2,1)S(1)}, u32[]{:S(2)}, u32[]{:S(2)}) collective-permute-start(bf16[48,1536]{1,0:T(8,128)(2,1)S(1)} %get-tuple-element.112), channel_id=1, source_target_pairs={{0,32},{1,33},{2,34},{3,35},{4,36},{5,37},{6,38},{7,39},{8,40},{9,... | collective-permute-start | bytes 442376 | tf_op jit(solution)/shard_map/ppermute | solution.py:42
  65.7 19.8 %copy-start = (bf16[1,256,1536]{2,1,0:T(8,128)(2,1)S(1)}, bf16[1,256,1536]{2,1,0:T(8,128)(2,1)}, u32[]{:S(2)}) copy-start(bf16[1,256,1536]{2,1,0:T(8,128)(2,1)} %param.6) | copy-start | bytes 2359300
  66.5 18.9 %collective-permute-start.12 = (bf16[128,1536]{1,0:T(8,128)(2,1)}, bf16[128,1536]{1,0:T(8,128)(2,1)}, u32[]{:S(2)}, u32[]{:S(2)}) collective-permute-start(bf16[128,1536]{1,0:T(8,128)(2,1)} %slice.134), channel_id=1, source_target_pairs={{0,15},{1,0},{2,1},{3,2},{4,3},{5,4},{6,5},{7,6},{8,7},{9,8},{10,9... | collective-permute-start | bytes 1179656 | tf_op jit(solution)/shard_map/ppermute | solution.py:31
  79.6 16.7 %all-to-all-start = ((bf16[8,144,128]{2,1,0:T(8,128)(2,1)}), bf16[8,144,128]{2,1,0:T(8,128)(2,1)S(1)}, u32[]{:S(2)}, u32[]{:S(2)}) async-start(bf16[8,144,128]{2,1,0:T(8,128)(2,1)} %pieces.1), calls=%async_computation | async-start | bytes 589824 | tf_op jit(solution)/shard_map/all_to_all | solution.py:561

commit v6 on v5

--- a/solution.py
+++ b/solution.py
@@ -70,15 +70,19 @@
     return y ^ 2, xh, core, z, xl
 
 
+def along_z(step):
+    return lambda y, xh, core, z, xl: (y, xh, core, (z + step) % Z, xl)
+
+
 ROUTES = (
+    (to_y_near, to_y_mirror),
+    (to_y_mirror, to_y_near),
     (to_x_near, to_x_mirror),
     (to_x_mirror, to_x_near),
-    (to_y_near, to_y_mirror),
-    (to_y_mirror, to_y_near),
 )
 OWNERS = (
+    (to_x_mirror, to_x_near, to_x_far),
     (to_y_mirror, to_y_near, to_y_far),
-    (to_x_mirror, to_x_near, to_x_far),
 )
 
 
@@ -88,7 +92,7 @@
 
 def chunk_at(route, slot, y, xh, xl):
     bits = [(slot >> (3 - i)) & 1 for i in range(4)]
-    x_first = route < 2
+    x_first = route >= 2
     x_bits, y_bits = (bits[:2], bits[2:]) if x_first else (bits[2:], bits[:2])
     found = []
     for hi, lo, pair, order in ((y >> 1, y & 1, y_bits, 0 if x_first else route), (xh, xl, x_bits, route if x_first else 0)):
@@ -110,12 +114,6 @@
     centered = rows_in - average
     variance = jnp.mean(centered * centered, axis=-1, keepdims=True)
     return average, lax.rsqrt(variance + epsilon)
-
-
-def normalize_grad(rows_in, average, inverse, grad):
-    normed = (rows_in - average) * inverse
-    along = jnp.mean(grad * normed, axis=-1, keepdims=True)
-    return inverse * (grad - jnp.mean(grad, axis=-1, keepdims=True) - normed * along)
 
 
 SMEM_SPEC = pl.BlockSpec(memory_space=pltpu.SMEM)
@@ -443,6 +441,47 @@
     return outs[:routes], outs[routes:]
 
 
+def finish_kernel(back_ref, grad_ref, frames_ref, stats_ref, out_ref, rows, grads, sems):
+    tiles = rows.shape[0] // CONTEXT
+    copies = []
+    for i in range(tiles):
+        here = pl.ds(i * CONTEXT, CONTEXT)
+        copies.append(pltpu.make_async_copy(frames_ref.at[here], rows.at[here], sems.at[i]))
+        copies.append(pltpu.make_async_copy(grad_ref.at[here], grads.at[here], sems.at[tiles + i]))
+    for copy in copies:
+        copy.start()
+    columns = jnp.concatenate([stats_ref[...]] * 4, axis=0).T
+    for i in range(tiles):
+        here = slice(i * CONTEXT, (i + 1) * CONTEXT)
+        copies[2 * i].wait()
+        copies[2 * i + 1].wait()
+        grad = grads[here]
+        if (i + 1) * CONTEXT == rows.shape[0]:
+            grad += back_ref[...].astype(F32)
+        grad = grad.astype(BF16).astype(F32)
+        inverse = columns[here, 1:2]
+        normed = (rows[here].astype(F32) - columns[here, 0:1]) * inverse
+        along = jnp.mean(grad * normed, axis=-1, keepdims=True)
+        out_ref[here] = (inverse * (grad - jnp.mean(grad, axis=-1, keepdims=True) - normed * along)).astype(BF16)
+
+
+def finish(back, grad, frames, stats):
+    return pl.pallas_call(
+        finish_kernel,
+        in_specs=[VMEM_SPEC, HBM_SPEC, HBM_SPEC, VMEM_SPEC],
+        out_specs=VMEM_SPEC,
+        out_shape=jax.ShapeDtypeStruct(frames.shape, BF16),
+        scratch_shapes=[
+            pltpu.VMEM(frames.shape, BF16),
+            pltpu.VMEM(frames.shape, F32),
+            pltpu.SemaphoreType.DMA((2 * frames.shape[0] // CONTEXT,)),
+        ],
+        compiler_params=params(12),
+        cost_estimate=cost(1, 1),
+        name="finish",
+    )(in_vmem(back), in_hbm(grad), in_hbm(frames), in_vmem(stats))
+
+
 def plus(*terms):
     return sum(t.astype(F32) for t in terms).astype(BF16)
 
@@ -469,25 +508,42 @@
     return outs[:2], outs[2:]
 
 
-def pieces_kernel(*refs):
-    ins, out_ref, held = refs[:-2], refs[-2], refs[-1]
-    for ref, places in zip(ins, ((3, 0), (1, 2))):
+def pieces_kernel(place, first_ref, second_ref, *refs):
+    outs, held = refs[:-1], refs[-1]
+    for ref, places in ((first_ref, (3, 0)), (second_ref, (1, 2))):
         block = ref[...].astype(F32)
         tiles = block.shape[1] // PAIR // 2
         share = block.shape[0] // Z
-        for n, place in enumerate(places):
+        for n, at in enumerate(places):
             for t in range(tiles):
-                rows = slice((place * tiles + t) * share, (place * tiles + t + 1) * share)
+                rows = slice((at * tiles + t) * share, (at * tiles + t + 1) * share)
                 column = (n * tiles + t) * PAIR
                 for z in range(Z):
                     held[z, rows, :] = block[z * share : (z + 1) * share, column : column + PAIR]
-    out_ref[...] = held[...].astype(BF16)
-
-
-def total_kernel(in_ref, out_ref):
-    total = in_ref[0].astype(F32)
-    for z in range(1, Z):
-        total += in_ref[z].astype(F32)
+    for step, ref in enumerate(outs):
+        ref[...] = held[lax.rem(place[0] + step, Z)].astype(BF16)
+
+
+def pieces(place, groups):
+    rows, columns = groups[0].shape
+    size = (rows // Z * 2 * columns // PAIR, PAIR)
+    return pl.pallas_call(
+        pieces_kernel,
+        in_specs=[SMEM_SPEC] + [VMEM_SPEC] * 2,
+        out_specs=[VMEM_SPEC] * Z,
+        out_shape=[pltpu.VMEM(size, BF16)] * Z,
+        scratch_shapes=[pltpu.VMEM((Z, *size), F32)],
+        compiler_params=params(16),
+        cost_estimate=cost(1, 1),
+        name="pieces",
+    )(jnp.reshape(place, (1,)), *[in_vmem(g) for g in groups])
+
+
+def total_kernel(*refs):
+    ins, out_ref = refs[:-1], refs[-1]
+    total = ins[0][...].astype(F32)
+    for ref in ins[1:]:
+        total += ref[...].astype(F32)
     share = out_ref.shape[0]
     for t in range(out_ref.shape[1] // PAIR):
         out_ref[:, t * PAIR : (t + 1) * PAIR] = total[t * share : (t + 1) * share]
@@ -544,29 +600,20 @@
     second_group, normed_grad = second_ring(kept_b, gots_b, 1, normed_grad)
     groups = [first_group, second_group]
     returned = from_behind(normed_grad[row_count:].astype(BF16), "seq", -1)
-    returned = jnp.concatenate([jnp.zeros((row_count - CONTEXT, width), BF16), returned], axis=0)
-    normed_grad = (normed_grad[:row_count] + returned.astype(F32)).astype(BF16)
-    frame_grad = normalize_grad(frame_rows.astype(F32), stats[0][:, None], stats[1][:, None], normed_grad.astype(F32))
+    frame_grad = finish(returned, normed_grad, frame_rows, stats)
+    shares = pieces(seq_index // XL, groups)
+    shares = [shares[0]] + [to_device(shares[step], along_z(step)) for step in (4, 3, 5, 2, 6, 1, 7)]
+    shares, frame_grad = lax.optimization_barrier((shares, frame_grad))
     share = width // (CHUNKS * CORES * Z)
-    tiles = 4 * inner // PAIR
-    shares = pl.pallas_call(
-        pieces_kernel,
-        in_specs=[VMEM_SPEC] * 2,
-        out_shape=jax.ShapeDtypeStruct((Z, tiles * share, PAIR), BF16),
-        scratch_shapes=[pltpu.VMEM((Z, tiles * share, PAIR), F32)],
-        compiler_params=params(24),
-        name="pieces",
-    )(*[in_vmem(g) for g in groups])
-    rings = [[place * XL + x for place in range(Z)] for x in range(XL)]
-    shares = lax.all_to_all(shares, "seq", 0, 0, axis_index_groups=rings, tiled=True)
     total = pl.pallas_call(
         total_kernel,
-        in_specs=[VMEM_SPEC],
+        in_specs=[VMEM_SPEC] * Z,
         out_shape=jax.ShapeDtypeStruct((share, 4 * inner), F32),
-        compiler_params=params(24),
+        compiler_params=params(8),
+        cost_estimate=cost(1, 1),
         name="total",
-    )(in_vmem(shares))
-    return block_out[None], frame_grad.astype(BF16)[None], total
+    )(*[in_vmem(o) for o in shares])
+    return block_out[None], frame_grad[None], total
 
 
 def solution(mesh):

time: 97.8 us -> 98.9 us (1.011)
  waiting for transfers between devices: 33.9 us -> 13.7 us
  starting transfers between devices: 29.4 us -> 43.6 us
  Pallas kernels: 22.9 us -> 28.1 us
  matrix products: 4.59 us -> 8.64 us
  other arithmetic: 3.65 us -> 1.97 us
    ppermute x17 -> x24, starting transfers between devices: 20.4 us -> 39.7 us  [to_device(): return lax.ppermute(value, ('dp', 'seq'), pairs)]
    ppermute x17 -> x24, waiting for transfers between devices: 22.4 us -> 10.1 us  [to_device(): return lax.ppermute(value, ('dp', 'seq'), pairs)]
    all_to_all x1 -> x0, waiting for transfers between devices: 7.9 us -> none  [on_device(): lax.all_to_all(shares, 'seq', 0, 0, axis_index_groups=rings, tiled=True)]
    all_to_all x1 -> x0, starting transfers between devices: 5.83 us -> none  [on_device(): lax.all_to_all(shares, 'seq', 0, 0, axis_index_groups=rings, tiled=True)]
    dot_general x2, matrix products: 4.59 us -> 8.64 us  [dot(): return lax.dot_general(a, b, dims, preferred_element_type=F32)]
    pallas_call x2 -> x3, Pallas kernels: 1.49 us -> 3.73 us  [the longest x1 2.94 us: finish(): pl.pallas_call(finish_kernel, in_specs=[VMEM_SPEC, HBM_SPEC, HBM_SPEC, VM...]
    pallas_call x2, Pallas kernels: 4.46 us -> 6.22 us  [weight_sections(): pl.pallas_call(kernel, in_specs=[SMEM_SPEC] + [VMEM_SPEC] * len(operands)...]
    reduce_sum x1 -> x0, other arithmetic: 1.48 us -> none  [normalize_grad(): jnp.mean(grad, axis=-1, keepdims=True)]
  transfers between devices with their start and end apart: 20 -> 26, of which waited for: 9 -> 9; matrix products, arithmetic and copies ran while one was open for 9% -> 12% of each run, Pallas kernels for 22% -> 27%
where the time goes in v6:
time: 98.9 us; the launch traced here: 98.6 us
  starting transfers between devices  43.6 us (44%)
  Pallas kernels  28.1 us (28%)
  waiting for transfers between devices  13.7 us (14%)
  matrix products  8.64 us (9%)
  other arithmetic  1.97 us (2%)
  between operations  1.54 us (2%)
    ppermute x24, starting transfers between devices, to_device(): return lax.ppermute(value, ('dp', 'seq'), pairs)  39.7 us
    ppermute x24, waiting for transfers between devices, to_device(): return lax.ppermute(value, ('dp', 'seq'), pairs)  10.1 us
    pallas_call x1, Pallas kernels, front(): pl.pallas_call(front_kernel, in_specs=[SMEM_SPEC] + [HBM_SPEC] * 6, out_s...  9.89 us
    dot_general x2, matrix products, dot(): return lax.dot_general(a, b, dims, preferred_element_type=F32)  8.64 us
    pallas_call x2, Pallas kernels, weight_sections(): pl.pallas_call(kernel, in_specs=[SMEM_SPEC] + [VMEM_SPEC] * len(operands)...  6.22 us
    pallas_call x1, Pallas kernels, early_tile(): pl.pallas_call(early_kernel, in_specs=[SMEM_SPEC, HBM_SPEC] + [VMEM_SPEC]...  4.69 us
    ppermute x2, starting transfers between devices, from_behind(): lax.ppermute(value, axis, [(i, (i + by) % peers) for i in range(peers)])  3.97 us
    ppermute x2, waiting for transfers between devices, from_behind(): lax.ppermute(value, axis, [(i, (i + by) % peers) for i in range(peers)])  3.62 us
  transfers between devices with their start and end apart: 26, of which 9 were waited for; matrix products, arithmetic and copies ran while one was open for 12% of the time, Pallas kernels for 27%

profile of v6, /device:TPU:8, one launch (start us, length us, event | category | flops | bytes accessed | tf_op | source)
XLA Modules:
  0.0 98.6 jit_solution(11080048135775146591)
XLA Ops:
  0.6 1.0 %last_rows.1 = bf16[128,1536]{1,0:T(8,128)(2,1)S(1)} custom-call(bf16[256,1536]{1,0:T(8,128)(2,1)} %bitcast.41), custom_call_target="tpu_custom_call" | custom-call | flops 1 | bytes 1 | tf_op jit(solution)/shard_map/last_rows/pallas_call | solution.py:168
  1.7 1.6 %collective-permute-start = (bf16[128,1536]{1,0:T(8,128)(2,1)S(1)}, bf16[128,1536]{1,0:T(8,128)(2,1)S(1)}, u32[]{:S(2)}, u32[]{:S(2)}) collective-permute-start(bf16[128,1536]{1,0:T(8,128)(2,1)S(1)} %last_rows.1), channel_id=1, source_target_pairs={{0,1},{1,2},{2,3},{3,4},{4,5},{5,6},{6,7},{7,8},{8,9},{9,10},{10,1... | collective-permute-start | bytes 1179656 | tf_op jit(solution)/shard_map/ppermute | solution.py:31
  3.3 0.1 pad_add_fusion.1.places
  4.0 9.9 %front.1 = (bf16[256,2304]{1,0:T(8,128)(2,1)S(1)}, bf16[256,768]{1,0:T(8,128)(2,1)S(1)}, bf16[768,512]{1,0:T(8,128)(2,1)S(1)}, bf16[768,512]{1,0:T(8,128)(2,1)S(...) custom-call(s32[2]{0:T(128)S(1)} %pad_add_fusion.1.places, ...), custom_call_target="tpu_custom_call" | custom-call | flops 3623878656 | bytes 11796480 | tf_op jit(solution)/shard_map/front/pallas_call | solution.py:249
  13.9 0.1 collective-permute-start.2
  14.0 3.6 %collective-permute-done.frames_ref = bf16[128,1536]{1,0:T(8,128)(2,1)S(1)} collective-permute-done((bf16[128,1536]{1,0:T(8,128)(2,1)S(1)}, bf16[128,1536]{1,0:T(8,128)(2,1)S(1)}, u32[]{:S(2)}, u32[]{:S(2)}) %collective-permute-start) | collective-permute-done | bytes 393248 | tf_op jit(solution)/shard_map/ppermute | solution.py:31
  17.6 4.7 %attention_early.1 = (bf16[2,256,768]{2,1,0:T(8,128)(2,1)S(1)}, bf16[2,384,896]{2,1,0:T(8,128)(2,1)S(1)}, bf16[768,128]{1,0:T(8,128)(2,1)S(1)}) custom-call(s32[2]{0:T(128)S(1)} %pad_add_fusion.1.places, s32[1]{0:T(128)S(6)} %copy.9.lengths_ref, bf16[384,384]{1,0:T(8,128)(2,1)S(1)} %get-tuple-element.78.order_ref, ...), custom_call_target="tpu_custom_call" | custom-call | flops 704643072 | bytes 1572864 | tf_op jit(solution)/shard_map/attention_early/pallas_call | solution.py:365
  22.3 0.3 collective-permute-start.1
  22.6 0.8 first_own.1.own_ref
  23.4 1.5 %collective-permute-done.1.right_other_ref = bf16[2,256,768]{2,1,0:T(8,128)(2,1)S(1)} collective-permute-done((bf16[2,256,768]{2,1,0:T(8,128)(2,1)S(1)}, bf16[2,256,768]{2,1,0:T(8,128)(2,1)S(1)}, u32[]{:S(2)}, u32[]{:S(2)}) %collective-permute-start.1) | collective-permute-done | bytes 786464 | tf_op jit(solution)/shard_map/ppermute | solution.py:42
  24.9 0.1 collective-permute-start.5
  25.0 0.8 slice_bitcast_fusion.2
  25.8 2.6 %first_wave.1 = (bf16[8,48,768]{2,1,0:T(8,128)(2,1)S(1)}, bf16[8,48,768]{2,1,0:T(8,128)(2,1)S(1)}, bf16[8,48,768]{2,1,0:T(8,128)(2,1)}, bf16[8,48,768]{2,1,0:T(8,128)(2,1)}) custom-call(s32[4,16]{1,0:T(4,128)S(1)} %pad_add_fusion.chunks, bf16[768,512]{1,0:T(8,128)(2,1)S(1)} %collective-permute-done.2.left_other_ref, ...), custom_call_target="tpu_custom_call" | custom-call | flops 1 | bytes 1 | tf_op jit(solution)/shard_map/first_wave/pallas_call | solution.py:431
  28.5 0.5 collective-permute-start.3
  28.9 2.4 %collective-permute-start.4 = (bf16[8,48,768]{2,1,0:T(8,128)(2,1)}, bf16[8,48,768]{2,1,0:T(8,128)(2,1)S(1)}, u32[]{:S(2)}, u32[]{:S(2)}) collective-permute-start(bf16[8,48,768]{2,1,0:T(8,128)(2,1)} %get-tuple-element.92), channel_id=1, source_target_pairs={{0,192},{1,193},{2,194},{3,195},{4,196},{5,197},{6,198},{7,199},{8... | collective-permute-start | bytes 1769480 | tf_op jit(solution)/shard_map/ppermute | solution.py:42
  31.3 0.1 slice_bitcast_fusion.1
  31.4 1.3 %fusion.2 = bf16[384,2304]{1,0:T(8,128)(2,1)} fusion(bf16[256,768]{1,0:T(8,128)(2,1)S(1)} %get-tuple-element.149, bf16[384,768]{1,0:T(8,128)(2,1)S(1)} %get-tuple-element.148, bf16[384,768]{1,0:T(8,128)(2,1)S(1)} %get-tuple-element.147), kind=kLoop, calls=%fused_computation.4 | loop fusion | flops 7077888 | bytes 3342336 | tf_op jit(solution)/shard_map/concatenate | solution.py:580
  32.8 0.0 collective-permute-done.5.right_other_ref
  32.8 3.6 %second_wave.1 = (bf16[8,48,768]{2,1,0:T(8,128)(2,1)S(1)}, bf16[8,48,768]{2,1,0:T(8,128)(2,1)S(1)}, bf16[8,48,768]{2,1,0:T(8,128)(2,1)}, bf16[8,48,768]{2,1,0:T(8,128)(2,1)}) custom-call(s32[4,16]{1,0:T(4,128)S(1)} %pad_add_fusion.chunks, bf16[768,512]{1,0:T(8,128)(2,1)S(1)} %get-tuple-element.86.left_ref, ...), custom_call_target="tpu_custom_call" | custom-call | flops 3000000000 | bytes 1 | tf_op jit(solution)/shard_map/second_wave/pallas_call | solution.py:431
  36.4 3.3 %collective-permute-start.9 = (bf16[8,48,768]{2,1,0:T(8,128)(2,1)}, bf16[8,48,768]{2,1,0:T(8,128)(2,1)}, u32[]{:S(2)}, u32[]{:S(2)}) collective-permute-start(bf16[8,48,768]{2,1,0:T(8,128)(2,1)} %get-tuple-element.110), channel_id=1, source_target_pairs={{0,33},{1,32},{2,35},{3,34},{4,37},{5,36},{6,39},{7,38},{8,41},{9,... | collective-permute-start | bytes 1769480 | tf_op jit(solution)/shard_map/ppermute | solution.py:42
  39.7 3.5 %convolution_convert_fusion = bf16[256,1536]{1,0:T(8,128)(2,1)} fusion(bf16[256,768]{1,0:T(8,128)(2,1)} %get-tuple-element.97, bf16[768,1536]{1,0:T(8,128)(2,1)} %out_ref.1), kind=kOutput, calls=%fused_computation.2 | convolution fusion | flops 604372992 | bytes 3538944 | tf_op jit(solution)/shard_map/dot_general | solution.py:26
  43.1 1.2 %collective-permute-done.3.refs_2_ = bf16[8,48,768]{2,1,0:T(8,128)(2,1)S(1)} collective-permute-done((bf16[8,48,768]{2,1,0:T(8,128)(2,1)}, bf16[8,48,768]{2,1,0:T(8,128)(2,1)S(1)}, u32[]{:S(2)}, u32[]{:S(2)}) %collective-permute-start.3) | collective-permute-done | bytes 589856 | tf_op jit(solution)/shard_map/ppermute | solution.py:42
  44.3 0.8 collective-permute-done.4.refs_3_
  45.1 0.3 halve.2
  45.4 1.8 %collective-permute-start.6 = (bf16[4,48,768]{2,1,0:T(8,128)(2,1)S(1)}, bf16[4,48,768]{2,1,0:T(8,128)(2,1)S(1)}, u32[]{:S(2)}, u32[]{:S(2)}) collective-permute-start(bf16[4,48,768]{2,1,0:T(8,128)(2,1)S(1)} %get-tuple-element.104), channel_id=1, source_target_pairs={{0,192},{1,193},{2,194},{3,195},{4,196},{5,197},{6,198},{7,199},{8... | collective-permute-start | bytes 884744 | tf_op jit(solution)/shard_map/ppermute | solution.py:42
  47.2 2.6 %collective-permute-start.7 = (bf16[4,48,768]{2,1,0:T(8,128)(2,1)S(1)}, bf16[4,48,768]{2,1,0:T(8,128)(2,1)S(1)}, u32[]{:S(2)}, u32[]{:S(2)}) collective-permute-start(bf16[4,48,768]{2,1,0:T(8,128)(2,1)S(1)} %get-tuple-element.105), channel_id=1, source_target_pairs={{0,64},{1,65},{2,66},{3,67},{4,68},{5,69},{6,70},{7,71},{8,72},{9,... | collective-permute-start | bytes 884744 | tf_op jit(solution)/shard_map/ppermute | solution.py:42
  49.8 1.9 %collective-permute-done.8.refs_2_ = bf16[8,48,768]{2,1,0:T(8,128)(2,1)} collective-permute-done((bf16[8,48,768]{2,1,0:T(8,128)(2,1)}, bf16[8,48,768]{2,1,0:T(8,128)(2,1)}, u32[]{:S(2)}, u32[]{:S(2)}) %collective-permute-start.8) | collective-permute-done | bytes 589856 | tf_op jit(solution)/shard_map/ppermute | solution.py:42
  51.7 1.3 %collective-permute-done.9.refs_3_ = bf16[8,48,768]{2,1,0:T(8,128)(2,1)} collective-permute-done((bf16[8,48,768]{2,1,0:T(8,128)(2,1)}, bf16[8,48,768]{2,1,0:T(8,128)(2,1)}, u32[]{:S(2)}, u32[]{:S(2)}) %collective-permute-start.9) | collective-permute-done | bytes 589856 | tf_op jit(solution)/shard_map/ppermute | solution.py:42
  53.0 1.5 %halve.3 = (bf16[4,48,768]{2,1,0:T(8,128)(2,1)S(1)}, bf16[4,48,768]{2,1,0:T(8,128)(2,1)S(1)}, bf16[4,48,768]{2,1,0:T(8,128)(2,1)S(1)}, bf16[4,48,768]{2,1,0:T(8,128)(2,1)S(1)}) custom-call(bf16[8,48,768]{2,1,0:T(8,128)(2,1)S(1)} %get-tuple-element.107.refs_0_, bf16[8,48,768]{2,1,0:T(8,128)(2,1)S(1)} %get-tuple-element.108.refs_1_, ...), custom_call_target="tpu_custom_call" | custom-call | flops 1 | bytes 1 | tf_op jit(solution)/shard_map/halve/pallas_call | solution.py:499
  54.5 3.0 %collective-permute-start.13 = (bf16[4,48,768]{2,1,0:T(8,128)(2,1)S(1)}, bf16[4,48,768]{2,1,0:T(8,128)(2,1)S(1)}, u32[]{:S(2)}, u32[]{:S(2)}) collective-permute-start(bf16[4,48,768]{2,1,0:T(8,128)(2,1)S(1)} %get-tuple-element.121), channel_id=1, source_target_pairs={{0,33},{1,32},{2,35},{3,34},{4,37},{5,36},{6,39},{7,38},{8,41},{9,... | collective-permute-start | bytes 884744 | tf_op jit(solution)/shard_map/ppermute | solution.py:42
  57.5 0.0 collective-permute-start.14
  57.5 5.2 %fusion.24.grad_ref = f32[384,1536]{1,0:T(8,128)S(1)} fusion(bf16[384,2304]{1,0:T(8,128)(2,1)S(1)} %copy-done.1, bf16[1536,2304]{1,0:T(8,128)(2,1)} %weight_ref.1), kind=kOutput, calls=%fused_computation.63 | convolution fusion | flops 2717908992 | bytes 11206656 | tf_op jit(solution)/shard_map/dot_general | solution.py:26
  62.7 0.0 collective-permute-done.6
  62.8 0.1 add_convert_fusion.3
  62.8 0.1 add_convert_fusion.2
  63.0 0.4 collective-permute-start.10
  63.3 1.8 %collective-permute-start.11 = (bf16[48,1536]{1,0:T(8,128)(2,1)S(1)}, bf16[48,1536]{1,0:T(8,128)(2,1)S(1)}, u32[]{:S(2)}, u32[]{:S(2)}) collective-permute-start(bf16[48,1536]{1,0:T(8,128)(2,1)S(1)} %get-tuple-element.118), channel_id=1, source_target_pairs={{0,1},{1,0},{2,3},{3,2},{4,5},{5,4},{6,7},{7,6},{8,9},{9,8},{10,11... | collective-permute-start | bytes 442376 | tf_op jit(solution)/shard_map/ppermute | solution.py:42
  65.2 2.6 %collective-permute-start.12 = (bf16[48,1536]{1,0:T(8,128)(2,1)S(1)}, bf16[48,1536]{1,0:T(8,128)(2,1)S(1)}, u32[]{:S(2)}, u32[]{:S(2)}) collective-permute-start(bf16[48,1536]{1,0:T(8,128)(2,1)S(1)} %get-tuple-element.119), channel_id=1, source_target_pairs={{0,32},{1,33},{2,34},{3,35},{4,36},{5,37},{6,38},{7,39},{8,40},{9,... | collective-permute-start | bytes 442376 | tf_op jit(solution)/shard_map/ppermute | solution.py:42
  67.8 0.0 collective-permute-done.13
  67.8 0.1 add_convert_fusion.1
  67.8 0.1 add_convert_fusion
  68.0 0.4 collective-permute-start.15
  68.3 2.1 %collective-permute-start.16 = (bf16[48,1536]{1,0:T(8,128)(2,1)S(1)}, bf16[48,1536]{1,0:T(8,128)(2,1)S(1)}, u32[]{:S(2)}, u32[]{:S(2)}) collective-permute-start(bf16[48,1536]{1,0:T(8,128)(2,1)S(1)} %get-tuple-element.126), channel_id=1, source_target_pairs={{0,64},{1,65},{2,66},{3,67},{4,68},{5,69},{6,70},{7,71},{8,72},{9,... | collective-permute-start | bytes 442376 | tf_op jit(solution)/shard_map/ppermute | solution.py:42
  70.5 0.5 collective-permute-done.10
  71.0 1.2 %collective-permute-start.17 = (bf16[48,1536]{1,0:T(8,128)(2,1)S(1)}, bf16[48,1536]{1,0:T(8,128)(2,1)S(1)}, u32[]{:S(2)}, u32[]{:S(2)}) collective-permute-start(bf16[48,1536]{1,0:T(8,128)(2,1)S(1)} %get-tuple-element.127), channel_id=1, source_target_pairs={{0,128},{1,129},{2,130},{3,131},{4,132},{5,133},{6,134},{7,135},{8... | collective-permute-start | bytes 442376 | tf_op jit(solution)/shard_map/ppermute | solution.py:42
  72.2 0.5 collective-permute-done.12
  72.7 0.1 fusion.8.first_ref
  72.9 2.4 %collective-permute-start.25 = (bf16[128,1536]{1,0:T(8,128)(2,1)S(1)}, bf16[128,1536]{1,0:T(8,128)(2,1)S(1)}, u32[]{:S(2)}, u32[]{:S(2)}) collective-permute-start(bf16[128,1536]{1,0:T(8,128)(2,1)S(1)} %slice.123), channel_id=1, source_target_pairs={{0,15},{1,0},{2,1},{3,2},{4,3},{5,4},{6,5},{7,6},{8,7},{9,8},{10,9... | collective-permute-start | bytes 1179656 | tf_op jit(solution)/shard_map/ppermute | solution.py:31
  75.3 0.0 collective-permute-done.15
  75.3 2.4 %collective-permute-done.17 = bf16[48,1536]{1,0:T(8,128)(2,1)S(1)} collective-permute-done((bf16[48,1536]{1,0:T(8,128)(2,1)S(1)}, bf16[48,1536]{1,0:T(8,128)(2,1)S(1)}, u32[]{:S(2)}, u32[]{:S(2)}) %collective-permute-start.17) | collective-permute-done | bytes 147488 | tf_op jit(solution)/shard_map/ppermute | solution.py:42
  77.6 0.1 fusion.5.second_ref
  77.7 0.1 pieces.1
  77.8 4.6 %collective-permute-start.18 = (bf16[144,128]{1,0:T(8,128)(2,1)S(1)}, bf16[144,128]{1,0:T(8,128)(2,1)S(1)}, u32[]{:S(2)}, u32[]{:S(2)}) collective-permute-start(bf16[144,128]{1,0:T(8,128)(2,1)S(1)} %get-tuple-element.129), channel_id=1, source_target_pairs={{0,8},{1,9},{2,10},{3,11},{4,12},{5,13},{6,14},{7,15},{8,0},{9,1},... | collective-permute-start | bytes 110600 | tf_op jit(solution)/shard_map/ppermute | solution.py:42
  82.5 0.9 collective-permute-start.19
  83.4 4.1 %collective-permute-start.20 = (bf16[144,128]{1,0:T(8,128)(2,1)S(1)}, bf16[144,128]{1,0:T(8,128)(2,1)S(1)}, u32[]{:S(2)}, u32[]{:S(2)}) collective-permute-start(bf16[144,128]{1,0:T(8,128)(2,1)S(1)} %get-tuple-element.131), channel_id=1, source_target_pairs={{0,10},{1,11},{2,12},{3,13},{4,14},{5,15},{6,0},{7,1},{8,2},{9,3},... | collective-permute-start | bytes 110600 | tf_op jit(solution)/shard_map/ppermute | solution.py:42
  87.5 0.5 collective-permute-start.21
  88.0 3.6 %collective-permute-start.22 = (bf16[144,128]{1,0:T(8,128)(2,1)S(1)}, bf16[144,128]{1,0:T(8,128)(2,1)S(1)}, u32[]{:S(2)}, u32[]{:S(2)}) collective-permute-start(bf16[144,128]{1,0:T(8,128)(2,1)S(1)} %get-tuple-element.133), channel_id=1, source_target_pairs={{0,12},{1,13},{2,14},{3,15},{4,0},{5,1},{6,2},{7,3},{8,4},{9,5},{1... | collective-permute-start | bytes 110600 | tf_op jit(solution)/shard_map/ppermute | solution.py:42
  91.6 0.0 collective-permute-done.19.refs_2_
  91.6 0.1 collective-permute-start.23
  91.7 0.0 collective-permute-done.25.back_ref
  91.7 3.2 %collective-permute-start.24 = (bf16[144,128]{1,0:T(8,128)(2,1)S(1)}, bf16[144,128]{1,0:T(8,128)(2,1)S(1)}, u32[]{:S(2)}, u32[]{:S(2)}) collective-permute-start(bf16[144,128]{1,0:T(8,128)(2,1)S(1)} %get-tuple-element.135), channel_id=1, source_target_pairs={{0,14},{1,15},{2,0},{3,1},{4,2},{5,3},{6,4},{7,5},{8,6},{9,7},{10,... | collective-permute-start | bytes 110600 | tf_op jit(solution)/shard_map/ppermute | solution.py:42
  94.9 2.9 %finish.1 = bf16[256,1536]{1,0:T(8,128)(2,1)} custom-call(bf16[128,1536]{1,0:T(8,128)(2,1)S(1)} %collective-permute-done.25.back_ref, f32[384,1536]{1,0:T(8,128)} %copy-done, bf16[256,1536]{1,0:T(8,128)(2,1)} %bitcast.43, f32[2,256]{1,0:T(2,128)S(1)} %get-tuple-element.137.stats_ref), custom_call_target="tpu_custom_call" | custom-call | flops 1 | bytes 1 | tf_op jit(solution)/shard_map/finish/pallas_call | solution.py:469
  97.8 0.0 collective-permute-done.20.refs_3_
  97.9 0.7 total.1
  (21 shorter events, 0.2 us)
Async XLA Ops:
  1.7 16.0 %collective-permute-start = (bf16[128,1536]{1,0:T(8,128)(2,1)S(1)}, bf16[128,1536]{1,0:T(8,128)(2,1)S(1)}, u32[]{:S(2)}, u32[]{:S(2)}) collective-permute-start(bf16[128,1536]{1,0:T(8,128)(2,1)S(1)} %last_rows.1), channel_id=1, source_target_pairs={{0,1},{1,2},{2,3},{3,4},{4,5},{5,6},{6,7},{7,8},{8,9},{9,10},{10,1... | collective-permute-start | bytes 1179656 | tf_op jit(solution)/shard_map/ppermute | solution.py:31
  13.9 9.5 %collective-permute-start.2 = (bf16[768,512]{1,0:T(8,128)(2,1)S(1)}, bf16[768,512]{1,0:T(8,128)(2,1)S(1)}, u32[]{:S(2)}, u32[]{:S(2)}) collective-permute-start(bf16[768,512]{1,0:T(8,128)(2,1)S(1)} %get-tuple-element.85), channel_id=1, source_target_pairs={{0,16},{1,17},{2,18},{3,19},{4,20},{5,21},{6,22},{7,23},{8,24},{9,... | collective-permute-start | bytes 2359304 | tf_op jit(solution)/shard_map/ppermute | solution.py:42
  22.3 2.6 %collective-permute-start.1 = (bf16[2,256,768]{2,1,0:T(8,128)(2,1)S(1)}, bf16[2,256,768]{2,1,0:T(8,128)(2,1)S(1)}, u32[]{:S(2)}, u32[]{:S(2)}) collective-permute-start(bf16[2,256,768]{2,1,0:T(8,128)(2,1)S(1)} %get-tuple-element.84.right_ref), channel_id=1, source_target_pairs={{0,16},{1,17},{2,18},{3,19},{4,20},{5,21},{6,22},{7,23},{8,24},{9,... | collective-permute-start | bytes 2359304 | tf_op jit(solution)/shard_map/ppermute | solution.py:42
  24.9 7.9 %collective-permute-start.5 = (bf16[2,384,896]{2,1,0:T(8,128)(2,1)S(1)}, bf16[2,384,896]{2,1,0:T(8,128)(2,1)S(1)}, u32[]{:S(2)}, u32[]{:S(2)}) collective-permute-start(bf16[2,384,896]{2,1,0:T(8,128)(2,1)S(1)} %get-tuple-element.93.right_ref), channel_id=1, source_target_pairs={{0,16},{1,17},{2,18},{3,19},{4,20},{5,21},{6,22},{7,23},{8,24},{9,... | collective-permute-start | bytes 4128776 | tf_op jit(solution)/shard_map/ppermute | solution.py:42
  28.5 15.8 %collective-permute-start.3 = (bf16[8,48,768]{2,1,0:T(8,128)(2,1)}, bf16[8,48,768]{2,1,0:T(8,128)(2,1)S(1)}, u32[]{:S(2)}, u32[]{:S(2)}) collective-permute-start(bf16[8,48,768]{2,1,0:T(8,128)(2,1)} %get-tuple-element.91), channel_id=1, source_target_pairs={{0,64},{1,65},{2,66},{3,67},{4,68},{5,69},{6,70},{7,71},{8,72},{9,... | collective-permute-start | bytes 1769480 | tf_op jit(solution)/shard_map/ppermute | solution.py:42
  28.9 16.2 %collective-permute-start.4 = (bf16[8,48,768]{2,1,0:T(8,128)(2,1)}, bf16[8,48,768]{2,1,0:T(8,128)(2,1)S(1)}, u32[]{:S(2)}, u32[]{:S(2)}) collective-permute-start(bf16[8,48,768]{2,1,0:T(8,128)(2,1)} %get-tuple-element.92), channel_id=1, source_target_pairs={{0,192},{1,193},{2,194},{3,195},{4,196},{5,197},{6,198},{7,199},{8... | collective-permute-start | bytes 1769480 | tf_op jit(solution)/shard_map/ppermute | solution.py:42
  36.4 15.3 %collective-permute-start.8 = (bf16[8,48,768]{2,1,0:T(8,128)(2,1)}, bf16[8,48,768]{2,1,0:T(8,128)(2,1)}, u32[]{:S(2)}, u32[]{:S(2)}) collective-permute-start(bf16[8,48,768]{2,1,0:T(8,128)(2,1)} %get-tuple-element.109), channel_id=1, source_target_pairs={{0,1},{1,0},{2,3},{3,2},{4,5},{5,4},{6,7},{7,6},{8,9},{9,8},{10,11... | collective-permute-start | bytes 1769480 | tf_op jit(solution)/shard_map/ppermute | solution.py:42
  36.4 16.6 %collective-permute-start.9 = (bf16[8,48,768]{2,1,0:T(8,128)(2,1)}, bf16[8,48,768]{2,1,0:T(8,128)(2,1)}, u32[]{:S(2)}, u32[]{:S(2)}) collective-permute-start(bf16[8,48,768]{2,1,0:T(8,128)(2,1)} %get-tuple-element.110), channel_id=1, source_target_pairs={{0,33},{1,32},{2,35},{3,34},{4,37},{5,36},{6,39},{7,38},{8,41},{9,... | collective-permute-start | bytes 1769480 | tf_op jit(solution)/shard_map/ppermute | solution.py:42
  45.1 12.4 %copy-start.1 = (bf16[384,2304]{1,0:T(8,128)(2,1)S(1)}, bf16[384,2304]{1,0:T(8,128)(2,1)}, u32[]{:S(2)}) copy-start(bf16[384,2304]{1,0:T(8,128)(2,1)} %fusion.2) | copy-start | bytes 5308420
  45.4 17.4 %collective-permute-start.6 = (bf16[4,48,768]{2,1,0:T(8,128)(2,1)S(1)}, bf16[4,48,768]{2,1,0:T(8,128)(2,1)S(1)}, u32[]{:S(2)}, u32[]{:S(2)}) collective-permute-start(bf16[4,48,768]{2,1,0:T(8,128)(2,1)S(1)} %get-tuple-element.104), channel_id=1, source_target_pairs={{0,192},{1,193},{2,194},{3,195},{4,196},{5,197},{6,198},{7,199},{8... | collective-permute-start | bytes 884744 | tf_op jit(solution)/shard_map/ppermute | solution.py:42
  47.2 15.5 %collective-permute-start.7 = (bf16[4,48,768]{2,1,0:T(8,128)(2,1)S(1)}, bf16[4,48,768]{2,1,0:T(8,128)(2,1)S(1)}, u32[]{:S(2)}, u32[]{:S(2)}) collective-permute-start(bf16[4,48,768]{2,1,0:T(8,128)(2,1)S(1)} %get-tuple-element.105), channel_id=1, source_target_pairs={{0,64},{1,65},{2,66},{3,67},{4,68},{5,69},{6,70},{7,71},{8,72},{9,... | collective-permute-start | bytes 884744 | tf_op jit(solution)/shard_map/ppermute | solution.py:42
  54.5 13.3 %collective-permute-start.13 = (bf16[4,48,768]{2,1,0:T(8,128)(2,1)S(1)}, bf16[4,48,768]{2,1,0:T(8,128)(2,1)S(1)}, u32[]{:S(2)}, u32[]{:S(2)}) collective-permute-start(bf16[4,48,768]{2,1,0:T(8,128)(2,1)S(1)} %get-tuple-element.121), channel_id=1, source_target_pairs={{0,33},{1,32},{2,35},{3,34},{4,37},{5,36},{6,39},{7,38},{8,41},{9,... | collective-permute-start | bytes 884744 | tf_op jit(solution)/shard_map/ppermute | solution.py:42
  57.5 10.3 %collective-permute-start.14 = (bf16[4,48,768]{2,1,0:T(8,128)(2,1)S(1)}, bf16[4,48,768]{2,1,0:T(8,128)(2,1)S(1)}, u32[]{:S(2)}, u32[]{:S(2)}) collective-permute-start(bf16[4,48,768]{2,1,0:T(8,128)(2,1)S(1)} %get-tuple-element.123), channel_id=1, source_target_pairs={{0,1},{1,0},{2,3},{3,2},{4,5},{5,4},{6,7},{7,6},{8,9},{9,8},{10,11... | collective-permute-start | bytes 884744 | tf_op jit(solution)/shard_map/ppermute | solution.py:42
  62.7 10.1 %copy-start = (f32[384,1536]{1,0:T(8,128)}, f32[384,1536]{1,0:T(8,128)S(1)}, u32[]{:S(2)}) copy-start(f32[384,1536]{1,0:T(8,128)S(1)} %fusion.24.grad_ref) | copy-start | bytes 7077892
  63.0 8.0 %collective-permute-start.10 = (bf16[48,1536]{1,0:T(8,128)(2,1)S(1)}, bf16[48,1536]{1,0:T(8,128)(2,1)S(1)}, u32[]{:S(2)}, u32[]{:S(2)}) collective-permute-start(bf16[48,1536]{1,0:T(8,128)(2,1)S(1)} %get-tuple-element.117), channel_id=1, source_target_pairs={{0,33},{1,32},{2,35},{3,34},{4,37},{5,36},{6,39},{7,38},{8,41},{9,... | collective-permute-start | bytes 442376 | tf_op jit(solution)/shard_map/ppermute | solution.py:42
  63.3 8.9 %collective-permute-start.11 = (bf16[48,1536]{1,0:T(8,128)(2,1)S(1)}, bf16[48,1536]{1,0:T(8,128)(2,1)S(1)}, u32[]{:S(2)}, u32[]{:S(2)}) collective-permute-start(bf16[48,1536]{1,0:T(8,128)(2,1)S(1)} %get-tuple-element.118), channel_id=1, source_target_pairs={{0,1},{1,0},{2,3},{3,2},{4,5},{5,4},{6,7},{7,6},{8,9},{9,8},{10,11... | collective-permute-start | bytes 442376 | tf_op jit(solution)/shard_map/ppermute | solution.py:42
  65.2 7.6 %collective-permute-start.12 = (bf16[48,1536]{1,0:T(8,128)(2,1)S(1)}, bf16[48,1536]{1,0:T(8,128)(2,1)S(1)}, u32[]{:S(2)}, u32[]{:S(2)}) collective-permute-start(bf16[48,1536]{1,0:T(8,128)(2,1)S(1)} %get-tuple-element.119), channel_id=1, source_target_pairs={{0,32},{1,33},{2,34},{3,35},{4,36},{5,37},{6,38},{7,39},{8,40},{9,... | collective-permute-start | bytes 442376 | tf_op jit(solution)/shard_map/ppermute | solution.py:42
  68.0 7.3 %collective-permute-start.15 = (bf16[48,1536]{1,0:T(8,128)(2,1)S(1)}, bf16[48,1536]{1,0:T(8,128)(2,1)S(1)}, u32[]{:S(2)}, u32[]{:S(2)}) collective-permute-start(bf16[48,1536]{1,0:T(8,128)(2,1)S(1)} %get-tuple-element.125), channel_id=1, source_target_pairs={{0,192},{1,193},{2,194},{3,195},{4,196},{5,197},{6,198},{7,199},{8... | collective-permute-start | bytes 442376 | tf_op jit(solution)/shard_map/ppermute | solution.py:42
  68.3 6.9 %collective-permute-start.16 = (bf16[48,1536]{1,0:T(8,128)(2,1)S(1)}, bf16[48,1536]{1,0:T(8,128)(2,1)S(1)}, u32[]{:S(2)}, u32[]{:S(2)}) collective-permute-start(bf16[48,1536]{1,0:T(8,128)(2,1)S(1)} %get-tuple-element.126), channel_id=1, source_target_pairs={{0,64},{1,65},{2,66},{3,67},{4,68},{5,69},{6,70},{7,71},{8,72},{9,... | collective-permute-start | bytes 442376 | tf_op jit(solution)/shard_map/ppermute | solution.py:42
  71.0 6.6 %collective-permute-start.17 = (bf16[48,1536]{1,0:T(8,128)(2,1)S(1)}, bf16[48,1536]{1,0:T(8,128)(2,1)S(1)}, u32[]{:S(2)}, u32[]{:S(2)}) collective-permute-start(bf16[48,1536]{1,0:T(8,128)(2,1)S(1)} %get-tuple-element.127), channel_id=1, source_target_pairs={{0,128},{1,129},{2,130},{3,131},{4,132},{5,133},{6,134},{7,135},{8... | collective-permute-start | bytes 442376 | tf_op jit(solution)/shard_map/ppermute | solution.py:42
  72.9 18.8 %collective-permute-start.25 = (bf16[128,1536]{1,0:T(8,128)(2,1)S(1)}, bf16[128,1536]{1,0:T(8,128)(2,1)S(1)}, u32[]{:S(2)}, u32[]{:S(2)}) collective-permute-start(bf16[128,1536]{1,0:T(8,128)(2,1)S(1)} %slice.123), channel_id=1, source_target_pairs={{0,15},{1,0},{2,1},{3,2},{4,3},{5,4},{6,5},{7,6},{8,7},{9,8},{10,9... | collective-permute-start | bytes 1179656 | tf_op jit(solution)/shard_map/ppermute | solution.py:31
  77.8 10.2 %collective-permute-start.18 = (bf16[144,128]{1,0:T(8,128)(2,1)S(1)}, bf16[144,128]{1,0:T(8,128)(2,1)S(1)}, u32[]{:S(2)}, u32[]{:S(2)}) collective-permute-start(bf16[144,128]{1,0:T(8,128)(2,1)S(1)} %get-tuple-element.129), channel_id=1, source_target_pairs={{0,8},{1,9},{2,10},{3,11},{4,12},{5,13},{6,14},{7,15},{8,0},{9,1},... | collective-permute-start | bytes 110600 | tf_op jit(solution)/shard_map/ppermute | solution.py:42
  82.5 9.2 %collective-permute-start.19 = (bf16[144,128]{1,0:T(8,128)(2,1)S(1)}, bf16[144,128]{1,0:T(8,128)(2,1)S(1)}, u32[]{:S(2)}, u32[]{:S(2)}) collective-permute-start(bf16[144,128]{1,0:T(8,128)(2,1)S(1)} %get-tuple-element.130), channel_id=1, source_target_pairs={{0,6},{1,7},{2,8},{3,9},{4,10},{5,11},{6,12},{7,13},{8,14},{9,15},... | collective-permute-start | bytes 110600 | tf_op jit(solution)/shard_map/ppermute | solution.py:42
  83.4 14.4 %collective-permute-start.20 = (bf16[144,128]{1,0:T(8,128)(2,1)S(1)}, bf16[144,128]{1,0:T(8,128)(2,1)S(1)}, u32[]{:S(2)}, u32[]{:S(2)}) collective-permute-start(bf16[144,128]{1,0:T(8,128)(2,1)S(1)} %get-tuple-element.131), channel_id=1, source_target_pairs={{0,10},{1,11},{2,12},{3,13},{4,14},{5,15},{6,0},{7,1},{8,2},{9,3},... | collective-permute-start | bytes 110600 | tf_op jit(solution)/shard_map/ppermute | solution.py:42
  87.5 10.3 %collective-permute-start.21 = (bf16[144,128]{1,0:T(8,128)(2,1)S(1)}, bf16[144,128]{1,0:T(8,128)(2,1)S(1)}, u32[]{:S(2)}, u32[]{:S(2)}) collective-permute-start(bf16[144,128]{1,0:T(8,128)(2,1)S(1)} %get-tuple-element.132), channel_id=1, source_target_pairs={{0,4},{1,5},{2,6},{3,7},{4,8},{5,9},{6,10},{7,11},{8,12},{9,13},{1... | collective-permute-start | bytes 110600 | tf_op jit(solution)/shard_map/ppermute | solution.py:42
  88.0 9.8 %collective-permute-start.22 = (bf16[144,128]{1,0:T(8,128)(2,1)S(1)}, bf16[144,128]{1,0:T(8,128)(2,1)S(1)}, u32[]{:S(2)}, u32[]{:S(2)}) collective-permute-start(bf16[144,128]{1,0:T(8,128)(2,1)S(1)} %get-tuple-element.133), channel_id=1, source_target_pairs={{0,12},{1,13},{2,14},{3,15},{4,0},{5,1},{6,2},{7,3},{8,4},{9,5},{1... | collective-permute-start | bytes 110600 | tf_op jit(solution)/shard_map/ppermute | solution.py:42
  91.6 6.2 %collective-permute-start.23 = (bf16[144,128]{1,0:T(8,128)(2,1)S(1)}, bf16[144,128]{1,0:T(8,128)(2,1)S(1)}, u32[]{:S(2)}, u32[]{:S(2)}) collective-permute-start(bf16[144,128]{1,0:T(8,128)(2,1)S(1)} %get-tuple-element.134), channel_id=1, source_target_pairs={{0,2},{1,3},{2,4},{3,5},{4,6},{5,7},{6,8},{7,9},{8,10},{9,11},{10,... | collective-permute-start | bytes 110600 | tf_op jit(solution)/shard_map/ppermute | solution.py:42
  91.7 6.2 %collective-permute-start.24 = (bf16[144,128]{1,0:T(8,128)(2,1)S(1)}, bf16[144,128]{1,0:T(8,128)(2,1)S(1)}, u32[]{:S(2)}, u32[]{:S(2)}) collective-permute-start(bf16[144,128]{1,0:T(8,128)(2,1)S(1)} %get-tuple-element.135), channel_id=1, source_target_pairs={{0,14},{1,15},{2,0},{3,1},{4,2},{5,3},{6,4},{7,5},{8,6},{9,7},{10,... | collective-permute-start | bytes 110600 | tf_op jit(solution)/shard_map/ppermute | solution.py:42

commit v7 on v5

--- a/solution.py
+++ b/solution.py
@@ -70,15 +70,19 @@
     return y ^ 2, xh, core, z, xl
 
 
+def to_z_near(y, xh, core, z, xl):
+    return y, xh, core, z ^ 1, xl
+
+
 ROUTES = (
+    (to_y_near, to_y_mirror),
+    (to_y_mirror, to_y_near),
     (to_x_near, to_x_mirror),
     (to_x_mirror, to_x_near),
-    (to_y_near, to_y_mirror),
-    (to_y_mirror, to_y_near),
 )
 OWNERS = (
+    (to_x_mirror, to_x_near, to_x_far),
     (to_y_mirror, to_y_near, to_y_far),
-    (to_x_mirror, to_x_near, to_x_far),
 )
 
 
@@ -88,7 +92,7 @@
 
 def chunk_at(route, slot, y, xh, xl):
     bits = [(slot >> (3 - i)) & 1 for i in range(4)]
-    x_first = route < 2
+    x_first = route >= 2
     x_bits, y_bits = (bits[:2], bits[2:]) if x_first else (bits[2:], bits[:2])
     found = []
     for hi, lo, pair, order in ((y >> 1, y & 1, y_bits, 0 if x_first else route), (xh, xl, x_bits, route if x_first else 0)):
@@ -469,24 +473,41 @@
     return outs[:2], outs[2:]
 
 
-def pieces_kernel(*refs):
-    ins, out_ref, held = refs[:-2], refs[-2], refs[-1]
-    for ref, places in zip(ins, ((3, 0), (1, 2))):
+def pieces_kernel(place, first_ref, second_ref, keep_ref, send_ref, held):
+    for ref, places in ((first_ref, (3, 0)), (second_ref, (1, 2))):
         block = ref[...].astype(F32)
         tiles = block.shape[1] // PAIR // 2
         share = block.shape[0] // Z
-        for n, place in enumerate(places):
+        for n, at in enumerate(places):
             for t in range(tiles):
-                rows = slice((place * tiles + t) * share, (place * tiles + t + 1) * share)
+                rows = slice((at * tiles + t) * share, (at * tiles + t + 1) * share)
                 column = (n * tiles + t) * PAIR
                 for z in range(Z):
                     held[z, rows, :] = block[z * share : (z + 1) * share, column : column + PAIR]
-    out_ref[...] = held[...].astype(BF16)
+    parity = lax.rem(place[2], 2)
+    for step in range(Z // 2):
+        keep_ref[step] = held[2 * step + parity].astype(BF16)
+        send_ref[step] = held[2 * step + 1 - parity].astype(BF16)
+
+
+def pieces(place, groups):
+    rows, columns = groups[0].shape
+    size = (rows // Z * 2 * columns // PAIR, PAIR)
+    return pl.pallas_call(
+        pieces_kernel,
+        in_specs=[SMEM_SPEC] + [VMEM_SPEC] * 2,
+        out_specs=[VMEM_SPEC] * 2,
+        out_shape=[pltpu.VMEM((Z // 2, *size), BF16)] * 2,
+        scratch_shapes=[pltpu.VMEM((Z, *size), F32)],
+        compiler_params=params(16),
+        cost_estimate=cost(1, 1),
+        name="pieces",
+    )(place, *[in_vmem(g) for g in groups])
 
 
 def total_kernel(in_ref, out_ref):
     total = in_ref[0].astype(F32)
-    for z in range(1, Z):
+    for z in range(1, Z // 2):
         total += in_ref[z].astype(F32)
     share = out_ref.shape[0]
     for t in range(out_ref.shape[1] // PAIR):
@@ -502,7 +523,7 @@
     dp_index = lax.axis_index("dp")
     xl = seq_index % XL
     core, xh, y = dp_index % CORES, dp_index // CORES % XH, dp_index // (CORES * XH)
-    places = jnp.stack([seq_index * row_count, core])
+    places = jnp.stack([seq_index * row_count, core, seq_index // XL])
     chunks = jnp.stack([chunk_at(r, jnp.arange(CHUNKS), y, xh, xl) for r in range(len(ROUTES))])
 
     behind = from_behind(last_rows(frame_rows), "seq", 1)
@@ -547,18 +568,11 @@
     returned = jnp.concatenate([jnp.zeros((row_count - CONTEXT, width), BF16), returned], axis=0)
     normed_grad = (normed_grad[:row_count] + returned.astype(F32)).astype(BF16)
     frame_grad = normalize_grad(frame_rows.astype(F32), stats[0][:, None], stats[1][:, None], normed_grad.astype(F32))
+    kept, sent = pieces(places, groups)
+    shares = plus(kept, to_device(sent, to_z_near))
+    rings = [[place * XL + x for place in range(parity, Z, 2)] for parity in range(2) for x in range(XL)]
+    shares = lax.all_to_all(shares, "seq", 0, 0, axis_index_groups=rings, tiled=True)
     share = width // (CHUNKS * CORES * Z)
-    tiles = 4 * inner // PAIR
-    shares = pl.pallas_call(
-        pieces_kernel,
-        in_specs=[VMEM_SPEC] * 2,
-        out_shape=jax.ShapeDtypeStruct((Z, tiles * share, PAIR), BF16),
-        scratch_shapes=[pltpu.VMEM((Z, tiles * share, PAIR), F32)],
-        compiler_params=params(24),
-        name="pieces",
-    )(*[in_vmem(g) for g in groups])
-    rings = [[place * XL + x for place in range(Z)] for x in range(XL)]
-    shares = lax.all_to_all(shares, "seq", 0, 0, axis_index_groups=rings, tiled=True)
     total = pl.pallas_call(
         total_kernel,
         in_specs=[VMEM_SPEC],

time: 97.8 us -> 97.5 us (level)
  waiting for transfers between devices: 33.9 us -> 30.9 us
  starting transfers between devices: 29.4 us -> 31.3 us
    ppermute x17 -> x18, starting transfers between devices: 20.4 us -> 22.7 us  [to_device(): return lax.ppermute(value, ('dp', 'seq'), pairs)]
    all_to_all x1, waiting for transfers between devices: 7.9 us -> 5.94 us  [on_device(): lax.all_to_all(shares, 'seq', 0, 0, axis_index_groups=rings, tiled=True)]
    ppermute x17 -> x18, waiting for transfers between devices: 22.4 us -> 21.4 us  [to_device(): return lax.ppermute(value, ('dp', 'seq'), pairs)]
  transfers between devices with their start and end apart: 20 -> 21, of which waited for: 9 -> 11; matrix products, arithmetic and copies ran while one was open for 9% -> 10% of each run, Pallas kernels for 22% -> 22%
where the time goes in v7:
time: 97.5 us; the launch traced here: 96.4 us
  starting transfers between devices  31.3 us (32%)
  waiting for transfers between devices  30.9 us (32%)
  Pallas kernels  22.7 us (23%)
  matrix products  4.58 us (5%)
  other arithmetic  4.34 us (4%)
  between operations  1.59 us (2%)
    ppermute x18, starting transfers between devices, to_device(): return lax.ppermute(value, ('dp', 'seq'), pairs)  22.7 us
    ppermute x18, waiting for transfers between devices, to_device(): return lax.ppermute(value, ('dp', 'seq'), pairs)  21.4 us
    pallas_call x1, Pallas kernels, front(): pl.pallas_call(front_kernel, in_specs=[SMEM_SPEC] + [HBM_SPEC] * 6, out_s...  9.88 us
    all_to_all x1, waiting for transfers between devices, on_device(): lax.all_to_all(shares, 'seq', 0, 0, axis_index_groups=rings, tiled=True)  5.94 us
    all_to_all x1, starting transfers between devices, on_device(): lax.all_to_all(shares, 'seq', 0, 0, axis_index_groups=rings, tiled=True)  5.81 us
    pallas_call x1, Pallas kernels, early_tile(): pl.pallas_call(early_kernel, in_specs=[SMEM_SPEC, HBM_SPEC] + [VMEM_SPEC]...  4.69 us
    dot_general x2, matrix products, dot(): return lax.dot_general(a, b, dims, preferred_element_type=F32)  4.58 us
    pallas_call x2, Pallas kernels, weight_sections(): pl.pallas_call(kernel, in_specs=[SMEM_SPEC] + [VMEM_SPEC] * len(operands)...  4.44 us
  transfers between devices with their start and end apart: 21, of which 11 were waited for; matrix products, arithmetic and copies ran while one was open for 10% of the time, Pallas kernels for 22%

profile of v7, /device:TPU:8, one launch (start us, length us, event | category | flops | bytes accessed | tf_op | source)
XLA Modules:
  0.0 96.4 jit_solution(2829030585264607542)
XLA Ops:
  0.6 1.0 %last_rows.1 = bf16[128,1536]{1,0:T(8,128)(2,1)S(1)} custom-call(bf16[256,1536]{1,0:T(8,128)(2,1)} %bitcast.44), custom_call_target="tpu_custom_call" | custom-call | flops 1 | bytes 1 | tf_op jit(solution)/shard_map/last_rows/pallas_call | solution.py:174
  1.7 1.6 %collective-permute-start = (bf16[128,1536]{1,0:T(8,128)(2,1)S(1)}, bf16[128,1536]{1,0:T(8,128)(2,1)S(1)}, u32[]{:S(2)}, u32[]{:S(2)}) collective-permute-start(bf16[128,1536]{1,0:T(8,128)(2,1)S(1)} %last_rows.1), channel_id=1, source_target_pairs={{0,1},{1,2},{2,3},{3,4},{4,5},{5,6},{6,7},{7,8},{8,9},{9,10},{10,1... | collective-permute-start | bytes 1179656 | tf_op jit(solution)/shard_map/ppermute | solution.py:31
  3.3 0.1 pad_add_fusion.1.places.place
  4.1 9.9 %front.1 = (bf16[256,2304]{1,0:T(8,128)(2,1)S(1)}, bf16[256,768]{1,0:T(8,128)(2,1)S(1)}, bf16[768,512]{1,0:T(8,128)(2,1)S(1)}, bf16[768,512]{1,0:T(8,128)(2,1)S(...) custom-call(s32[3]{0:T(128)S(1)} %pad_add_fusion.1.places.place, ...), custom_call_target="tpu_custom_call" | custom-call | flops 3623878656 | bytes 11796480 | tf_op jit(solution)/shard_map/front/pallas_call | solution.py:255
  13.9 0.1 collective-permute-start.2
  14.0 3.6 %collective-permute-done.frames_ref = bf16[128,1536]{1,0:T(8,128)(2,1)S(1)} collective-permute-done((bf16[128,1536]{1,0:T(8,128)(2,1)S(1)}, bf16[128,1536]{1,0:T(8,128)(2,1)S(1)}, u32[]{:S(2)}, u32[]{:S(2)}) %collective-permute-start) | collective-permute-done | bytes 393248 | tf_op jit(solution)/shard_map/ppermute | solution.py:31
  17.6 4.7 %attention_early.1 = (bf16[2,256,768]{2,1,0:T(8,128)(2,1)S(1)}, bf16[2,384,896]{2,1,0:T(8,128)(2,1)S(1)}, bf16[768,128]{1,0:T(8,128)(2,1)S(1)}) custom-call(s32[3]{0:T(128)S(1)} %pad_add_fusion.1.places.place, s32[1]{0:T(128)S(6)} %copy.9.lengths_ref, bf16[384,384]{1,0:T(8,128)(2,1)S(1)} %get-tuple-element.63.order_ref, ...), custom_call_target="tpu_custom_call" | custom-call | flops 704643072 | bytes 1572864 | tf_op jit(solution)/shard_map/attention_early/pallas_call | solution.py:371
  22.3 0.3 collective-permute-start.1
  22.6 0.8 first_own.1.own_ref
  23.4 1.5 %collective-permute-done.1.right_other_ref = bf16[2,256,768]{2,1,0:T(8,128)(2,1)S(1)} collective-permute-done((bf16[2,256,768]{2,1,0:T(8,128)(2,1)S(1)}, bf16[2,256,768]{2,1,0:T(8,128)(2,1)S(1)}, u32[]{:S(2)}, u32[]{:S(2)}) %collective-permute-start.1) | collective-permute-done | bytes 786464 | tf_op jit(solution)/shard_map/ppermute | solution.py:42
  24.9 0.1 collective-permute-start.5
  25.0 0.1 slice_bitcast_fusion.2
  25.1 1.6 %first_wave.1 = (bf16[8,48,768]{2,1,0:T(8,128)(2,1)S(1)}, bf16[8,48,768]{2,1,0:T(8,128)(2,1)S(1)}, bf16[8,48,768]{2,1,0:T(8,128)(2,1)S(1)}, bf16[8,48,768]{2,1,0:T(8,128)(2,1)S(1)}) custom-call(s32[4,16]{1,0:T(4,128)S(1)} %pad_add_fusion.chunks, bf16[768,512]{1,0:T(8,128)(2,1)S(1)} %collective-permute-done.2.left_other_ref, ...), custom_call_target="tpu_custom_call" | custom-call | flops 1 | bytes 1 | tf_op jit(solution)/shard_map/first_wave/pallas_call | solution.py:437
  26.7 0.5 collective-permute-start.3
  27.3 2.4 %collective-permute-start.4 = (bf16[8,48,768]{2,1,0:T(8,128)(2,1)S(1)}, bf16[8,48,768]{2,1,0:T(8,128)(2,1)S(1)}, u32[]{:S(2)}, u32[]{:S(2)}) collective-permute-start(bf16[8,48,768]{2,1,0:T(8,128)(2,1)S(1)} %get-tuple-element.77), channel_id=1, source_target_pairs={{0,192},{1,193},{2,194},{3,195},{4,196},{5,197},{6,198},{7,199},{8... | collective-permute-start | bytes 1769480 | tf_op jit(solution)/shard_map/ppermute | solution.py:42
  29.7 0.1 slice_bitcast_fusion.1
  29.8 0.0 slice-start
  29.8 0.1 fusion.2
  29.9 0.0 collective-permute-done.5.right_other_ref
  29.9 0.0 copy-start.1
  29.9 0.0 slice-start.1
  30.0 2.8 %second_wave.1 = (bf16[8,48,768]{2,1,0:T(8,128)(2,1)S(1)}, bf16[8,48,768]{2,1,0:T(8,128)(2,1)S(1)}, bf16[8,48,768]{2,1,0:T(8,128)(2,1)S(1)}, bf16[8,48,768]{2,1,0:T(8,128)(2,1)S(1)}) custom-call(s32[4,16]{1,0:T(4,128)S(1)} %pad_add_fusion.chunks, bf16[768,512]{1,0:T(8,128)(2,1)S(1)} %get-tuple-element.71.left_ref, ...), custom_call_target="tpu_custom_call" | custom-call | flops 3000000000 | bytes 1 | tf_op jit(solution)/shard_map/second_wave/pallas_call | solution.py:437
  32.8 0.1 collective-permute-start.6
  32.9 3.3 %collective-permute-start.7 = (bf16[8,48,768]{2,1,0:T(8,128)(2,1)S(1)}, bf16[8,48,768]{2,1,0:T(8,128)(2,1)S(1)}, u32[]{:S(2)}, u32[]{:S(2)}) collective-permute-start(bf16[8,48,768]{2,1,0:T(8,128)(2,1)S(1)} %get-tuple-element.88), channel_id=1, source_target_pairs={{0,33},{1,32},{2,35},{3,34},{4,37},{5,36},{6,39},{7,38},{8,41},{9,... | collective-permute-start | bytes 1769480 | tf_op jit(solution)/shard_map/ppermute | solution.py:42
  36.1 1.7 %convolution_convert_fusion = bf16[256,1536]{1,0:T(8,128)(2,1)} fusion(bf16[256,768]{1,0:T(8,128)(2,1)S(1)} %get-tuple-element.82, bf16[768,1536]{1,0:T(8,128)(2,1)S(1)} %copy-done.1), kind=kOutput, calls=%fused_computation.2 | convolution fusion | flops 604372992 | bytes 3538944 | tf_op jit(solution)/shard_map/dot_general | solution.py:26
  37.8 4.6 %collective-permute-done.3.refs_2_ = bf16[8,48,768]{2,1,0:T(8,128)(2,1)S(1)} collective-permute-done((bf16[8,48,768]{2,1,0:T(8,128)(2,1)S(1)}, bf16[8,48,768]{2,1,0:T(8,128)(2,1)S(1)}, u32[]{:S(2)}, u32[]{:S(2)}) %collective-permute-start.3) | collective-permute-done | bytes 589856 | tf_op jit(solution)/shard_map/ppermute | solution.py:42
  42.4 0.8 collective-permute-done.4.refs_3_
  43.3 0.3 halve.3
  43.6 1.8 %collective-permute-start.10 = (bf16[4,48,768]{2,1,0:T(8,128)(2,1)S(1)}, bf16[4,48,768]{2,1,0:T(8,128)(2,1)S(1)}, u32[]{:S(2)}, u32[]{:S(2)}) collective-permute-start(bf16[4,48,768]{2,1,0:T(8,128)(2,1)S(1)} %get-tuple-element.100), channel_id=1, source_target_pairs={{0,192},{1,193},{2,194},{3,195},{4,196},{5,197},{6,198},{7,199},{8... | collective-permute-start | bytes 884744 | tf_op jit(solution)/shard_map/ppermute | solution.py:42
  45.4 2.6 %collective-permute-start.11 = (bf16[4,48,768]{2,1,0:T(8,128)(2,1)S(1)}, bf16[4,48,768]{2,1,0:T(8,128)(2,1)S(1)}, u32[]{:S(2)}, u32[]{:S(2)}) collective-permute-start(bf16[4,48,768]{2,1,0:T(8,128)(2,1)S(1)} %get-tuple-element.101), channel_id=1, source_target_pairs={{0,64},{1,65},{2,66},{3,67},{4,68},{5,69},{6,70},{7,71},{8,72},{9,... | collective-permute-start | bytes 884744 | tf_op jit(solution)/shard_map/ppermute | solution.py:42
  47.9 0.0 collective-permute-done.6.refs_2_
  47.9 1.3 %collective-permute-done.7.refs_3_ = bf16[8,48,768]{2,1,0:T(8,128)(2,1)S(1)} collective-permute-done((bf16[8,48,768]{2,1,0:T(8,128)(2,1)S(1)}, bf16[8,48,768]{2,1,0:T(8,128)(2,1)S(1)}, u32[]{:S(2)}, u32[]{:S(2)}) %collective-permute-start.7) | collective-permute-done | bytes 589856 | tf_op jit(solution)/shard_map/ppermute | solution.py:42
  49.2 0.3 halve.2
  49.5 3.0 %collective-permute-start.8 = (bf16[4,48,768]{2,1,0:T(8,128)(2,1)S(1)}, bf16[4,48,768]{2,1,0:T(8,128)(2,1)S(1)}, u32[]{:S(2)}, u32[]{:S(2)}) collective-permute-start(bf16[4,48,768]{2,1,0:T(8,128)(2,1)S(1)} %get-tuple-element.93), channel_id=1, source_target_pairs={{0,33},{1,32},{2,35},{3,34},{4,37},{5,36},{6,39},{7,38},{8,41},{9,... | collective-permute-start | bytes 884744 | tf_op jit(solution)/shard_map/ppermute | solution.py:42
  52.5 0.0 collective-permute-start.9
  52.5 2.9 %fusion.30 = f32[384,1536]{1,0:T(8,128)S(1)} fusion(bf16[384,2304]{1,0:T(8,128)(2,1)S(1)} %fusion.2, bf16[1536,2304]{1,0:T(8,128)(2,1)S(1)} %bitcast.53), kind=kOutput, calls=%fused_computation.77 | convolution fusion | flops 2717908992 | bytes 11206656 | tf_op jit(solution)/shard_map/dot_general | solution.py:26
  55.4 0.1 add_convert_fusion.1
  55.5 0.1 add_convert_fusion.2
  55.6 0.4 collective-permute-start.13
  56.0 2.0 %collective-permute-start.14 = (bf16[48,1536]{1,0:T(8,128)(2,1)S(1)}, bf16[48,1536]{1,0:T(8,128)(2,1)S(1)}, u32[]{:S(2)}, u32[]{:S(2)}) collective-permute-start(bf16[48,1536]{1,0:T(8,128)(2,1)S(1)} %get-tuple-element.110), channel_id=1, source_target_pairs={{0,1},{1,0},{2,3},{3,2},{4,5},{5,4},{6,7},{7,6},{8,9},{9,8},{10,11... | collective-permute-start | bytes 442376 | tf_op jit(solution)/shard_map/ppermute | solution.py:42
  58.1 2.4 %collective-permute-start.15 = (bf16[48,1536]{1,0:T(8,128)(2,1)S(1)}, bf16[48,1536]{1,0:T(8,128)(2,1)S(1)}, u32[]{:S(2)}, u32[]{:S(2)}) collective-permute-start(bf16[48,1536]{1,0:T(8,128)(2,1)S(1)} %get-tuple-element.111), channel_id=1, source_target_pairs={{0,32},{1,33},{2,34},{3,35},{4,36},{5,37},{6,38},{7,39},{8,40},{9,... | collective-permute-start | bytes 442376 | tf_op jit(solution)/shard_map/ppermute | solution.py:42
  60.4 0.1 add_convert_fusion.4
  60.5 1.9 %collective-permute-done.9 = bf16[4,48,768]{2,1,0:T(8,128)(2,1)S(1)} collective-permute-done((bf16[4,48,768]{2,1,0:T(8,128)(2,1)S(1)}, bf16[4,48,768]{2,1,0:T(8,128)(2,1)S(1)}, u32[]{:S(2)}, u32[]{:S(2)}) %collective-permute-start.9) | collective-permute-done | bytes 294944 | tf_op jit(solution)/shard_map/ppermute | solution.py:42
  62.4 0.1 add_convert_fusion.3
  62.5 0.4 collective-permute-start.16
  62.9 2.1 %collective-permute-start.17 = (bf16[48,1536]{1,0:T(8,128)(2,1)S(1)}, bf16[48,1536]{1,0:T(8,128)(2,1)S(1)}, u32[]{:S(2)}, u32[]{:S(2)}) collective-permute-start(bf16[48,1536]{1,0:T(8,128)(2,1)S(1)} %get-tuple-element.113), channel_id=1, source_target_pairs={{0,64},{1,65},{2,66},{3,67},{4,68},{5,69},{6,70},{7,71},{8,72},{9,... | collective-permute-start | bytes 442376 | tf_op jit(solution)/shard_map/ppermute | solution.py:42
  65.0 1.1 %collective-permute-start.18 = (bf16[48,1536]{1,0:T(8,128)(2,1)S(1)}, bf16[48,1536]{1,0:T(8,128)(2,1)S(1)}, u32[]{:S(2)}, u32[]{:S(2)}) collective-permute-start(bf16[48,1536]{1,0:T(8,128)(2,1)S(1)} %get-tuple-element.114), channel_id=1, source_target_pairs={{0,128},{1,129},{2,130},{3,131},{4,132},{5,133},{6,134},{7,135},{8... | collective-permute-start | bytes 442376 | tf_op jit(solution)/shard_map/ppermute | solution.py:42
  66.1 0.1 fusion.13.first_ref
  66.2 0.0 copy-start
  66.2 0.8 slice.134
  67.0 0.8 collective-permute-done.16
  67.8 0.4 collective-permute-done.17
  68.1 3.5 %collective-permute-done.18 = bf16[48,1536]{1,0:T(8,128)(2,1)S(1)} collective-permute-done((bf16[48,1536]{1,0:T(8,128)(2,1)S(1)}, bf16[48,1536]{1,0:T(8,128)(2,1)S(1)}, u32[]{:S(2)}, u32[]{:S(2)}) %collective-permute-start.18) | collective-permute-done | bytes 147488 | tf_op jit(solution)/shard_map/ppermute | solution.py:42
  71.7 0.1 fusion.10.second_ref
  71.7 1.3 %collective-permute-start.12 = (bf16[128,1536]{1,0:T(8,128)(2,1)}, bf16[128,1536]{1,0:T(8,128)(2,1)}, u32[]{:S(2)}, u32[]{:S(2)}) collective-permute-start(bf16[128,1536]{1,0:T(8,128)(2,1)} %slice.134), channel_id=1, source_target_pairs={{0,15},{1,0},{2,1},{3,2},{4,3},{5,4},{6,5},{7,6},{8,7},{9,8},{10,9... | collective-permute-start | bytes 1179656 | tf_op jit(solution)/shard_map/ppermute | solution.py:31
  73.0 0.6 pieces.1
  73.7 0.1 collective-permute-start.19
  73.8 6.6 %collective-permute-done.19 = bf16[4,144,128]{2,1,0:T(8,128)(2,1)S(1)} collective-permute-done((bf16[4,144,128]{2,1,0:T(8,128)(2,1)S(1)}, bf16[4,144,128]{2,1,0:T(8,128)(2,1)S(1)}, u32[]{:S(2)}, u32[]{:S(2)}) %collective-permute-start.19) | collective-permute-done | bytes 147488 | tf_op jit(solution)/shard_map/ppermute | solution.py:42
  80.4 0.7 add_convert_fusion.5
  81.1 5.8 %all-to-all-start = ((bf16[4,144,128]{2,1,0:T(8,128)(2,1)}), bf16[4,144,128]{2,1,0:T(8,128)(2,1)S(1)}, u32[]{:S(2)}, u32[]{:S(2)}) async-start(bf16[4,144,128]{2,1,0:T(8,128)(2,1)} %add_convert_fusion.5), calls=%async_computation | async-start | bytes 294912 | tf_op jit(solution)/shard_map/all_to_all | solution.py:574
  86.9 1.5 %convert_reduce_fusion = (f32[256]{0:T(256)S(1)}, f32[256]{0:T(256)S(1)}, bf16[256,1536]{1,0:T(8,128)(2,1)S(1)}) fusion(f32[256]{0:T(256)S(1)} %bitcast.50, f32[256]{0:T(256)S(1)} %bitcast.48, bf16[256,1536]{1,0:T(8,128)(2,1)S(1)} %bitcast.46, bf16[128,1536]{1,0:T(8,128)(2,1)} %collective-permute-done.12, f32[384,1536]{1,0:T(8,128)S(1)} %fusion.30), kind=kLoop, calls=%fused_computation.5 | loop fusion | flops 3931648 | bytes 3543040 | tf_op jit(solution)/shard_map/reduce_sum | solution.py:122
  88.4 1.4 %fusion.7 = bf16[1,256,1536]{2,1,0:T(8,128)(2,1)} fusion(bf16[256,1536]{1,0:T(8,128)(2,1)S(1)} %bitcast.47, bf16[256,1536]{1,0:T(8,128)(2,1)S(1)} %get-tuple-element.119, f32[256]{0:T(256)S(1)} %broadcast_multiply_fusion, f32[256]{0:T(256)S(1)} %bitcast.49, f32[256]{0:T(256)S(1)} %broadcast_multiply_fusion.1, f32[256]{0:T(256)S(1)} %bitcast.51), kind=kLoop, calls=%fused_computation.14 | loop fusion | flops 3538944 | bytes 2363392 | tf_op jit(solution)/shard_map/broadcast_in_dim | solution.py:583
  89.8 5.9 %all-to-all-done.in_ref = bf16[4,144,128]{2,1,0:T(8,128)(2,1)S(1)} async-done(((bf16[4,144,128]{2,1,0:T(8,128)(2,1)}), bf16[4,144,128]{2,1,0:T(8,128)(2,1)S(1)}, u32[]{:S(2)}, u32[]{:S(2)}) %all-to-all-start) | async-done | bytes 147488 | tf_op jit(solution)/shard_map/all_to_all | solution.py:574
  95.7 0.7 total.1
  (21 shorter events, 0.1 us)
Async XLA Ops:
  1.7 16.0 %collective-permute-start = (bf16[128,1536]{1,0:T(8,128)(2,1)S(1)}, bf16[128,1536]{1,0:T(8,128)(2,1)S(1)}, u32[]{:S(2)}, u32[]{:S(2)}) collective-permute-start(bf16[128,1536]{1,0:T(8,128)(2,1)S(1)} %last_rows.1), channel_id=1, source_target_pairs={{0,1},{1,2},{2,3},{3,4},{4,5},{5,6},{6,7},{7,8},{8,9},{9,10},{10,1... | collective-permute-start | bytes 1179656 | tf_op jit(solution)/shard_map/ppermute | solution.py:31
  13.9 9.5 %collective-permute-start.2 = (bf16[768,512]{1,0:T(8,128)(2,1)S(1)}, bf16[768,512]{1,0:T(8,128)(2,1)S(1)}, u32[]{:S(2)}, u32[]{:S(2)}) collective-permute-start(bf16[768,512]{1,0:T(8,128)(2,1)S(1)} %get-tuple-element.70), channel_id=1, source_target_pairs={{0,16},{1,17},{2,18},{3,19},{4,20},{5,21},{6,22},{7,23},{8,24},{9,... | collective-permute-start | bytes 2359304 | tf_op jit(solution)/shard_map/ppermute | solution.py:42
  22.3 2.6 %collective-permute-start.1 = (bf16[2,256,768]{2,1,0:T(8,128)(2,1)S(1)}, bf16[2,256,768]{2,1,0:T(8,128)(2,1)S(1)}, u32[]{:S(2)}, u32[]{:S(2)}) collective-permute-start(bf16[2,256,768]{2,1,0:T(8,128)(2,1)S(1)} %get-tuple-element.69.right_ref), channel_id=1, source_target_pairs={{0,16},{1,17},{2,18},{3,19},{4,20},{5,21},{6,22},{7,23},{8,24},{9,... | collective-permute-start | bytes 2359304 | tf_op jit(solution)/shard_map/ppermute | solution.py:42
  24.9 5.0 %collective-permute-start.5 = (bf16[2,384,896]{2,1,0:T(8,128)(2,1)S(1)}, bf16[2,384,896]{2,1,0:T(8,128)(2,1)S(1)}, u32[]{:S(2)}, u32[]{:S(2)}) collective-permute-start(bf16[2,384,896]{2,1,0:T(8,128)(2,1)S(1)} %get-tuple-element.78.right_ref), channel_id=1, source_target_pairs={{0,16},{1,17},{2,18},{3,19},{4,20},{5,21},{6,22},{7,23},{8,24},{9,... | collective-permute-start | bytes 4128776 | tf_op jit(solution)/shard_map/ppermute | solution.py:42
  26.7 15.7 %collective-permute-start.3 = (bf16[8,48,768]{2,1,0:T(8,128)(2,1)S(1)}, bf16[8,48,768]{2,1,0:T(8,128)(2,1)S(1)}, u32[]{:S(2)}, u32[]{:S(2)}) collective-permute-start(bf16[8,48,768]{2,1,0:T(8,128)(2,1)S(1)} %get-tuple-element.76), channel_id=1, source_target_pairs={{0,64},{1,65},{2,66},{3,67},{4,68},{5,69},{6,70},{7,71},{8,72},{9,... | collective-permute-start | bytes 1769480 | tf_op jit(solution)/shard_map/ppermute | solution.py:42
  27.3 16.0 %collective-permute-start.4 = (bf16[8,48,768]{2,1,0:T(8,128)(2,1)S(1)}, bf16[8,48,768]{2,1,0:T(8,128)(2,1)S(1)}, u32[]{:S(2)}, u32[]{:S(2)}) collective-permute-start(bf16[8,48,768]{2,1,0:T(8,128)(2,1)S(1)} %get-tuple-element.77), channel_id=1, source_target_pairs={{0,192},{1,193},{2,194},{3,195},{4,196},{5,197},{6,198},{7,199},{8... | collective-permute-start | bytes 1769480 | tf_op jit(solution)/shard_map/ppermute | solution.py:42
  29.8 22.7 %slice-start = ((s8[7077888]{0:T(1024)(128)(4,1)}), s8[4194304]{0:T(1024)(128)(4,1)S(1)}, s32[]{:S(2)}) async-start(s8[7077888]{0:T(1024)(128)(4,1)} %bitcast.52), calls=%async_computation.1 | async-start | bytes 8388608
  29.9 6.2 %copy-start.1 = (bf16[768,1536]{1,0:T(8,128)(2,1)S(1)}, bf16[768,1536]{1,0:T(8,128)(2,1)}, u32[]{:S(2)}) copy-start(bf16[768,1536]{1,0:T(8,128)(2,1)} %out_ref.1) | copy-start | bytes 7077892
  29.9 22.5 %slice-start.1 = ((s8[7077888]{0:T(1024)(128)(4,1)}), s8[2883584]{0:T(1024)(128)(4,1)S(1)}, s32[]{:S(2)}) async-start(s8[7077888]{0:T(1024)(128)(4,1)} %bitcast.52), calls=%async_computation.2 | async-start | bytes 5767168
  32.8 15.2 %collective-permute-start.6 = (bf16[8,48,768]{2,1,0:T(8,128)(2,1)S(1)}, bf16[8,48,768]{2,1,0:T(8,128)(2,1)S(1)}, u32[]{:S(2)}, u32[]{:S(2)}) collective-permute-start(bf16[8,48,768]{2,1,0:T(8,128)(2,1)S(1)} %get-tuple-element.87), channel_id=1, source_target_pairs={{0,1},{1,0},{2,3},{3,2},{4,5},{5,4},{6,7},{7,6},{8,9},{9,8},{10,11... | collective-permute-start | bytes 1769480 | tf_op jit(solution)/shard_map/ppermute | solution.py:42
  32.9 16.3 %collective-permute-start.7 = (bf16[8,48,768]{2,1,0:T(8,128)(2,1)S(1)}, bf16[8,48,768]{2,1,0:T(8,128)(2,1)S(1)}, u32[]{:S(2)}, u32[]{:S(2)}) collective-permute-start(bf16[8,48,768]{2,1,0:T(8,128)(2,1)S(1)} %get-tuple-element.88), channel_id=1, source_target_pairs={{0,33},{1,32},{2,35},{3,34},{4,37},{5,36},{6,39},{7,38},{8,41},{9,... | collective-permute-start | bytes 1769480 | tf_op jit(solution)/shard_map/ppermute | solution.py:42
  43.6 11.9 %collective-permute-start.10 = (bf16[4,48,768]{2,1,0:T(8,128)(2,1)S(1)}, bf16[4,48,768]{2,1,0:T(8,128)(2,1)S(1)}, u32[]{:S(2)}, u32[]{:S(2)}) collective-permute-start(bf16[4,48,768]{2,1,0:T(8,128)(2,1)S(1)} %get-tuple-element.100), channel_id=1, source_target_pairs={{0,192},{1,193},{2,194},{3,195},{4,196},{5,197},{6,198},{7,199},{8... | collective-permute-start | bytes 884744 | tf_op jit(solution)/shard_map/ppermute | solution.py:42
  45.4 10.1 %collective-permute-start.11 = (bf16[4,48,768]{2,1,0:T(8,128)(2,1)S(1)}, bf16[4,48,768]{2,1,0:T(8,128)(2,1)S(1)}, u32[]{:S(2)}, u32[]{:S(2)}) collective-permute-start(bf16[4,48,768]{2,1,0:T(8,128)(2,1)S(1)} %get-tuple-element.101), channel_id=1, source_target_pairs={{0,64},{1,65},{2,66},{3,67},{4,68},{5,69},{6,70},{7,71},{8,72},{9,... | collective-permute-start | bytes 884744 | tf_op jit(solution)/shard_map/ppermute | solution.py:42
  49.5 11.0 %collective-permute-start.8 = (bf16[4,48,768]{2,1,0:T(8,128)(2,1)S(1)}, bf16[4,48,768]{2,1,0:T(8,128)(2,1)S(1)}, u32[]{:S(2)}, u32[]{:S(2)}) collective-permute-start(bf16[4,48,768]{2,1,0:T(8,128)(2,1)S(1)} %get-tuple-element.93), channel_id=1, source_target_pairs={{0,33},{1,32},{2,35},{3,34},{4,37},{5,36},{6,39},{7,38},{8,41},{9,... | collective-permute-start | bytes 884744 | tf_op jit(solution)/shard_map/ppermute | solution.py:42
  52.5 9.9 %collective-permute-start.9 = (bf16[4,48,768]{2,1,0:T(8,128)(2,1)S(1)}, bf16[4,48,768]{2,1,0:T(8,128)(2,1)S(1)}, u32[]{:S(2)}, u32[]{:S(2)}) collective-permute-start(bf16[4,48,768]{2,1,0:T(8,128)(2,1)S(1)} %get-tuple-element.95), channel_id=1, source_target_pairs={{0,1},{1,0},{2,3},{3,2},{4,5},{5,4},{6,7},{7,6},{8,9},{9,8},{10,11... | collective-permute-start | bytes 884744 | tf_op jit(solution)/shard_map/ppermute | solution.py:42
  55.6 9.4 %collective-permute-start.13 = (bf16[48,1536]{1,0:T(8,128)(2,1)S(1)}, bf16[48,1536]{1,0:T(8,128)(2,1)S(1)}, u32[]{:S(2)}, u32[]{:S(2)}) collective-permute-start(bf16[48,1536]{1,0:T(8,128)(2,1)S(1)} %get-tuple-element.109), channel_id=1, source_target_pairs={{0,33},{1,32},{2,35},{3,34},{4,37},{5,36},{6,39},{7,38},{8,41},{9,... | collective-permute-start | bytes 442376 | tf_op jit(solution)/shard_map/ppermute | solution.py:42
  56.0 10.1 %collective-permute-start.14 = (bf16[48,1536]{1,0:T(8,128)(2,1)S(1)}, bf16[48,1536]{1,0:T(8,128)(2,1)S(1)}, u32[]{:S(2)}, u32[]{:S(2)}) collective-permute-start(bf16[48,1536]{1,0:T(8,128)(2,1)S(1)} %get-tuple-element.110), channel_id=1, source_target_pairs={{0,1},{1,0},{2,3},{3,2},{4,5},{5,4},{6,7},{7,6},{8,9},{9,8},{10,11... | collective-permute-start | bytes 442376 | tf_op jit(solution)/shard_map/ppermute | solution.py:42
  58.1 8.1 %collective-permute-start.15 = (bf16[48,1536]{1,0:T(8,128)(2,1)S(1)}, bf16[48,1536]{1,0:T(8,128)(2,1)S(1)}, u32[]{:S(2)}, u32[]{:S(2)}) collective-permute-start(bf16[48,1536]{1,0:T(8,128)(2,1)S(1)} %get-tuple-element.111), channel_id=1, source_target_pairs={{0,32},{1,33},{2,34},{3,35},{4,36},{5,37},{6,38},{7,39},{8,40},{9,... | collective-permute-start | bytes 442376 | tf_op jit(solution)/shard_map/ppermute | solution.py:42
  62.5 5.2 %collective-permute-start.16 = (bf16[48,1536]{1,0:T(8,128)(2,1)S(1)}, bf16[48,1536]{1,0:T(8,128)(2,1)S(1)}, u32[]{:S(2)}, u32[]{:S(2)}) collective-permute-start(bf16[48,1536]{1,0:T(8,128)(2,1)S(1)} %get-tuple-element.112), channel_id=1, source_target_pairs={{0,192},{1,193},{2,194},{3,195},{4,196},{5,197},{6,198},{7,199},{8... | collective-permute-start | bytes 442376 | tf_op jit(solution)/shard_map/ppermute | solution.py:42
  62.9 5.2 %collective-permute-start.17 = (bf16[48,1536]{1,0:T(8,128)(2,1)S(1)}, bf16[48,1536]{1,0:T(8,128)(2,1)S(1)}, u32[]{:S(2)}, u32[]{:S(2)}) collective-permute-start(bf16[48,1536]{1,0:T(8,128)(2,1)S(1)} %get-tuple-element.113), channel_id=1, source_target_pairs={{0,64},{1,65},{2,66},{3,67},{4,68},{5,69},{6,70},{7,71},{8,72},{9,... | collective-permute-start | bytes 442376 | tf_op jit(solution)/shard_map/ppermute | solution.py:42
  65.0 6.6 %collective-permute-start.18 = (bf16[48,1536]{1,0:T(8,128)(2,1)S(1)}, bf16[48,1536]{1,0:T(8,128)(2,1)S(1)}, u32[]{:S(2)}, u32[]{:S(2)}) collective-permute-start(bf16[48,1536]{1,0:T(8,128)(2,1)S(1)} %get-tuple-element.114), channel_id=1, source_target_pairs={{0,128},{1,129},{2,130},{3,131},{4,132},{5,133},{6,134},{7,135},{8... | collective-permute-start | bytes 442376 | tf_op jit(solution)/shard_map/ppermute | solution.py:42
  66.2 20.7 %copy-start = (bf16[1,256,1536]{2,1,0:T(8,128)(2,1)S(1)}, bf16[1,256,1536]{2,1,0:T(8,128)(2,1)}, u32[]{:S(2)}) copy-start(bf16[1,256,1536]{2,1,0:T(8,128)(2,1)} %param.6) | copy-start | bytes 2359300
  71.7 15.1 %collective-permute-start.12 = (bf16[128,1536]{1,0:T(8,128)(2,1)}, bf16[128,1536]{1,0:T(8,128)(2,1)}, u32[]{:S(2)}, u32[]{:S(2)}) collective-permute-start(bf16[128,1536]{1,0:T(8,128)(2,1)} %slice.134), channel_id=1, source_target_pairs={{0,15},{1,0},{2,1},{3,2},{4,3},{5,4},{6,5},{7,6},{8,7},{9,8},{10,9... | collective-permute-start | bytes 1179656 | tf_op jit(solution)/shard_map/ppermute | solution.py:31
  73.7 6.7 %collective-permute-start.19 = (bf16[4,144,128]{2,1,0:T(8,128)(2,1)S(1)}, bf16[4,144,128]{2,1,0:T(8,128)(2,1)S(1)}, u32[]{:S(2)}, u32[]{:S(2)}) collective-permute-start(bf16[4,144,128]{2,1,0:T(8,128)(2,1)S(1)} %get-tuple-element.116), channel_id=1, source_target_pairs={{0,2},{1,3},{2,0},{3,1},{4,6},{5,7},{6,4},{7,5},{8,10},{9,11},{10,... | collective-permute-start | bytes 442376 | tf_op jit(solution)/shard_map/ppermute | solution.py:42
  81.1 14.7 %all-to-all-start = ((bf16[4,144,128]{2,1,0:T(8,128)(2,1)}), bf16[4,144,128]{2,1,0:T(8,128)(2,1)S(1)}, u32[]{:S(2)}, u32[]{:S(2)}) async-start(bf16[4,144,128]{2,1,0:T(8,128)(2,1)} %add_convert_fusion.5), calls=%async_computation | async-start | bytes 294912 | tf_op jit(solution)/shard_map/all_to_all | solution.py:574

commit v8 on v5

--- a/solution.py
+++ b/solution.py
@@ -71,14 +71,14 @@
 
 
 ROUTES = (
+    (to_y_near, to_y_mirror),
+    (to_y_mirror, to_y_near),
     (to_x_near, to_x_mirror),
     (to_x_mirror, to_x_near),
-    (to_y_near, to_y_mirror),
-    (to_y_mirror, to_y_near),
 )
 OWNERS = (
+    (to_x_mirror, to_x_near, to_x_far),
     (to_y_mirror, to_y_near, to_y_far),
-    (to_x_mirror, to_x_near, to_x_far),
 )
 
 
@@ -88,7 +88,7 @@
 
 def chunk_at(route, slot, y, xh, xl):
     bits = [(slot >> (3 - i)) & 1 for i in range(4)]
-    x_first = route < 2
+    x_first = route >= 2
     x_bits, y_bits = (bits[:2], bits[2:]) if x_first else (bits[2:], bits[:2])
     found = []
     for hi, lo, pair, order in ((y >> 1, y & 1, y_bits, 0 if x_first else route), (xh, xl, x_bits, route if x_first else 0)):

time: 97.8 us -> 90.2 us (0.922)
  waiting for transfers between devices: 33.9 us -> 24.7 us
  starting transfers between devices: 29.4 us -> 31.6 us
    ppermute x17, waiting for transfers between devices: 22.4 us -> 13.2 us  [to_device(): return lax.ppermute(value, ('dp', 'seq'), pairs)]
    ppermute x17, starting transfers between devices: 20.4 us -> 22.6 us  [to_device(): return lax.ppermute(value, ('dp', 'seq'), pairs)]
  transfers between devices with their start and end apart: 20 -> 20, of which waited for: 9 -> 8; matrix products, arithmetic and copies ran while one was open for 9% -> 10% of each run, Pallas kernels for 22% -> 24%
where the time goes in v8:
time: 90.2 us; the launch traced here: 89.9 us
  starting transfers between devices  31.6 us (35%)
  waiting for transfers between devices  24.7 us (27%)
  Pallas kernels  22.9 us (25%)
  matrix products  4.59 us (5%)
  other arithmetic  3.64 us (4%)
  between operations  1.56 us (2%)
  local copies, waits for them, and re-layouts  0.95 us (1%)
    ppermute x17, starting transfers between devices, to_device(): return lax.ppermute(value, ('dp', 'seq'), pairs)  22.6 us
    ppermute x17, waiting for transfers between devices, to_device(): return lax.ppermute(value, ('dp', 'seq'), pairs)  13.2 us
    pallas_call x1, Pallas kernels, front(): pl.pallas_call(front_kernel, in_specs=[SMEM_SPEC] + [HBM_SPEC] * 6, out_s...  9.88 us
    all_to_all x1, waiting for transfers between devices, on_device(): lax.all_to_all(shares, 'seq', 0, 0, axis_index_groups=rings, tiled=True)  7.9 us
    all_to_all x1, starting transfers between devices, on_device(): lax.all_to_all(shares, 'seq', 0, 0, axis_index_groups=rings, tiled=True)  5.84 us
    pallas_call x1, Pallas kernels, early_tile(): pl.pallas_call(early_kernel, in_specs=[SMEM_SPEC, HBM_SPEC] + [VMEM_SPEC]...  4.69 us
    dot_general x2, matrix products, dot(): return lax.dot_general(a, b, dims, preferred_element_type=F32)  4.59 us
    pallas_call x2, Pallas kernels, weight_sections(): pl.pallas_call(kernel, in_specs=[SMEM_SPEC] + [VMEM_SPEC] * len(operands)...  4.46 us
  transfers between devices with their start and end apart: 20, of which 8 were waited for; matrix products, arithmetic and copies ran while one was open for 10% of the time, Pallas kernels for 24%

profile of v8, /device:TPU:8, one launch (start us, length us, event | category | flops | bytes accessed | tf_op | source)
XLA Modules:
  0.0 89.9 jit_solution(17240097195066212256)
XLA Ops:
  0.6 1.0 %last_rows.1 = bf16[128,1536]{1,0:T(8,128)(2,1)S(1)} custom-call(bf16[256,1536]{1,0:T(8,128)(2,1)} %bitcast.43), custom_call_target="tpu_custom_call" | custom-call | flops 1 | bytes 1 | tf_op jit(solution)/shard_map/last_rows/pallas_call | solution.py:170
  1.7 1.6 %collective-permute-start = (bf16[128,1536]{1,0:T(8,128)(2,1)S(1)}, bf16[128,1536]{1,0:T(8,128)(2,1)S(1)}, u32[]{:S(2)}, u32[]{:S(2)}) collective-permute-start(bf16[128,1536]{1,0:T(8,128)(2,1)S(1)} %last_rows.1), channel_id=1, source_target_pairs={{0,1},{1,2},{2,3},{3,4},{4,5},{5,6},{6,7},{7,8},{8,9},{9,10},{10,1... | collective-permute-start | bytes 1179656 | tf_op jit(solution)/shard_map/ppermute | solution.py:31
  3.3 0.1 pad_add_fusion.1.places
  4.0 9.9 %front.1 = (bf16[256,2304]{1,0:T(8,128)(2,1)S(1)}, bf16[256,768]{1,0:T(8,128)(2,1)S(1)}, bf16[768,512]{1,0:T(8,128)(2,1)S(1)}, bf16[768,512]{1,0:T(8,128)(2,1)S(...) custom-call(s32[2]{0:T(128)S(1)} %pad_add_fusion.1.places, ...), custom_call_target="tpu_custom_call" | custom-call | flops 3623878656 | bytes 11796480 | tf_op jit(solution)/shard_map/front/pallas_call | solution.py:251
  13.9 0.1 collective-permute-start.2
  14.0 3.6 %collective-permute-done.frames_ref = bf16[128,1536]{1,0:T(8,128)(2,1)S(1)} collective-permute-done((bf16[128,1536]{1,0:T(8,128)(2,1)S(1)}, bf16[128,1536]{1,0:T(8,128)(2,1)S(1)}, u32[]{:S(2)}, u32[]{:S(2)}) %collective-permute-start) | collective-permute-done | bytes 393248 | tf_op jit(solution)/shard_map/ppermute | solution.py:31
  17.6 4.7 %attention_early.1 = (bf16[2,256,768]{2,1,0:T(8,128)(2,1)S(1)}, bf16[2,384,896]{2,1,0:T(8,128)(2,1)S(1)}, bf16[768,128]{1,0:T(8,128)(2,1)S(1)}) custom-call(s32[2]{0:T(128)S(1)} %pad_add_fusion.1.places, s32[1]{0:T(128)S(6)} %copy.9.lengths_ref, bf16[384,384]{1,0:T(8,128)(2,1)S(1)} %get-tuple-element.61.order_ref, ...), custom_call_target="tpu_custom_call" | custom-call | flops 704643072 | bytes 1572864 | tf_op jit(solution)/shard_map/attention_early/pallas_call | solution.py:367
  22.3 0.3 collective-permute-start.1
  22.6 0.8 first_own.1.own_ref
  23.4 1.5 %collective-permute-done.1.right_other_ref = bf16[2,256,768]{2,1,0:T(8,128)(2,1)S(1)} collective-permute-done((bf16[2,256,768]{2,1,0:T(8,128)(2,1)S(1)}, bf16[2,256,768]{2,1,0:T(8,128)(2,1)S(1)}, u32[]{:S(2)}, u32[]{:S(2)}) %collective-permute-start.1) | collective-permute-done | bytes 786464 | tf_op jit(solution)/shard_map/ppermute | solution.py:42
  24.9 0.1 collective-permute-start.5
  25.0 0.1 slice_bitcast_fusion.2
  25.1 1.6 %first_wave.1 = (bf16[8,48,768]{2,1,0:T(8,128)(2,1)S(1)}, bf16[8,48,768]{2,1,0:T(8,128)(2,1)S(1)}, bf16[8,48,768]{2,1,0:T(8,128)(2,1)S(1)}, bf16[8,48,768]{2,1,0:T(8,128)(2,1)S(1)}) custom-call(s32[4,16]{1,0:T(4,128)S(1)} %pad_add_fusion.chunks, bf16[768,512]{1,0:T(8,128)(2,1)S(1)} %collective-permute-done.2.left_other_ref, ...), custom_call_target="tpu_custom_call" | custom-call | flops 1 | bytes 1 | tf_op jit(solution)/shard_map/first_wave/pallas_call | solution.py:433
  26.7 0.5 collective-permute-start.3
  27.3 2.4 %collective-permute-start.4 = (bf16[8,48,768]{2,1,0:T(8,128)(2,1)S(1)}, bf16[8,48,768]{2,1,0:T(8,128)(2,1)S(1)}, u32[]{:S(2)}, u32[]{:S(2)}) collective-permute-start(bf16[8,48,768]{2,1,0:T(8,128)(2,1)S(1)} %get-tuple-element.75), channel_id=1, source_target_pairs={{0,192},{1,193},{2,194},{3,195},{4,196},{5,197},{6,198},{7,199},{8... | collective-permute-start | bytes 1769480 | tf_op jit(solution)/shard_map/ppermute | solution.py:42
  29.7 0.1 slice_bitcast_fusion.1
  29.8 0.0 slice-start
  29.8 0.1 fusion.2
  29.9 0.0 collective-permute-done.5.right_other_ref
  29.9 0.0 copy-start.1
  29.9 0.0 slice-start.1
  30.0 2.8 %second_wave.1 = (bf16[8,48,768]{2,1,0:T(8,128)(2,1)S(1)}, bf16[8,48,768]{2,1,0:T(8,128)(2,1)S(1)}, bf16[8,48,768]{2,1,0:T(8,128)(2,1)S(1)}, bf16[8,48,768]{2,1,0:T(8,128)(2,1)S(1)}) custom-call(s32[4,16]{1,0:T(4,128)S(1)} %pad_add_fusion.chunks, bf16[768,512]{1,0:T(8,128)(2,1)S(1)} %get-tuple-element.69.left_ref, ...), custom_call_target="tpu_custom_call" | custom-call | flops 3000000000 | bytes 1 | tf_op jit(solution)/shard_map/second_wave/pallas_call | solution.py:433
  32.8 0.1 collective-permute-start.6
  32.9 3.3 %collective-permute-start.7 = (bf16[8,48,768]{2,1,0:T(8,128)(2,1)S(1)}, bf16[8,48,768]{2,1,0:T(8,128)(2,1)S(1)}, u32[]{:S(2)}, u32[]{:S(2)}) collective-permute-start(bf16[8,48,768]{2,1,0:T(8,128)(2,1)S(1)} %get-tuple-element.86), channel_id=1, source_target_pairs={{0,33},{1,32},{2,35},{3,34},{4,37},{5,36},{6,39},{7,38},{8,41},{9,... | collective-permute-start | bytes 1769480 | tf_op jit(solution)/shard_map/ppermute | solution.py:42
  36.2 1.7 %convolution_convert_fusion = bf16[256,1536]{1,0:T(8,128)(2,1)} fusion(bf16[256,768]{1,0:T(8,128)(2,1)S(1)} %get-tuple-element.80, bf16[768,1536]{1,0:T(8,128)(2,1)S(1)} %copy-done.1), kind=kOutput, calls=%fused_computation.2 | convolution fusion | flops 604372992 | bytes 3538944 | tf_op jit(solution)/shard_map/dot_general | solution.py:26
  37.8 4.6 %collective-permute-done.3.refs_2_ = bf16[8,48,768]{2,1,0:T(8,128)(2,1)S(1)} collective-permute-done((bf16[8,48,768]{2,1,0:T(8,128)(2,1)S(1)}, bf16[8,48,768]{2,1,0:T(8,128)(2,1)S(1)}, u32[]{:S(2)}, u32[]{:S(2)}) %collective-permute-start.3) | collective-permute-done | bytes 589856 | tf_op jit(solution)/shard_map/ppermute | solution.py:42
  42.4 0.8 collective-permute-done.4.refs_3_
  43.3 0.3 halve.3
  43.6 1.8 %collective-permute-start.10 = (bf16[4,48,768]{2,1,0:T(8,128)(2,1)S(1)}, bf16[4,48,768]{2,1,0:T(8,128)(2,1)S(1)}, u32[]{:S(2)}, u32[]{:S(2)}) collective-permute-start(bf16[4,48,768]{2,1,0:T(8,128)(2,1)S(1)} %get-tuple-element.98), channel_id=1, source_target_pairs={{0,192},{1,193},{2,194},{3,195},{4,196},{5,197},{6,198},{7,199},{8... | collective-permute-start | bytes 884744 | tf_op jit(solution)/shard_map/ppermute | solution.py:42
  45.4 2.6 %collective-permute-start.11 = (bf16[4,48,768]{2,1,0:T(8,128)(2,1)S(1)}, bf16[4,48,768]{2,1,0:T(8,128)(2,1)S(1)}, u32[]{:S(2)}, u32[]{:S(2)}) collective-permute-start(bf16[4,48,768]{2,1,0:T(8,128)(2,1)S(1)} %get-tuple-element.99), channel_id=1, source_target_pairs={{0,64},{1,65},{2,66},{3,67},{4,68},{5,69},{6,70},{7,71},{8,72},{9,... | collective-permute-start | bytes 884744 | tf_op jit(solution)/shard_map/ppermute | solution.py:42
  47.9 1.3 %collective-permute-done.7.refs_3_ = bf16[8,48,768]{2,1,0:T(8,128)(2,1)S(1)} collective-permute-done((bf16[8,48,768]{2,1,0:T(8,128)(2,1)S(1)}, bf16[8,48,768]{2,1,0:T(8,128)(2,1)S(1)}, u32[]{:S(2)}, u32[]{:S(2)}) %collective-permute-start.7) | collective-permute-done | bytes 589856 | tf_op jit(solution)/shard_map/ppermute | solution.py:42
  49.2 0.3 halve.2
  49.5 3.0 %collective-permute-start.8 = (bf16[4,48,768]{2,1,0:T(8,128)(2,1)S(1)}, bf16[4,48,768]{2,1,0:T(8,128)(2,1)S(1)}, u32[]{:S(2)}, u32[]{:S(2)}) collective-permute-start(bf16[4,48,768]{2,1,0:T(8,128)(2,1)S(1)} %get-tuple-element.91), channel_id=1, source_target_pairs={{0,33},{1,32},{2,35},{3,34},{4,37},{5,36},{6,39},{7,38},{8,41},{9,... | collective-permute-start | bytes 884744 | tf_op jit(solution)/shard_map/ppermute | solution.py:42
  52.5 0.0 collective-permute-start.9
  52.5 2.9 %fusion.30 = f32[384,1536]{1,0:T(8,128)S(1)} fusion(bf16[384,2304]{1,0:T(8,128)(2,1)S(1)} %fusion.2, bf16[1536,2304]{1,0:T(8,128)(2,1)S(1)} %bitcast.52), kind=kOutput, calls=%fused_computation.76 | convolution fusion | flops 2717908992 | bytes 11206656 | tf_op jit(solution)/shard_map/dot_general | solution.py:26
  55.5 0.1 add_convert_fusion.1
  55.5 0.1 add_convert_fusion.2
  55.7 0.4 collective-permute-start.13
  56.1 2.0 %collective-permute-start.14 = (bf16[48,1536]{1,0:T(8,128)(2,1)S(1)}, bf16[48,1536]{1,0:T(8,128)(2,1)S(1)}, u32[]{:S(2)}, u32[]{:S(2)}) collective-permute-start(bf16[48,1536]{1,0:T(8,128)(2,1)S(1)} %get-tuple-element.108), channel_id=1, source_target_pairs={{0,1},{1,0},{2,3},{3,2},{4,5},{5,4},{6,7},{7,6},{8,9},{9,8},{10,11... | collective-permute-start | bytes 442376 | tf_op jit(solution)/shard_map/ppermute | solution.py:42
  58.1 2.4 %collective-permute-start.15 = (bf16[48,1536]{1,0:T(8,128)(2,1)S(1)}, bf16[48,1536]{1,0:T(8,128)(2,1)S(1)}, u32[]{:S(2)}, u32[]{:S(2)}) collective-permute-start(bf16[48,1536]{1,0:T(8,128)(2,1)S(1)} %get-tuple-element.109), channel_id=1, source_target_pairs={{0,32},{1,33},{2,34},{3,35},{4,36},{5,37},{6,38},{7,39},{8,40},{9,... | collective-permute-start | bytes 442376 | tf_op jit(solution)/shard_map/ppermute | solution.py:42
  60.5 0.0 collective-permute-done.8
  60.5 0.1 add_convert_fusion.4
  60.5 1.9 %collective-permute-done.9 = bf16[4,48,768]{2,1,0:T(8,128)(2,1)S(1)} collective-permute-done((bf16[4,48,768]{2,1,0:T(8,128)(2,1)S(1)}, bf16[4,48,768]{2,1,0:T(8,128)(2,1)S(1)}, u32[]{:S(2)}, u32[]{:S(2)}) %collective-permute-start.9) | collective-permute-done | bytes 294944 | tf_op jit(solution)/shard_map/ppermute | solution.py:42
  62.4 0.1 add_convert_fusion.3
  62.5 0.4 collective-permute-start.16
  62.9 2.1 %collective-permute-start.17 = (bf16[48,1536]{1,0:T(8,128)(2,1)S(1)}, bf16[48,1536]{1,0:T(8,128)(2,1)S(1)}, u32[]{:S(2)}, u32[]{:S(2)}) collective-permute-start(bf16[48,1536]{1,0:T(8,128)(2,1)S(1)} %get-tuple-element.111), channel_id=1, source_target_pairs={{0,64},{1,65},{2,66},{3,67},{4,68},{5,69},{6,70},{7,71},{8,72},{9,... | collective-permute-start | bytes 442376 | tf_op jit(solution)/shard_map/ppermute | solution.py:42
  65.0 0.0 collective-permute-done.13
  65.0 1.1 %collective-permute-start.18 = (bf16[48,1536]{1,0:T(8,128)(2,1)S(1)}, bf16[48,1536]{1,0:T(8,128)(2,1)S(1)}, u32[]{:S(2)}, u32[]{:S(2)}) collective-permute-start(bf16[48,1536]{1,0:T(8,128)(2,1)S(1)} %get-tuple-element.112), channel_id=1, source_target_pairs={{0,128},{1,129},{2,130},{3,131},{4,132},{5,133},{6,134},{7,135},{8... | collective-permute-start | bytes 442376 | tf_op jit(solution)/shard_map/ppermute | solution.py:42
  66.1 0.0 collective-permute-done.14
  66.1 0.0 collective-permute-done.15
  66.1 0.1 fusion.13.refs_0_
  66.2 0.0 copy-start
  66.2 0.8 slice.134
  67.0 1.6 %collective-permute-start.12 = (bf16[128,1536]{1,0:T(8,128)(2,1)}, bf16[128,1536]{1,0:T(8,128)(2,1)}, u32[]{:S(2)}, u32[]{:S(2)}) collective-permute-start(bf16[128,1536]{1,0:T(8,128)(2,1)} %slice.134), channel_id=1, source_target_pairs={{0,15},{1,0},{2,1},{3,2},{4,3},{5,4},{6,5},{7,6},{8,7},{9,8},{10,9... | collective-permute-start | bytes 1179656 | tf_op jit(solution)/shard_map/ppermute | solution.py:31
  68.6 0.0 collective-permute-done.16
  68.6 0.0 collective-permute-done.17
  68.6 3.1 %collective-permute-done.18 = bf16[48,1536]{1,0:T(8,128)(2,1)S(1)} collective-permute-done((bf16[48,1536]{1,0:T(8,128)(2,1)S(1)}, bf16[48,1536]{1,0:T(8,128)(2,1)S(1)}, u32[]{:S(2)}, u32[]{:S(2)}) %collective-permute-start.18) | collective-permute-done | bytes 147488 | tf_op jit(solution)/shard_map/ppermute | solution.py:42
  71.7 0.1 fusion.10.refs_1_
  71.8 0.8 pieces.1
  72.6 5.8 %all-to-all-start = ((bf16[8,144,128]{2,1,0:T(8,128)(2,1)}), bf16[8,144,128]{2,1,0:T(8,128)(2,1)S(1)}, u32[]{:S(2)}, u32[]{:S(2)}) async-start(bf16[8,144,128]{2,1,0:T(8,128)(2,1)} %pieces.1), calls=%async_computation | async-start | bytes 589824 | tf_op jit(solution)/shard_map/all_to_all | solution.py:561
  78.4 1.5 %convert_reduce_fusion = (f32[256]{0:T(256)S(1)}, f32[256]{0:T(256)S(1)}, bf16[256,1536]{1,0:T(8,128)(2,1)S(1)}) fusion(f32[256]{0:T(256)S(1)} %bitcast.49, f32[256]{0:T(256)S(1)} %bitcast.47, bf16[256,1536]{1,0:T(8,128)(2,1)S(1)} %bitcast.45, bf16[128,1536]{1,0:T(8,128)(2,1)} %collective-permute-done.12, f32[384,1536]{1,0:T(8,128)S(1)} %fusion.30), kind=kLoop, calls=%fused_computation.5 | loop fusion | flops 3931648 | bytes 3543040 | tf_op jit(solution)/shard_map/reduce_sum | solution.py:118
  79.9 1.4 %fusion.7 = bf16[1,256,1536]{2,1,0:T(8,128)(2,1)} fusion(bf16[256,1536]{1,0:T(8,128)(2,1)S(1)} %bitcast.46, bf16[256,1536]{1,0:T(8,128)(2,1)S(1)} %get-tuple-element.115, f32[256]{0:T(256)S(1)} %broadcast_multiply_fusion, f32[256]{0:T(256)S(1)} %bitcast.48, f32[256]{0:T(256)S(1)} %broadcast_multiply_fusion.1, f32[256]{0:T(256)S(1)} %bitcast.50), kind=kLoop, calls=%fused_computation.14 | loop fusion | flops 3538944 | bytes 2363392 | tf_op jit(solution)/shard_map/broadcast_in_dim | solution.py:569
  81.3 7.9 %all-to-all-done.in_ref = bf16[8,144,128]{2,1,0:T(8,128)(2,1)S(1)} async-done(((bf16[8,144,128]{2,1,0:T(8,128)(2,1)}), bf16[8,144,128]{2,1,0:T(8,128)(2,1)S(1)}, u32[]{:S(2)}, u32[]{:S(2)}) %all-to-all-start) | async-done | bytes 294944 | tf_op jit(solution)/shard_map/all_to_all | solution.py:561
  89.2 0.7 total.1
  (18 shorter events, 0.1 us)
Async XLA Ops:
  1.7 16.0 %collective-permute-start = (bf16[128,1536]{1,0:T(8,128)(2,1)S(1)}, bf16[128,1536]{1,0:T(8,128)(2,1)S(1)}, u32[]{:S(2)}, u32[]{:S(2)}) collective-permute-start(bf16[128,1536]{1,0:T(8,128)(2,1)S(1)} %last_rows.1), channel_id=1, source_target_pairs={{0,1},{1,2},{2,3},{3,4},{4,5},{5,6},{6,7},{7,8},{8,9},{9,10},{10,1... | collective-permute-start | bytes 1179656 | tf_op jit(solution)/shard_map/ppermute | solution.py:31
  13.9 9.5 %collective-permute-start.2 = (bf16[768,512]{1,0:T(8,128)(2,1)S(1)}, bf16[768,512]{1,0:T(8,128)(2,1)S(1)}, u32[]{:S(2)}, u32[]{:S(2)}) collective-permute-start(bf16[768,512]{1,0:T(8,128)(2,1)S(1)} %get-tuple-element.68), channel_id=1, source_target_pairs={{0,16},{1,17},{2,18},{3,19},{4,20},{5,21},{6,22},{7,23},{8,24},{9,... | collective-permute-start | bytes 2359304 | tf_op jit(solution)/shard_map/ppermute | solution.py:42
  22.3 2.6 %collective-permute-start.1 = (bf16[2,256,768]{2,1,0:T(8,128)(2,1)S(1)}, bf16[2,256,768]{2,1,0:T(8,128)(2,1)S(1)}, u32[]{:S(2)}, u32[]{:S(2)}) collective-permute-start(bf16[2,256,768]{2,1,0:T(8,128)(2,1)S(1)} %get-tuple-element.67.right_ref), channel_id=1, source_target_pairs={{0,16},{1,17},{2,18},{3,19},{4,20},{5,21},{6,22},{7,23},{8,24},{9,... | collective-permute-start | bytes 2359304 | tf_op jit(solution)/shard_map/ppermute | solution.py:42
  24.9 5.0 %collective-permute-start.5 = (bf16[2,384,896]{2,1,0:T(8,128)(2,1)S(1)}, bf16[2,384,896]{2,1,0:T(8,128)(2,1)S(1)}, u32[]{:S(2)}, u32[]{:S(2)}) collective-permute-start(bf16[2,384,896]{2,1,0:T(8,128)(2,1)S(1)} %get-tuple-element.76.right_ref), channel_id=1, source_target_pairs={{0,16},{1,17},{2,18},{3,19},{4,20},{5,21},{6,22},{7,23},{8,24},{9,... | collective-permute-start | bytes 4128776 | tf_op jit(solution)/shard_map/ppermute | solution.py:42
  26.7 15.7 %collective-permute-start.3 = (bf16[8,48,768]{2,1,0:T(8,128)(2,1)S(1)}, bf16[8,48,768]{2,1,0:T(8,128)(2,1)S(1)}, u32[]{:S(2)}, u32[]{:S(2)}) collective-permute-start(bf16[8,48,768]{2,1,0:T(8,128)(2,1)S(1)} %get-tuple-element.74), channel_id=1, source_target_pairs={{0,64},{1,65},{2,66},{3,67},{4,68},{5,69},{6,70},{7,71},{8,72},{9,... | collective-permute-start | bytes 1769480 | tf_op jit(solution)/shard_map/ppermute | solution.py:42
  27.3 16.0 %collective-permute-start.4 = (bf16[8,48,768]{2,1,0:T(8,128)(2,1)S(1)}, bf16[8,48,768]{2,1,0:T(8,128)(2,1)S(1)}, u32[]{:S(2)}, u32[]{:S(2)}) collective-permute-start(bf16[8,48,768]{2,1,0:T(8,128)(2,1)S(1)} %get-tuple-element.75), channel_id=1, source_target_pairs={{0,192},{1,193},{2,194},{3,195},{4,196},{5,197},{6,198},{7,199},{8... | collective-permute-start | bytes 1769480 | tf_op jit(solution)/shard_map/ppermute | solution.py:42
  29.8 22.7 %slice-start = ((s8[7077888]{0:T(1024)(128)(4,1)}), s8[4194304]{0:T(1024)(128)(4,1)S(1)}, s32[]{:S(2)}) async-start(s8[7077888]{0:T(1024)(128)(4,1)} %bitcast.51), calls=%async_computation.1 | async-start | bytes 8388608
  29.9 6.2 %copy-start.1 = (bf16[768,1536]{1,0:T(8,128)(2,1)S(1)}, bf16[768,1536]{1,0:T(8,128)(2,1)}, u32[]{:S(2)}) copy-start(bf16[768,1536]{1,0:T(8,128)(2,1)} %out_ref.1) | copy-start | bytes 7077892
  29.9 22.6 %slice-start.1 = ((s8[7077888]{0:T(1024)(128)(4,1)}), s8[2883584]{0:T(1024)(128)(4,1)S(1)}, s32[]{:S(2)}) async-start(s8[7077888]{0:T(1024)(128)(4,1)} %bitcast.51), calls=%async_computation.2 | async-start | bytes 5767168
  32.8 15.2 %collective-permute-start.6 = (bf16[8,48,768]{2,1,0:T(8,128)(2,1)S(1)}, bf16[8,48,768]{2,1,0:T(8,128)(2,1)S(1)}, u32[]{:S(2)}, u32[]{:S(2)}) collective-permute-start(bf16[8,48,768]{2,1,0:T(8,128)(2,1)S(1)} %get-tuple-element.85), channel_id=1, source_target_pairs={{0,1},{1,0},{2,3},{3,2},{4,5},{5,4},{6,7},{7,6},{8,9},{9,8},{10,11... | collective-permute-start | bytes 1769480 | tf_op jit(solution)/shard_map/ppermute | solution.py:42
  32.9 16.3 %collective-permute-start.7 = (bf16[8,48,768]{2,1,0:T(8,128)(2,1)S(1)}, bf16[8,48,768]{2,1,0:T(8,128)(2,1)S(1)}, u32[]{:S(2)}, u32[]{:S(2)}) collective-permute-start(bf16[8,48,768]{2,1,0:T(8,128)(2,1)S(1)} %get-tuple-element.86), channel_id=1, source_target_pairs={{0,33},{1,32},{2,35},{3,34},{4,37},{5,36},{6,39},{7,38},{8,41},{9,... | collective-permute-start | bytes 1769480 | tf_op jit(solution)/shard_map/ppermute | solution.py:42
  43.6 11.9 %collective-permute-start.10 = (bf16[4,48,768]{2,1,0:T(8,128)(2,1)S(1)}, bf16[4,48,768]{2,1,0:T(8,128)(2,1)S(1)}, u32[]{:S(2)}, u32[]{:S(2)}) collective-permute-start(bf16[4,48,768]{2,1,0:T(8,128)(2,1)S(1)} %get-tuple-element.98), channel_id=1, source_target_pairs={{0,192},{1,193},{2,194},{3,195},{4,196},{5,197},{6,198},{7,199},{8... | collective-permute-start | bytes 884744 | tf_op jit(solution)/shard_map/ppermute | solution.py:42
  45.4 10.1 %collective-permute-start.11 = (bf16[4,48,768]{2,1,0:T(8,128)(2,1)S(1)}, bf16[4,48,768]{2,1,0:T(8,128)(2,1)S(1)}, u32[]{:S(2)}, u32[]{:S(2)}) collective-permute-start(bf16[4,48,768]{2,1,0:T(8,128)(2,1)S(1)} %get-tuple-element.99), channel_id=1, source_target_pairs={{0,64},{1,65},{2,66},{3,67},{4,68},{5,69},{6,70},{7,71},{8,72},{9,... | collective-permute-start | bytes 884744 | tf_op jit(solution)/shard_map/ppermute | solution.py:42
  49.5 11.0 %collective-permute-start.8 = (bf16[4,48,768]{2,1,0:T(8,128)(2,1)S(1)}, bf16[4,48,768]{2,1,0:T(8,128)(2,1)S(1)}, u32[]{:S(2)}, u32[]{:S(2)}) collective-permute-start(bf16[4,48,768]{2,1,0:T(8,128)(2,1)S(1)} %get-tuple-element.91), channel_id=1, source_target_pairs={{0,33},{1,32},{2,35},{3,34},{4,37},{5,36},{6,39},{7,38},{8,41},{9,... | collective-permute-start | bytes 884744 | tf_op jit(solution)/shard_map/ppermute | solution.py:42
  52.5 9.9 %collective-permute-start.9 = (bf16[4,48,768]{2,1,0:T(8,128)(2,1)S(1)}, bf16[4,48,768]{2,1,0:T(8,128)(2,1)S(1)}, u32[]{:S(2)}, u32[]{:S(2)}) collective-permute-start(bf16[4,48,768]{2,1,0:T(8,128)(2,1)S(1)} %get-tuple-element.93), channel_id=1, source_target_pairs={{0,1},{1,0},{2,3},{3,2},{4,5},{5,4},{6,7},{7,6},{8,9},{9,8},{10,11... | collective-permute-start | bytes 884744 | tf_op jit(solution)/shard_map/ppermute | solution.py:42
  55.7 9.4 %collective-permute-start.13 = (bf16[48,1536]{1,0:T(8,128)(2,1)S(1)}, bf16[48,1536]{1,0:T(8,128)(2,1)S(1)}, u32[]{:S(2)}, u32[]{:S(2)}) collective-permute-start(bf16[48,1536]{1,0:T(8,128)(2,1)S(1)} %get-tuple-element.107), channel_id=1, source_target_pairs={{0,33},{1,32},{2,35},{3,34},{4,37},{5,36},{6,39},{7,38},{8,41},{9,... | collective-permute-start | bytes 442376 | tf_op jit(solution)/shard_map/ppermute | solution.py:42
  56.1 10.1 %collective-permute-start.14 = (bf16[48,1536]{1,0:T(8,128)(2,1)S(1)}, bf16[48,1536]{1,0:T(8,128)(2,1)S(1)}, u32[]{:S(2)}, u32[]{:S(2)}) collective-permute-start(bf16[48,1536]{1,0:T(8,128)(2,1)S(1)} %get-tuple-element.108), channel_id=1, source_target_pairs={{0,1},{1,0},{2,3},{3,2},{4,5},{5,4},{6,7},{7,6},{8,9},{9,8},{10,11... | collective-permute-start | bytes 442376 | tf_op jit(solution)/shard_map/ppermute | solution.py:42
  58.1 8.0 %collective-permute-start.15 = (bf16[48,1536]{1,0:T(8,128)(2,1)S(1)}, bf16[48,1536]{1,0:T(8,128)(2,1)S(1)}, u32[]{:S(2)}, u32[]{:S(2)}) collective-permute-start(bf16[48,1536]{1,0:T(8,128)(2,1)S(1)} %get-tuple-element.109), channel_id=1, source_target_pairs={{0,32},{1,33},{2,34},{3,35},{4,36},{5,37},{6,38},{7,39},{8,40},{9,... | collective-permute-start | bytes 442376 | tf_op jit(solution)/shard_map/ppermute | solution.py:42
  62.5 6.1 %collective-permute-start.16 = (bf16[48,1536]{1,0:T(8,128)(2,1)S(1)}, bf16[48,1536]{1,0:T(8,128)(2,1)S(1)}, u32[]{:S(2)}, u32[]{:S(2)}) collective-permute-start(bf16[48,1536]{1,0:T(8,128)(2,1)S(1)} %get-tuple-element.110), channel_id=1, source_target_pairs={{0,192},{1,193},{2,194},{3,195},{4,196},{5,197},{6,198},{7,199},{8... | collective-permute-start | bytes 442376 | tf_op jit(solution)/shard_map/ppermute | solution.py:42
  62.9 5.7 %collective-permute-start.17 = (bf16[48,1536]{1,0:T(8,128)(2,1)S(1)}, bf16[48,1536]{1,0:T(8,128)(2,1)S(1)}, u32[]{:S(2)}, u32[]{:S(2)}) collective-permute-start(bf16[48,1536]{1,0:T(8,128)(2,1)S(1)} %get-tuple-element.111), channel_id=1, source_target_pairs={{0,64},{1,65},{2,66},{3,67},{4,68},{5,69},{6,70},{7,71},{8,72},{9,... | collective-permute-start | bytes 442376 | tf_op jit(solution)/shard_map/ppermute | solution.py:42
  65.0 6.6 %collective-permute-start.18 = (bf16[48,1536]{1,0:T(8,128)(2,1)S(1)}, bf16[48,1536]{1,0:T(8,128)(2,1)S(1)}, u32[]{:S(2)}, u32[]{:S(2)}) collective-permute-start(bf16[48,1536]{1,0:T(8,128)(2,1)S(1)} %get-tuple-element.112), channel_id=1, source_target_pairs={{0,128},{1,129},{2,130},{3,131},{4,132},{5,133},{6,134},{7,135},{8... | collective-permute-start | bytes 442376 | tf_op jit(solution)/shard_map/ppermute | solution.py:42
  66.2 12.2 %copy-start = (bf16[1,256,1536]{2,1,0:T(8,128)(2,1)S(1)}, bf16[1,256,1536]{2,1,0:T(8,128)(2,1)}, u32[]{:S(2)}) copy-start(bf16[1,256,1536]{2,1,0:T(8,128)(2,1)} %param.6) | copy-start | bytes 2359300
  67.0 11.4 %collective-permute-start.12 = (bf16[128,1536]{1,0:T(8,128)(2,1)}, bf16[128,1536]{1,0:T(8,128)(2,1)}, u32[]{:S(2)}, u32[]{:S(2)}) collective-permute-start(bf16[128,1536]{1,0:T(8,128)(2,1)} %slice.134), channel_id=1, source_target_pairs={{0,15},{1,0},{2,1},{3,2},{4,3},{5,4},{6,5},{7,6},{8,7},{9,8},{10,9... | collective-permute-start | bytes 1179656 | tf_op jit(solution)/shard_map/ppermute | solution.py:31
  72.6 16.7 %all-to-all-start = ((bf16[8,144,128]{2,1,0:T(8,128)(2,1)}), bf16[8,144,128]{2,1,0:T(8,128)(2,1)S(1)}, u32[]{:S(2)}, u32[]{:S(2)}) async-start(bf16[8,144,128]{2,1,0:T(8,128)(2,1)} %pieces.1), calls=%async_computation | async-start | bytes 589824 | tf_op jit(solution)/shard_map/all_to_all | solution.py:561

commit v9 on v8

--- a/solution.py
+++ b/solution.py
@@ -392,22 +392,27 @@
         outs[n if slot < half else 2 + n][slot % half] = held[n, chunks[route, slot]].astype(BF16)
 
 
-def first_own_kernel(left_ref, right_ref, out_ref):
-    tokens = right_ref.shape[1]
-    out_ref[0] = dot(left_ref[:, tokens:], right_ref[0])
-    out_ref[1] = dot(left_ref[:, :tokens], right_ref[1])
-
-
-def first_own(left, right):
+def own_kernel(left_ref, behind_ref, first_ref, second_ref, first_out, second_out):
+    tokens = first_ref.shape[1]
+    inner = first_ref.shape[2]
+    left = jnp.concatenate([left_ref[:, :tokens], behind_ref[...]], axis=1)
+    first_out[0] = dot(left_ref[:, tokens:], first_ref[0])
+    first_out[1] = dot(left_ref[:, :tokens], first_ref[1])
+    for n in range(2):
+        second_out[n] = dot(left, second_ref[n, :, :inner])
+
+
+def own_sums(left, behind, first, second):
+    rows, inner = left.shape[0], first.shape[2]
     return pl.pallas_call(
-        first_own_kernel,
-        in_specs=[VMEM_SPEC] * 2,
-        out_specs=VMEM_SPEC,
-        out_shape=pltpu.VMEM((2, left.shape[0], right.shape[2]), F32),
+        own_kernel,
+        in_specs=[VMEM_SPEC] * 4,
+        out_specs=[VMEM_SPEC] * 2,
+        out_shape=[pltpu.VMEM((2, rows, inner), F32)] * 2,
         compiler_params=params(8),
-        cost_estimate=cost(2 * 10**9, 1),
-        name="first_own",
-    )(in_vmem(left), in_vmem(right))
+        cost_estimate=cost(4 * 10**9, 1),
+        name="own_sums",
+    )(*[in_vmem(o) for o in (left, behind, first, second)])
 
 
 def first_wave_kernel(chunks, left_other_ref, right_other_ref, own_ref, *refs):
@@ -417,13 +422,13 @@
         store_section(chunks, n, n, total, refs[:-1], refs[-1])
 
 
-def second_wave_kernel(chunks, left_ref, left_other_ref, behind_ref, right_ref, right_other_ref, *refs):
-    tokens = left_ref.shape[1] // 2
-    inner = right_ref.shape[2] - CONTEXT
-    behind_other = jnp.concatenate([right_other_ref[n, :, inner:] for n in range(2)], axis=0)
-    left = jnp.concatenate([left_ref[:, :tokens], behind_ref[...], left_other_ref[:, :tokens], behind_other], axis=1)
+def second_wave_kernel(chunks, left_other_ref, right_other_ref, own_ref, *refs):
+    tokens = left_other_ref.shape[1] // 2
+    inner = right_other_ref.shape[2] - CONTEXT
+    behind = jnp.concatenate([right_other_ref[n, :, inner:] for n in range(2)], axis=0)
+    left = jnp.concatenate([left_other_ref[:, :tokens], behind], axis=1)
     for n in range(2):
-        total = dot(left, jnp.concatenate([right_ref[n, :, :inner], right_other_ref[n, :, :inner]], axis=0))
+        total = own_ref[n] + dot(left, right_other_ref[n, :, :inner])
         store_section(chunks, 2 + n, n, total, refs[:-1], refs[-1])
 
 
@@ -513,12 +518,14 @@
     left_other = to_device(left_out, to_core)
     own, grads, left_behind = early_tile(places, lengths, order, behind, weight, qkv, attended_grad, late, late_grad)
     own_other = to_device(own, to_core)
-    own_sum = first_own(left, own)
-    own_other, left_other, own_sum, grads = lax.optimization_barrier((own_other, left_other, own_sum, grads))
+    own_sum, grads_sum = own_sums(left, left_behind, own, grads)
+    own_other, left_other, own_sum, grads_sum, grads = lax.optimization_barrier(
+        (own_other, left_other, own_sum, grads_sum, grads)
+    )
     grads_other = to_device(grads, to_core)
     keep_a, send_a = weight_sections(first_wave_kernel, chunks, (left_other, own_other, own_sum), inner, 1, "first_wave")
     keep_b, send_b = weight_sections(
-        second_wave_kernel, chunks, (left, left_other, left_behind, grads, grads_other), inner, 3 * 10**9, "second_wave"
+        second_wave_kernel, chunks, (left_other, grads_other, grads_sum), inner, 3 * 10**9, "second_wave"
     )
     query_grad = jnp.concatenate([own[1], jnp.zeros((CONTEXT, inner), BF16)], axis=0)
     projected_grad = jnp.concatenate([query_grad, grads[0, :, :inner], grads[1, :, :inner]], axis=1)
@@ -527,7 +534,7 @@
     def second_ring(kept, gots, n, *after):
         group = jnp.concatenate([plus(kept[r], gots[r]) for r in range(2)], axis=-1)
         slots, *after = lax.optimization_barrier(([group[slot] for slot in range(1, 4)], *after))
-        others = [to_device(slots[i], OWNERS[n][i]) for i in range(3)]
+        others = [to_device(slots[i], OWNERS[n][i]) for i in (2, 0, 1)]
         return plus(group[0], *others), *after
 
     gots_a = [to_device(send_a[r], ROUTES[r][0]) for r in range(2)]

time: 90.2 us -> 88.7 us (0.983)
  waiting for transfers between devices: 24.7 us -> 19.7 us
  starting transfers between devices: 31.6 us -> 33.7 us
    ppermute x17, waiting for transfers between devices: 13.2 us -> 8.16 us  [to_device(): return lax.ppermute(value, ('dp', 'seq'), pairs)]
    ppermute x2, waiting for transfers between devices: 3.63 us -> 6.72 us  [from_behind(): lax.ppermute(value, axis, [(i, (i + by) % peers) for i in range(peers)])]
    all_to_all x1, waiting for transfers between devices: 7.9 us -> 4.83 us  [on_device(): lax.all_to_all(shares, 'seq', 0, 0, axis_index_groups=rings, tiled=True)]
    ppermute x17, starting transfers between devices: 22.6 us -> 24 us  [to_device(): return lax.ppermute(value, ('dp', 'seq'), pairs)]
    pallas_call x1, Pallas kernels: 0.78 us -> 2 us  [own_sums(): pl.pallas_call(own_kernel, in_specs=[VMEM_SPEC] * 4, out_specs=[VMEM_SPEC...]
    ppermute x2, starting transfers between devices: 3.17 us -> 4.24 us  [from_behind(): lax.ppermute(value, axis, [(i, (i + by) % peers) for i in range(peers)])]
  transfers between devices with their start and end apart: 20 -> 20, of which waited for: 8 -> 8; matrix products, arithmetic and copies ran while one was open for 10% -> 10% of each run, Pallas kernels for 24% -> 25%
where the time goes in v9:
time: 88.7 us; the launch traced here: 87.7 us
  starting transfers between devices  33.7 us (38%)
  Pallas kernels  23.6 us (27%)
  waiting for transfers between devices  19.7 us (22%)
  matrix products  4.58 us (5%)
  other arithmetic  3.64 us (4%)
  between operations  1.55 us (2%)
  local copies, waits for them, and re-layouts  0.95 us (1%)
    ppermute x17, starting transfers between devices, to_device(): return lax.ppermute(value, ('dp', 'seq'), pairs)  24 us
    pallas_call x1, Pallas kernels, front(): pl.pallas_call(front_kernel, in_specs=[SMEM_SPEC] + [HBM_SPEC] * 6, out_s...  9.88 us
    ppermute x17, waiting for transfers between devices, to_device(): return lax.ppermute(value, ('dp', 'seq'), pairs)  8.16 us
    ppermute x2, waiting for transfers between devices, from_behind(): lax.ppermute(value, axis, [(i, (i + by) % peers) for i in range(peers)])  6.72 us
    all_to_all x1, starting transfers between devices, on_device(): lax.all_to_all(shares, 'seq', 0, 0, axis_index_groups=rings, tiled=True)  5.5 us
    all_to_all x1, waiting for transfers between devices, on_device(): lax.all_to_all(shares, 'seq', 0, 0, axis_index_groups=rings, tiled=True)  4.83 us
    pallas_call x1, Pallas kernels, early_tile(): pl.pallas_call(early_kernel, in_specs=[SMEM_SPEC, HBM_SPEC] + [VMEM_SPEC]...  4.69 us
    dot_general x2, matrix products, dot(): return lax.dot_general(a, b, dims, preferred_element_type=F32)  4.58 us
  transfers between devices with their start and end apart: 20, of which 8 were waited for; matrix products, arithmetic and copies ran while one was open for 10% of the time, Pallas kernels for 25%

profile of v9, /device:TPU:8, one launch (start us, length us, event | category | flops | bytes accessed | tf_op | source)
XLA Modules:
  0.0 87.7 jit_solution(18009935923118928789)
XLA Ops:
  0.6 1.0 %last_rows.1 = bf16[128,1536]{1,0:T(8,128)(2,1)S(1)} custom-call(bf16[256,1536]{1,0:T(8,128)(2,1)} %bitcast.43), custom_call_target="tpu_custom_call" | custom-call | flops 1 | bytes 1 | tf_op jit(solution)/shard_map/last_rows/pallas_call | solution.py:170
  1.7 1.6 %collective-permute-start = (bf16[128,1536]{1,0:T(8,128)(2,1)S(1)}, bf16[128,1536]{1,0:T(8,128)(2,1)S(1)}, u32[]{:S(2)}, u32[]{:S(2)}) collective-permute-start(bf16[128,1536]{1,0:T(8,128)(2,1)S(1)} %last_rows.1), channel_id=1, source_target_pairs={{0,1},{1,2},{2,3},{3,4},{4,5},{5,6},{6,7},{7,8},{8,9},{9,10},{10,1... | collective-permute-start | bytes 1179656 | tf_op jit(solution)/shard_map/ppermute | solution.py:31
  3.3 0.1 pad_add_fusion.1.places
  4.0 9.9 %front.1 = (bf16[256,2304]{1,0:T(8,128)(2,1)S(1)}, bf16[256,768]{1,0:T(8,128)(2,1)S(1)}, bf16[768,512]{1,0:T(8,128)(2,1)S(1)}, bf16[768,512]{1,0:T(8,128)(2,1)S(...) custom-call(s32[2]{0:T(128)S(1)} %pad_add_fusion.1.places, ...), custom_call_target="tpu_custom_call" | custom-call | flops 3623878656 | bytes 11796480 | tf_op jit(solution)/shard_map/front/pallas_call | solution.py:251
  13.9 0.1 collective-permute-start.2
  14.0 3.6 %collective-permute-done.frames_ref = bf16[128,1536]{1,0:T(8,128)(2,1)S(1)} collective-permute-done((bf16[128,1536]{1,0:T(8,128)(2,1)S(1)}, bf16[128,1536]{1,0:T(8,128)(2,1)S(1)}, u32[]{:S(2)}, u32[]{:S(2)}) %collective-permute-start) | collective-permute-done | bytes 393248 | tf_op jit(solution)/shard_map/ppermute | solution.py:31
  17.6 4.7 %attention_early.1 = (bf16[2,256,768]{2,1,0:T(8,128)(2,1)S(1)}, bf16[2,384,896]{2,1,0:T(8,128)(2,1)S(1)}, bf16[768,128]{1,0:T(8,128)(2,1)S(1)}) custom-call(s32[2]{0:T(128)S(1)} %pad_add_fusion.1.places, s32[1]{0:T(128)S(6)} %copy.9.lengths_ref, bf16[384,384]{1,0:T(8,128)(2,1)S(1)} %get-tuple-element.64.order_ref, ...), custom_call_target="tpu_custom_call" | custom-call | flops 704643072 | bytes 1572864 | tf_op jit(solution)/shard_map/attention_early/pallas_call | solution.py:367
  22.3 0.3 collective-permute-start.1
  22.6 2.0 %own_sums.1 = (f32[2,768,768]{2,1,0:T(8,128)S(1)}, f32[2,768,768]{2,1,0:T(8,128)S(1)}) custom-call(bf16[768,512]{1,0:T(8,128)(2,1)S(1)} %get-tuple-element.72.left_ref, bf16[768,128]{1,0:T(8,128)(2,1)S(1)} %get-tuple-element.73.behind_ref, bf16[2,256,768]{2,1,0:T(8,128)(2,1)S(1)} %get-tuple-element.70.first_ref, ...), custom_call_target="tpu_custom_call" | custom-call | flops 4000000000 | bytes 1 | tf_op jit(solution)/shard_map/own_sums/pallas_call | solution.py:407
  24.6 0.0 collective-permute-done.2.left_other_ref
  24.6 0.3 collective-permute-done.1.right_other_ref
  24.9 0.3 collective-permute-start.5
  25.2 0.1 slice_bitcast_fusion.2
  25.3 1.6 %first_wave.1 = (bf16[8,48,768]{2,1,0:T(8,128)(2,1)S(1)}, bf16[8,48,768]{2,1,0:T(8,128)(2,1)S(1)}, bf16[8,48,768]{2,1,0:T(8,128)(2,1)S(1)}, bf16[8,48,768]{2,1,0:T(8,128)(2,1)S(1)}) custom-call(s32[4,16]{1,0:T(4,128)S(1)} %pad_add_fusion.chunks, bf16[768,512]{1,0:T(8,128)(2,1)S(1)} %collective-permute-done.2.left_other_ref, ...), custom_call_target="tpu_custom_call" | custom-call | flops 1 | bytes 1 | tf_op jit(solution)/shard_map/first_wave/pallas_call | solution.py:438
  26.9 0.5 collective-permute-start.3
  27.5 2.4 %collective-permute-start.4 = (bf16[8,48,768]{2,1,0:T(8,128)(2,1)S(1)}, bf16[8,48,768]{2,1,0:T(8,128)(2,1)S(1)}, u32[]{:S(2)}, u32[]{:S(2)}) collective-permute-start(bf16[8,48,768]{2,1,0:T(8,128)(2,1)S(1)} %get-tuple-element.81), channel_id=1, source_target_pairs={{0,192},{1,193},{2,194},{3,195},{4,196},{5,197},{6,198},{7,199},{8... | collective-permute-start | bytes 1769480 | tf_op jit(solution)/shard_map/ppermute | solution.py:42
  29.9 0.1 slice_bitcast_fusion.1
  30.0 0.0 slice-start
  30.0 0.1 fusion.2
  30.1 0.0 copy-start.1
  30.1 0.0 slice-start.1
  30.1 0.0 collective-permute-done.5.right_other_ref
  30.1 2.3 %second_wave.1 = (bf16[8,48,768]{2,1,0:T(8,128)(2,1)S(1)}, bf16[8,48,768]{2,1,0:T(8,128)(2,1)S(1)}, bf16[8,48,768]{2,1,0:T(8,128)(2,1)S(1)}, bf16[8,48,768]{2,1,0:T(8,128)(2,1)S(1)}) custom-call(s32[4,16]{1,0:T(4,128)S(1)} %pad_add_fusion.chunks, bf16[768,512]{1,0:T(8,128)(2,1)S(1)} %collective-permute-done.2.left_other_ref, ...), custom_call_target="tpu_custom_call" | custom-call | flops 3000000000 | bytes 1 | tf_op jit(solution)/shard_map/second_wave/pallas_call | solution.py:438
  32.4 0.1 collective-permute-start.6
  32.5 3.3 %collective-permute-start.7 = (bf16[8,48,768]{2,1,0:T(8,128)(2,1)S(1)}, bf16[8,48,768]{2,1,0:T(8,128)(2,1)S(1)}, u32[]{:S(2)}, u32[]{:S(2)}) collective-permute-start(bf16[8,48,768]{2,1,0:T(8,128)(2,1)S(1)} %get-tuple-element.92), channel_id=1, source_target_pairs={{0,33},{1,32},{2,35},{3,34},{4,37},{5,36},{6,39},{7,38},{8,41},{9,... | collective-permute-start | bytes 1769480 | tf_op jit(solution)/shard_map/ppermute | solution.py:42
  35.8 1.7 %convolution_convert_fusion = bf16[256,1536]{1,0:T(8,128)(2,1)} fusion(bf16[256,768]{1,0:T(8,128)(2,1)S(1)} %get-tuple-element.86, bf16[768,1536]{1,0:T(8,128)(2,1)S(1)} %copy-done.1), kind=kOutput, calls=%fused_computation.2 | convolution fusion | flops 604372992 | bytes 3538944 | tf_op jit(solution)/shard_map/dot_general | solution.py:26
  37.5 5.0 %collective-permute-done.3.refs_2_ = bf16[8,48,768]{2,1,0:T(8,128)(2,1)S(1)} collective-permute-done((bf16[8,48,768]{2,1,0:T(8,128)(2,1)S(1)}, bf16[8,48,768]{2,1,0:T(8,128)(2,1)S(1)}, u32[]{:S(2)}, u32[]{:S(2)}) %collective-permute-start.3) | collective-permute-done | bytes 589856 | tf_op jit(solution)/shard_map/ppermute | solution.py:42
  42.4 0.8 collective-permute-done.4.refs_3_
  43.3 0.3 halve.3
  43.6 1.8 %collective-permute-start.10 = (bf16[4,48,768]{2,1,0:T(8,128)(2,1)S(1)}, bf16[4,48,768]{2,1,0:T(8,128)(2,1)S(1)}, u32[]{:S(2)}, u32[]{:S(2)}) collective-permute-start(bf16[4,48,768]{2,1,0:T(8,128)(2,1)S(1)} %get-tuple-element.104), channel_id=1, source_target_pairs={{0,192},{1,193},{2,194},{3,195},{4,196},{5,197},{6,198},{7,199},{8... | collective-permute-start | bytes 884744 | tf_op jit(solution)/shard_map/ppermute | solution.py:42
  45.4 2.6 %collective-permute-start.11 = (bf16[4,48,768]{2,1,0:T(8,128)(2,1)S(1)}, bf16[4,48,768]{2,1,0:T(8,128)(2,1)S(1)}, u32[]{:S(2)}, u32[]{:S(2)}) collective-permute-start(bf16[4,48,768]{2,1,0:T(8,128)(2,1)S(1)} %get-tuple-element.105), channel_id=1, source_target_pairs={{0,64},{1,65},{2,66},{3,67},{4,68},{5,69},{6,70},{7,71},{8,72},{9,... | collective-permute-start | bytes 884744 | tf_op jit(solution)/shard_map/ppermute | solution.py:42
  47.9 0.7 collective-permute-done.7.refs_3_
  48.7 0.3 halve.2
  49.0 3.0 %collective-permute-start.8 = (bf16[4,48,768]{2,1,0:T(8,128)(2,1)S(1)}, bf16[4,48,768]{2,1,0:T(8,128)(2,1)S(1)}, u32[]{:S(2)}, u32[]{:S(2)}) collective-permute-start(bf16[4,48,768]{2,1,0:T(8,128)(2,1)S(1)} %get-tuple-element.97), channel_id=1, source_target_pairs={{0,33},{1,32},{2,35},{3,34},{4,37},{5,36},{6,39},{7,38},{8,41},{9,... | collective-permute-start | bytes 884744 | tf_op jit(solution)/shard_map/ppermute | solution.py:42
  52.0 0.0 collective-permute-start.9
  52.0 2.9 %fusion.30 = f32[384,1536]{1,0:T(8,128)S(1)} fusion(bf16[384,2304]{1,0:T(8,128)(2,1)S(1)} %fusion.2, bf16[1536,2304]{1,0:T(8,128)(2,1)S(1)} %bitcast.52), kind=kOutput, calls=%fused_computation.76 | convolution fusion | flops 2717908992 | bytes 11206656 | tf_op jit(solution)/shard_map/dot_general | solution.py:26
  54.9 0.0 collective-permute-done.10
  54.9 0.0 collective-permute-done.11
  54.9 0.1 add_convert_fusion.1
  55.0 0.1 add_convert_fusion.2
  55.1 1.9 %collective-permute-start.13 = (bf16[48,1536]{1,0:T(8,128)(2,1)S(1)}, bf16[48,1536]{1,0:T(8,128)(2,1)S(1)}, u32[]{:S(2)}, u32[]{:S(2)}) collective-permute-start(bf16[48,1536]{1,0:T(8,128)(2,1)S(1)} %get-tuple-element.113), channel_id=1, source_target_pairs={{0,32},{1,33},{2,34},{3,35},{4,36},{5,37},{6,38},{7,39},{8,40},{9,... | collective-permute-start | bytes 442376 | tf_op jit(solution)/shard_map/ppermute | solution.py:42
  57.0 2.9 %collective-permute-start.14 = (bf16[48,1536]{1,0:T(8,128)(2,1)S(1)}, bf16[48,1536]{1,0:T(8,128)(2,1)S(1)}, u32[]{:S(2)}, u32[]{:S(2)}) collective-permute-start(bf16[48,1536]{1,0:T(8,128)(2,1)S(1)} %get-tuple-element.114), channel_id=1, source_target_pairs={{0,33},{1,32},{2,35},{3,34},{4,37},{5,36},{6,39},{7,38},{8,41},{9,... | collective-permute-start | bytes 442376 | tf_op jit(solution)/shard_map/ppermute | solution.py:42
  59.9 0.0 collective-permute-start.15
  59.9 0.1 add_convert_fusion.4
  60.0 1.3 %collective-permute-done.9 = bf16[4,48,768]{2,1,0:T(8,128)(2,1)S(1)} collective-permute-done((bf16[4,48,768]{2,1,0:T(8,128)(2,1)S(1)}, bf16[4,48,768]{2,1,0:T(8,128)(2,1)S(1)}, u32[]{:S(2)}, u32[]{:S(2)}) %collective-permute-start.9) | collective-permute-done | bytes 294944 | tf_op jit(solution)/shard_map/ppermute | solution.py:42
  61.3 0.1 add_convert_fusion.3
  61.4 1.3 %collective-permute-start.16 = (bf16[48,1536]{1,0:T(8,128)(2,1)S(1)}, bf16[48,1536]{1,0:T(8,128)(2,1)S(1)}, u32[]{:S(2)}, u32[]{:S(2)}) collective-permute-start(bf16[48,1536]{1,0:T(8,128)(2,1)S(1)} %get-tuple-element.116), channel_id=1, source_target_pairs={{0,128},{1,129},{2,130},{3,131},{4,132},{5,133},{6,134},{7,135},{8... | collective-permute-start | bytes 442376 | tf_op jit(solution)/shard_map/ppermute | solution.py:42
  62.8 1.6 %collective-permute-start.17 = (bf16[48,1536]{1,0:T(8,128)(2,1)S(1)}, bf16[48,1536]{1,0:T(8,128)(2,1)S(1)}, u32[]{:S(2)}, u32[]{:S(2)}) collective-permute-start(bf16[48,1536]{1,0:T(8,128)(2,1)S(1)} %get-tuple-element.117), channel_id=1, source_target_pairs={{0,192},{1,193},{2,194},{3,195},{4,196},{5,197},{6,198},{7,199},{8... | collective-permute-start | bytes 442376 | tf_op jit(solution)/shard_map/ppermute | solution.py:42
  64.3 1.9 %collective-permute-start.18 = (bf16[48,1536]{1,0:T(8,128)(2,1)S(1)}, bf16[48,1536]{1,0:T(8,128)(2,1)S(1)}, u32[]{:S(2)}, u32[]{:S(2)}) collective-permute-start(bf16[48,1536]{1,0:T(8,128)(2,1)S(1)} %get-tuple-element.118), channel_id=1, source_target_pairs={{0,64},{1,65},{2,66},{3,67},{4,68},{5,69},{6,70},{7,71},{8,72},{9,... | collective-permute-start | bytes 442376 | tf_op jit(solution)/shard_map/ppermute | solution.py:42
  66.2 0.0 collective-permute-done.15
  66.2 0.1 fusion.13.refs_0_
  66.3 0.0 copy-start
  66.3 0.8 slice.134
  67.1 2.7 %collective-permute-start.12 = (bf16[128,1536]{1,0:T(8,128)(2,1)}, bf16[128,1536]{1,0:T(8,128)(2,1)}, u32[]{:S(2)}, u32[]{:S(2)}) collective-permute-start(bf16[128,1536]{1,0:T(8,128)(2,1)} %slice.134), channel_id=1, source_target_pairs={{0,15},{1,0},{2,1},{3,2},{4,3},{5,4},{6,5},{7,6},{8,7},{9,8},{10,9... | collective-permute-start | bytes 1179656 | tf_op jit(solution)/shard_map/ppermute | solution.py:31
  69.8 0.0 collective-permute-done.16
  69.8 0.0 collective-permute-done.17
  69.8 0.1 fusion.10.refs_1_
  69.9 0.8 pieces.1
  70.7 5.5 %all-to-all-start = ((bf16[8,144,128]{2,1,0:T(8,128)(2,1)}), bf16[8,144,128]{2,1,0:T(8,128)(2,1)S(1)}, u32[]{:S(2)}, u32[]{:S(2)}) async-start(bf16[8,144,128]{2,1,0:T(8,128)(2,1)} %pieces.1), calls=%async_computation | async-start | bytes 589824 | tf_op jit(solution)/shard_map/all_to_all | solution.py:568
  76.2 3.1 %collective-permute-done.12 = bf16[128,1536]{1,0:T(8,128)(2,1)} collective-permute-done((bf16[128,1536]{1,0:T(8,128)(2,1)}, bf16[128,1536]{1,0:T(8,128)(2,1)}, u32[]{:S(2)}, u32[]{:S(2)}) %collective-permute-start.12) | collective-permute-done | bytes 393248 | tf_op jit(solution)/shard_map/ppermute | solution.py:31
  79.3 1.5 %convert_reduce_fusion = (f32[256]{0:T(256)S(1)}, f32[256]{0:T(256)S(1)}, bf16[256,1536]{1,0:T(8,128)(2,1)S(1)}) fusion(f32[256]{0:T(256)S(1)} %bitcast.49, f32[256]{0:T(256)S(1)} %bitcast.47, bf16[256,1536]{1,0:T(8,128)(2,1)S(1)} %bitcast.45, bf16[128,1536]{1,0:T(8,128)(2,1)} %collective-permute-done.12, f32[384,1536]{1,0:T(8,128)S(1)} %fusion.30), kind=kLoop, calls=%fused_computation.5 | loop fusion | flops 3931648 | bytes 3543040 | tf_op jit(solution)/shard_map/reduce_sum | solution.py:118
  80.8 1.4 %fusion.7 = bf16[1,256,1536]{2,1,0:T(8,128)(2,1)} fusion(bf16[256,1536]{1,0:T(8,128)(2,1)S(1)} %bitcast.46, bf16[256,1536]{1,0:T(8,128)(2,1)S(1)} %get-tuple-element.121, f32[256]{0:T(256)S(1)} %broadcast_multiply_fusion, f32[256]{0:T(256)S(1)} %bitcast.48, f32[256]{0:T(256)S(1)} %broadcast_multiply_fusion.1, f32[256]{0:T(256)S(1)} %bitcast.50), kind=kLoop, calls=%fused_computation.14 | loop fusion | flops 3538944 | bytes 2363392 | tf_op jit(solution)/shard_map/broadcast_in_dim | solution.py:576
  82.2 4.8 %all-to-all-done.in_ref = bf16[8,144,128]{2,1,0:T(8,128)(2,1)S(1)} async-done(((bf16[8,144,128]{2,1,0:T(8,128)(2,1)}), bf16[8,144,128]{2,1,0:T(8,128)(2,1)S(1)}, u32[]{:S(2)}, u32[]{:S(2)}) %all-to-all-start) | async-done | bytes 294944 | tf_op jit(solution)/shard_map/all_to_all | solution.py:568
  87.1 0.7 total.1
  (18 shorter events, 0.1 us)
Async XLA Ops:
  1.7 16.0 %collective-permute-start = (bf16[128,1536]{1,0:T(8,128)(2,1)S(1)}, bf16[128,1536]{1,0:T(8,128)(2,1)S(1)}, u32[]{:S(2)}, u32[]{:S(2)}) collective-permute-start(bf16[128,1536]{1,0:T(8,128)(2,1)S(1)} %last_rows.1), channel_id=1, source_target_pairs={{0,1},{1,2},{2,3},{3,4},{4,5},{5,6},{6,7},{7,8},{8,9},{9,10},{10,1... | collective-permute-start | bytes 1179656 | tf_op jit(solution)/shard_map/ppermute | solution.py:31
  13.9 10.7 %collective-permute-start.2 = (bf16[768,512]{1,0:T(8,128)(2,1)S(1)}, bf16[768,512]{1,0:T(8,128)(2,1)S(1)}, u32[]{:S(2)}, u32[]{:S(2)}) collective-permute-start(bf16[768,512]{1,0:T(8,128)(2,1)S(1)} %get-tuple-element.71), channel_id=1, source_target_pairs={{0,16},{1,17},{2,18},{3,19},{4,20},{5,21},{6,22},{7,23},{8,24},{9,... | collective-permute-start | bytes 2359304 | tf_op jit(solution)/shard_map/ppermute | solution.py:42
  22.3 2.6 %collective-permute-start.1 = (bf16[2,256,768]{2,1,0:T(8,128)(2,1)S(1)}, bf16[2,256,768]{2,1,0:T(8,128)(2,1)S(1)}, u32[]{:S(2)}, u32[]{:S(2)}) collective-permute-start(bf16[2,256,768]{2,1,0:T(8,128)(2,1)S(1)} %get-tuple-element.70.first_ref), channel_id=1, source_target_pairs={{0,16},{1,17},{2,18},{3,19},{4,20},{5,21},{6,22},{7,23},{8,24},{9,... | collective-permute-start | bytes 2359304 | tf_op jit(solution)/shard_map/ppermute | solution.py:42
  24.9 5.2 %collective-permute-start.5 = (bf16[2,384,896]{2,1,0:T(8,128)(2,1)S(1)}, bf16[2,384,896]{2,1,0:T(8,128)(2,1)S(1)}, u32[]{:S(2)}, u32[]{:S(2)}) collective-permute-start(bf16[2,384,896]{2,1,0:T(8,128)(2,1)S(1)} %get-tuple-element.82.second_ref), channel_id=1, source_target_pairs={{0,16},{1,17},{2,18},{3,19},{4,20},{5,21},{6,22},{7,23},{8,24},{9,... | collective-permute-start | bytes 4128776 | tf_op jit(solution)/shard_map/ppermute | solution.py:42
  26.9 15.5 %collective-permute-start.3 = (bf16[8,48,768]{2,1,0:T(8,128)(2,1)S(1)}, bf16[8,48,768]{2,1,0:T(8,128)(2,1)S(1)}, u32[]{:S(2)}, u32[]{:S(2)}) collective-permute-start(bf16[8,48,768]{2,1,0:T(8,128)(2,1)S(1)} %get-tuple-element.80), channel_id=1, source_target_pairs={{0,64},{1,65},{2,66},{3,67},{4,68},{5,69},{6,70},{7,71},{8,72},{9,... | collective-permute-start | bytes 1769480 | tf_op jit(solution)/shard_map/ppermute | solution.py:42
  27.5 15.8 %collective-permute-start.4 = (bf16[8,48,768]{2,1,0:T(8,128)(2,1)S(1)}, bf16[8,48,768]{2,1,0:T(8,128)(2,1)S(1)}, u32[]{:S(2)}, u32[]{:S(2)}) collective-permute-start(bf16[8,48,768]{2,1,0:T(8,128)(2,1)S(1)} %get-tuple-element.81), channel_id=1, source_target_pairs={{0,192},{1,193},{2,194},{3,195},{4,196},{5,197},{6,198},{7,199},{8... | collective-permute-start | bytes 1769480 | tf_op jit(solution)/shard_map/ppermute | solution.py:42
  30.0 22.0 %slice-start = ((s8[7077888]{0:T(1024)(128)(4,1)}), s8[4194304]{0:T(1024)(128)(4,1)S(1)}, s32[]{:S(2)}) async-start(s8[7077888]{0:T(1024)(128)(4,1)} %bitcast.51), calls=%async_computation.1 | async-start | bytes 8388608
  30.1 5.7 %copy-start.1 = (bf16[768,1536]{1,0:T(8,128)(2,1)S(1)}, bf16[768,1536]{1,0:T(8,128)(2,1)}, u32[]{:S(2)}) copy-start(bf16[768,1536]{1,0:T(8,128)(2,1)} %out_ref.1) | copy-start | bytes 7077892
  30.1 21.9 %slice-start.1 = ((s8[7077888]{0:T(1024)(128)(4,1)}), s8[2883584]{0:T(1024)(128)(4,1)S(1)}, s32[]{:S(2)}) async-start(s8[7077888]{0:T(1024)(128)(4,1)} %bitcast.51), calls=%async_computation.2 | async-start | bytes 5767168
  32.4 15.5 %collective-permute-start.6 = (bf16[8,48,768]{2,1,0:T(8,128)(2,1)S(1)}, bf16[8,48,768]{2,1,0:T(8,128)(2,1)S(1)}, u32[]{:S(2)}, u32[]{:S(2)}) collective-permute-start(bf16[8,48,768]{2,1,0:T(8,128)(2,1)S(1)} %get-tuple-element.91), channel_id=1, source_target_pairs={{0,1},{1,0},{2,3},{3,2},{4,5},{5,4},{6,7},{7,6},{8,9},{9,8},{10,11... | collective-permute-start | bytes 1769480 | tf_op jit(solution)/shard_map/ppermute | solution.py:42
  32.5 16.2 %collective-permute-start.7 = (bf16[8,48,768]{2,1,0:T(8,128)(2,1)S(1)}, bf16[8,48,768]{2,1,0:T(8,128)(2,1)S(1)}, u32[]{:S(2)}, u32[]{:S(2)}) collective-permute-start(bf16[8,48,768]{2,1,0:T(8,128)(2,1)S(1)} %get-tuple-element.92), channel_id=1, source_target_pairs={{0,33},{1,32},{2,35},{3,34},{4,37},{5,36},{6,39},{7,38},{8,41},{9,... | collective-permute-start | bytes 1769480 | tf_op jit(solution)/shard_map/ppermute | solution.py:42
  43.6 11.4 %collective-permute-start.10 = (bf16[4,48,768]{2,1,0:T(8,128)(2,1)S(1)}, bf16[4,48,768]{2,1,0:T(8,128)(2,1)S(1)}, u32[]{:S(2)}, u32[]{:S(2)}) collective-permute-start(bf16[4,48,768]{2,1,0:T(8,128)(2,1)S(1)} %get-tuple-element.104), channel_id=1, source_target_pairs={{0,192},{1,193},{2,194},{3,195},{4,196},{5,197},{6,198},{7,199},{8... | collective-permute-start | bytes 884744 | tf_op jit(solution)/shard_map/ppermute | solution.py:42
  45.4 9.5 %collective-permute-start.11 = (bf16[4,48,768]{2,1,0:T(8,128)(2,1)S(1)}, bf16[4,48,768]{2,1,0:T(8,128)(2,1)S(1)}, u32[]{:S(2)}, u32[]{:S(2)}) collective-permute-start(bf16[4,48,768]{2,1,0:T(8,128)(2,1)S(1)} %get-tuple-element.105), channel_id=1, source_target_pairs={{0,64},{1,65},{2,66},{3,67},{4,68},{5,69},{6,70},{7,71},{8,72},{9,... | collective-permute-start | bytes 884744 | tf_op jit(solution)/shard_map/ppermute | solution.py:42
  49.0 11.0 %collective-permute-start.8 = (bf16[4,48,768]{2,1,0:T(8,128)(2,1)S(1)}, bf16[4,48,768]{2,1,0:T(8,128)(2,1)S(1)}, u32[]{:S(2)}, u32[]{:S(2)}) collective-permute-start(bf16[4,48,768]{2,1,0:T(8,128)(2,1)S(1)} %get-tuple-element.97), channel_id=1, source_target_pairs={{0,33},{1,32},{2,35},{3,34},{4,37},{5,36},{6,39},{7,38},{8,41},{9,... | collective-permute-start | bytes 884744 | tf_op jit(solution)/shard_map/ppermute | solution.py:42
  52.0 9.4 %collective-permute-start.9 = (bf16[4,48,768]{2,1,0:T(8,128)(2,1)S(1)}, bf16[4,48,768]{2,1,0:T(8,128)(2,1)S(1)}, u32[]{:S(2)}, u32[]{:S(2)}) collective-permute-start(bf16[4,48,768]{2,1,0:T(8,128)(2,1)S(1)} %get-tuple-element.99), channel_id=1, source_target_pairs={{0,1},{1,0},{2,3},{3,2},{4,5},{5,4},{6,7},{7,6},{8,9},{9,8},{10,11... | collective-permute-start | bytes 884744 | tf_op jit(solution)/shard_map/ppermute | solution.py:42
  55.1 9.2 %collective-permute-start.13 = (bf16[48,1536]{1,0:T(8,128)(2,1)S(1)}, bf16[48,1536]{1,0:T(8,128)(2,1)S(1)}, u32[]{:S(2)}, u32[]{:S(2)}) collective-permute-start(bf16[48,1536]{1,0:T(8,128)(2,1)S(1)} %get-tuple-element.113), channel_id=1, source_target_pairs={{0,32},{1,33},{2,34},{3,35},{4,36},{5,37},{6,38},{7,39},{8,40},{9,... | collective-permute-start | bytes 442376 | tf_op jit(solution)/shard_map/ppermute | solution.py:42
  57.0 9.2 %collective-permute-start.14 = (bf16[48,1536]{1,0:T(8,128)(2,1)S(1)}, bf16[48,1536]{1,0:T(8,128)(2,1)S(1)}, u32[]{:S(2)}, u32[]{:S(2)}) collective-permute-start(bf16[48,1536]{1,0:T(8,128)(2,1)S(1)} %get-tuple-element.114), channel_id=1, source_target_pairs={{0,33},{1,32},{2,35},{3,34},{4,37},{5,36},{6,39},{7,38},{8,41},{9,... | collective-permute-start | bytes 442376 | tf_op jit(solution)/shard_map/ppermute | solution.py:42
  59.9 6.3 %collective-permute-start.15 = (bf16[48,1536]{1,0:T(8,128)(2,1)S(1)}, bf16[48,1536]{1,0:T(8,128)(2,1)S(1)}, u32[]{:S(2)}, u32[]{:S(2)}) collective-permute-start(bf16[48,1536]{1,0:T(8,128)(2,1)S(1)} %get-tuple-element.115), channel_id=1, source_target_pairs={{0,1},{1,0},{2,3},{3,2},{4,5},{5,4},{6,7},{7,6},{8,9},{9,8},{10,11... | collective-permute-start | bytes 442376 | tf_op jit(solution)/shard_map/ppermute | solution.py:42
  61.4 8.4 %collective-permute-start.16 = (bf16[48,1536]{1,0:T(8,128)(2,1)S(1)}, bf16[48,1536]{1,0:T(8,128)(2,1)S(1)}, u32[]{:S(2)}, u32[]{:S(2)}) collective-permute-start(bf16[48,1536]{1,0:T(8,128)(2,1)S(1)} %get-tuple-element.116), channel_id=1, source_target_pairs={{0,128},{1,129},{2,130},{3,131},{4,132},{5,133},{6,134},{7,135},{8... | collective-permute-start | bytes 442376 | tf_op jit(solution)/shard_map/ppermute | solution.py:42
  62.8 7.0 %collective-permute-start.17 = (bf16[48,1536]{1,0:T(8,128)(2,1)S(1)}, bf16[48,1536]{1,0:T(8,128)(2,1)S(1)}, u32[]{:S(2)}, u32[]{:S(2)}) collective-permute-start(bf16[48,1536]{1,0:T(8,128)(2,1)S(1)} %get-tuple-element.117), channel_id=1, source_target_pairs={{0,192},{1,193},{2,194},{3,195},{4,196},{5,197},{6,198},{7,199},{8... | collective-permute-start | bytes 442376 | tf_op jit(solution)/shard_map/ppermute | solution.py:42
  64.3 5.5 %collective-permute-start.18 = (bf16[48,1536]{1,0:T(8,128)(2,1)S(1)}, bf16[48,1536]{1,0:T(8,128)(2,1)S(1)}, u32[]{:S(2)}, u32[]{:S(2)}) collective-permute-start(bf16[48,1536]{1,0:T(8,128)(2,1)S(1)} %get-tuple-element.118), channel_id=1, source_target_pairs={{0,64},{1,65},{2,66},{3,67},{4,68},{5,69},{6,70},{7,71},{8,72},{9,... | collective-permute-start | bytes 442376 | tf_op jit(solution)/shard_map/ppermute | solution.py:42
  66.3 13.0 %copy-start = (bf16[1,256,1536]{2,1,0:T(8,128)(2,1)S(1)}, bf16[1,256,1536]{2,1,0:T(8,128)(2,1)}, u32[]{:S(2)}) copy-start(bf16[1,256,1536]{2,1,0:T(8,128)(2,1)} %param.6) | copy-start | bytes 2359300
  67.1 12.2 %collective-permute-start.12 = (bf16[128,1536]{1,0:T(8,128)(2,1)}, bf16[128,1536]{1,0:T(8,128)(2,1)}, u32[]{:S(2)}, u32[]{:S(2)}) collective-permute-start(bf16[128,1536]{1,0:T(8,128)(2,1)} %slice.134), channel_id=1, source_target_pairs={{0,15},{1,0},{2,1},{3,2},{4,3},{5,4},{6,5},{7,6},{8,7},{9,8},{10,9... | collective-permute-start | bytes 1179656 | tf_op jit(solution)/shard_map/ppermute | solution.py:31
  70.7 16.3 %all-to-all-start = ((bf16[8,144,128]{2,1,0:T(8,128)(2,1)}), bf16[8,144,128]{2,1,0:T(8,128)(2,1)S(1)}, u32[]{:S(2)}, u32[]{:S(2)}) async-start(bf16[8,144,128]{2,1,0:T(8,128)(2,1)} %pieces.1), calls=%async_computation | async-start | bytes 589824 | tf_op jit(solution)/shard_map/all_to_all | solution.py:568

commit v10 on v9

--- a/solution.py
+++ b/solution.py
@@ -530,7 +530,7 @@
     query_grad = jnp.concatenate([own[1], jnp.zeros((CONTEXT, inner), BF16)], axis=0)
     projected_grad = jnp.concatenate([query_grad, grads[0, :, :inner], grads[1, :, :inner]], axis=1)
     attended, projected_grad, send_b = lax.optimization_barrier((own[0], projected_grad, send_b))
-    block_out = dot(attended, w_out).astype(BF16)
+    normed_grad = dot(projected_grad, w_qkv, NT)
     def second_ring(kept, gots, n, *after):
         group = jnp.concatenate([plus(kept[r], gots[r]) for r in range(2)], axis=-1)
         slots, *after = lax.optimization_barrier(([group[slot] for slot in range(1, 4)], *after))
@@ -539,14 +539,14 @@
 
     gots_a = [to_device(send_a[r], ROUTES[r][0]) for r in range(2)]
     gots_b = [to_device(send_b[r], ROUTES[2 + r][0]) for r in range(2)]
-    gots_a, block_out = lax.optimization_barrier((gots_a, block_out))
+    gots_a, normed_grad = lax.optimization_barrier((gots_a, normed_grad))
     kept_a, sent_a = halve(keep_a, gots_a)
     gots_a = [to_device(sent_a[r], ROUTES[r][1]) for r in range(2)]
     kept_b, sent_b = halve(keep_b, gots_b)
-    projected_grad, sent_b = lax.optimization_barrier((projected_grad, sent_b))
+    attended, sent_b = lax.optimization_barrier((attended, sent_b))
     gots_b = [to_device(sent_b[r], ROUTES[2 + r][1]) for r in range(2)]
-    normed_grad = dot(projected_grad, w_qkv, NT)
-    gots_a, normed_grad = lax.optimization_barrier((gots_a, normed_grad))
+    block_out = dot(attended, w_out).astype(BF16)
+    gots_a, block_out = lax.optimization_barrier((gots_a, block_out))
     first_group, = second_ring(kept_a, gots_a, 0)
     second_group, normed_grad = second_ring(kept_b, gots_b, 1, normed_grad)
     groups = [first_group, second_group]

time: 88.7 us -> 88.6 us (level)
  waiting for transfers between devices: 19.7 us -> 21.4 us
  starting transfers between devices: 33.7 us -> 32.7 us
    ppermute x17, waiting for transfers between devices: 8.16 us -> 9.81 us  [to_device(): return lax.ppermute(value, ('dp', 'seq'), pairs)]
    ppermute x2, starting transfers between devices: 4.24 us -> 3.09 us  [from_behind(): lax.ppermute(value, axis, [(i, (i + by) % peers) for i in range(peers)])]
  transfers between devices with their start and end apart: 20 -> 20, of which waited for: 8 -> 11; matrix products, arithmetic and copies ran while one was open for 10% -> 10% of each run, Pallas kernels for 25% -> 25%
where the time goes in v10:
time: 88.6 us; the launch traced here: 88.3 us
  starting transfers between devices  32.7 us (37%)
  Pallas kernels  23.6 us (27%)
  waiting for transfers between devices  21.4 us (24%)
  matrix products  4.58 us (5%)
  other arithmetic  3.64 us (4%)
  between operations  1.52 us (2%)
  local copies, waits for them, and re-layouts  0.95 us (1%)
    ppermute x17, starting transfers between devices, to_device(): return lax.ppermute(value, ('dp', 'seq'), pairs)  23.8 us
    pallas_call x1, Pallas kernels, front(): pl.pallas_call(front_kernel, in_specs=[SMEM_SPEC] + [HBM_SPEC] * 6, out_s...  9.88 us
    ppermute x17, waiting for transfers between devices, to_device(): return lax.ppermute(value, ('dp', 'seq'), pairs)  9.81 us
    ppermute x2, waiting for transfers between devices, from_behind(): lax.ppermute(value, axis, [(i, (i + by) % peers) for i in range(peers)])  6.18 us
    all_to_all x1, starting transfers between devices, on_device(): lax.all_to_all(shares, 'seq', 0, 0, axis_index_groups=rings, tiled=True)  5.82 us
    all_to_all x1, waiting for transfers between devices, on_device(): lax.all_to_all(shares, 'seq', 0, 0, axis_index_groups=rings, tiled=True)  5.37 us
    pallas_call x1, Pallas kernels, early_tile(): pl.pallas_call(early_kernel, in_specs=[SMEM_SPEC, HBM_SPEC] + [VMEM_SPEC]...  4.69 us
    dot_general x2, matrix products, dot(): return lax.dot_general(a, b, dims, preferred_element_type=F32)  4.58 us
  transfers between devices with their start and end apart: 20, of which 11 were waited for; matrix products, arithmetic and copies ran while one was open for 10% of the time, Pallas kernels for 25%

profile of v10, /device:TPU:8, one launch (start us, length us, event | category | flops | bytes accessed | tf_op | source)
XLA Modules:
  0.0 88.3 jit_solution(6551000229830515465)
XLA Ops:
  0.6 1.0 %last_rows.1 = bf16[128,1536]{1,0:T(8,128)(2,1)S(1)} custom-call(bf16[256,1536]{1,0:T(8,128)(2,1)} %bitcast.43), custom_call_target="tpu_custom_call" | custom-call | flops 1 | bytes 1 | tf_op jit(solution)/shard_map/last_rows/pallas_call | solution.py:170
  1.7 1.6 %collective-permute-start = (bf16[128,1536]{1,0:T(8,128)(2,1)S(1)}, bf16[128,1536]{1,0:T(8,128)(2,1)S(1)}, u32[]{:S(2)}, u32[]{:S(2)}) collective-permute-start(bf16[128,1536]{1,0:T(8,128)(2,1)S(1)} %last_rows.1), channel_id=1, source_target_pairs={{0,1},{1,2},{2,3},{3,4},{4,5},{5,6},{6,7},{7,8},{8,9},{9,10},{10,1... | collective-permute-start | bytes 1179656 | tf_op jit(solution)/shard_map/ppermute | solution.py:31
  3.3 0.1 pad_add_fusion.1.places
  4.0 9.9 %front.1 = (bf16[256,2304]{1,0:T(8,128)(2,1)S(1)}, bf16[256,768]{1,0:T(8,128)(2,1)S(1)}, bf16[768,512]{1,0:T(8,128)(2,1)S(1)}, bf16[768,512]{1,0:T(8,128)(2,1)S(...) custom-call(s32[2]{0:T(128)S(1)} %pad_add_fusion.1.places, ...), custom_call_target="tpu_custom_call" | custom-call | flops 3623878656 | bytes 11796480 | tf_op jit(solution)/shard_map/front/pallas_call | solution.py:251
  13.9 0.1 collective-permute-start.2
  14.0 3.6 %collective-permute-done.frames_ref = bf16[128,1536]{1,0:T(8,128)(2,1)S(1)} collective-permute-done((bf16[128,1536]{1,0:T(8,128)(2,1)S(1)}, bf16[128,1536]{1,0:T(8,128)(2,1)S(1)}, u32[]{:S(2)}, u32[]{:S(2)}) %collective-permute-start) | collective-permute-done | bytes 393248 | tf_op jit(solution)/shard_map/ppermute | solution.py:31
  17.6 4.7 %attention_early.1 = (bf16[2,256,768]{2,1,0:T(8,128)(2,1)S(1)}, bf16[2,384,896]{2,1,0:T(8,128)(2,1)S(1)}, bf16[768,128]{1,0:T(8,128)(2,1)S(1)}) custom-call(s32[2]{0:T(128)S(1)} %pad_add_fusion.1.places, s32[1]{0:T(128)S(6)} %copy.9.lengths_ref, bf16[384,384]{1,0:T(8,128)(2,1)S(1)} %get-tuple-element.64.order_ref, ...), custom_call_target="tpu_custom_call" | custom-call | flops 704643072 | bytes 1572864 | tf_op jit(solution)/shard_map/attention_early/pallas_call | solution.py:367
  22.3 0.3 collective-permute-start.1
  22.6 2.0 %own_sums.1 = (f32[2,768,768]{2,1,0:T(8,128)S(1)}, f32[2,768,768]{2,1,0:T(8,128)S(1)}) custom-call(bf16[768,512]{1,0:T(8,128)(2,1)S(1)} %get-tuple-element.72.left_ref, bf16[768,128]{1,0:T(8,128)(2,1)S(1)} %get-tuple-element.73.behind_ref, bf16[2,256,768]{2,1,0:T(8,128)(2,1)S(1)} %get-tuple-element.70.first_ref, ...), custom_call_target="tpu_custom_call" | custom-call | flops 4000000000 | bytes 1 | tf_op jit(solution)/shard_map/own_sums/pallas_call | solution.py:407
  24.6 0.3 collective-permute-done.1.right_other_ref
  24.9 0.3 collective-permute-start.5
  25.2 0.1 slice_bitcast_fusion.2
  25.3 1.6 %first_wave.1 = (bf16[8,48,768]{2,1,0:T(8,128)(2,1)S(1)}, bf16[8,48,768]{2,1,0:T(8,128)(2,1)S(1)}, bf16[8,48,768]{2,1,0:T(8,128)(2,1)S(1)}, bf16[8,48,768]{2,1,0:T(8,128)(2,1)S(1)}) custom-call(s32[4,16]{1,0:T(4,128)S(1)} %pad_add_fusion.chunks, bf16[768,512]{1,0:T(8,128)(2,1)S(1)} %collective-permute-done.2.left_other_ref, ...), custom_call_target="tpu_custom_call" | custom-call | flops 1 | bytes 1 | tf_op jit(solution)/shard_map/first_wave/pallas_call | solution.py:438
  27.0 0.5 collective-permute-start.3
  27.5 2.4 %collective-permute-start.4 = (bf16[8,48,768]{2,1,0:T(8,128)(2,1)S(1)}, bf16[8,48,768]{2,1,0:T(8,128)(2,1)S(1)}, u32[]{:S(2)}, u32[]{:S(2)}) collective-permute-start(bf16[8,48,768]{2,1,0:T(8,128)(2,1)S(1)} %get-tuple-element.83), channel_id=1, source_target_pairs={{0,192},{1,193},{2,194},{3,195},{4,196},{5,197},{6,198},{7,199},{8... | collective-permute-start | bytes 1769480 | tf_op jit(solution)/shard_map/ppermute | solution.py:42
  29.9 0.1 slice_bitcast_fusion.1
  30.0 0.0 slice-start
  30.0 0.1 fusion.2
  30.1 0.0 slice-start.1
  30.1 0.0 collective-permute-done.5.right_other_ref
  30.1 2.3 %second_wave.1 = (bf16[8,48,768]{2,1,0:T(8,128)(2,1)S(1)}, bf16[8,48,768]{2,1,0:T(8,128)(2,1)S(1)}, bf16[8,48,768]{2,1,0:T(8,128)(2,1)S(1)}, bf16[8,48,768]{2,1,0:T(8,128)(2,1)S(1)}) custom-call(s32[4,16]{1,0:T(4,128)S(1)} %pad_add_fusion.chunks, bf16[768,512]{1,0:T(8,128)(2,1)S(1)} %collective-permute-done.2.left_other_ref, ...), custom_call_target="tpu_custom_call" | custom-call | flops 3000000000 | bytes 1 | tf_op jit(solution)/shard_map/second_wave/pallas_call | solution.py:438
  32.4 0.1 collective-permute-start.8
  32.5 3.3 %collective-permute-start.9 = (bf16[8,48,768]{2,1,0:T(8,128)(2,1)S(1)}, bf16[8,48,768]{2,1,0:T(8,128)(2,1)S(1)}, u32[]{:S(2)}, u32[]{:S(2)}) collective-permute-start(bf16[8,48,768]{2,1,0:T(8,128)(2,1)S(1)} %get-tuple-element.97), channel_id=1, source_target_pairs={{0,33},{1,32},{2,35},{3,34},{4,37},{5,36},{6,39},{7,38},{8,41},{9,... | collective-permute-start | bytes 1769480 | tf_op jit(solution)/shard_map/ppermute | solution.py:42
  35.8 2.9 %fusion.30 = f32[384,1536]{1,0:T(8,128)S(1)} fusion(bf16[384,2304]{1,0:T(8,128)(2,1)S(1)} %fusion.2, bf16[1536,2304]{1,0:T(8,128)(2,1)S(1)} %bitcast.52), kind=kOutput, calls=%fused_computation.76 | convolution fusion | flops 2717908992 | bytes 11206656 | tf_op jit(solution)/shard_map/dot_general | solution.py:26
  38.8 3.7 %collective-permute-done.3.refs_2_ = bf16[8,48,768]{2,1,0:T(8,128)(2,1)S(1)} collective-permute-done((bf16[8,48,768]{2,1,0:T(8,128)(2,1)S(1)}, bf16[8,48,768]{2,1,0:T(8,128)(2,1)S(1)}, u32[]{:S(2)}, u32[]{:S(2)}) %collective-permute-start.3) | collective-permute-done | bytes 589856 | tf_op jit(solution)/shard_map/ppermute | solution.py:42
  42.4 0.8 collective-permute-done.4.refs_3_
  43.3 0.3 halve.2
  43.6 0.0 copy-start.1
  43.6 1.8 %collective-permute-start.6 = (bf16[4,48,768]{2,1,0:T(8,128)(2,1)S(1)}, bf16[4,48,768]{2,1,0:T(8,128)(2,1)S(1)}, u32[]{:S(2)}, u32[]{:S(2)}) collective-permute-start(bf16[4,48,768]{2,1,0:T(8,128)(2,1)S(1)} %get-tuple-element.91), channel_id=1, source_target_pairs={{0,192},{1,193},{2,194},{3,195},{4,196},{5,197},{6,198},{7,199},{8... | collective-permute-start | bytes 884744 | tf_op jit(solution)/shard_map/ppermute | solution.py:42
  45.4 2.6 %collective-permute-start.7 = (bf16[4,48,768]{2,1,0:T(8,128)(2,1)S(1)}, bf16[4,48,768]{2,1,0:T(8,128)(2,1)S(1)}, u32[]{:S(2)}, u32[]{:S(2)}) collective-permute-start(bf16[4,48,768]{2,1,0:T(8,128)(2,1)S(1)} %get-tuple-element.92), channel_id=1, source_target_pairs={{0,64},{1,65},{2,66},{3,67},{4,68},{5,69},{6,70},{7,71},{8,72},{9,... | collective-permute-start | bytes 884744 | tf_op jit(solution)/shard_map/ppermute | solution.py:42
  48.0 0.0 collective-permute-done.8.refs_2_
  48.0 0.7 collective-permute-done.9.refs_3_
  48.7 0.3 halve.3
  49.0 3.0 %collective-permute-start.10 = (bf16[4,48,768]{2,1,0:T(8,128)(2,1)S(1)}, bf16[4,48,768]{2,1,0:T(8,128)(2,1)S(1)}, u32[]{:S(2)}, u32[]{:S(2)}) collective-permute-start(bf16[4,48,768]{2,1,0:T(8,128)(2,1)S(1)} %get-tuple-element.104), channel_id=1, source_target_pairs={{0,33},{1,32},{2,35},{3,34},{4,37},{5,36},{6,39},{7,38},{8,41},{9,... | collective-permute-start | bytes 884744 | tf_op jit(solution)/shard_map/ppermute | solution.py:42
  52.0 0.0 collective-permute-start.11
  52.0 1.7 %convolution_convert_fusion = bf16[256,1536]{1,0:T(8,128)(2,1)} fusion(bf16[256,768]{1,0:T(8,128)(2,1)S(1)} %get-tuple-element.100, bf16[768,1536]{1,0:T(8,128)(2,1)S(1)} %copy-done.1), kind=kOutput, calls=%fused_computation.2 | convolution fusion | flops 604372992 | bytes 3538944 | tf_op jit(solution)/shard_map/dot_general | solution.py:26
  53.6 0.0 collective-permute-done.6
  53.6 0.2 collective-permute-done.7
  53.9 0.1 add_convert_fusion.1
  53.9 0.1 add_convert_fusion.2
  54.1 2.8 %collective-permute-start.13 = (bf16[48,1536]{1,0:T(8,128)(2,1)S(1)}, bf16[48,1536]{1,0:T(8,128)(2,1)S(1)}, u32[]{:S(2)}, u32[]{:S(2)}) collective-permute-start(bf16[48,1536]{1,0:T(8,128)(2,1)S(1)} %get-tuple-element.113), channel_id=1, source_target_pairs={{0,32},{1,33},{2,34},{3,35},{4,36},{5,37},{6,38},{7,39},{8,40},{9,... | collective-permute-start | bytes 442376 | tf_op jit(solution)/shard_map/ppermute | solution.py:42
  56.9 1.7 %collective-permute-start.14 = (bf16[48,1536]{1,0:T(8,128)(2,1)S(1)}, bf16[48,1536]{1,0:T(8,128)(2,1)S(1)}, u32[]{:S(2)}, u32[]{:S(2)}) collective-permute-start(bf16[48,1536]{1,0:T(8,128)(2,1)S(1)} %get-tuple-element.114), channel_id=1, source_target_pairs={{0,33},{1,32},{2,35},{3,34},{4,37},{5,36},{6,39},{7,38},{8,41},{9,... | collective-permute-start | bytes 442376 | tf_op jit(solution)/shard_map/ppermute | solution.py:42
  58.6 0.0 collective-permute-start.15
  58.6 1.2 %collective-permute-done.10 = bf16[4,48,768]{2,1,0:T(8,128)(2,1)S(1)} collective-permute-done((bf16[4,48,768]{2,1,0:T(8,128)(2,1)S(1)}, bf16[4,48,768]{2,1,0:T(8,128)(2,1)S(1)}, u32[]{:S(2)}, u32[]{:S(2)}) %collective-permute-start.10) | collective-permute-done | bytes 294944 | tf_op jit(solution)/shard_map/ppermute | solution.py:42
  59.8 0.1 add_convert_fusion.4
  59.9 2.1 %collective-permute-done.11 = bf16[4,48,768]{2,1,0:T(8,128)(2,1)S(1)} collective-permute-done((bf16[4,48,768]{2,1,0:T(8,128)(2,1)S(1)}, bf16[4,48,768]{2,1,0:T(8,128)(2,1)S(1)}, u32[]{:S(2)}, u32[]{:S(2)}) %collective-permute-start.11) | collective-permute-done | bytes 294944 | tf_op jit(solution)/shard_map/ppermute | solution.py:42
  61.9 0.1 add_convert_fusion.3
  62.0 1.3 %collective-permute-start.16 = (bf16[48,1536]{1,0:T(8,128)(2,1)S(1)}, bf16[48,1536]{1,0:T(8,128)(2,1)S(1)}, u32[]{:S(2)}, u32[]{:S(2)}) collective-permute-start(bf16[48,1536]{1,0:T(8,128)(2,1)S(1)} %get-tuple-element.116), channel_id=1, source_target_pairs={{0,128},{1,129},{2,130},{3,131},{4,132},{5,133},{6,134},{7,135},{8... | collective-permute-start | bytes 442376 | tf_op jit(solution)/shard_map/ppermute | solution.py:42
  63.3 1.6 %collective-permute-start.17 = (bf16[48,1536]{1,0:T(8,128)(2,1)S(1)}, bf16[48,1536]{1,0:T(8,128)(2,1)S(1)}, u32[]{:S(2)}, u32[]{:S(2)}) collective-permute-start(bf16[48,1536]{1,0:T(8,128)(2,1)S(1)} %get-tuple-element.117), channel_id=1, source_target_pairs={{0,192},{1,193},{2,194},{3,195},{4,196},{5,197},{6,198},{7,199},{8... | collective-permute-start | bytes 442376 | tf_op jit(solution)/shard_map/ppermute | solution.py:42
  64.9 1.9 %collective-permute-start.18 = (bf16[48,1536]{1,0:T(8,128)(2,1)S(1)}, bf16[48,1536]{1,0:T(8,128)(2,1)S(1)}, u32[]{:S(2)}, u32[]{:S(2)}) collective-permute-start(bf16[48,1536]{1,0:T(8,128)(2,1)S(1)} %get-tuple-element.118), channel_id=1, source_target_pairs={{0,64},{1,65},{2,66},{3,67},{4,68},{5,69},{6,70},{7,71},{8,72},{9,... | collective-permute-start | bytes 442376 | tf_op jit(solution)/shard_map/ppermute | solution.py:42
  66.8 0.0 collective-permute-done.14
  66.8 0.1 fusion.13.refs_0_
  66.9 0.0 copy-start
  66.9 0.8 slice.134
  67.7 1.5 %collective-permute-start.12 = (bf16[128,1536]{1,0:T(8,128)(2,1)}, bf16[128,1536]{1,0:T(8,128)(2,1)}, u32[]{:S(2)}, u32[]{:S(2)}) collective-permute-start(bf16[128,1536]{1,0:T(8,128)(2,1)} %slice.134), channel_id=1, source_target_pairs={{0,15},{1,0},{2,1},{3,2},{4,3},{5,4},{6,5},{7,6},{8,7},{9,8},{10,9... | collective-permute-start | bytes 1179656 | tf_op jit(solution)/shard_map/ppermute | solution.py:31
  69.2 0.8 collective-permute-done.17
  70.1 0.1 fusion.10.refs_1_
  70.2 0.8 pieces.1
  71.0 5.8 %all-to-all-start = ((bf16[8,144,128]{2,1,0:T(8,128)(2,1)}), bf16[8,144,128]{2,1,0:T(8,128)(2,1)S(1)}, u32[]{:S(2)}, u32[]{:S(2)}) async-start(bf16[8,144,128]{2,1,0:T(8,128)(2,1)} %pieces.1), calls=%async_computation | async-start | bytes 589824 | tf_op jit(solution)/shard_map/all_to_all | solution.py:568
  76.8 2.5 %collective-permute-done.12 = bf16[128,1536]{1,0:T(8,128)(2,1)} collective-permute-done((bf16[128,1536]{1,0:T(8,128)(2,1)}, bf16[128,1536]{1,0:T(8,128)(2,1)}, u32[]{:S(2)}, u32[]{:S(2)}) %collective-permute-start.12) | collective-permute-done | bytes 393248 | tf_op jit(solution)/shard_map/ppermute | solution.py:31
  79.3 1.5 %convert_reduce_fusion = (f32[256]{0:T(256)S(1)}, f32[256]{0:T(256)S(1)}, bf16[256,1536]{1,0:T(8,128)(2,1)S(1)}) fusion(f32[256]{0:T(256)S(1)} %bitcast.49, f32[256]{0:T(256)S(1)} %bitcast.47, bf16[256,1536]{1,0:T(8,128)(2,1)S(1)} %bitcast.45, bf16[128,1536]{1,0:T(8,128)(2,1)} %collective-permute-done.12, f32[384,1536]{1,0:T(8,128)S(1)} %fusion.30), kind=kLoop, calls=%fused_computation.5 | loop fusion | flops 3931648 | bytes 3543040 | tf_op jit(solution)/shard_map/reduce_sum | solution.py:118
  80.8 1.4 %fusion.7 = bf16[1,256,1536]{2,1,0:T(8,128)(2,1)} fusion(bf16[256,1536]{1,0:T(8,128)(2,1)S(1)} %bitcast.46, bf16[256,1536]{1,0:T(8,128)(2,1)S(1)} %get-tuple-element.121, f32[256]{0:T(256)S(1)} %broadcast_multiply_fusion, f32[256]{0:T(256)S(1)} %bitcast.48, f32[256]{0:T(256)S(1)} %broadcast_multiply_fusion.1, f32[256]{0:T(256)S(1)} %bitcast.50), kind=kLoop, calls=%fused_computation.14 | loop fusion | flops 3538944 | bytes 2363392 | tf_op jit(solution)/shard_map/broadcast_in_dim | solution.py:576
  82.3 5.4 %all-to-all-done.in_ref = bf16[8,144,128]{2,1,0:T(8,128)(2,1)S(1)} async-done(((bf16[8,144,128]{2,1,0:T(8,128)(2,1)}), bf16[8,144,128]{2,1,0:T(8,128)(2,1)S(1)}, u32[]{:S(2)}, u32[]{:S(2)}) %all-to-all-start) | async-done | bytes 294944 | tf_op jit(solution)/shard_map/all_to_all | solution.py:568
  87.6 0.7 total.1
  (18 shorter events, 0.1 us)
Async XLA Ops:
  1.7 16.0 %collective-permute-start = (bf16[128,1536]{1,0:T(8,128)(2,1)S(1)}, bf16[128,1536]{1,0:T(8,128)(2,1)S(1)}, u32[]{:S(2)}, u32[]{:S(2)}) collective-permute-start(bf16[128,1536]{1,0:T(8,128)(2,1)S(1)} %last_rows.1), channel_id=1, source_target_pairs={{0,1},{1,2},{2,3},{3,4},{4,5},{5,6},{6,7},{7,8},{8,9},{9,10},{10,1... | collective-permute-start | bytes 1179656 | tf_op jit(solution)/shard_map/ppermute | solution.py:31
  13.9 10.7 %collective-permute-start.2 = (bf16[768,512]{1,0:T(8,128)(2,1)S(1)}, bf16[768,512]{1,0:T(8,128)(2,1)S(1)}, u32[]{:S(2)}, u32[]{:S(2)}) collective-permute-start(bf16[768,512]{1,0:T(8,128)(2,1)S(1)} %get-tuple-element.71), channel_id=1, source_target_pairs={{0,16},{1,17},{2,18},{3,19},{4,20},{5,21},{6,22},{7,23},{8,24},{9,... | collective-permute-start | bytes 2359304 | tf_op jit(solution)/shard_map/ppermute | solution.py:42
  22.3 2.6 %collective-permute-start.1 = (bf16[2,256,768]{2,1,0:T(8,128)(2,1)S(1)}, bf16[2,256,768]{2,1,0:T(8,128)(2,1)S(1)}, u32[]{:S(2)}, u32[]{:S(2)}) collective-permute-start(bf16[2,256,768]{2,1,0:T(8,128)(2,1)S(1)} %get-tuple-element.70.first_ref), channel_id=1, source_target_pairs={{0,16},{1,17},{2,18},{3,19},{4,20},{5,21},{6,22},{7,23},{8,24},{9,... | collective-permute-start | bytes 2359304 | tf_op jit(solution)/shard_map/ppermute | solution.py:42
  24.9 5.2 %collective-permute-start.5 = (bf16[2,384,896]{2,1,0:T(8,128)(2,1)S(1)}, bf16[2,384,896]{2,1,0:T(8,128)(2,1)S(1)}, u32[]{:S(2)}, u32[]{:S(2)}) collective-permute-start(bf16[2,384,896]{2,1,0:T(8,128)(2,1)S(1)} %get-tuple-element.84.second_ref), channel_id=1, source_target_pairs={{0,16},{1,17},{2,18},{3,19},{4,20},{5,21},{6,22},{7,23},{8,24},{9,... | collective-permute-start | bytes 4128776 | tf_op jit(solution)/shard_map/ppermute | solution.py:42
  27.0 15.5 %collective-permute-start.3 = (bf16[8,48,768]{2,1,0:T(8,128)(2,1)S(1)}, bf16[8,48,768]{2,1,0:T(8,128)(2,1)S(1)}, u32[]{:S(2)}, u32[]{:S(2)}) collective-permute-start(bf16[8,48,768]{2,1,0:T(8,128)(2,1)S(1)} %get-tuple-element.82), channel_id=1, source_target_pairs={{0,64},{1,65},{2,66},{3,67},{4,68},{5,69},{6,70},{7,71},{8,72},{9,... | collective-permute-start | bytes 1769480 | tf_op jit(solution)/shard_map/ppermute | solution.py:42
  27.5 15.8 %collective-permute-start.4 = (bf16[8,48,768]{2,1,0:T(8,128)(2,1)S(1)}, bf16[8,48,768]{2,1,0:T(8,128)(2,1)S(1)}, u32[]{:S(2)}, u32[]{:S(2)}) collective-permute-start(bf16[8,48,768]{2,1,0:T(8,128)(2,1)S(1)} %get-tuple-element.83), channel_id=1, source_target_pairs={{0,192},{1,193},{2,194},{3,195},{4,196},{5,197},{6,198},{7,199},{8... | collective-permute-start | bytes 1769480 | tf_op jit(solution)/shard_map/ppermute | solution.py:42
  30.0 5.8 %slice-start = ((s8[7077888]{0:T(1024)(128)(4,1)}), s8[4194304]{0:T(1024)(128)(4,1)S(1)}, s32[]{:S(2)}) async-start(s8[7077888]{0:T(1024)(128)(4,1)} %bitcast.51), calls=%async_computation.1 | async-start | bytes 8388608
  30.1 5.7 %slice-start.1 = ((s8[7077888]{0:T(1024)(128)(4,1)}), s8[2883584]{0:T(1024)(128)(4,1)S(1)}, s32[]{:S(2)}) async-start(s8[7077888]{0:T(1024)(128)(4,1)} %bitcast.51), calls=%async_computation.2 | async-start | bytes 5767168
  32.4 15.5 %collective-permute-start.8 = (bf16[8,48,768]{2,1,0:T(8,128)(2,1)S(1)}, bf16[8,48,768]{2,1,0:T(8,128)(2,1)S(1)}, u32[]{:S(2)}, u32[]{:S(2)}) collective-permute-start(bf16[8,48,768]{2,1,0:T(8,128)(2,1)S(1)} %get-tuple-element.96), channel_id=1, source_target_pairs={{0,1},{1,0},{2,3},{3,2},{4,5},{5,4},{6,7},{7,6},{8,9},{9,8},{10,11... | collective-permute-start | bytes 1769480 | tf_op jit(solution)/shard_map/ppermute | solution.py:42
  32.5 16.1 %collective-permute-start.9 = (bf16[8,48,768]{2,1,0:T(8,128)(2,1)S(1)}, bf16[8,48,768]{2,1,0:T(8,128)(2,1)S(1)}, u32[]{:S(2)}, u32[]{:S(2)}) collective-permute-start(bf16[8,48,768]{2,1,0:T(8,128)(2,1)S(1)} %get-tuple-element.97), channel_id=1, source_target_pairs={{0,33},{1,32},{2,35},{3,34},{4,37},{5,36},{6,39},{7,38},{8,41},{9,... | collective-permute-start | bytes 1769480 | tf_op jit(solution)/shard_map/ppermute | solution.py:42
  43.6 8.4 %copy-start.1 = (bf16[768,1536]{1,0:T(8,128)(2,1)S(1)}, bf16[768,1536]{1,0:T(8,128)(2,1)}, u32[]{:S(2)}) copy-start(bf16[768,1536]{1,0:T(8,128)(2,1)} %out_ref.1) | copy-start | bytes 7077892
  43.6 10.1 %collective-permute-start.6 = (bf16[4,48,768]{2,1,0:T(8,128)(2,1)S(1)}, bf16[4,48,768]{2,1,0:T(8,128)(2,1)S(1)}, u32[]{:S(2)}, u32[]{:S(2)}) collective-permute-start(bf16[4,48,768]{2,1,0:T(8,128)(2,1)S(1)} %get-tuple-element.91), channel_id=1, source_target_pairs={{0,192},{1,193},{2,194},{3,195},{4,196},{5,197},{6,198},{7,199},{8... | collective-permute-start | bytes 884744 | tf_op jit(solution)/shard_map/ppermute | solution.py:42
  45.4 8.5 %collective-permute-start.7 = (bf16[4,48,768]{2,1,0:T(8,128)(2,1)S(1)}, bf16[4,48,768]{2,1,0:T(8,128)(2,1)S(1)}, u32[]{:S(2)}, u32[]{:S(2)}) collective-permute-start(bf16[4,48,768]{2,1,0:T(8,128)(2,1)S(1)} %get-tuple-element.92), channel_id=1, source_target_pairs={{0,64},{1,65},{2,66},{3,67},{4,68},{5,69},{6,70},{7,71},{8,72},{9,... | collective-permute-start | bytes 884744 | tf_op jit(solution)/shard_map/ppermute | solution.py:42
  49.0 10.8 %collective-permute-start.10 = (bf16[4,48,768]{2,1,0:T(8,128)(2,1)S(1)}, bf16[4,48,768]{2,1,0:T(8,128)(2,1)S(1)}, u32[]{:S(2)}, u32[]{:S(2)}) collective-permute-start(bf16[4,48,768]{2,1,0:T(8,128)(2,1)S(1)} %get-tuple-element.104), channel_id=1, source_target_pairs={{0,33},{1,32},{2,35},{3,34},{4,37},{5,36},{6,39},{7,38},{8,41},{9,... | collective-permute-start | bytes 884744 | tf_op jit(solution)/shard_map/ppermute | solution.py:42
  52.0 9.9 %collective-permute-start.11 = (bf16[4,48,768]{2,1,0:T(8,128)(2,1)S(1)}, bf16[4,48,768]{2,1,0:T(8,128)(2,1)S(1)}, u32[]{:S(2)}, u32[]{:S(2)}) collective-permute-start(bf16[4,48,768]{2,1,0:T(8,128)(2,1)S(1)} %get-tuple-element.106), channel_id=1, source_target_pairs={{0,1},{1,0},{2,3},{3,2},{4,5},{5,4},{6,7},{7,6},{8,9},{9,8},{10,11... | collective-permute-start | bytes 884744 | tf_op jit(solution)/shard_map/ppermute | solution.py:42
  54.1 10.9 %collective-permute-start.13 = (bf16[48,1536]{1,0:T(8,128)(2,1)S(1)}, bf16[48,1536]{1,0:T(8,128)(2,1)S(1)}, u32[]{:S(2)}, u32[]{:S(2)}) collective-permute-start(bf16[48,1536]{1,0:T(8,128)(2,1)S(1)} %get-tuple-element.113), channel_id=1, source_target_pairs={{0,32},{1,33},{2,34},{3,35},{4,36},{5,37},{6,38},{7,39},{8,40},{9,... | collective-permute-start | bytes 442376 | tf_op jit(solution)/shard_map/ppermute | solution.py:42
  56.9 9.9 %collective-permute-start.14 = (bf16[48,1536]{1,0:T(8,128)(2,1)S(1)}, bf16[48,1536]{1,0:T(8,128)(2,1)S(1)}, u32[]{:S(2)}, u32[]{:S(2)}) collective-permute-start(bf16[48,1536]{1,0:T(8,128)(2,1)S(1)} %get-tuple-element.114), channel_id=1, source_target_pairs={{0,33},{1,32},{2,35},{3,34},{4,37},{5,36},{6,39},{7,38},{8,41},{9,... | collective-permute-start | bytes 442376 | tf_op jit(solution)/shard_map/ppermute | solution.py:42
  58.6 8.2 %collective-permute-start.15 = (bf16[48,1536]{1,0:T(8,128)(2,1)S(1)}, bf16[48,1536]{1,0:T(8,128)(2,1)S(1)}, u32[]{:S(2)}, u32[]{:S(2)}) collective-permute-start(bf16[48,1536]{1,0:T(8,128)(2,1)S(1)} %get-tuple-element.115), channel_id=1, source_target_pairs={{0,1},{1,0},{2,3},{3,2},{4,5},{5,4},{6,7},{7,6},{8,9},{9,8},{10,11... | collective-permute-start | bytes 442376 | tf_op jit(solution)/shard_map/ppermute | solution.py:42
  62.0 7.2 %collective-permute-start.16 = (bf16[48,1536]{1,0:T(8,128)(2,1)S(1)}, bf16[48,1536]{1,0:T(8,128)(2,1)S(1)}, u32[]{:S(2)}, u32[]{:S(2)}) collective-permute-start(bf16[48,1536]{1,0:T(8,128)(2,1)S(1)} %get-tuple-element.116), channel_id=1, source_target_pairs={{0,128},{1,129},{2,130},{3,131},{4,132},{5,133},{6,134},{7,135},{8... | collective-permute-start | bytes 442376 | tf_op jit(solution)/shard_map/ppermute | solution.py:42
  63.3 6.7 %collective-permute-start.17 = (bf16[48,1536]{1,0:T(8,128)(2,1)S(1)}, bf16[48,1536]{1,0:T(8,128)(2,1)S(1)}, u32[]{:S(2)}, u32[]{:S(2)}) collective-permute-start(bf16[48,1536]{1,0:T(8,128)(2,1)S(1)} %get-tuple-element.117), channel_id=1, source_target_pairs={{0,192},{1,193},{2,194},{3,195},{4,196},{5,197},{6,198},{7,199},{8... | collective-permute-start | bytes 442376 | tf_op jit(solution)/shard_map/ppermute | solution.py:42
  64.9 5.1 %collective-permute-start.18 = (bf16[48,1536]{1,0:T(8,128)(2,1)S(1)}, bf16[48,1536]{1,0:T(8,128)(2,1)S(1)}, u32[]{:S(2)}, u32[]{:S(2)}) collective-permute-start(bf16[48,1536]{1,0:T(8,128)(2,1)S(1)} %get-tuple-element.118), channel_id=1, source_target_pairs={{0,64},{1,65},{2,66},{3,67},{4,68},{5,69},{6,70},{7,71},{8,72},{9,... | collective-permute-start | bytes 442376 | tf_op jit(solution)/shard_map/ppermute | solution.py:42
  66.9 12.4 %copy-start = (bf16[1,256,1536]{2,1,0:T(8,128)(2,1)S(1)}, bf16[1,256,1536]{2,1,0:T(8,128)(2,1)}, u32[]{:S(2)}) copy-start(bf16[1,256,1536]{2,1,0:T(8,128)(2,1)} %param.6) | copy-start | bytes 2359300
  67.7 11.6 %collective-permute-start.12 = (bf16[128,1536]{1,0:T(8,128)(2,1)}, bf16[128,1536]{1,0:T(8,128)(2,1)}, u32[]{:S(2)}, u32[]{:S(2)}) collective-permute-start(bf16[128,1536]{1,0:T(8,128)(2,1)} %slice.134), channel_id=1, source_target_pairs={{0,15},{1,0},{2,1},{3,2},{4,3},{5,4},{6,5},{7,6},{8,7},{9,8},{10,9... | collective-permute-start | bytes 1179656 | tf_op jit(solution)/shard_map/ppermute | solution.py:31
  71.0 16.7 %all-to-all-start = ((bf16[8,144,128]{2,1,0:T(8,128)(2,1)}), bf16[8,144,128]{2,1,0:T(8,128)(2,1)S(1)}, u32[]{:S(2)}, u32[]{:S(2)}) async-start(bf16[8,144,128]{2,1,0:T(8,128)(2,1)} %pieces.1), calls=%async_computation | async-start | bytes 589824 | tf_op jit(solution)/shard_map/all_to_all | solution.py:568

commit v11 on v10

--- a/solution.py
+++ b/solution.py
@@ -385,11 +385,11 @@
     )(places, lengths, *[in_vmem(o) for o in (order, frames, weight, qkv, attended_grad, late, late_grad)])
 
 
-def store_section(chunks, route, n, total, outs, held):
+def store_section(places, route, n, total, outs, held):
     half = CHUNKS // 2
     held[n] = total.reshape(held.shape[1:])
     for slot in range(CHUNKS):
-        outs[n if slot < half else 2 + n][slot % half] = held[n, chunks[route, slot]].astype(BF16)
+        outs[n if slot < half else 2 + n][slot % half] = held[n, chunk_at(route, slot, places[2], places[3], places[4])].astype(BF16)
 
 
 def own_kernel(left_ref, behind_ref, first_ref, second_ref, first_out, second_out):
@@ -415,24 +415,24 @@
     )(*[in_vmem(o) for o in (left, behind, first, second)])
 
 
-def first_wave_kernel(chunks, left_other_ref, right_other_ref, own_ref, *refs):
+def first_wave_kernel(places, left_other_ref, right_other_ref, own_ref, *refs):
     tokens = right_other_ref.shape[1]
     for n, at in enumerate((slice(tokens, 2 * tokens), slice(0, tokens))):
         total = own_ref[n] + dot(left_other_ref[:, at], right_other_ref[n])
-        store_section(chunks, n, n, total, refs[:-1], refs[-1])
-
-
-def second_wave_kernel(chunks, left_other_ref, right_other_ref, own_ref, *refs):
+        store_section(places, n, n, total, refs[:-1], refs[-1])
+
+
+def second_wave_kernel(places, left_other_ref, right_other_ref, own_ref, *refs):
     tokens = left_other_ref.shape[1] // 2
     inner = right_other_ref.shape[2] - CONTEXT
     behind = jnp.concatenate([right_other_ref[n, :, inner:] for n in range(2)], axis=0)
     left = jnp.concatenate([left_other_ref[:, :tokens], behind], axis=1)
     for n in range(2):
         total = own_ref[n] + dot(left, right_other_ref[n, :, :inner])
-        store_section(chunks, 2 + n, n, total, refs[:-1], refs[-1])
-
-
-def weight_sections(kernel, chunks, operands, inner, flops, name):
+        store_section(places, 2 + n, n, total, refs[:-1], refs[-1])
+
+
+def weight_sections(kernel, places, operands, inner, flops, name):
     size = (operands[0].shape[0] // CHUNKS, inner)
     routes = 2
     outs = pl.pallas_call(
@@ -444,7 +444,7 @@
         compiler_params=params(24),
         cost_estimate=cost(flops, 1),
         name=name,
-    )(chunks, *[in_vmem(o) for o in operands])
+    )(places, *[in_vmem(o) for o in operands])
     return outs[:routes], outs[routes:]
 
 
@@ -507,11 +507,10 @@
     dp_index = lax.axis_index("dp")
     xl = seq_index % XL
     core, xh, y = dp_index % CORES, dp_index // CORES % XH, dp_index // (CORES * XH)
-    places = jnp.stack([seq_index * row_count, core])
-    chunks = jnp.stack([chunk_at(r, jnp.arange(CHUNKS), y, xh, xl) for r in range(len(ROUTES))])
+    places = jnp.stack([seq_index * row_count, core, y, xh, xl])
 
     behind = from_behind(last_rows(frame_rows), "seq", 1)
-    frame_rows, places, chunks = lax.optimization_barrier((frame_rows, places, chunks))
+    frame_rows, places = lax.optimization_barrier((frame_rows, places))
     qkv, attended_grad, left, left_out, stats, weight, late, late_grad, order = front(
         places, lengths, frame_rows, grad_rows, w_qkv, w_out
     )
@@ -523,9 +522,9 @@
         (own_other, left_other, own_sum, grads_sum, grads)
     )
     grads_other = to_device(grads, to_core)
-    keep_a, send_a = weight_sections(first_wave_kernel, chunks, (left_other, own_other, own_sum), inner, 1, "first_wave")
+    keep_a, send_a = weight_sections(first_wave_kernel, places, (left_other, own_other, own_sum), inner, 1, "first_wave")
     keep_b, send_b = weight_sections(
-        second_wave_kernel, chunks, (left_other, grads_other, grads_sum), inner, 3 * 10**9, "second_wave"
+        second_wave_kernel, places, (left_other, grads_other, grads_sum), inner, 3 * 10**9, "second_wave"
     )
     query_grad = jnp.concatenate([own[1], jnp.zeros((CONTEXT, inner), BF16)], axis=0)
     projected_grad = jnp.concatenate([query_grad, grads[0, :, :inner], grads[1, :, :inner]], axis=1)

time: 88.6 us -> 88.7 us (level)
  no operation moved by 1% of the time
where the time goes in v11:
time: 88.7 us; the launch traced here: 88.4 us
  starting transfers between devices  32.6 us (37%)
  Pallas kernels  23.6 us (27%)
  waiting for transfers between devices  21.5 us (24%)
  matrix products  4.58 us (5%)
  other arithmetic  3.53 us (4%)
  between operations  1.5 us (2%)
  local copies, waits for them, and re-layouts  1.03 us (1%)
    ppermute x17, starting transfers between devices, to_device(): return lax.ppermute(value, ('dp', 'seq'), pairs)  23.7 us
    ppermute x17, waiting for transfers between devices, to_device(): return lax.ppermute(value, ('dp', 'seq'), pairs)  9.88 us
    pallas_call x1, Pallas kernels, front(): pl.pallas_call(front_kernel, in_specs=[SMEM_SPEC] + [HBM_SPEC] * 6, out_s...  9.87 us
    ppermute x2, waiting for transfers between devices, from_behind(): lax.ppermute(value, axis, [(i, (i + by) % peers) for i in range(peers)])  6.21 us
    all_to_all x1, starting transfers between devices, on_device(): lax.all_to_all(shares, 'seq', 0, 0, axis_index_groups=rings, tiled=True)  5.83 us
    all_to_all x1, waiting for transfers between devices, on_device(): lax.all_to_all(shares, 'seq', 0, 0, axis_index_groups=rings, tiled=True)  5.4 us
    pallas_call x1, Pallas kernels, early_tile(): pl.pallas_call(early_kernel, in_specs=[SMEM_SPEC, HBM_SPEC] + [VMEM_SPEC]...  4.69 us
    dot_general x2, matrix products, dot(): return lax.dot_general(a, b, dims, preferred_element_type=F32)  4.58 us
  transfers between devices with their start and end apart: 20, of which 11 were waited for; matrix products, arithmetic and copies ran while one was open for 10% of the time, Pallas kernels for 25%

profile of v11, /device:TPU:8, one launch (start us, length us, event | category | flops | bytes accessed | tf_op | source)
XLA Modules:
  0.0 88.4 jit_solution(2681672951059529082)
XLA Ops:
  0.6 1.0 %last_rows.1 = bf16[128,1536]{1,0:T(8,128)(2,1)S(1)} custom-call(bf16[256,1536]{1,0:T(8,128)(2,1)} %bitcast.46), custom_call_target="tpu_custom_call" | custom-call | flops 1 | bytes 1 | tf_op jit(solution)/shard_map/last_rows/pallas_call | solution.py:170
  1.7 1.6 %collective-permute-start = (bf16[128,1536]{1,0:T(8,128)(2,1)S(1)}, bf16[128,1536]{1,0:T(8,128)(2,1)S(1)}, u32[]{:S(2)}, u32[]{:S(2)}) collective-permute-start(bf16[128,1536]{1,0:T(8,128)(2,1)S(1)} %last_rows.1), channel_id=1, source_target_pairs={{0,1},{1,2},{2,3},{3,4},{4,5},{5,6},{6,7},{7,8},{8,9},{9,10},{10,1... | collective-permute-start | bytes 1179656 | tf_op jit(solution)/shard_map/ppermute | solution.py:31
  3.9 0.1 stack.23.places
  4.0 9.9 %front.1 = (bf16[256,2304]{1,0:T(8,128)(2,1)S(1)}, bf16[256,768]{1,0:T(8,128)(2,1)S(1)}, bf16[768,512]{1,0:T(8,128)(2,1)S(1)}, bf16[768,512]{1,0:T(8,128)(2,1)S(...) custom-call(s32[5]{0:T(128)S(1)} %stack.23.places, ...), custom_call_target="tpu_custom_call" | custom-call | flops 3623878656 | bytes 11796480 | tf_op jit(solution)/shard_map/front/pallas_call | solution.py:251
  13.9 0.1 collective-permute-start.2
  14.0 3.7 %collective-permute-done.frames_ref = bf16[128,1536]{1,0:T(8,128)(2,1)S(1)} collective-permute-done((bf16[128,1536]{1,0:T(8,128)(2,1)S(1)}, bf16[128,1536]{1,0:T(8,128)(2,1)S(1)}, u32[]{:S(2)}, u32[]{:S(2)}) %collective-permute-start) | collective-permute-done | bytes 393248 | tf_op jit(solution)/shard_map/ppermute | solution.py:31
  17.6 4.7 %attention_early.1 = (bf16[2,256,768]{2,1,0:T(8,128)(2,1)S(1)}, bf16[2,384,896]{2,1,0:T(8,128)(2,1)S(1)}, bf16[768,128]{1,0:T(8,128)(2,1)S(1)}) custom-call(s32[5]{0:T(128)S(1)} %stack.23.places, s32[1]{0:T(128)S(6)} %copy.9.lengths_ref, bf16[384,384]{1,0:T(8,128)(2,1)S(1)} %get-tuple-element.62.order_ref, ...), custom_call_target="tpu_custom_call" | custom-call | flops 704643072 | bytes 1572864 | tf_op jit(solution)/shard_map/attention_early/pallas_call | solution.py:367
  22.3 0.3 collective-permute-start.1
  22.6 2.0 %own_sums.1 = (f32[2,768,768]{2,1,0:T(8,128)S(1)}, f32[2,768,768]{2,1,0:T(8,128)S(1)}) custom-call(bf16[768,512]{1,0:T(8,128)(2,1)S(1)} %get-tuple-element.70.left_ref, bf16[768,128]{1,0:T(8,128)(2,1)S(1)} %get-tuple-element.71.behind_ref, bf16[2,256,768]{2,1,0:T(8,128)(2,1)S(1)} %get-tuple-element.68.first_ref, ...), custom_call_target="tpu_custom_call" | custom-call | flops 4000000000 | bytes 1 | tf_op jit(solution)/shard_map/own_sums/pallas_call | solution.py:407
  24.6 0.0 collective-permute-done.2.left_other_ref
  24.6 0.3 collective-permute-done.1.right_other_ref
  24.9 0.3 collective-permute-start.5
  25.2 0.1 slice_bitcast_fusion.2
  25.3 1.7 %first_wave.1 = (bf16[8,48,768]{2,1,0:T(8,128)(2,1)S(1)}, bf16[8,48,768]{2,1,0:T(8,128)(2,1)S(1)}, bf16[8,48,768]{2,1,0:T(8,128)(2,1)S(1)}, bf16[8,48,768]{2,1,0:T(8,128)(2,1)S(1)}) custom-call(s32[5]{0:T(128)S(1)} %stack.23.places, bf16[768,512]{1,0:T(8,128)(2,1)S(1)} %collective-permute-done.2.left_other_ref, ...), custom_call_target="tpu_custom_call" | custom-call | flops 1 | bytes 1 | tf_op jit(solution)/shard_map/first_wave/pallas_call | solution.py:438
  27.0 0.5 collective-permute-start.3
  27.6 2.4 %collective-permute-start.4 = (bf16[8,48,768]{2,1,0:T(8,128)(2,1)S(1)}, bf16[8,48,768]{2,1,0:T(8,128)(2,1)S(1)}, u32[]{:S(2)}, u32[]{:S(2)}) collective-permute-start(bf16[8,48,768]{2,1,0:T(8,128)(2,1)S(1)} %get-tuple-element.81), channel_id=1, source_target_pairs={{0,192},{1,193},{2,194},{3,195},{4,196},{5,197},{6,198},{7,199},{8... | collective-permute-start | bytes 1769480 | tf_op jit(solution)/shard_map/ppermute | solution.py:42
  30.0 0.1 slice_bitcast_fusion.1
  30.0 0.0 slice-start
  30.1 0.1 fusion.2
  30.2 0.0 slice-start.1
  30.2 0.0 collective-permute-done.5.right_other_ref
  30.2 2.3 %second_wave.1 = (bf16[8,48,768]{2,1,0:T(8,128)(2,1)S(1)}, bf16[8,48,768]{2,1,0:T(8,128)(2,1)S(1)}, bf16[8,48,768]{2,1,0:T(8,128)(2,1)S(1)}, bf16[8,48,768]{2,1,0:T(8,128)(2,1)S(1)}) custom-call(s32[5]{0:T(128)S(1)} %stack.23.places, bf16[768,512]{1,0:T(8,128)(2,1)S(1)} %collective-permute-done.2.left_other_ref, ...), custom_call_target="tpu_custom_call" | custom-call | flops 3000000000 | bytes 1 | tf_op jit(solution)/shard_map/second_wave/pallas_call | solution.py:438
  32.5 0.1 collective-permute-start.8
  32.6 3.3 %collective-permute-start.9 = (bf16[8,48,768]{2,1,0:T(8,128)(2,1)S(1)}, bf16[8,48,768]{2,1,0:T(8,128)(2,1)S(1)}, u32[]{:S(2)}, u32[]{:S(2)}) collective-permute-start(bf16[8,48,768]{2,1,0:T(8,128)(2,1)S(1)} %get-tuple-element.95), channel_id=1, source_target_pairs={{0,33},{1,32},{2,35},{3,34},{4,37},{5,36},{6,39},{7,38},{8,41},{9,... | collective-permute-start | bytes 1769480 | tf_op jit(solution)/shard_map/ppermute | solution.py:42
  35.9 2.9 %fusion.29 = f32[384,1536]{1,0:T(8,128)S(1)} fusion(bf16[384,2304]{1,0:T(8,128)(2,1)S(1)} %fusion.2, bf16[1536,2304]{1,0:T(8,128)(2,1)S(1)} %bitcast.55), kind=kOutput, calls=%fused_computation.63 | convolution fusion | flops 2717908992 | bytes 11206656 | tf_op jit(solution)/shard_map/dot_general | solution.py:26
  38.8 3.7 %collective-permute-done.3.refs_2_ = bf16[8,48,768]{2,1,0:T(8,128)(2,1)S(1)} collective-permute-done((bf16[8,48,768]{2,1,0:T(8,128)(2,1)S(1)}, bf16[8,48,768]{2,1,0:T(8,128)(2,1)S(1)}, u32[]{:S(2)}, u32[]{:S(2)}) %collective-permute-start.3) | collective-permute-done | bytes 589856 | tf_op jit(solution)/shard_map/ppermute | solution.py:42
  42.5 0.8 collective-permute-done.4.refs_3_
  43.3 0.3 halve.2
  43.6 0.0 copy-start.1
  43.6 1.8 %collective-permute-start.6 = (bf16[4,48,768]{2,1,0:T(8,128)(2,1)S(1)}, bf16[4,48,768]{2,1,0:T(8,128)(2,1)S(1)}, u32[]{:S(2)}, u32[]{:S(2)}) collective-permute-start(bf16[4,48,768]{2,1,0:T(8,128)(2,1)S(1)} %get-tuple-element.89), channel_id=1, source_target_pairs={{0,192},{1,193},{2,194},{3,195},{4,196},{5,197},{6,198},{7,199},{8... | collective-permute-start | bytes 884744 | tf_op jit(solution)/shard_map/ppermute | solution.py:42
  45.5 2.6 %collective-permute-start.7 = (bf16[4,48,768]{2,1,0:T(8,128)(2,1)S(1)}, bf16[4,48,768]{2,1,0:T(8,128)(2,1)S(1)}, u32[]{:S(2)}, u32[]{:S(2)}) collective-permute-start(bf16[4,48,768]{2,1,0:T(8,128)(2,1)S(1)} %get-tuple-element.90), channel_id=1, source_target_pairs={{0,64},{1,65},{2,66},{3,67},{4,68},{5,69},{6,70},{7,71},{8,72},{9,... | collective-permute-start | bytes 884744 | tf_op jit(solution)/shard_map/ppermute | solution.py:42
  48.0 0.7 collective-permute-done.9.refs_3_
  48.7 0.3 halve.3
  49.0 3.0 %collective-permute-start.10 = (bf16[4,48,768]{2,1,0:T(8,128)(2,1)S(1)}, bf16[4,48,768]{2,1,0:T(8,128)(2,1)S(1)}, u32[]{:S(2)}, u32[]{:S(2)}) collective-permute-start(bf16[4,48,768]{2,1,0:T(8,128)(2,1)S(1)} %get-tuple-element.102), channel_id=1, source_target_pairs={{0,33},{1,32},{2,35},{3,34},{4,37},{5,36},{6,39},{7,38},{8,41},{9,... | collective-permute-start | bytes 884744 | tf_op jit(solution)/shard_map/ppermute | solution.py:42
  52.0 0.0 collective-permute-start.11
  52.0 1.7 %convolution_convert_fusion = bf16[256,1536]{1,0:T(8,128)(2,1)} fusion(bf16[256,768]{1,0:T(8,128)(2,1)S(1)} %get-tuple-element.98, bf16[768,1536]{1,0:T(8,128)(2,1)S(1)} %copy-done.1), kind=kOutput, calls=%fused_computation.2 | convolution fusion | flops 604372992 | bytes 3538944 | tf_op jit(solution)/shard_map/dot_general | solution.py:26
  53.7 0.3 collective-permute-done.7
  53.9 0.1 add_convert_fusion.1
  54.1 2.8 %collective-permute-start.13 = (bf16[48,1536]{1,0:T(8,128)(2,1)S(1)}, bf16[48,1536]{1,0:T(8,128)(2,1)S(1)}, u32[]{:S(2)}, u32[]{:S(2)}) collective-permute-start(bf16[48,1536]{1,0:T(8,128)(2,1)S(1)} %get-tuple-element.111), channel_id=1, source_target_pairs={{0,32},{1,33},{2,34},{3,35},{4,36},{5,37},{6,38},{7,39},{8,40},{9,... | collective-permute-start | bytes 442376 | tf_op jit(solution)/shard_map/ppermute | solution.py:42
  56.9 1.7 %collective-permute-start.14 = (bf16[48,1536]{1,0:T(8,128)(2,1)S(1)}, bf16[48,1536]{1,0:T(8,128)(2,1)S(1)}, u32[]{:S(2)}, u32[]{:S(2)}) collective-permute-start(bf16[48,1536]{1,0:T(8,128)(2,1)S(1)} %get-tuple-element.112), channel_id=1, source_target_pairs={{0,33},{1,32},{2,35},{3,34},{4,37},{5,36},{6,39},{7,38},{8,41},{9,... | collective-permute-start | bytes 442376 | tf_op jit(solution)/shard_map/ppermute | solution.py:42
  58.6 0.0 collective-permute-start.15
  58.6 1.2 %collective-permute-done.10 = bf16[4,48,768]{2,1,0:T(8,128)(2,1)S(1)} collective-permute-done((bf16[4,48,768]{2,1,0:T(8,128)(2,1)S(1)}, bf16[4,48,768]{2,1,0:T(8,128)(2,1)S(1)}, u32[]{:S(2)}, u32[]{:S(2)}) %collective-permute-start.10) | collective-permute-done | bytes 294944 | tf_op jit(solution)/shard_map/ppermute | solution.py:42
  59.8 0.1 add_convert_fusion.4
  59.9 2.1 %collective-permute-done.11 = bf16[4,48,768]{2,1,0:T(8,128)(2,1)S(1)} collective-permute-done((bf16[4,48,768]{2,1,0:T(8,128)(2,1)S(1)}, bf16[4,48,768]{2,1,0:T(8,128)(2,1)S(1)}, u32[]{:S(2)}, u32[]{:S(2)}) %collective-permute-start.11) | collective-permute-done | bytes 294944 | tf_op jit(solution)/shard_map/ppermute | solution.py:42
  61.9 0.1 add_convert_fusion.3
  62.1 1.3 %collective-permute-start.16 = (bf16[48,1536]{1,0:T(8,128)(2,1)S(1)}, bf16[48,1536]{1,0:T(8,128)(2,1)S(1)}, u32[]{:S(2)}, u32[]{:S(2)}) collective-permute-start(bf16[48,1536]{1,0:T(8,128)(2,1)S(1)} %get-tuple-element.114), channel_id=1, source_target_pairs={{0,128},{1,129},{2,130},{3,131},{4,132},{5,133},{6,134},{7,135},{8... | collective-permute-start | bytes 442376 | tf_op jit(solution)/shard_map/ppermute | solution.py:42
  63.4 1.6 %collective-permute-start.17 = (bf16[48,1536]{1,0:T(8,128)(2,1)S(1)}, bf16[48,1536]{1,0:T(8,128)(2,1)S(1)}, u32[]{:S(2)}, u32[]{:S(2)}) collective-permute-start(bf16[48,1536]{1,0:T(8,128)(2,1)S(1)} %get-tuple-element.115), channel_id=1, source_target_pairs={{0,192},{1,193},{2,194},{3,195},{4,196},{5,197},{6,198},{7,199},{8... | collective-permute-start | bytes 442376 | tf_op jit(solution)/shard_map/ppermute | solution.py:42
  65.0 0.0 collective-permute-done.13
  65.0 1.9 %collective-permute-start.18 = (bf16[48,1536]{1,0:T(8,128)(2,1)S(1)}, bf16[48,1536]{1,0:T(8,128)(2,1)S(1)}, u32[]{:S(2)}, u32[]{:S(2)}) collective-permute-start(bf16[48,1536]{1,0:T(8,128)(2,1)S(1)} %get-tuple-element.116), channel_id=1, source_target_pairs={{0,64},{1,65},{2,66},{3,67},{4,68},{5,69},{6,70},{7,71},{8,72},{9,... | collective-permute-start | bytes 442376 | tf_op jit(solution)/shard_map/ppermute | solution.py:42
  66.8 0.0 collective-permute-done.14
  66.9 0.1 fusion.13.refs_0_
  66.9 0.0 copy-start
  67.0 0.8 slice.134
  67.7 1.5 %collective-permute-start.12 = (bf16[128,1536]{1,0:T(8,128)(2,1)}, bf16[128,1536]{1,0:T(8,128)(2,1)}, u32[]{:S(2)}, u32[]{:S(2)}) collective-permute-start(bf16[128,1536]{1,0:T(8,128)(2,1)} %slice.134), channel_id=1, source_target_pairs={{0,15},{1,0},{2,1},{3,2},{4,3},{5,4},{6,5},{7,6},{8,7},{9,8},{10,9... | collective-permute-start | bytes 1179656 | tf_op jit(solution)/shard_map/ppermute | solution.py:31
  69.2 0.0 collective-permute-done.16
  69.2 0.9 collective-permute-done.17
  70.1 0.1 fusion.10.refs_1_
  70.2 0.8 pieces.1
  71.0 5.8 %all-to-all-start = ((bf16[8,144,128]{2,1,0:T(8,128)(2,1)}), bf16[8,144,128]{2,1,0:T(8,128)(2,1)S(1)}, u32[]{:S(2)}, u32[]{:S(2)}) async-start(bf16[8,144,128]{2,1,0:T(8,128)(2,1)} %pieces.1), calls=%async_computation | async-start | bytes 589824 | tf_op jit(solution)/shard_map/all_to_all | solution.py:567
  76.8 2.5 %collective-permute-done.12 = bf16[128,1536]{1,0:T(8,128)(2,1)} collective-permute-done((bf16[128,1536]{1,0:T(8,128)(2,1)}, bf16[128,1536]{1,0:T(8,128)(2,1)}, u32[]{:S(2)}, u32[]{:S(2)}) %collective-permute-start.12) | collective-permute-done | bytes 393248 | tf_op jit(solution)/shard_map/ppermute | solution.py:31
  79.4 1.5 %convert_reduce_fusion = (f32[256]{0:T(256)S(1)}, f32[256]{0:T(256)S(1)}, bf16[256,1536]{1,0:T(8,128)(2,1)S(1)}) fusion(f32[256]{0:T(256)S(1)} %bitcast.52, f32[256]{0:T(256)S(1)} %bitcast.50, bf16[256,1536]{1,0:T(8,128)(2,1)S(1)} %bitcast.48, bf16[128,1536]{1,0:T(8,128)(2,1)} %collective-permute-done.12, f32[384,1536]{1,0:T(8,128)S(1)} %fusion.29), kind=kLoop, calls=%fused_computation.5 | loop fusion | flops 3931648 | bytes 3543040 | tf_op jit(solution)/shard_map/reduce_sum | solution.py:118
  80.8 1.4 %fusion.7 = bf16[1,256,1536]{2,1,0:T(8,128)(2,1)} fusion(bf16[256,1536]{1,0:T(8,128)(2,1)S(1)} %bitcast.49, bf16[256,1536]{1,0:T(8,128)(2,1)S(1)} %get-tuple-element.119, f32[256]{0:T(256)S(1)} %get-tuple-element.134, f32[256]{0:T(256)S(1)} %bitcast.51, f32[256]{0:T(256)S(1)} %get-tuple-element.135, f32[256]{0:T(256)S(1)} %bitcast.53), kind=kLoop, calls=%fused_computation.14 | loop fusion | flops 3538944 | bytes 2363392 | tf_op jit(solution)/shard_map/broadcast_in_dim | solution.py:575
  82.3 5.4 %all-to-all-done.in_ref = bf16[8,144,128]{2,1,0:T(8,128)(2,1)S(1)} async-done(((bf16[8,144,128]{2,1,0:T(8,128)(2,1)}), bf16[8,144,128]{2,1,0:T(8,128)(2,1)S(1)}, u32[]{:S(2)}, u32[]{:S(2)}) %all-to-all-start) | async-done | bytes 294944 | tf_op jit(solution)/shard_map/all_to_all | solution.py:567
  87.7 0.7 total.1
  (13 shorter events, 0.1 us)
Async XLA Ops:
  1.7 16.0 %collective-permute-start = (bf16[128,1536]{1,0:T(8,128)(2,1)S(1)}, bf16[128,1536]{1,0:T(8,128)(2,1)S(1)}, u32[]{:S(2)}, u32[]{:S(2)}) collective-permute-start(bf16[128,1536]{1,0:T(8,128)(2,1)S(1)} %last_rows.1), channel_id=1, source_target_pairs={{0,1},{1,2},{2,3},{3,4},{4,5},{5,6},{6,7},{7,8},{8,9},{9,10},{10,1... | collective-permute-start | bytes 1179656 | tf_op jit(solution)/shard_map/ppermute | solution.py:31
  13.9 10.8 %collective-permute-start.2 = (bf16[768,512]{1,0:T(8,128)(2,1)S(1)}, bf16[768,512]{1,0:T(8,128)(2,1)S(1)}, u32[]{:S(2)}, u32[]{:S(2)}) collective-permute-start(bf16[768,512]{1,0:T(8,128)(2,1)S(1)} %get-tuple-element.69), channel_id=1, source_target_pairs={{0,16},{1,17},{2,18},{3,19},{4,20},{5,21},{6,22},{7,23},{8,24},{9,... | collective-permute-start | bytes 2359304 | tf_op jit(solution)/shard_map/ppermute | solution.py:42
  22.3 2.6 %collective-permute-start.1 = (bf16[2,256,768]{2,1,0:T(8,128)(2,1)S(1)}, bf16[2,256,768]{2,1,0:T(8,128)(2,1)S(1)}, u32[]{:S(2)}, u32[]{:S(2)}) collective-permute-start(bf16[2,256,768]{2,1,0:T(8,128)(2,1)S(1)} %get-tuple-element.68.first_ref), channel_id=1, source_target_pairs={{0,16},{1,17},{2,18},{3,19},{4,20},{5,21},{6,22},{7,23},{8,24},{9,... | collective-permute-start | bytes 2359304 | tf_op jit(solution)/shard_map/ppermute | solution.py:42
  24.9 5.3 %collective-permute-start.5 = (bf16[2,384,896]{2,1,0:T(8,128)(2,1)S(1)}, bf16[2,384,896]{2,1,0:T(8,128)(2,1)S(1)}, u32[]{:S(2)}, u32[]{:S(2)}) collective-permute-start(bf16[2,384,896]{2,1,0:T(8,128)(2,1)S(1)} %get-tuple-element.82.second_ref), channel_id=1, source_target_pairs={{0,16},{1,17},{2,18},{3,19},{4,20},{5,21},{6,22},{7,23},{8,24},{9,... | collective-permute-start | bytes 4128776 | tf_op jit(solution)/shard_map/ppermute | solution.py:42
  27.0 15.5 %collective-permute-start.3 = (bf16[8,48,768]{2,1,0:T(8,128)(2,1)S(1)}, bf16[8,48,768]{2,1,0:T(8,128)(2,1)S(1)}, u32[]{:S(2)}, u32[]{:S(2)}) collective-permute-start(bf16[8,48,768]{2,1,0:T(8,128)(2,1)S(1)} %get-tuple-element.80), channel_id=1, source_target_pairs={{0,64},{1,65},{2,66},{3,67},{4,68},{5,69},{6,70},{7,71},{8,72},{9,... | collective-permute-start | bytes 1769480 | tf_op jit(solution)/shard_map/ppermute | solution.py:42
  27.6 15.8 %collective-permute-start.4 = (bf16[8,48,768]{2,1,0:T(8,128)(2,1)S(1)}, bf16[8,48,768]{2,1,0:T(8,128)(2,1)S(1)}, u32[]{:S(2)}, u32[]{:S(2)}) collective-permute-start(bf16[8,48,768]{2,1,0:T(8,128)(2,1)S(1)} %get-tuple-element.81), channel_id=1, source_target_pairs={{0,192},{1,193},{2,194},{3,195},{4,196},{5,197},{6,198},{7,199},{8... | collective-permute-start | bytes 1769480 | tf_op jit(solution)/shard_map/ppermute | solution.py:42
  30.0 5.8 %slice-start = ((s8[7077888]{0:T(1024)(128)(4,1)}), s8[4194304]{0:T(1024)(128)(4,1)S(1)}, s32[]{:S(2)}) async-start(s8[7077888]{0:T(1024)(128)(4,1)} %bitcast.54), calls=%async_computation.1 | async-start | bytes 8388608
  30.2 5.7 %slice-start.1 = ((s8[7077888]{0:T(1024)(128)(4,1)}), s8[2883584]{0:T(1024)(128)(4,1)S(1)}, s32[]{:S(2)}) async-start(s8[7077888]{0:T(1024)(128)(4,1)} %bitcast.54), calls=%async_computation.2 | async-start | bytes 5767168
  32.5 15.5 %collective-permute-start.8 = (bf16[8,48,768]{2,1,0:T(8,128)(2,1)S(1)}, bf16[8,48,768]{2,1,0:T(8,128)(2,1)S(1)}, u32[]{:S(2)}, u32[]{:S(2)}) collective-permute-start(bf16[8,48,768]{2,1,0:T(8,128)(2,1)S(1)} %get-tuple-element.94), channel_id=1, source_target_pairs={{0,1},{1,0},{2,3},{3,2},{4,5},{5,4},{6,7},{7,6},{8,9},{9,8},{10,11... | collective-permute-start | bytes 1769480 | tf_op jit(solution)/shard_map/ppermute | solution.py:42
  32.6 16.1 %collective-permute-start.9 = (bf16[8,48,768]{2,1,0:T(8,128)(2,1)S(1)}, bf16[8,48,768]{2,1,0:T(8,128)(2,1)S(1)}, u32[]{:S(2)}, u32[]{:S(2)}) collective-permute-start(bf16[8,48,768]{2,1,0:T(8,128)(2,1)S(1)} %get-tuple-element.95), channel_id=1, source_target_pairs={{0,33},{1,32},{2,35},{3,34},{4,37},{5,36},{6,39},{7,38},{8,41},{9,... | collective-permute-start | bytes 1769480 | tf_op jit(solution)/shard_map/ppermute | solution.py:42
  43.6 8.4 %copy-start.1 = (bf16[768,1536]{1,0:T(8,128)(2,1)S(1)}, bf16[768,1536]{1,0:T(8,128)(2,1)}, u32[]{:S(2)}) copy-start(bf16[768,1536]{1,0:T(8,128)(2,1)} %out_ref.1) | copy-start | bytes 7077892
  43.6 10.0 %collective-permute-start.6 = (bf16[4,48,768]{2,1,0:T(8,128)(2,1)S(1)}, bf16[4,48,768]{2,1,0:T(8,128)(2,1)S(1)}, u32[]{:S(2)}, u32[]{:S(2)}) collective-permute-start(bf16[4,48,768]{2,1,0:T(8,128)(2,1)S(1)} %get-tuple-element.89), channel_id=1, source_target_pairs={{0,192},{1,193},{2,194},{3,195},{4,196},{5,197},{6,198},{7,199},{8... | collective-permute-start | bytes 884744 | tf_op jit(solution)/shard_map/ppermute | solution.py:42
  45.5 8.5 %collective-permute-start.7 = (bf16[4,48,768]{2,1,0:T(8,128)(2,1)S(1)}, bf16[4,48,768]{2,1,0:T(8,128)(2,1)S(1)}, u32[]{:S(2)}, u32[]{:S(2)}) collective-permute-start(bf16[4,48,768]{2,1,0:T(8,128)(2,1)S(1)} %get-tuple-element.90), channel_id=1, source_target_pairs={{0,64},{1,65},{2,66},{3,67},{4,68},{5,69},{6,70},{7,71},{8,72},{9,... | collective-permute-start | bytes 884744 | tf_op jit(solution)/shard_map/ppermute | solution.py:42
  49.0 10.8 %collective-permute-start.10 = (bf16[4,48,768]{2,1,0:T(8,128)(2,1)S(1)}, bf16[4,48,768]{2,1,0:T(8,128)(2,1)S(1)}, u32[]{:S(2)}, u32[]{:S(2)}) collective-permute-start(bf16[4,48,768]{2,1,0:T(8,128)(2,1)S(1)} %get-tuple-element.102), channel_id=1, source_target_pairs={{0,33},{1,32},{2,35},{3,34},{4,37},{5,36},{6,39},{7,38},{8,41},{9,... | collective-permute-start | bytes 884744 | tf_op jit(solution)/shard_map/ppermute | solution.py:42
  52.0 9.9 %collective-permute-start.11 = (bf16[4,48,768]{2,1,0:T(8,128)(2,1)S(1)}, bf16[4,48,768]{2,1,0:T(8,128)(2,1)S(1)}, u32[]{:S(2)}, u32[]{:S(2)}) collective-permute-start(bf16[4,48,768]{2,1,0:T(8,128)(2,1)S(1)} %get-tuple-element.104), channel_id=1, source_target_pairs={{0,1},{1,0},{2,3},{3,2},{4,5},{5,4},{6,7},{7,6},{8,9},{9,8},{10,11... | collective-permute-start | bytes 884744 | tf_op jit(solution)/shard_map/ppermute | solution.py:42
  54.1 10.8 %collective-permute-start.13 = (bf16[48,1536]{1,0:T(8,128)(2,1)S(1)}, bf16[48,1536]{1,0:T(8,128)(2,1)S(1)}, u32[]{:S(2)}, u32[]{:S(2)}) collective-permute-start(bf16[48,1536]{1,0:T(8,128)(2,1)S(1)} %get-tuple-element.111), channel_id=1, source_target_pairs={{0,32},{1,33},{2,34},{3,35},{4,36},{5,37},{6,38},{7,39},{8,40},{9,... | collective-permute-start | bytes 442376 | tf_op jit(solution)/shard_map/ppermute | solution.py:42
  56.9 9.9 %collective-permute-start.14 = (bf16[48,1536]{1,0:T(8,128)(2,1)S(1)}, bf16[48,1536]{1,0:T(8,128)(2,1)S(1)}, u32[]{:S(2)}, u32[]{:S(2)}) collective-permute-start(bf16[48,1536]{1,0:T(8,128)(2,1)S(1)} %get-tuple-element.112), channel_id=1, source_target_pairs={{0,33},{1,32},{2,35},{3,34},{4,37},{5,36},{6,39},{7,38},{8,41},{9,... | collective-permute-start | bytes 442376 | tf_op jit(solution)/shard_map/ppermute | solution.py:42
  58.6 8.2 %collective-permute-start.15 = (bf16[48,1536]{1,0:T(8,128)(2,1)S(1)}, bf16[48,1536]{1,0:T(8,128)(2,1)S(1)}, u32[]{:S(2)}, u32[]{:S(2)}) collective-permute-start(bf16[48,1536]{1,0:T(8,128)(2,1)S(1)} %get-tuple-element.113), channel_id=1, source_target_pairs={{0,1},{1,0},{2,3},{3,2},{4,5},{5,4},{6,7},{7,6},{8,9},{9,8},{10,11... | collective-permute-start | bytes 442376 | tf_op jit(solution)/shard_map/ppermute | solution.py:42
  62.1 7.2 %collective-permute-start.16 = (bf16[48,1536]{1,0:T(8,128)(2,1)S(1)}, bf16[48,1536]{1,0:T(8,128)(2,1)S(1)}, u32[]{:S(2)}, u32[]{:S(2)}) collective-permute-start(bf16[48,1536]{1,0:T(8,128)(2,1)S(1)} %get-tuple-element.114), channel_id=1, source_target_pairs={{0,128},{1,129},{2,130},{3,131},{4,132},{5,133},{6,134},{7,135},{8... | collective-permute-start | bytes 442376 | tf_op jit(solution)/shard_map/ppermute | solution.py:42
  63.4 6.7 %collective-permute-start.17 = (bf16[48,1536]{1,0:T(8,128)(2,1)S(1)}, bf16[48,1536]{1,0:T(8,128)(2,1)S(1)}, u32[]{:S(2)}, u32[]{:S(2)}) collective-permute-start(bf16[48,1536]{1,0:T(8,128)(2,1)S(1)} %get-tuple-element.115), channel_id=1, source_target_pairs={{0,192},{1,193},{2,194},{3,195},{4,196},{5,197},{6,198},{7,199},{8... | collective-permute-start | bytes 442376 | tf_op jit(solution)/shard_map/ppermute | solution.py:42
  65.0 5.1 %collective-permute-start.18 = (bf16[48,1536]{1,0:T(8,128)(2,1)S(1)}, bf16[48,1536]{1,0:T(8,128)(2,1)S(1)}, u32[]{:S(2)}, u32[]{:S(2)}) collective-permute-start(bf16[48,1536]{1,0:T(8,128)(2,1)S(1)} %get-tuple-element.116), channel_id=1, source_target_pairs={{0,64},{1,65},{2,66},{3,67},{4,68},{5,69},{6,70},{7,71},{8,72},{9,... | collective-permute-start | bytes 442376 | tf_op jit(solution)/shard_map/ppermute | solution.py:42
  66.9 12.4 %copy-start = (bf16[1,256,1536]{2,1,0:T(8,128)(2,1)S(1)}, bf16[1,256,1536]{2,1,0:T(8,128)(2,1)}, u32[]{:S(2)}) copy-start(bf16[1,256,1536]{2,1,0:T(8,128)(2,1)} %param.6) | copy-start | bytes 2359300
  67.7 11.6 %collective-permute-start.12 = (bf16[128,1536]{1,0:T(8,128)(2,1)}, bf16[128,1536]{1,0:T(8,128)(2,1)}, u32[]{:S(2)}, u32[]{:S(2)}) collective-permute-start(bf16[128,1536]{1,0:T(8,128)(2,1)} %slice.134), channel_id=1, source_target_pairs={{0,15},{1,0},{2,1},{3,2},{4,3},{5,4},{6,5},{7,6},{8,7},{9,8},{10,9... | collective-permute-start | bytes 1179656 | tf_op jit(solution)/shard_map/ppermute | solution.py:31
  71.0 16.7 %all-to-all-start = ((bf16[8,144,128]{2,1,0:T(8,128)(2,1)}), bf16[8,144,128]{2,1,0:T(8,128)(2,1)S(1)}, u32[]{:S(2)}, u32[]{:S(2)}) async-start(bf16[8,144,128]{2,1,0:T(8,128)(2,1)} %pieces.1), calls=%async_computation | async-start | bytes 589824 | tf_op jit(solution)/shard_map/all_to_all | solution.py:567

commit v12 on v10

--- a/solution.py
+++ b/solution.py
@@ -387,9 +387,9 @@
 
 def store_section(chunks, route, n, total, outs, held):
     half = CHUNKS // 2
-    held[n] = total.reshape(held.shape[1:])
+    held[n] = total.astype(BF16).reshape(held.shape[1:])
     for slot in range(CHUNKS):
-        outs[n if slot < half else 2 + n][slot % half] = held[n, chunks[route, slot]].astype(BF16)
+        outs[n if slot < half else 2 + n][slot % half] = held[n, chunks[route, slot]]
 
 
 def own_kernel(left_ref, behind_ref, first_ref, second_ref, first_out, second_out):
@@ -440,7 +440,7 @@
         in_specs=[SMEM_SPEC] + [VMEM_SPEC] * len(operands),
         out_specs=[VMEM_SPEC] * (2 * routes),
         out_shape=[pltpu.VMEM((CHUNKS // 2, *size), BF16)] * (2 * routes),
-        scratch_shapes=[pltpu.VMEM((routes, CHUNKS, *size), F32)],
+        scratch_shapes=[pltpu.VMEM((routes, CHUNKS, *size), BF16)],
         compiler_params=params(24),
         cost_estimate=cost(flops, 1),
         name=name,

time: 88.6 us -> 88.1 us (level)
  no operation moved by 1% of the time
where the time goes in v12:
time: 88.1 us; the launch traced here: 87.7 us
  starting transfers between devices  32.3 us (37%)
  Pallas kernels  23.3 us (26%)
  waiting for transfers between devices  21.3 us (24%)
  matrix products  4.58 us (5%)
  other arithmetic  3.64 us (4%)
  between operations  1.52 us (2%)
  local copies, waits for them, and re-layouts  0.95 us (1%)
    ppermute x17, starting transfers between devices, to_device(): return lax.ppermute(value, ('dp', 'seq'), pairs)  23.8 us
    pallas_call x1, Pallas kernels, front(): pl.pallas_call(front_kernel, in_specs=[SMEM_SPEC] + [HBM_SPEC] * 6, out_s...  9.88 us
    ppermute x17, waiting for transfers between devices, to_device(): return lax.ppermute(value, ('dp', 'seq'), pairs)  9.77 us
    ppermute x2, waiting for transfers between devices, from_behind(): lax.ppermute(value, axis, [(i, (i + by) % peers) for i in range(peers)])  6.09 us
    all_to_all x1, waiting for transfers between devices, on_device(): lax.all_to_all(shares, 'seq', 0, 0, axis_index_groups=rings, tiled=True)  5.45 us
    all_to_all x1, starting transfers between devices, on_device(): lax.all_to_all(shares, 'seq', 0, 0, axis_index_groups=rings, tiled=True)  5.45 us
    pallas_call x1, Pallas kernels, early_tile(): pl.pallas_call(early_kernel, in_specs=[SMEM_SPEC, HBM_SPEC] + [VMEM_SPEC]...  4.69 us
    dot_general x2, matrix products, dot(): return lax.dot_general(a, b, dims, preferred_element_type=F32)  4.58 us
  transfers between devices with their start and end apart: 20, of which 11 were waited for; matrix products, arithmetic and copies ran while one was open for 10% of the time, Pallas kernels for 25%

profile of v12, /device:TPU:8, one launch (start us, length us, event | category | flops | bytes accessed | tf_op | source)
XLA Modules:
  0.0 87.7 jit_solution(12516980552425200090)
XLA Ops:
  0.6 1.0 %last_rows.1 = bf16[128,1536]{1,0:T(8,128)(2,1)S(1)} custom-call(bf16[256,1536]{1,0:T(8,128)(2,1)} %bitcast.43), custom_call_target="tpu_custom_call" | custom-call | flops 1 | bytes 1 | tf_op jit(solution)/shard_map/last_rows/pallas_call | solution.py:170
  1.7 1.6 %collective-permute-start = (bf16[128,1536]{1,0:T(8,128)(2,1)S(1)}, bf16[128,1536]{1,0:T(8,128)(2,1)S(1)}, u32[]{:S(2)}, u32[]{:S(2)}) collective-permute-start(bf16[128,1536]{1,0:T(8,128)(2,1)S(1)} %last_rows.1), channel_id=1, source_target_pairs={{0,1},{1,2},{2,3},{3,4},{4,5},{5,6},{6,7},{7,8},{8,9},{9,10},{10,1... | collective-permute-start | bytes 1179656 | tf_op jit(solution)/shard_map/ppermute | solution.py:31
  3.3 0.1 pad_add_fusion.1.places
  4.0 9.9 %front.1 = (bf16[256,2304]{1,0:T(8,128)(2,1)S(1)}, bf16[256,768]{1,0:T(8,128)(2,1)S(1)}, bf16[768,512]{1,0:T(8,128)(2,1)S(1)}, bf16[768,512]{1,0:T(8,128)(2,1)S(...) custom-call(s32[2]{0:T(128)S(1)} %pad_add_fusion.1.places, ...), custom_call_target="tpu_custom_call" | custom-call | flops 3623878656 | bytes 11796480 | tf_op jit(solution)/shard_map/front/pallas_call | solution.py:251
  13.9 0.1 collective-permute-start.2
  14.0 3.6 %collective-permute-done.frames_ref = bf16[128,1536]{1,0:T(8,128)(2,1)S(1)} collective-permute-done((bf16[128,1536]{1,0:T(8,128)(2,1)S(1)}, bf16[128,1536]{1,0:T(8,128)(2,1)S(1)}, u32[]{:S(2)}, u32[]{:S(2)}) %collective-permute-start) | collective-permute-done | bytes 393248 | tf_op jit(solution)/shard_map/ppermute | solution.py:31
  17.6 4.7 %attention_early.1 = (bf16[2,256,768]{2,1,0:T(8,128)(2,1)S(1)}, bf16[2,384,896]{2,1,0:T(8,128)(2,1)S(1)}, bf16[768,128]{1,0:T(8,128)(2,1)S(1)}) custom-call(s32[2]{0:T(128)S(1)} %pad_add_fusion.1.places, s32[1]{0:T(128)S(6)} %copy.9.lengths_ref, bf16[384,384]{1,0:T(8,128)(2,1)S(1)} %get-tuple-element.64.order_ref, ...), custom_call_target="tpu_custom_call" | custom-call | flops 704643072 | bytes 1572864 | tf_op jit(solution)/shard_map/attention_early/pallas_call | solution.py:367
  22.3 0.3 collective-permute-start.1
  22.6 2.0 %own_sums.1 = (f32[2,768,768]{2,1,0:T(8,128)S(1)}, f32[2,768,768]{2,1,0:T(8,128)S(1)}) custom-call(bf16[768,512]{1,0:T(8,128)(2,1)S(1)} %get-tuple-element.72.left_ref, bf16[768,128]{1,0:T(8,128)(2,1)S(1)} %get-tuple-element.73.behind_ref, bf16[2,256,768]{2,1,0:T(8,128)(2,1)S(1)} %get-tuple-element.70.first_ref, ...), custom_call_target="tpu_custom_call" | custom-call | flops 4000000000 | bytes 1 | tf_op jit(solution)/shard_map/own_sums/pallas_call | solution.py:407
  24.6 0.0 collective-permute-done.2.left_other_ref
  24.6 0.3 collective-permute-done.1.right_other_ref
  24.9 0.3 collective-permute-start.5
  25.2 0.1 slice_bitcast_fusion.2
  25.3 1.5 %first_wave.1 = (bf16[8,48,768]{2,1,0:T(8,128)(2,1)S(1)}, bf16[8,48,768]{2,1,0:T(8,128)(2,1)S(1)}, bf16[8,48,768]{2,1,0:T(8,128)(2,1)S(1)}, bf16[8,48,768]{2,1,0:T(8,128)(2,1)S(1)}) custom-call(s32[4,16]{1,0:T(4,128)S(1)} %pad_add_fusion.chunks, bf16[768,512]{1,0:T(8,128)(2,1)S(1)} %collective-permute-done.2.left_other_ref, ...), custom_call_target="tpu_custom_call" | custom-call | flops 1 | bytes 1 | tf_op jit(solution)/shard_map/first_wave/pallas_call | solution.py:438
  26.9 0.5 collective-permute-start.3
  27.4 2.4 %collective-permute-start.4 = (bf16[8,48,768]{2,1,0:T(8,128)(2,1)S(1)}, bf16[8,48,768]{2,1,0:T(8,128)(2,1)S(1)}, u32[]{:S(2)}, u32[]{:S(2)}) collective-permute-start(bf16[8,48,768]{2,1,0:T(8,128)(2,1)S(1)} %get-tuple-element.83), channel_id=1, source_target_pairs={{0,192},{1,193},{2,194},{3,195},{4,196},{5,197},{6,198},{7,199},{8... | collective-permute-start | bytes 1769480 | tf_op jit(solution)/shard_map/ppermute | solution.py:42
  29.8 0.1 slice_bitcast_fusion.1
  29.9 0.0 slice-start
  29.9 0.1 fusion.2
  30.0 0.0 slice-start.1
  30.0 2.1 %second_wave.1 = (bf16[8,48,768]{2,1,0:T(8,128)(2,1)S(1)}, bf16[8,48,768]{2,1,0:T(8,128)(2,1)S(1)}, bf16[8,48,768]{2,1,0:T(8,128)(2,1)S(1)}, bf16[8,48,768]{2,1,0:T(8,128)(2,1)S(1)}) custom-call(s32[4,16]{1,0:T(4,128)S(1)} %pad_add_fusion.chunks, bf16[768,512]{1,0:T(8,128)(2,1)S(1)} %collective-permute-done.2.left_other_ref, ...), custom_call_target="tpu_custom_call" | custom-call | flops 3000000000 | bytes 1 | tf_op jit(solution)/shard_map/second_wave/pallas_call | solution.py:438
  32.2 0.1 collective-permute-start.8
  32.3 3.3 %collective-permute-start.9 = (bf16[8,48,768]{2,1,0:T(8,128)(2,1)S(1)}, bf16[8,48,768]{2,1,0:T(8,128)(2,1)S(1)}, u32[]{:S(2)}, u32[]{:S(2)}) collective-permute-start(bf16[8,48,768]{2,1,0:T(8,128)(2,1)S(1)} %get-tuple-element.97), channel_id=1, source_target_pairs={{0,33},{1,32},{2,35},{3,34},{4,37},{5,36},{6,39},{7,38},{8,41},{9,... | collective-permute-start | bytes 1769480 | tf_op jit(solution)/shard_map/ppermute | solution.py:42
  35.6 2.9 %fusion.30 = f32[384,1536]{1,0:T(8,128)S(1)} fusion(bf16[384,2304]{1,0:T(8,128)(2,1)S(1)} %fusion.2, bf16[1536,2304]{1,0:T(8,128)(2,1)S(1)} %bitcast.52), kind=kOutput, calls=%fused_computation.76 | convolution fusion | flops 2717908992 | bytes 11206656 | tf_op jit(solution)/shard_map/dot_general | solution.py:26
  38.5 3.9 %collective-permute-done.3.refs_2_ = bf16[8,48,768]{2,1,0:T(8,128)(2,1)S(1)} collective-permute-done((bf16[8,48,768]{2,1,0:T(8,128)(2,1)S(1)}, bf16[8,48,768]{2,1,0:T(8,128)(2,1)S(1)}, u32[]{:S(2)}, u32[]{:S(2)}) %collective-permute-start.3) | collective-permute-done | bytes 589856 | tf_op jit(solution)/shard_map/ppermute | solution.py:42
  42.3 0.8 collective-permute-done.4.refs_3_
  43.2 0.3 halve.2
  43.5 0.0 copy-start.1
  43.5 1.8 %collective-permute-start.6 = (bf16[4,48,768]{2,1,0:T(8,128)(2,1)S(1)}, bf16[4,48,768]{2,1,0:T(8,128)(2,1)S(1)}, u32[]{:S(2)}, u32[]{:S(2)}) collective-permute-start(bf16[4,48,768]{2,1,0:T(8,128)(2,1)S(1)} %get-tuple-element.91), channel_id=1, source_target_pairs={{0,192},{1,193},{2,194},{3,195},{4,196},{5,197},{6,198},{7,199},{8... | collective-permute-start | bytes 884744 | tf_op jit(solution)/shard_map/ppermute | solution.py:42
  45.3 2.6 %collective-permute-start.7 = (bf16[4,48,768]{2,1,0:T(8,128)(2,1)S(1)}, bf16[4,48,768]{2,1,0:T(8,128)(2,1)S(1)}, u32[]{:S(2)}, u32[]{:S(2)}) collective-permute-start(bf16[4,48,768]{2,1,0:T(8,128)(2,1)S(1)} %get-tuple-element.92), channel_id=1, source_target_pairs={{0,64},{1,65},{2,66},{3,67},{4,68},{5,69},{6,70},{7,71},{8,72},{9,... | collective-permute-start | bytes 884744 | tf_op jit(solution)/shard_map/ppermute | solution.py:42
  47.9 0.6 collective-permute-done.9.refs_3_
  48.4 0.3 halve.3
  48.7 3.0 %collective-permute-start.10 = (bf16[4,48,768]{2,1,0:T(8,128)(2,1)S(1)}, bf16[4,48,768]{2,1,0:T(8,128)(2,1)S(1)}, u32[]{:S(2)}, u32[]{:S(2)}) collective-permute-start(bf16[4,48,768]{2,1,0:T(8,128)(2,1)S(1)} %get-tuple-element.104), channel_id=1, source_target_pairs={{0,33},{1,32},{2,35},{3,34},{4,37},{5,36},{6,39},{7,38},{8,41},{9,... | collective-permute-start | bytes 884744 | tf_op jit(solution)/shard_map/ppermute | solution.py:42
  51.7 0.0 collective-permute-start.11
  51.7 1.7 %convolution_convert_fusion = bf16[256,1536]{1,0:T(8,128)(2,1)} fusion(bf16[256,768]{1,0:T(8,128)(2,1)S(1)} %get-tuple-element.100, bf16[768,1536]{1,0:T(8,128)(2,1)S(1)} %copy-done.1), kind=kOutput, calls=%fused_computation.2 | convolution fusion | flops 604372992 | bytes 3538944 | tf_op jit(solution)/shard_map/dot_general | solution.py:26
  53.3 0.0 collective-permute-done.6
  53.4 0.4 collective-permute-done.7
  53.8 0.1 add_convert_fusion.1
  53.8 0.1 add_convert_fusion.2
  54.0 3.0 %collective-permute-start.13 = (bf16[48,1536]{1,0:T(8,128)(2,1)S(1)}, bf16[48,1536]{1,0:T(8,128)(2,1)S(1)}, u32[]{:S(2)}, u32[]{:S(2)}) collective-permute-start(bf16[48,1536]{1,0:T(8,128)(2,1)S(1)} %get-tuple-element.113), channel_id=1, source_target_pairs={{0,32},{1,33},{2,34},{3,35},{4,36},{5,37},{6,38},{7,39},{8,40},{9,... | collective-permute-start | bytes 442376 | tf_op jit(solution)/shard_map/ppermute | solution.py:42
  57.0 1.6 %collective-permute-start.14 = (bf16[48,1536]{1,0:T(8,128)(2,1)S(1)}, bf16[48,1536]{1,0:T(8,128)(2,1)S(1)}, u32[]{:S(2)}, u32[]{:S(2)}) collective-permute-start(bf16[48,1536]{1,0:T(8,128)(2,1)S(1)} %get-tuple-element.114), channel_id=1, source_target_pairs={{0,33},{1,32},{2,35},{3,34},{4,37},{5,36},{6,39},{7,38},{8,41},{9,... | collective-permute-start | bytes 442376 | tf_op jit(solution)/shard_map/ppermute | solution.py:42
  58.6 0.0 collective-permute-start.15
  58.6 0.3 collective-permute-done.10
  58.9 0.1 add_convert_fusion.4
  59.0 2.7 %collective-permute-done.11 = bf16[4,48,768]{2,1,0:T(8,128)(2,1)S(1)} collective-permute-done((bf16[4,48,768]{2,1,0:T(8,128)(2,1)S(1)}, bf16[4,48,768]{2,1,0:T(8,128)(2,1)S(1)}, u32[]{:S(2)}, u32[]{:S(2)}) %collective-permute-start.11) | collective-permute-done | bytes 294944 | tf_op jit(solution)/shard_map/ppermute | solution.py:42
  61.6 0.1 add_convert_fusion.3
  61.7 1.3 %collective-permute-start.16 = (bf16[48,1536]{1,0:T(8,128)(2,1)S(1)}, bf16[48,1536]{1,0:T(8,128)(2,1)S(1)}, u32[]{:S(2)}, u32[]{:S(2)}) collective-permute-start(bf16[48,1536]{1,0:T(8,128)(2,1)S(1)} %get-tuple-element.116), channel_id=1, source_target_pairs={{0,128},{1,129},{2,130},{3,131},{4,132},{5,133},{6,134},{7,135},{8... | collective-permute-start | bytes 442376 | tf_op jit(solution)/shard_map/ppermute | solution.py:42
  63.1 1.6 %collective-permute-start.17 = (bf16[48,1536]{1,0:T(8,128)(2,1)S(1)}, bf16[48,1536]{1,0:T(8,128)(2,1)S(1)}, u32[]{:S(2)}, u32[]{:S(2)}) collective-permute-start(bf16[48,1536]{1,0:T(8,128)(2,1)S(1)} %get-tuple-element.117), channel_id=1, source_target_pairs={{0,192},{1,193},{2,194},{3,195},{4,196},{5,197},{6,198},{7,199},{8... | collective-permute-start | bytes 442376 | tf_op jit(solution)/shard_map/ppermute | solution.py:42
  64.6 1.9 %collective-permute-start.18 = (bf16[48,1536]{1,0:T(8,128)(2,1)S(1)}, bf16[48,1536]{1,0:T(8,128)(2,1)S(1)}, u32[]{:S(2)}, u32[]{:S(2)}) collective-permute-start(bf16[48,1536]{1,0:T(8,128)(2,1)S(1)} %get-tuple-element.118), channel_id=1, source_target_pairs={{0,64},{1,65},{2,66},{3,67},{4,68},{5,69},{6,70},{7,71},{8,72},{9,... | collective-permute-start | bytes 442376 | tf_op jit(solution)/shard_map/ppermute | solution.py:42
  66.5 0.0 collective-permute-done.14
  66.5 0.0 collective-permute-done.15
  66.5 0.1 fusion.13.refs_0_
  66.6 0.0 copy-start
  66.6 0.8 slice.134
  67.4 1.5 %collective-permute-start.12 = (bf16[128,1536]{1,0:T(8,128)(2,1)}, bf16[128,1536]{1,0:T(8,128)(2,1)}, u32[]{:S(2)}, u32[]{:S(2)}) collective-permute-start(bf16[128,1536]{1,0:T(8,128)(2,1)} %slice.134), channel_id=1, source_target_pairs={{0,15},{1,0},{2,1},{3,2},{4,3},{5,4},{6,5},{7,6},{8,7},{9,8},{10,9... | collective-permute-start | bytes 1179656 | tf_op jit(solution)/shard_map/ppermute | solution.py:31
  68.9 0.8 collective-permute-done.17
  69.8 0.1 fusion.10.refs_1_
  69.9 0.8 pieces.1
  70.7 5.5 %all-to-all-start = ((bf16[8,144,128]{2,1,0:T(8,128)(2,1)}), bf16[8,144,128]{2,1,0:T(8,128)(2,1)S(1)}, u32[]{:S(2)}, u32[]{:S(2)}) async-start(bf16[8,144,128]{2,1,0:T(8,128)(2,1)} %pieces.1), calls=%async_computation | async-start | bytes 589824 | tf_op jit(solution)/shard_map/all_to_all | solution.py:568
  76.1 2.5 %collective-permute-done.12 = bf16[128,1536]{1,0:T(8,128)(2,1)} collective-permute-done((bf16[128,1536]{1,0:T(8,128)(2,1)}, bf16[128,1536]{1,0:T(8,128)(2,1)}, u32[]{:S(2)}, u32[]{:S(2)}) %collective-permute-start.12) | collective-permute-done | bytes 393248 | tf_op jit(solution)/shard_map/ppermute | solution.py:31
  78.6 1.5 %convert_reduce_fusion = (f32[256]{0:T(256)S(1)}, f32[256]{0:T(256)S(1)}, bf16[256,1536]{1,0:T(8,128)(2,1)S(1)}) fusion(f32[256]{0:T(256)S(1)} %bitcast.49, f32[256]{0:T(256)S(1)} %bitcast.47, bf16[256,1536]{1,0:T(8,128)(2,1)S(1)} %bitcast.45, bf16[128,1536]{1,0:T(8,128)(2,1)} %collective-permute-done.12, f32[384,1536]{1,0:T(8,128)S(1)} %fusion.30), kind=kLoop, calls=%fused_computation.5 | loop fusion | flops 3931648 | bytes 3543040 | tf_op jit(solution)/shard_map/reduce_sum | solution.py:118
  80.1 1.4 %fusion.7 = bf16[1,256,1536]{2,1,0:T(8,128)(2,1)} fusion(bf16[256,1536]{1,0:T(8,128)(2,1)S(1)} %bitcast.46, bf16[256,1536]{1,0:T(8,128)(2,1)S(1)} %get-tuple-element.121, f32[256]{0:T(256)S(1)} %broadcast_multiply_fusion, f32[256]{0:T(256)S(1)} %bitcast.48, f32[256]{0:T(256)S(1)} %broadcast_multiply_fusion.1, f32[256]{0:T(256)S(1)} %bitcast.50), kind=kLoop, calls=%fused_computation.14 | loop fusion | flops 3538944 | bytes 2363392 | tf_op jit(solution)/shard_map/broadcast_in_dim | solution.py:576
  81.5 5.5 %all-to-all-done.in_ref = bf16[8,144,128]{2,1,0:T(8,128)(2,1)S(1)} async-done(((bf16[8,144,128]{2,1,0:T(8,128)(2,1)}), bf16[8,144,128]{2,1,0:T(8,128)(2,1)S(1)}, u32[]{:S(2)}, u32[]{:S(2)}) %all-to-all-start) | async-done | bytes 294944 | tf_op jit(solution)/shard_map/all_to_all | solution.py:568
  87.0 0.7 total.1
  (18 shorter events, 0.1 us)
Async XLA Ops:
  1.7 16.0 %collective-permute-start = (bf16[128,1536]{1,0:T(8,128)(2,1)S(1)}, bf16[128,1536]{1,0:T(8,128)(2,1)S(1)}, u32[]{:S(2)}, u32[]{:S(2)}) collective-permute-start(bf16[128,1536]{1,0:T(8,128)(2,1)S(1)} %last_rows.1), channel_id=1, source_target_pairs={{0,1},{1,2},{2,3},{3,4},{4,5},{5,6},{6,7},{7,8},{8,9},{9,10},{10,1... | collective-permute-start | bytes 1179656 | tf_op jit(solution)/shard_map/ppermute | solution.py:31
  13.9 10.7 %collective-permute-start.2 = (bf16[768,512]{1,0:T(8,128)(2,1)S(1)}, bf16[768,512]{1,0:T(8,128)(2,1)S(1)}, u32[]{:S(2)}, u32[]{:S(2)}) collective-permute-start(bf16[768,512]{1,0:T(8,128)(2,1)S(1)} %get-tuple-element.71), channel_id=1, source_target_pairs={{0,16},{1,17},{2,18},{3,19},{4,20},{5,21},{6,22},{7,23},{8,24},{9,... | collective-permute-start | bytes 2359304 | tf_op jit(solution)/shard_map/ppermute | solution.py:42
  22.3 2.6 %collective-permute-start.1 = (bf16[2,256,768]{2,1,0:T(8,128)(2,1)S(1)}, bf16[2,256,768]{2,1,0:T(8,128)(2,1)S(1)}, u32[]{:S(2)}, u32[]{:S(2)}) collective-permute-start(bf16[2,256,768]{2,1,0:T(8,128)(2,1)S(1)} %get-tuple-element.70.first_ref), channel_id=1, source_target_pairs={{0,16},{1,17},{2,18},{3,19},{4,20},{5,21},{6,22},{7,23},{8,24},{9,... | collective-permute-start | bytes 2359304 | tf_op jit(solution)/shard_map/ppermute | solution.py:42
  24.9 5.1 %collective-permute-start.5 = (bf16[2,384,896]{2,1,0:T(8,128)(2,1)S(1)}, bf16[2,384,896]{2,1,0:T(8,128)(2,1)S(1)}, u32[]{:S(2)}, u32[]{:S(2)}) collective-permute-start(bf16[2,384,896]{2,1,0:T(8,128)(2,1)S(1)} %get-tuple-element.84.second_ref), channel_id=1, source_target_pairs={{0,16},{1,17},{2,18},{3,19},{4,20},{5,21},{6,22},{7,23},{8,24},{9,... | collective-permute-start | bytes 4128776 | tf_op jit(solution)/shard_map/ppermute | solution.py:42
  26.9 15.5 %collective-permute-start.3 = (bf16[8,48,768]{2,1,0:T(8,128)(2,1)S(1)}, bf16[8,48,768]{2,1,0:T(8,128)(2,1)S(1)}, u32[]{:S(2)}, u32[]{:S(2)}) collective-permute-start(bf16[8,48,768]{2,1,0:T(8,128)(2,1)S(1)} %get-tuple-element.82), channel_id=1, source_target_pairs={{0,64},{1,65},{2,66},{3,67},{4,68},{5,69},{6,70},{7,71},{8,72},{9,... | collective-permute-start | bytes 1769480 | tf_op jit(solution)/shard_map/ppermute | solution.py:42
  27.4 15.8 %collective-permute-start.4 = (bf16[8,48,768]{2,1,0:T(8,128)(2,1)S(1)}, bf16[8,48,768]{2,1,0:T(8,128)(2,1)S(1)}, u32[]{:S(2)}, u32[]{:S(2)}) collective-permute-start(bf16[8,48,768]{2,1,0:T(8,128)(2,1)S(1)} %get-tuple-element.83), channel_id=1, source_target_pairs={{0,192},{1,193},{2,194},{3,195},{4,196},{5,197},{6,198},{7,199},{8... | collective-permute-start | bytes 1769480 | tf_op jit(solution)/shard_map/ppermute | solution.py:42
  29.9 5.7 %slice-start = ((s8[7077888]{0:T(1024)(128)(4,1)}), s8[4194304]{0:T(1024)(128)(4,1)S(1)}, s32[]{:S(2)}) async-start(s8[7077888]{0:T(1024)(128)(4,1)} %bitcast.51), calls=%async_computation.1 | async-start | bytes 8388608
  30.0 5.5 %slice-start.1 = ((s8[7077888]{0:T(1024)(128)(4,1)}), s8[2883584]{0:T(1024)(128)(4,1)S(1)}, s32[]{:S(2)}) async-start(s8[7077888]{0:T(1024)(128)(4,1)} %bitcast.51), calls=%async_computation.2 | async-start | bytes 5767168
  32.2 15.7 %collective-permute-start.8 = (bf16[8,48,768]{2,1,0:T(8,128)(2,1)S(1)}, bf16[8,48,768]{2,1,0:T(8,128)(2,1)S(1)}, u32[]{:S(2)}, u32[]{:S(2)}) collective-permute-start(bf16[8,48,768]{2,1,0:T(8,128)(2,1)S(1)} %get-tuple-element.96), channel_id=1, source_target_pairs={{0,1},{1,0},{2,3},{3,2},{4,5},{5,4},{6,7},{7,6},{8,9},{9,8},{10,11... | collective-permute-start | bytes 1769480 | tf_op jit(solution)/shard_map/ppermute | solution.py:42
  32.3 16.1 %collective-permute-start.9 = (bf16[8,48,768]{2,1,0:T(8,128)(2,1)S(1)}, bf16[8,48,768]{2,1,0:T(8,128)(2,1)S(1)}, u32[]{:S(2)}, u32[]{:S(2)}) collective-permute-start(bf16[8,48,768]{2,1,0:T(8,128)(2,1)S(1)} %get-tuple-element.97), channel_id=1, source_target_pairs={{0,33},{1,32},{2,35},{3,34},{4,37},{5,36},{6,39},{7,38},{8,41},{9,... | collective-permute-start | bytes 1769480 | tf_op jit(solution)/shard_map/ppermute | solution.py:42
  43.5 8.2 %copy-start.1 = (bf16[768,1536]{1,0:T(8,128)(2,1)S(1)}, bf16[768,1536]{1,0:T(8,128)(2,1)}, u32[]{:S(2)}) copy-start(bf16[768,1536]{1,0:T(8,128)(2,1)} %out_ref.1) | copy-start | bytes 7077892
  43.5 9.9 %collective-permute-start.6 = (bf16[4,48,768]{2,1,0:T(8,128)(2,1)S(1)}, bf16[4,48,768]{2,1,0:T(8,128)(2,1)S(1)}, u32[]{:S(2)}, u32[]{:S(2)}) collective-permute-start(bf16[4,48,768]{2,1,0:T(8,128)(2,1)S(1)} %get-tuple-element.91), channel_id=1, source_target_pairs={{0,192},{1,193},{2,194},{3,195},{4,196},{5,197},{6,198},{7,199},{8... | collective-permute-start | bytes 884744 | tf_op jit(solution)/shard_map/ppermute | solution.py:42
  45.3 8.5 %collective-permute-start.7 = (bf16[4,48,768]{2,1,0:T(8,128)(2,1)S(1)}, bf16[4,48,768]{2,1,0:T(8,128)(2,1)S(1)}, u32[]{:S(2)}, u32[]{:S(2)}) collective-permute-start(bf16[4,48,768]{2,1,0:T(8,128)(2,1)S(1)} %get-tuple-element.92), channel_id=1, source_target_pairs={{0,64},{1,65},{2,66},{3,67},{4,68},{5,69},{6,70},{7,71},{8,72},{9,... | collective-permute-start | bytes 884744 | tf_op jit(solution)/shard_map/ppermute | solution.py:42
  48.7 10.2 %collective-permute-start.10 = (bf16[4,48,768]{2,1,0:T(8,128)(2,1)S(1)}, bf16[4,48,768]{2,1,0:T(8,128)(2,1)S(1)}, u32[]{:S(2)}, u32[]{:S(2)}) collective-permute-start(bf16[4,48,768]{2,1,0:T(8,128)(2,1)S(1)} %get-tuple-element.104), channel_id=1, source_target_pairs={{0,33},{1,32},{2,35},{3,34},{4,37},{5,36},{6,39},{7,38},{8,41},{9,... | collective-permute-start | bytes 884744 | tf_op jit(solution)/shard_map/ppermute | solution.py:42
  51.7 9.9 %collective-permute-start.11 = (bf16[4,48,768]{2,1,0:T(8,128)(2,1)S(1)}, bf16[4,48,768]{2,1,0:T(8,128)(2,1)S(1)}, u32[]{:S(2)}, u32[]{:S(2)}) collective-permute-start(bf16[4,48,768]{2,1,0:T(8,128)(2,1)S(1)} %get-tuple-element.106), channel_id=1, source_target_pairs={{0,1},{1,0},{2,3},{3,2},{4,5},{5,4},{6,7},{7,6},{8,9},{9,8},{10,11... | collective-permute-start | bytes 884744 | tf_op jit(solution)/shard_map/ppermute | solution.py:42
  54.0 10.7 %collective-permute-start.13 = (bf16[48,1536]{1,0:T(8,128)(2,1)S(1)}, bf16[48,1536]{1,0:T(8,128)(2,1)S(1)}, u32[]{:S(2)}, u32[]{:S(2)}) collective-permute-start(bf16[48,1536]{1,0:T(8,128)(2,1)S(1)} %get-tuple-element.113), channel_id=1, source_target_pairs={{0,32},{1,33},{2,34},{3,35},{4,36},{5,37},{6,38},{7,39},{8,40},{9,... | collective-permute-start | bytes 442376 | tf_op jit(solution)/shard_map/ppermute | solution.py:42
  57.0 9.5 %collective-permute-start.14 = (bf16[48,1536]{1,0:T(8,128)(2,1)S(1)}, bf16[48,1536]{1,0:T(8,128)(2,1)S(1)}, u32[]{:S(2)}, u32[]{:S(2)}) collective-permute-start(bf16[48,1536]{1,0:T(8,128)(2,1)S(1)} %get-tuple-element.114), channel_id=1, source_target_pairs={{0,33},{1,32},{2,35},{3,34},{4,37},{5,36},{6,39},{7,38},{8,41},{9,... | collective-permute-start | bytes 442376 | tf_op jit(solution)/shard_map/ppermute | solution.py:42
  58.6 8.0 %collective-permute-start.15 = (bf16[48,1536]{1,0:T(8,128)(2,1)S(1)}, bf16[48,1536]{1,0:T(8,128)(2,1)S(1)}, u32[]{:S(2)}, u32[]{:S(2)}) collective-permute-start(bf16[48,1536]{1,0:T(8,128)(2,1)S(1)} %get-tuple-element.115), channel_id=1, source_target_pairs={{0,1},{1,0},{2,3},{3,2},{4,5},{5,4},{6,7},{7,6},{8,9},{9,8},{10,11... | collective-permute-start | bytes 442376 | tf_op jit(solution)/shard_map/ppermute | solution.py:42
  61.7 7.2 %collective-permute-start.16 = (bf16[48,1536]{1,0:T(8,128)(2,1)S(1)}, bf16[48,1536]{1,0:T(8,128)(2,1)S(1)}, u32[]{:S(2)}, u32[]{:S(2)}) collective-permute-start(bf16[48,1536]{1,0:T(8,128)(2,1)S(1)} %get-tuple-element.116), channel_id=1, source_target_pairs={{0,128},{1,129},{2,130},{3,131},{4,132},{5,133},{6,134},{7,135},{8... | collective-permute-start | bytes 442376 | tf_op jit(solution)/shard_map/ppermute | solution.py:42
  63.1 6.7 %collective-permute-start.17 = (bf16[48,1536]{1,0:T(8,128)(2,1)S(1)}, bf16[48,1536]{1,0:T(8,128)(2,1)S(1)}, u32[]{:S(2)}, u32[]{:S(2)}) collective-permute-start(bf16[48,1536]{1,0:T(8,128)(2,1)S(1)} %get-tuple-element.117), channel_id=1, source_target_pairs={{0,192},{1,193},{2,194},{3,195},{4,196},{5,197},{6,198},{7,199},{8... | collective-permute-start | bytes 442376 | tf_op jit(solution)/shard_map/ppermute | solution.py:42
  64.6 5.1 %collective-permute-start.18 = (bf16[48,1536]{1,0:T(8,128)(2,1)S(1)}, bf16[48,1536]{1,0:T(8,128)(2,1)S(1)}, u32[]{:S(2)}, u32[]{:S(2)}) collective-permute-start(bf16[48,1536]{1,0:T(8,128)(2,1)S(1)} %get-tuple-element.118), channel_id=1, source_target_pairs={{0,64},{1,65},{2,66},{3,67},{4,68},{5,69},{6,70},{7,71},{8,72},{9,... | collective-permute-start | bytes 442376 | tf_op jit(solution)/shard_map/ppermute | solution.py:42
  66.6 12.0 %copy-start = (bf16[1,256,1536]{2,1,0:T(8,128)(2,1)S(1)}, bf16[1,256,1536]{2,1,0:T(8,128)(2,1)}, u32[]{:S(2)}) copy-start(bf16[1,256,1536]{2,1,0:T(8,128)(2,1)} %param.6) | copy-start | bytes 2359300
  67.4 11.2 %collective-permute-start.12 = (bf16[128,1536]{1,0:T(8,128)(2,1)}, bf16[128,1536]{1,0:T(8,128)(2,1)}, u32[]{:S(2)}, u32[]{:S(2)}) collective-permute-start(bf16[128,1536]{1,0:T(8,128)(2,1)} %slice.134), channel_id=1, source_target_pairs={{0,15},{1,0},{2,1},{3,2},{4,3},{5,4},{6,5},{7,6},{8,7},{9,8},{10,9... | collective-permute-start | bytes 1179656 | tf_op jit(solution)/shard_map/ppermute | solution.py:31
  70.7 16.3 %all-to-all-start = ((bf16[8,144,128]{2,1,0:T(8,128)(2,1)}), bf16[8,144,128]{2,1,0:T(8,128)(2,1)S(1)}, u32[]{:S(2)}, u32[]{:S(2)}) async-start(bf16[8,144,128]{2,1,0:T(8,128)(2,1)} %pieces.1), calls=%async_computation | async-start | bytes 589824 | tf_op jit(solution)/shard_map/all_to_all | solution.py:568
